TPU v7x, 32 devices: a whole 2x2x4 slice. The times are simulated.
32 devices in a mesh: pb: 8 (over y, x, core), kv: 4 (over z).
Axes of the slice: x: 2, y: 2, z: 4, core: 2. Of those that a mesh axis runs over, the one named last changes fastest.
Arguments:
- queries: float32 [4096, 256], P(('pb', 'kv')), may hold values from -200 to 200
- keys: float32 [4096, 256], P(('pb', 'kv')), may hold values from -8 to 8
- values: float32 [4096, 256], P(('pb', 'kv')), may hold values from -192 to 192
- query_tangent: float32 [4096, 256], P(('pb', 'kv')), may hold values from -6 to 6
- key_tangent: float32 [4096, 256], P(('pb', 'kv')), may hold values from -6 to 6
- value_tangent: float32 [4096, 256], P(('pb', 'kv')), may hold values from -192 to 192
Outputs:
- attended: float32 [4096, 256], P(('pb', 'kv'))
- attended_tangent: float32 [4096, 256], P(('pb', 'kv'))
All inputs are finite; a program needn't handle non-finite values.
Results may differ from a plain program's by a relative error of at most 0.0003.
Values sent between devices are 32-bit elements; how exact they have to be, the bound alone decides.
No kernel may reach another device: no remote copies, remote signals or barrier semaphores. Data moves between devices by JAX's collectives and lax.ppermute only.
A program may use at most 128 MiB of HBM per device.

v0:
```python
import math

import jax
import jax.numpy as jnp
from jax import lax
from jax.sharding import PartitionSpec as P

DH = 128


def cross(left, right):
    return lax.dot_general(
        left,
        right,
        (((1,), (1,)), ((), ())),
        precision=lax.Precision.HIGHEST,
        preferred_element_type=jnp.float32,
    )


def product(left, right):
    return jnp.dot(left, right, precision=lax.Precision.HIGHEST, preferred_element_type=jnp.float32)


def widen(factor):
    return jnp.repeat(factor, DH, axis=1)


def finish(total, total_t, numer, numer_t):
    attended = numer / widen(total)
    tangent = (numer_t - attended * widen(total_t)) / widen(total)
    return (attended, tangent)


def per_device(queries, keys, values, query_tangent, key_tangent, value_tangent):
    heads = queries.shape[1] // DH
    scale = 1.0 / math.sqrt(DH)
    block_q, block_dq = (
        lax.all_gather(queries, "kv", axis=0, tiled=True),
        lax.all_gather(query_tangent, "kv", axis=0, tiled=True),
    )
    q_count = block_q.shape[0]
    peak = jnp.full((q_count, heads), -1e30, jnp.float32)
    key_p = lax.all_gather(keys, "pb", axis=0, tiled=True)
    val_p = lax.all_gather(values, "pb", axis=0, tiled=True)
    dkey_p = lax.all_gather(key_tangent, "pb", axis=0, tiled=True)
    dval_p = lax.all_gather(value_tangent, "pb", axis=0, tiled=True)
    peaks = []
    totals = []
    totals_t = []
    numers = []
    numers_t = []
    for head in range(heads):
        cols = slice(head * DH, (head + 1) * DH)
        q_h = block_q[:, cols]
        k_h = key_p[:, cols]
        scores = cross(q_h, k_h) * scale
        score_t = (cross(block_dq[:, cols], k_h) + cross(q_h, dkey_p[:, cols])) * scale
        old = peak[:, head]
        fresh = jnp.maximum(old, jnp.max(scores, axis=1))
        expo = jnp.exp(scores - fresh[:, None])
        weighted = expo * score_t
        peaks.append(fresh)
        totals.append(jnp.sum(expo, axis=1))
        totals_t.append(jnp.sum(weighted, axis=1))
        numers.append(product(expo, val_p[:, cols]))
        numers_t.append(product(weighted, val_p[:, cols]) + product(expo, dval_p[:, cols]))
    peak = jnp.stack(peaks, axis=1)
    total = jnp.stack(totals, axis=1)
    total_t = jnp.stack(totals_t, axis=1)
    numer = jnp.concatenate(numers, axis=1)
    numer_t = jnp.concatenate(numers_t, axis=1)
    top = lax.pmax(peak, "kv")
    factor = jnp.exp(peak - top)
    wide = widen(factor)
    own = (
        lax.psum_scatter(factor * total, "kv", scatter_dimension=0, tiled=True),
        lax.psum_scatter(factor * total_t, "kv", scatter_dimension=0, tiled=True),
        lax.psum_scatter(wide * numer, "kv", scatter_dimension=0, tiled=True),
        lax.psum_scatter(wide * numer_t, "kv", scatter_dimension=0, tiled=True),
    )
    return finish(own[0], own[1], own[2], own[3])


def solution(mesh):
    in_specs = (
        P(("pb", "kv"), None),
        P(("pb", "kv"), None),
        P(("pb", "kv"), None),
        P(("pb", "kv"), None),
        P(("pb", "kv"), None),
        P(("pb", "kv"), None),
    )
    out_specs = (P(("pb", "kv"), None), P(("pb", "kv"), None))
    return jax.shard_map(
        per_device, mesh=mesh, in_specs=in_specs, out_specs=out_specs, check_vma=False
    )
```

profile of v0, /device:TPU:0, one launch (start us, length us, event | category | flops | bytes accessed | tf_op | source)
XLA Modules:
  0.0 207.9 jit_solution(16006234253488915892)
XLA Ops:
  7.9 0.7 all-gather.9.cloned.1.call-update
  10.0 17.6 %all_gather.21 = f32[512,256]{1,0:T(8,128)S(1)} all-gather(f32[128,256]{1,0:T(8,128)} %param.9), channel_id=1, replica_groups=mesh['pb'=8,'kv'=4] {'kv'}, dimensions={0}, use_global_device_ids=true | all-gather | bytes 655360 | tf_op jit(solution)/shard_map/all_gather | solution.py:40
  27.6 16.6 %all_gather.18 = f32[512,256]{1,0:T(8,128)S(1)} all-gather(f32[128,256]{1,0:T(8,128)} %param.6), channel_id=1, replica_groups=mesh['pb'=8,'kv'=4] {'kv'}, dimensions={0}, use_global_device_ids=true | all-gather | bytes 655360 | tf_op jit(solution)/shard_map/all_gather | solution.py:39
  44.1 4.4 %multiply_reduce_fusion = (f32[512]{0:T(512)S(1)}, f32[512,1024]{1,0:T(8,128)}) fusion(f32[1024,256]{1,0:T(8,128)} %all-gather.5.cloned.1.call-done, f32[512,256]{1,0:T(8,128)S(1)} %all_gather.18), kind=kOutput, calls=%fused_computation.4 | convolution fusion | flops 806354432 | bytes 2885632 | tf_op jit(solution)/shard_map/dot_general | solution.py:12
  48.5 1.9 multiply_reduce_fusion.1
  50.5 11.3 %pmax.7 = f32[512,2]{0,1:T(2,128)S(1)} all-reduce(f32[512,2]{0,1:T(2,128)S(1)} %pad_maximum_fusion), channel_id=1, replica_groups=mesh['pb'=8,'kv'=4] {'kv'}, use_global_device_ids=true, to_apply=%region_2.0 | all-reduce | flops 1024 | bytes 8192 | tf_op jit(solution)/shard_map/pmax | solution.py:73
  61.8 4.3 %fusion.12 = f32[512,1024]{1,0:T(8,128)} fusion(f32[1024,256]{1,0:T(8,128)} %all-gather.5.cloned.1.call-done, f32[512,256]{1,0:T(8,128)S(1)} %all_gather.21), kind=kOutput, calls=%fused_computation.22 | convolution fusion | flops 805306368 | bytes 2883584 | tf_op jit(solution)/shard_map/dot_general | solution.py:12
  66.0 3.1 %fusion.16 = f32[512,1024]{1,0:T(8,128)} fusion(f32[1024,256]{1,0:T(8,128)S(1)} %copy-done.5, f32[512,256]{1,0:T(8,128)S(1)} %all_gather.21), kind=kOutput, calls=%fused_computation.26 | convolution fusion | flops 805306368 | bytes 2883584 | tf_op jit(solution)/shard_map/dot_general | solution.py:12
  69.1 6.2 %fusion.29 = (f32[512]{0:T(512)S(1)}, f32[512,1024]{1,0:T(8,128)}) fusion(f32[512,1024]{1,0:T(8,128)} %fusion.12, f32[1024,256]{1,0:T(8,128)} %all-gather.9.cloned.1.call-done, f32[512,256]{1,0:T(8,128)S(1)} %all_gather.18, f32[512]{0:T(512)S(1)} %broadcast_maximum_fusion, f32[512,1024]{1,0:T(8,128)} %get-tuple-element.13), kind=kOutput, calls=%fused_computation.48 | convolution fusion | flops 808451584 | bytes 7081984 | tf_op jit(solution)/shard_map/dot_general | solution.py:12
  75.3 3.6 %fusion.30 = (f32[512]{0:T(512)S(1)}, f32[512,1024]{1,0:T(8,128)}) fusion(f32[512,1024]{1,0:T(8,128)S(1)} %copy-done.2, f32[1024,256]{1,0:T(8,128)S(1)} %copy-done.6, f32[512,256]{1,0:T(8,128)S(1)} %all_gather.18, f32[512]{0:T(512)S(1)} %broadcast_maximum_fusion.1, f32[512,1024]{1,0:T(8,128)S(1)} %get-tuple-element.15), kind=kOutput, calls=%fused_computation.49 | convolution fusion | flops 808451584 | bytes 7081984 | tf_op jit(solution)/shard_map/dot_general | solution.py:12
  78.9 0.9 copy.14
  79.8 2.6 %fusion.27 = (f32[512]{0:T(512)S(1)}, f32[512]{0:T(512)S(1)}) fusion(f32[512]{0:T(512)S(1)} %broadcast_maximum_fusion.1, f32[512,1024]{1,0:T(8,128)S(1)} %get-tuple-element.15, f32[512]{0:T(512)S(1)} %broadcast_maximum_fusion, f32[512,1024]{1,0:T(8,128)} %get-tuple-element.13), kind=kLoop, calls=%fused_computation.46 | loop fusion | flops 3144704 | bytes 4202496 | tf_op jit(solution)/shard_map/reduce_sum | solution.py:64
  82.5 0.9 copy.12
  83.7 3.3 %all-gather.7.cloned.1.call-done = f32[1024,256]{1,0:T(8,128)} async-done(((f32[128,256]{1,0:T(8,128)}), f32[1024,256]{1,0:T(8,128)}) %all-gather.7.cloned.1.call-update) | async-done | bytes 1048592 | tf_op jit(solution)/shard_map/all_gather | solution.py:45
  87.0 4.5 %fusion.6 = f32[512,128]{0,1:T(8,128)S(1)} fusion(f32[1024,256]{1,0:T(8,128)} %all-gather.7.cloned.1.call-done, f32[512,1024]{1,0:T(8,128)} %get-tuple-element.13, f32[512]{0:T(512)S(1)} %broadcast_maximum_fusion), kind=kOutput, calls=%fused_computation.16 | convolution fusion | flops 806354944 | bytes 2885632 | tf_op jit(solution)/shard_map/dot_general | solution.py:22
  91.5 4.2 %fusion.4 = f32[512,128]{0,1:T(8,128)} fusion(f32[512,1024]{1,0:T(8,128)S(1)} %copy-done, f32[1024,256]{1,0:T(8,128)} %all-gather.7.cloned.1.call-done), kind=kOutput, calls=%fused_computation.14 | convolution fusion | flops 805306368 | bytes 2883584 | tf_op jit(solution)/shard_map/dot_general | solution.py:22
  95.7 3.0 %fusion.8 = f32[512,128]{0,1:T(8,128)} fusion(f32[512,1024]{1,0:T(8,128)S(1)} %copy-done.1, f32[1024,256]{1,0:T(8,128)S(1)} %copy-done.3), kind=kOutput, calls=%fused_computation.18 | convolution fusion | flops 805306368 | bytes 2883584 | tf_op jit(solution)/shard_map/dot_general | solution.py:22
  98.6 13.6 %all-gather.11.cloned.1.call-done = f32[1024,256]{1,0:T(8,128)} async-done(((f32[128,256]{1,0:T(8,128)}), f32[1024,256]{1,0:T(8,128)}) %all-gather.11.cloned.1.call-update) | async-done | bytes 1048592 | tf_op jit(solution)/shard_map/all_gather | solution.py:47
  112.2 4.5 %convolution_add_fusion = f32[512,128]{0,1:T(8,128)S(1)} fusion(f32[512,128]{0,1:T(8,128)} %fusion.4, f32[1024,256]{1,0:T(8,128)} %all-gather.11.cloned.1.call-done, f32[512,1024]{1,0:T(8,128)} %get-tuple-element.13, f32[512]{0:T(512)S(1)} %broadcast_maximum_fusion), kind=kOutput, calls=%fused_computation.6 | convolution fusion | flops 806420480 | bytes 3147776 | tf_op jit(solution)/shard_map/dot_general | solution.py:22
  116.8 2.7 %convolution_add_fusion.1 = f32[512,128]{0,1:T(8,128)S(1)} fusion(f32[512,128]{0,1:T(8,128)S(1)} %copy-done.8, f32[1024,256]{1,0:T(8,128)S(1)} %copy-done.7, f32[512,1024]{1,0:T(8,128)S(1)} %get-tuple-element.15, f32[512]{0:T(512)S(1)} %broadcast_maximum_fusion.1), kind=kOutput, calls=%fused_computation.7 | convolution fusion | flops 806420480 | bytes 3147776 | tf_op jit(solution)/shard_map/dot_general | solution.py:22
  119.4 2.7 %fusion.10 = f32[512,128]{0,1:T(8,128)S(1)} fusion(f32[1024,256]{1,0:T(8,128)S(1)} %copy-done.3, f32[512,1024]{1,0:T(8,128)S(1)} %get-tuple-element.15, f32[512]{0:T(512)S(1)} %broadcast_maximum_fusion.1), kind=kOutput, calls=%fused_computation.20 | convolution fusion | flops 806354944 | bytes 2885632 | tf_op jit(solution)/shard_map/dot_general | solution.py:22
  122.1 1.1 bitcast_multiply_fusion
  123.3 0.7 reduce-scatter.9.cloned.1.call-update
  124.0 10.1 %reduce-scatter.15.cloned.1.call-done = f32[128,2]{1,0:T(8,128)} async-done(((f32[512,2]{1,0:T(8,128)}), f32[128,2]{1,0:T(8,128)}) %reduce-scatter.15.cloned.1.call-update) | async-done | bytes 1040
  134.1 0.9 copy.15
  135.0 19.1 %reduce-scatter.13.cloned.1.call-done = f32[128,2]{1,0:T(8,128)} async-done(((f32[512,2]{1,0:T(8,128)}), f32[128,2]{1,0:T(8,128)}) %reduce-scatter.13.cloned.1.call-update) | async-done | bytes 1040
  154.1 0.9 copy.13
  155.0 21.4 %reduce-scatter.11.cloned.1.call-done = f32[128,256]{0,1:T(8,128)} async-done(((f32[512,256]{0,1:T(8,128)}), f32[128,256]{0,1:T(8,128)}) %reduce-scatter.11.cloned.1.call-update) | async-done | bytes 131088 | tf_op jit(solution)/shard_map/reduce_scatter | solution.py:80
  176.3 22.2 %reduce-scatter.9.cloned.1.call-done = f32[128,256]{0,1:T(8,128)} async-done(((f32[512,256]{0,1:T(8,128)}), f32[128,256]{0,1:T(8,128)}) %reduce-scatter.9.cloned.1.call-update) | async-done | bytes 131088 | tf_op jit(solution)/shard_map/reduce_scatter | solution.py:79
  198.5 1.0 bitcast_divide_fusion
  199.5 0.8 copy.10
  200.3 0.8 copy.11
  (39 shorter events, 2.6 us)
Async XLA Ops:
  7.2 37.0 %all-gather.5.cloned.1.call-start = ((), (), s32[]{:S(2)}) async-start(), calls=%async_computation.4 | async-start | bytes 1179648 | tf_op jit(solution)/shard_map/all_gather | solution.py:44
  7.9 61.2 %all-gather.9.cloned.1.call-start = ((), (), s32[]{:S(2)}) async-start(), calls=%async_computation.7 | async-start | bytes 1179648 | tf_op jit(solution)/shard_map/all_gather | solution.py:46
  8.6 78.3 %all-gather.7.cloned.1.call-start = ((), (), s32[]{:S(2)}) async-start(), calls=%async_computation.5 | async-start | bytes 1179648 | tf_op jit(solution)/shard_map/all_gather | solution.py:45
  9.4 102.9 %all-gather.11.cloned.1.call-start = ((), (), s32[]{:S(2)}) async-start(), calls=%async_computation.8 | async-start | bytes 1179648 | tf_op jit(solution)/shard_map/all_gather | solution.py:47
  10.0 124.1 %reduce-scatter.15.cloned.1.call-start = ((), (), s32[]{:S(2)}) async-start(), calls=%async_computation.11 | async-start | bytes 327680
  44.1 4.4 %copy-start.4 = (f32[1024,256]{1,0:T(8,128)S(1)}, f32[1024,256]{1,0:T(8,128)}, u32[]{:S(2)}) copy-start(f32[1024,256]{1,0:T(8,128)} %all-gather.5.cloned.1.call-done) | copy-start | bytes 3145732
  61.8 4.3 %copy-start.5 = (f32[1024,256]{1,0:T(8,128)S(1)}, f32[1024,256]{1,0:T(8,128)}, u32[]{:S(2)}) copy-start(f32[1024,256]{1,0:T(8,128)} %all-gather.5.cloned.1.call-done) | copy-start | bytes 3145732
  69.1 6.2 %copy-start.2 = (f32[512,1024]{1,0:T(8,128)S(1)}, f32[512,1024]{1,0:T(8,128)}, u32[]{:S(2)}) copy-start(f32[512,1024]{1,0:T(8,128)} %fusion.16) | copy-start | bytes 6291460
  69.1 6.2 %copy-start.6 = (f32[1024,256]{1,0:T(8,128)S(1)}, f32[1024,256]{1,0:T(8,128)}, u32[]{:S(2)}) copy-start(f32[1024,256]{1,0:T(8,128)} %all-gather.9.cloned.1.call-done) | copy-start | bytes 3145732
  82.4 71.6 %reduce-scatter.13.cloned.1.call-start = ((), (), s32[]{:S(2)}) async-start(), calls=%async_computation.10 | async-start | bytes 327680
  83.4 92.9 %reduce-scatter.11.cloned.1.call-start = ((), (), s32[]{:S(2)}) async-start(), calls=%async_computation.9 | async-start | bytes 655360 | tf_op jit(solution)/shard_map/reduce_scatter | solution.py:80
  87.0 4.5 %copy-start = (f32[512,1024]{1,0:T(8,128)S(1)}, f32[512,1024]{1,0:T(8,128)}, u32[]{:S(2)}) copy-start(f32[512,1024]{1,0:T(8,128)} %get-tuple-element.17) | copy-start | bytes 6291460
  87.0 8.7 %copy-start.3 = (f32[1024,256]{1,0:T(8,128)S(1)}, f32[1024,256]{1,0:T(8,128)}, u32[]{:S(2)}) copy-start(f32[1024,256]{1,0:T(8,128)} %all-gather.7.cloned.1.call-done) | copy-start | bytes 3145732
  91.5 4.2 %copy-start.1 = (f32[512,1024]{1,0:T(8,128)S(1)}, f32[512,1024]{1,0:T(8,128)}, u32[]{:S(2)}) copy-start(f32[512,1024]{1,0:T(8,128)} %get-tuple-element.19) | copy-start | bytes 6291460
  112.2 4.5 %copy-start.7 = (f32[1024,256]{1,0:T(8,128)S(1)}, f32[1024,256]{1,0:T(8,128)}, u32[]{:S(2)}) copy-start(f32[1024,256]{1,0:T(8,128)} %all-gather.11.cloned.1.call-done) | copy-start | bytes 3145732
  112.2 4.5 %copy-start.8 = (f32[512,128]{0,1:T(8,128)S(1)}, f32[512,128]{0,1:T(8,128)}, u32[]{:S(2)}) copy-start(f32[512,128]{0,1:T(8,128)} %fusion.8) | copy-start | bytes 786436
  123.2 75.3 %reduce-scatter.9.cloned.1.call-start = ((), (), s32[]{:S(2)}) async-start(), calls=%async_computation.6 | async-start | bytes 655360 | tf_op jit(solution)/shard_map/reduce_scatter | solution.py:79
Sparse Core Ops, SparseCore 0:
  9.9 26.1 all-gather.4
  38.0 23.5 all-gather.8
  63.5 23.4 all-gather.6
  88.7 23.4 all-gather.10
  114.3 19.6 reduce-scatter.14
  136.3 17.7 reduce-scatter.12
  156.4 19.9 reduce-scatter.10
  178.6 19.8 reduce-scatter.8
where the time goes:
time: 208 us
  waiting for transfers between devices  93 us (45%)
  blocking collectives  45.4 us (22%)
  matrix products  44.9 us (22%)
  between operations  14.2 us (7%)
  local copies, waits for them, and re-layouts  5.09 us (2%)
  other arithmetic  4.74 us (2%)
    unnamed x10, waiting for transfers between devices  32.5 us
    dot_general x6, matrix products, cross(): lax.dot_general(left, right, (((1,), (1,)), ((), ())), precision=lax.Prec...  23.4 us
    reduce_scatter x1, waiting for transfers between devices, per_device(): lax.psum_scatter(wide * numer, 'kv', scatter_dimension=0, tiled=True)  22.2 us
    dot_general x6, matrix products, product(): jnp.dot(left, right, precision=lax.Precision.HIGHEST, preferred_element_t...  21.4 us
    reduce_scatter x1, waiting for transfers between devices, per_device(): lax.psum_scatter(wide * numer_t, 'kv', scatter_dimension=0, tiled=True)  21.4 us
    all_gather x1, blocking collectives, per_device(): lax.all_gather(query_tangent, 'kv', axis=0, tiled=True)  17.6 us
    all_gather x1, blocking collectives, per_device(): lax.all_gather(queries, 'kv', axis=0, tiled=True)  16.6 us
    all_gather x1, waiting for transfers between devices, per_device(): dval_p = lax.all_gather(value_tangent, 'pb', axis=0, tiled=True)  13.6 us
  transfers between devices with their start and end apart: 8, of which 6 were waited for; matrix products, arithmetic and copies ran while one was open for 25% of the time, Pallas kernels for 0%

commit v1 on v0

v1 whole, which is shorter than its diff:
```python
import functools
import math

import jax
import jax.numpy as jnp
from jax import lax
from jax.experimental import pallas as pl
from jax.experimental.pallas import tpu as pltpu
from jax.sharding import PartitionSpec as P

DH = 128
LOG2E = 1.4426950408889634
STAT_ROWS = 8
AXES = ("pb", "kv")
PARAMS = pltpu.CompilerParams(vmem_limit_bytes=56 * 1024 * 1024)


def split2(x):
    high = x.astype(jnp.bfloat16)
    return high, (x - high.astype(jnp.float32)).astype(jnp.bfloat16)


def split3(x):
    high = x.astype(jnp.bfloat16)
    rest = x - high.astype(jnp.float32)
    mid = rest.astype(jnp.bfloat16)
    return high, mid, (rest - mid.astype(jnp.float32)).astype(jnp.bfloat16)


def dot_nt(left, right):
    return lax.dot_general(
        left, right, (((1,), (1,)), ((), ())), preferred_element_type=jnp.float32
    )


def dot_nn(left, right):
    return jnp.dot(left, right, preferred_element_type=jnp.float32)


def f32(*shape):
    return jax.ShapeDtypeStruct(shape, jnp.float32)


def give_kernel(core_ref, *refs):
    *ins, out = refs
    column = pl.multiple_of((1 - core_ref[0]) * DH, DH)
    for i, ref in enumerate(ins):
        out[:, i * DH : (i + 1) * DH] = ref[:, pl.ds(column, DH)]


def join_kernel(core_ref, *refs):
    *ins, got, out_q, out_k = refs
    rows = got.shape[0]
    column = pl.multiple_of(core_ref[0] * DH, DH)
    for i, ref in enumerate(ins):
        out, at = (out_q, i) if i < 2 else (out_k, i - 2)
        out[0:rows, at * DH : (at + 1) * DH] = ref[:, pl.ds(column, DH)]
    out_q[rows:, :] = got[:, 0 : 2 * DH]
    out_k[rows:, :] = got[:, 2 * DH :]


def attend_kernel(n_q, n_k, rows, has_prev, last, *refs):
    refs = list(refs)

    def take(count):
        head, refs[:] = refs[:count], refs[count:]
        return head

    q_refs, k_refs = take(n_q), take(n_k)
    prev = take(2 * n_q) if has_prev else None
    outs = take(n_q if last else 2 * n_q)
    ka, kb, va, vb, vc = refs
    scale = 1.0 / math.sqrt(DH)
    for b, ref in enumerate(k_refs):
        at = slice(b * rows, (b + 1) * rows)
        k1, k2, k3 = split3(ref[:, 0:DH])
        d1, d2 = split2(ref[:, DH : 2 * DH])
        v1, v2 = split2(ref[:, 2 * DH : 3 * DH])
        w1, w2 = split2(ref[:, 3 * DH : 4 * DH])
        ka[at, :] = jnp.concatenate([k1, k2, k1, k3, k1, k2], axis=1)
        kb[at, :] = jnp.concatenate([k1, d1, k2, d2, k1, d1], axis=1)
        va[at, :] = jnp.concatenate([v1, w1], axis=1)
        vb[at, :] = jnp.concatenate([v2, w2], axis=1)
        vc[at, :] = jnp.concatenate([v1, v2], axis=1)
    lane = lax.broadcasted_iota(jnp.int32, (rows, DH), 1)
    for b, ref in enumerate(q_refs):
        q = ref[:, 0:DH]
        a1, a2, a3 = split3(q * (scale * LOG2E))
        q1, q2 = split2(q * scale)
        d1, d2 = split2(ref[:, DH : 2 * DH] * scale)
        s = dot_nt(jnp.concatenate([a1, a1, a2, a1, a3, a2], axis=1), ka[...])
        st = dot_nt(jnp.concatenate([d1, q1, d1, q1, d2, q2], axis=1), kb[...])
        peak = jnp.max(s, axis=1, keepdims=True)
        if has_prev:
            old = prev[2 * b + 1][:, 0:3]
            peak = jnp.maximum(peak, old[:, 0:1])
        e = jnp.exp2(s - peak)
        w = e * st
        total = jnp.sum(e, axis=1, keepdims=True)
        total_t = jnp.sum(w, axis=1, keepdims=True)
        e1, e2 = split2(e)
        w1, w2 = split2(w)
        both = dot_nn(e1, va[...]) + dot_nn(e1, vb[...]) + dot_nn(e2, va[...])
        first = dot_nn(w1, vc[...])
        numer = both[:, :DH]
        numer_t = both[:, DH:] + first[:, :DH] + first[:, DH:] + dot_nn(w2, vc[:, :DH])
        if has_prev:
            factor = jnp.exp2(old[:, 0:1] - peak)
            total += factor * old[:, 1:2]
            total_t += factor * old[:, 2:3]
            numer += factor * prev[2 * b][:, :DH]
            numer_t += factor * prev[2 * b][:, DH:]
        stats = jnp.where(lane == 0, peak, jnp.where(lane == 1, total, total_t))
        if last:
            outs[b][0:rows, :DH] = numer
            outs[b][0:rows, DH:] = numer_t
            outs[b][rows:, :] = stats.T[0:STAT_ROWS, :]
        else:
            outs[2 * b][:, :DH] = numer
            outs[2 * b][:, DH:] = numer_t
            outs[2 * b + 1][...] = stats


def attend(q_blocks, k_blocks, prev, last):
    n_q, n_k, rows = len(q_blocks), len(k_blocks), q_blocks[0].shape[0]
    assert rows == 2 * DH
    keys = n_k * rows
    if last:
        shapes = [f32(rows + STAT_ROWS, 2 * DH)] * n_q
    else:
        shapes = [f32(rows, 2 * DH), f32(rows, DH)] * n_q
    work = n_q * rows * keys
    return pl.pallas_call(
        functools.partial(attend_kernel, n_q, n_k, rows, bool(prev), last),
        out_shape=shapes,
        scratch_shapes=[pltpu.VMEM((keys, w * DH), jnp.bfloat16) for w in (6, 6, 2, 2, 2)],
        compiler_params=PARAMS,
        cost_estimate=pl.CostEstimate(
            flops=work * 2 * 256 * 18, transcendentals=work, bytes_accessed=n_q * rows * 4096 + keys * 2048
        ),
    )(*q_blocks, *k_blocks, *prev)


def finish_kernel(n_q, rows, *refs):
    part_refs = refs[:n_q]
    keep, give = refs[n_q:]
    half = rows // 2
    wides = [
        jnp.concatenate(
            [ref[rows:, :], jnp.zeros((DH - STAT_ROWS, rows), jnp.float32)], axis=0
        ).T
        for ref in part_refs
    ]
    peaks = [wide[:, 0:1] for wide in wides]
    top = functools.reduce(jnp.maximum, peaks)
    total = total_t = numer = numer_t = 0.0
    for ref, wide, peak in zip(part_refs, wides, peaks):
        factor = jnp.exp2(peak - top)
        total += factor * wide[:, 1:2]
        total_t += factor * wide[:, 2:3]
        numer += factor * ref[0:rows, :DH]
        numer_t += factor * ref[0:rows, DH:]
    attended = numer / total
    tangent = (numer_t - attended * total_t) / total
    for ref, at in ((keep, slice(0, half)), (give, slice(half, rows))):
        ref[:, :DH] = attended[at]
        ref[:, DH:] = tangent[at]


def place_kernel(core_ref, keep, got, out, tan):
    for ref, core in ((keep, core_ref[0]), (got, 1 - core_ref[0])):
        column = pl.multiple_of(core * DH, DH)
        out[:, pl.ds(column, DH)] = ref[:, :DH]
        tan[:, pl.ds(column, DH)] = ref[:, DH:]


def bits_of(n_pb, n_kv):
    low = n_kv.bit_length() - 1
    far = [1 << i for i in range(low)]
    near = [1 << (low + i) for i in range(1, n_pb.bit_length() - 1)]
    one = far[0::2] + near[1::2]
    two = far[1::2] + near[0::2]
    return ((one, two), (two, one)) if len(one) == len(two) else ((one, one), (two, two))


def per_device(n_pb, n_kv, *arrays):
    rows, width = arrays[0].shape
    assert width == 2 * DH and n_pb & (n_pb - 1) == 0 and n_kv & (n_kv - 1) == 0
    q_bits, k_bits = bits_of(n_pb, n_kv)
    core = (lax.axis_index("pb") % 2).astype(jnp.int32).reshape(1)

    def swap(x, masks):
        return lax.ppermute(
            x, AXES, [(i, i ^ masks[i // n_kv % 2]) for i in range(n_pb * n_kv)]
        )

    smem = pl.BlockSpec(memory_space=pltpu.SMEM)
    vmem = pl.BlockSpec(memory_space=pltpu.VMEM)
    order = (0, 3, 1, 4, 2, 5)
    arrays = [arrays[i] for i in order]
    give = pl.pallas_call(
        give_kernel,
        out_shape=f32(rows, 6 * DH),
        in_specs=[smem] + [vmem] * 6,
        compiler_params=PARAMS,
    )(core, *arrays)
    got = swap(give, (n_kv, n_kv))
    mine_q, mine_k = pl.pallas_call(
        join_kernel,
        out_shape=[f32(2 * rows, 2 * DH), f32(2 * rows, 4 * DH)],
        in_specs=[smem] + [vmem] * 7,
        compiler_params=PARAMS,
    )(core, *arrays, got)

    q_blocks, k_blocks = [mine_q], [mine_k]
    for one, two in zip(*k_bits):
        k_blocks += [swap(x, (one, two)) for x in k_blocks]
    for one, two in zip(*q_bits):
        q_blocks += [swap(x, (one, two)) for x in q_blocks]
    n_q = len(q_blocks)
    states = attend(q_blocks, k_blocks[0::2], [], False)
    parts = [None] * n_q
    for start in (1, 0):
        which = list(range(start, n_q, 2))
        prev = [states[2 * b + i] for b in which for i in range(2)]
        for b, part in zip(which, attend([q_blocks[b] for b in which], k_blocks[1::2], prev, True)):
            parts[b] = part

    def mask(bits, index):
        return sum(bit for i, bit in enumerate(bits) if index >> i & 1)

    back = [parts[0]] + [
        swap(parts[b], (mask(q_bits[0], b), mask(q_bits[1], b))) for b in range(n_q - 1, 0, -1)
    ]
    keep, give = pl.pallas_call(
        functools.partial(finish_kernel, n_q, 2 * rows),
        out_shape=[f32(rows, 2 * DH)] * 2,
        compiler_params=PARAMS,
    )(*back)
    got = swap(give, (n_kv, n_kv))
    return tuple(
        pl.pallas_call(
            place_kernel,
            out_shape=[f32(rows, width)] * 2,
            in_specs=[smem, vmem, vmem],
            compiler_params=PARAMS,
        )(core, keep, got)
    )


def solution(mesh):
    spec = P(AXES, None)
    body = functools.partial(per_device, mesh.shape["pb"], mesh.shape["kv"])
    return jax.shard_map(body, mesh=mesh, in_specs=(spec,) * 6, out_specs=(spec,) * 2, check_vma=False)
```

time: 208 us -> 71.8 us (0.35)
  waiting for transfers between devices: 93 us -> 27 us
  blocking collectives: 45.4 us -> 0 us
  matrix products: 44.9 us -> 0 us
  Pallas kernels: 0 us -> 23.6 us
  starting transfers between devices: 0.54 us -> 15.9 us
  between operations: 14.2 us -> 0.69 us
  other arithmetic: 4.74 us -> 0 us
    dot_general x12 -> x0, matrix products: 44.9 us -> none  [the longest x6 23.4 us: cross(): lax.dot_general(left, right, (((1,), (1,)), ((), ())), precision=lax.Prec...]
    reduce_scatter x2 -> x0, waiting for transfers between devices: 43.5 us -> none  [the longest x1 22.2 us: per_device(): lax.psum_scatter(wide * numer, 'kv', scatter_dimension=0, tiled=True)]
    all_gather x2 -> x0, blocking collectives: 34.1 us -> none  [the longest x1 17.6 us: per_device(): lax.all_gather(query_tangent, 'kv', axis=0, tiled=True)]
    unnamed x10 -> x0, waiting for transfers between devices: 32.5 us -> none
    ppermute x0 -> x11, waiting for transfers between devices: none -> 27 us  [swap(): lax.ppermute(x, AXES, [(i, i ^ masks[i // n_kv % 2]) for i in range(n_pb...]
    pallas_call x0 -> x7, Pallas kernels: none -> 23.6 us  [the longest x3 15 us: attend(): pl.pallas_call(functools.partial(attend_kernel, n_q, n_k, rows, bool(prev...]
    all_gather x4 -> x0, waiting for transfers between devices: 16.9 us -> none  [the longest x1 13.6 us: per_device(): dval_p = lax.all_gather(value_tangent, 'pb', axis=0, tiled=True)]
    ppermute x0 -> x11, starting transfers between devices: none -> 15.9 us  [swap(): lax.ppermute(x, AXES, [(i, i ^ masks[i // n_kv % 2]) for i in range(n_pb...]
  transfers between devices with their start and end apart: 8 -> 11, of which waited for: 6 -> 8; matrix products, arithmetic and copies ran while one was open for 25% -> 0% of each run, Pallas kernels for 0% -> 14%
where the time goes in v1:
time: 71.8 us; the launch traced here: 71.5 us
  waiting for transfers between devices  27 us (38%)
  Pallas kernels  23.6 us (33%)
  starting transfers between devices  15.9 us (22%)
  local copies, waits for them, and re-layouts  4.36 us (6%)
    ppermute x11, waiting for transfers between devices, swap(): lax.ppermute(x, AXES, [(i, i ^ masks[i // n_kv % 2]) for i in range(n_pb...  27 us
    ppermute x11, starting transfers between devices, swap(): lax.ppermute(x, AXES, [(i, i ^ masks[i // n_kv % 2]) for i in range(n_pb...  15.9 us
    pallas_call x3, Pallas kernels, attend(): pl.pallas_call(functools.partial(attend_kernel, n_q, n_k, rows, bool(prev...  15 us
    unnamed x22, local copies, waits for them, and re-layouts  4.36 us
    pallas_call x1, Pallas kernels, per_device(): pl.pallas_call(functools.partial(finish_kernel, n_q, 2 * rows), out_shape...  2.6 us
    pallas_call x1, Pallas kernels, per_device(): pl.pallas_call(join_kernel, out_shape=[f32(2 * rows, 2 * DH), f32(2 * row...  2.27 us
    pallas_call x1, Pallas kernels, per_device(): pl.pallas_call(give_kernel, out_shape=f32(rows, 6 * DH), in_specs=[smem]...  1.98 us
    pallas_call x1, Pallas kernels, per_device(): pl.pallas_call(place_kernel, out_shape=[f32(rows, width)] * 2, in_specs=[...  1.68 us
  transfers between devices with their start and end apart: 11, of which 8 were waited for; matrix products, arithmetic and copies ran while one was open for 0% of the time, Pallas kernels for 14%

profile of v1, /device:TPU:0, one launch (start us, length us, event | category | flops | bytes accessed | tf_op | source)
XLA Modules:
  0.0 71.5 jit_solution(16605550084745676386)
XLA Ops:
  0.6 2.0 %shard_map.77 = f32[128,768]{1,0:T(8,128)} custom-call(s32[1]{0:T(128)} %bitcast.core_ref, f32[128,256]{1,0:T(8,128)} %refs_0_.3, f32[128,256]{1,0:T(8,128)} %refs_1_.3, f32[128,256]{1,0:T(8,128)} %refs_2_.3, f32[128,256]{1,0:T(8,128)} %refs_3_.3, f32[128,256]{1,0:T(8,128)} %refs_4_.3, f32[128,256]{1,0:T(8,128)} %refs_5_.3), custom_call_target="tpu_custom_call" | custom-call | tf_op jit(solution)/shard_map/pallas_call | solution.py:201
  2.6 0.5 collective-permute-start
  3.1 1.6 %collective-permute-done.refs_6_ = f32[128,768]{1,0:T(8,128)S(1)} collective-permute-done((f32[128,768]{1,0:T(8,128)}, f32[128,768]{1,0:T(8,128)S(1)}, u32[]{:S(2)}, u32[]{:S(2)}) %collective-permute-start) | collective-permute-done | bytes 393248 | tf_op jit(solution)/shard_map/ppermute | solution.py:193
  4.6 0.7 %copy-done = f32[128,768]{1,0:T(8,128)} copy-done((f32[128,768]{1,0:T(8,128)}, f32[128,768]{1,0:T(8,128)S(1)}, u32[]{:S(2)}) %copy-start) | copy-done | bytes 393240
  5.4 2.3 %shard_map.78 = (f32[256,256]{1,0:T(8,128)}, f32[256,512]{1,0:T(8,128)}) custom-call(s32[1]{0:T(128)} %bitcast.core_ref, f32[128,256]{1,0:T(8,128)} %refs_0_.3, f32[128,256]{1,0:T(8,128)} %refs_1_.3, f32[128,256]{1,0:T(8,128)} %refs_2_.3, f32[128,256]{1,0:T(8,128)} %refs_3_.3, f32[128,256]{1,0:T(8,128)} %refs_4_.3, f32[128,256]{1,0:T(8,128)} %refs_5_.3, ...), custom_call_target="tpu_custom_call" | custom-call | tf_op jit(solution)/shard_map/pallas_call | solution.py:208
  7.6 4.0 %collective-permute-start.2 = (f32[256,512]{1,0:T(8,128)}, f32[256,512]{1,0:T(8,128)S(1)}, u32[]{:S(2)}, u32[]{:S(2)}) collective-permute-start(f32[256,512]{1,0:T(8,128)} %get-tuple-element.19.refs_4_), channel_id=1, source_target_pairs={{0,2},{1,3},{2,0},{3,1},{4,5},{5,4},{6,7},{7,6},{8,10},{9,11},{10,... | collective-permute-start | bytes 1572872 | tf_op jit(solution)/shard_map/ppermute | solution.py:193
  11.6 1.6 %collective-permute-start.4 = (f32[256,256]{1,0:T(8,128)}, f32[256,256]{1,0:T(8,128)S(1)}, u32[]{:S(2)}, u32[]{:S(2)}) collective-permute-start(f32[256,256]{1,0:T(8,128)} %get-tuple-element.18.refs_0_), channel_id=1, source_target_pairs={{0,1},{1,0},{2,3},{3,2},{4,6},{5,7},{6,4},{7,5},{8,9},{9,8},{10,11... | collective-permute-start | bytes 786440 | tf_op jit(solution)/shard_map/ppermute | solution.py:193
  13.2 1.5 %collective-permute-start.6 = (f32[256,512]{1,0:T(8,128)}, f32[256,512]{1,0:T(8,128)S(1)}, u32[]{:S(2)}, u32[]{:S(2)}) collective-permute-start(f32[256,512]{1,0:T(8,128)} %get-tuple-element.19.refs_4_), channel_id=1, source_target_pairs={{0,8},{1,9},{2,10},{3,11},{4,20},{5,21},{6,22},{7,23},{8,0},{9,1},... | collective-permute-start | bytes 1572872 | tf_op jit(solution)/shard_map/ppermute | solution.py:193
  14.7 1.5 %collective-permute-start.1 = (f32[256,256]{1,0:T(8,128)}, f32[256,256]{1,0:T(8,128)S(1)}, u32[]{:S(2)}, u32[]{:S(2)}) collective-permute-start(f32[256,256]{1,0:T(8,128)} %get-tuple-element.18.refs_0_), channel_id=1, source_target_pairs={{0,16},{1,17},{2,18},{3,19},{4,12},{5,13},{6,14},{7,15},{8,24},{9,... | collective-permute-start | bytes 786440 | tf_op jit(solution)/shard_map/ppermute | solution.py:193
  16.2 11.9 %collective-permute-done.4.refs_1_.refs_0_ = f32[256,256]{1,0:T(8,128)S(1)} collective-permute-done((f32[256,256]{1,0:T(8,128)}, f32[256,256]{1,0:T(8,128)S(1)}, u32[]{:S(2)}, u32[]{:S(2)}) %collective-permute-start.4) | collective-permute-done | bytes 262176 | tf_op jit(solution)/shard_map/ppermute | solution.py:193
  28.1 1.5 %collective-permute-start.5 = (f32[256,256]{1,0:T(8,128)S(1)}, f32[256,256]{1,0:T(8,128)S(1)}, u32[]{:S(2)}, u32[]{:S(2)}) collective-permute-start(f32[256,256]{1,0:T(8,128)S(1)} %collective-permute-done.4.refs_1_.refs_0_), channel_id=1, source_target_pairs={{0,16},{1,17},{2,18},{3,19},{4,12},{5,13},{6,14},{7,15},{8,24},{9,... | collective-permute-start | bytes 786440 | tf_op jit(solution)/shard_map/ppermute | solution.py:193
  29.6 0.7 collective-permute-done.2.refs_2_
  30.2 1.8 %collective-permute-start.3 = (f32[256,512]{1,0:T(8,128)S(1)}, f32[256,512]{1,0:T(8,128)S(1)}, u32[]{:S(2)}, u32[]{:S(2)}) collective-permute-start(f32[256,512]{1,0:T(8,128)S(1)} %collective-permute-done.2.refs_2_), channel_id=1, source_target_pairs={{0,8},{1,9},{2,10},{3,11},{4,20},{5,21},{6,22},{7,23},{8,0},{9,1},... | collective-permute-start | bytes 1572872 | tf_op jit(solution)/shard_map/ppermute | solution.py:193
  32.1 5.2 %collective-permute-done.5.refs_3_.refs_1_ = f32[256,256]{1,0:T(8,128)S(1)} collective-permute-done((f32[256,256]{1,0:T(8,128)S(1)}, f32[256,256]{1,0:T(8,128)S(1)}, u32[]{:S(2)}, u32[]{:S(2)}) %collective-permute-start.5) | collective-permute-done | bytes 262176 | tf_op jit(solution)/shard_map/ppermute | solution.py:193
  37.3 0.7 copy-done.10
  38.0 0.8 %copy-done.7 = f32[256,512]{1,0:T(8,128)} copy-done((f32[256,512]{1,0:T(8,128)}, f32[256,512]{1,0:T(8,128)S(1)}, u32[]{:S(2)}) %copy-start.7) | copy-done | bytes 524312
  38.8 5.6 %shard_map.79 = (f32[256,256]{1,0:T(8,128)}, f32[256,128]{1,0:T(8,128)}, f32[256,256]{1,0:T(8,128)}, f32[256,128]{1,0:T(8,128)}, f32[256,256]{1,0:T(8,128)}, /*i...) custom-call(f32[256,256]{1,0:T(8,128)} %get-tuple-element.18.refs_0_, f32[256,256]{1,0:T(8,128)} %copy-done.9, ...), custom_call_target="tpu_custom_call" | custom-call | flops 4831838208 | bytes 5242880 | tf_op jit(solution)/shard_map/pallas_call | solution.py:133
  44.4 0.0 collective-permute-done.3.refs_3_
  44.4 0.8 %copy-done.6 = f32[256,512]{1,0:T(8,128)} copy-done((f32[256,512]{1,0:T(8,128)}, f32[256,512]{1,0:T(8,128)S(1)}, u32[]{:S(2)}) %copy-start.6) | copy-done | bytes 524312
  45.2 4.7 %shard_map.81 = (f32[264,256]{1,0:T(8,128)}, f32[264,256]{1,0:T(8,128)}) custom-call(f32[256,256]{1,0:T(8,128)} %copy-done.9, f32[256,256]{1,0:T(8,128)} %copy-done.10, f32[256,512]{1,0:T(8,128)} %copy-done.5, f32[256,512]{1,0:T(8,128)} %copy-done.6, f32[256,256]{1,0:T(8,128)} %get-tuple-element.25.refs_4_, f32[256,128]{1,0:T(8,128)} %get-tuple-element.26.refs_5_, ...), custom_call_target="tpu_custom_call" | custom-call | flops 2415919104 | bytes 3145728 | tf_op jit(solution)/shard_map/pallas_call | solution.py:133
  49.9 3.0 %collective-permute-start.7 = (f32[264,256]{1,0:T(8,128)}, f32[264,256]{1,0:T(8,128)S(1)}, u32[]{:S(2)}, u32[]{:S(2)}) collective-permute-start(f32[264,256]{1,0:T(8,128)} %get-tuple-element.29), channel_id=1, source_target_pairs={{0,17},{1,16},{2,19},{3,18},{4,14},{5,15},{6,12},{7,13},{8,25},{9,... | collective-permute-start | bytes 811016 | tf_op jit(solution)/shard_map/ppermute | solution.py:193
  52.9 0.0 collective-permute-start.9
  52.9 4.7 %shard_map.80 = (f32[264,256]{1,0:T(8,128)}, f32[264,256]{1,0:T(8,128)}) custom-call(f32[256,256]{1,0:T(8,128)} %get-tuple-element.18.refs_0_, f32[256,256]{1,0:T(8,128)} %copy-done.8, f32[256,512]{1,0:T(8,128)} %copy-done.5, f32[256,512]{1,0:T(8,128)} %copy-done.6, f32[256,256]{1,0:T(8,128)} %get-tuple-element.20.refs_4_, ...), custom_call_target="tpu_custom_call" | custom-call | flops 2415919104 | bytes 3145728 | tf_op jit(solution)/shard_map/pallas_call | solution.py:133
  57.6 0.6 collective-permute-start.8
  58.2 0.2 collective-permute-done.7.refs_1_
  58.4 3.4 %collective-permute-done.9.refs_3_ = f32[264,256]{1,0:T(8,128)S(1)} collective-permute-done((f32[264,256]{1,0:T(8,128)}, f32[264,256]{1,0:T(8,128)S(1)}, u32[]{:S(2)}, u32[]{:S(2)}) %collective-permute-start.9) | collective-permute-done | bytes 270368 | tf_op jit(solution)/shard_map/ppermute | solution.py:193
  61.8 2.5 %collective-permute-done.8.refs_2_ = f32[264,256]{1,0:T(8,128)S(1)} collective-permute-done((f32[264,256]{1,0:T(8,128)}, f32[264,256]{1,0:T(8,128)S(1)}, u32[]{:S(2)}, u32[]{:S(2)}) %collective-permute-start.8) | collective-permute-done | bytes 270368 | tf_op jit(solution)/shard_map/ppermute | solution.py:193
  64.3 0.7 copy-done.3
  65.0 2.6 %shard_map.82 = (f32[128,256]{1,0:T(8,128)}, f32[128,256]{1,0:T(8,128)}) custom-call(f32[264,256]{1,0:T(8,128)} %get-tuple-element.24.refs_0_, f32[264,256]{1,0:T(8,128)} %copy-done.1, f32[264,256]{1,0:T(8,128)} %copy-done.3, f32[264,256]{1,0:T(8,128)} %copy-done.2), custom_call_target="tpu_custom_call" | custom-call | tf_op jit(solution)/shard_map/pallas_call | solution.py:235
  67.6 1.6 %collective-permute-done.10.got = f32[128,256]{1,0:T(8,128)S(1)} collective-permute-done((f32[128,256]{1,0:T(8,128)}, f32[128,256]{1,0:T(8,128)S(1)}, u32[]{:S(2)}, u32[]{:S(2)}) %collective-permute-start.10) | collective-permute-done | bytes 131104 | tf_op jit(solution)/shard_map/ppermute | solution.py:193
  69.2 0.6 copy-done.4
  69.8 1.7 %shard_map.83 = (f32[128,256]{1,0:T(8,128)}, f32[128,256]{1,0:T(8,128)}) custom-call(s32[1]{0:T(128)} %bitcast.core_ref, f32[128,256]{1,0:T(8,128)} %get-tuple-element.32.keep, f32[128,256]{1,0:T(8,128)} %copy-done.4), custom_call_target="tpu_custom_call" | custom-call | tf_op jit(solution)/shard_map/pallas_call | solution.py:242
  (19 shorter events, 0.0 us)
Async XLA Ops:
  2.6 2.0 %collective-permute-start = (f32[128,768]{1,0:T(8,128)}, f32[128,768]{1,0:T(8,128)S(1)}, u32[]{:S(2)}, u32[]{:S(2)}) collective-permute-start(f32[128,768]{1,0:T(8,128)} %shard_map.77), channel_id=1, source_target_pairs={{0,4},{1,5},{2,6},{3,7},{4,0},{5,1},{6,2},{7,3},{8,12},{9,13},{10,... | collective-permute-start | bytes 1179656 | tf_op jit(solution)/shard_map/ppermute | solution.py:193
  4.6 0.7 %copy-start = (f32[128,768]{1,0:T(8,128)}, f32[128,768]{1,0:T(8,128)S(1)}, u32[]{:S(2)}) copy-start(f32[128,768]{1,0:T(8,128)S(1)} %collective-permute-done.refs_6_) | copy-start | bytes 1179652
  7.6 22.6 %collective-permute-start.2 = (f32[256,512]{1,0:T(8,128)}, f32[256,512]{1,0:T(8,128)S(1)}, u32[]{:S(2)}, u32[]{:S(2)}) collective-permute-start(f32[256,512]{1,0:T(8,128)} %get-tuple-element.19.refs_4_), channel_id=1, source_target_pairs={{0,2},{1,3},{2,0},{3,1},{4,5},{5,4},{6,7},{7,6},{8,10},{9,11},{10,... | collective-permute-start | bytes 1572872 | tf_op jit(solution)/shard_map/ppermute | solution.py:193
  11.6 16.4 %collective-permute-start.4 = (f32[256,256]{1,0:T(8,128)}, f32[256,256]{1,0:T(8,128)S(1)}, u32[]{:S(2)}, u32[]{:S(2)}) collective-permute-start(f32[256,256]{1,0:T(8,128)} %get-tuple-element.18.refs_0_), channel_id=1, source_target_pairs={{0,1},{1,0},{2,3},{3,2},{4,6},{5,7},{6,4},{7,5},{8,9},{9,8},{10,11... | collective-permute-start | bytes 786440 | tf_op jit(solution)/shard_map/ppermute | solution.py:193
  13.2 24.1 %collective-permute-start.6 = (f32[256,512]{1,0:T(8,128)}, f32[256,512]{1,0:T(8,128)S(1)}, u32[]{:S(2)}, u32[]{:S(2)}) collective-permute-start(f32[256,512]{1,0:T(8,128)} %get-tuple-element.19.refs_4_), channel_id=1, source_target_pairs={{0,8},{1,9},{2,10},{3,11},{4,20},{5,21},{6,22},{7,23},{8,0},{9,1},... | collective-permute-start | bytes 1572872 | tf_op jit(solution)/shard_map/ppermute | solution.py:193
  14.7 17.4 %collective-permute-start.1 = (f32[256,256]{1,0:T(8,128)}, f32[256,256]{1,0:T(8,128)S(1)}, u32[]{:S(2)}, u32[]{:S(2)}) collective-permute-start(f32[256,256]{1,0:T(8,128)} %get-tuple-element.18.refs_0_), channel_id=1, source_target_pairs={{0,16},{1,17},{2,18},{3,19},{4,12},{5,13},{6,14},{7,15},{8,24},{9,... | collective-permute-start | bytes 786440 | tf_op jit(solution)/shard_map/ppermute | solution.py:193
  28.0 9.3 %copy-start.9 = (f32[256,256]{1,0:T(8,128)}, f32[256,256]{1,0:T(8,128)S(1)}, u32[]{:S(2)}) copy-start(f32[256,256]{1,0:T(8,128)S(1)} %collective-permute-done.4.refs_1_.refs_0_) | copy-start | bytes 786436
  28.1 9.2 %collective-permute-start.5 = (f32[256,256]{1,0:T(8,128)S(1)}, f32[256,256]{1,0:T(8,128)S(1)}, u32[]{:S(2)}, u32[]{:S(2)}) collective-permute-start(f32[256,256]{1,0:T(8,128)S(1)} %collective-permute-done.4.refs_1_.refs_0_), channel_id=1, source_target_pairs={{0,16},{1,17},{2,18},{3,19},{4,12},{5,13},{6,14},{7,15},{8,24},{9,... | collective-permute-start | bytes 786440 | tf_op jit(solution)/shard_map/ppermute | solution.py:193
  30.2 14.2 %copy-start.5 = (f32[256,512]{1,0:T(8,128)}, f32[256,512]{1,0:T(8,128)S(1)}, u32[]{:S(2)}) copy-start(f32[256,512]{1,0:T(8,128)S(1)} %collective-permute-done.2.refs_2_) | copy-start | bytes 1572868
  30.2 14.2 %collective-permute-start.3 = (f32[256,512]{1,0:T(8,128)S(1)}, f32[256,512]{1,0:T(8,128)S(1)}, u32[]{:S(2)}, u32[]{:S(2)}) collective-permute-start(f32[256,512]{1,0:T(8,128)S(1)} %collective-permute-done.2.refs_2_), channel_id=1, source_target_pairs={{0,8},{1,9},{2,10},{3,11},{4,20},{5,21},{6,22},{7,23},{8,0},{9,1},... | collective-permute-start | bytes 1572872 | tf_op jit(solution)/shard_map/ppermute | solution.py:193
  32.1 5.2 %copy-start.8 = (f32[256,256]{1,0:T(8,128)}, f32[256,256]{1,0:T(8,128)S(1)}, u32[]{:S(2)}) copy-start(f32[256,256]{1,0:T(8,128)S(1)} %collective-permute-done.1.refs_2_.refs_1_) | copy-start | bytes 786436
  37.3 0.7 copy-start.10
  38.0 0.8 %copy-start.7 = (f32[256,512]{1,0:T(8,128)}, f32[256,512]{1,0:T(8,128)S(1)}, u32[]{:S(2)}) copy-start(f32[256,512]{1,0:T(8,128)S(1)} %collective-permute-done.6.refs_5_) | copy-start | bytes 1572868
  44.4 0.8 %copy-start.6 = (f32[256,512]{1,0:T(8,128)}, f32[256,512]{1,0:T(8,128)S(1)}, u32[]{:S(2)}) copy-start(f32[256,512]{1,0:T(8,128)S(1)} %collective-permute-done.3.refs_3_) | copy-start | bytes 1572868
  49.9 8.5 %collective-permute-start.7 = (f32[264,256]{1,0:T(8,128)}, f32[264,256]{1,0:T(8,128)S(1)}, u32[]{:S(2)}, u32[]{:S(2)}) collective-permute-start(f32[264,256]{1,0:T(8,128)} %get-tuple-element.29), channel_id=1, source_target_pairs={{0,17},{1,16},{2,19},{3,18},{4,14},{5,15},{6,12},{7,13},{8,25},{9,... | collective-permute-start | bytes 811016 | tf_op jit(solution)/shard_map/ppermute | solution.py:193
  52.9 8.9 %collective-permute-start.9 = (f32[264,256]{1,0:T(8,128)}, f32[264,256]{1,0:T(8,128)S(1)}, u32[]{:S(2)}, u32[]{:S(2)}) collective-permute-start(f32[264,256]{1,0:T(8,128)} %get-tuple-element.31), channel_id=1, source_target_pairs={{0,1},{1,0},{2,3},{3,2},{4,6},{5,7},{6,4},{7,5},{8,9},{9,8},{10,11... | collective-permute-start | bytes 811016 | tf_op jit(solution)/shard_map/ppermute | solution.py:193
  57.6 6.7 %collective-permute-start.8 = (f32[264,256]{1,0:T(8,128)}, f32[264,256]{1,0:T(8,128)S(1)}, u32[]{:S(2)}, u32[]{:S(2)}) collective-permute-start(f32[264,256]{1,0:T(8,128)} %get-tuple-element.30), channel_id=1, source_target_pairs={{0,16},{1,17},{2,18},{3,19},{4,12},{5,13},{6,14},{7,15},{8,24},{9,... | collective-permute-start | bytes 811016 | tf_op jit(solution)/shard_map/ppermute | solution.py:193
  58.4 5.9 %copy-start.1 = (f32[264,256]{1,0:T(8,128)}, f32[264,256]{1,0:T(8,128)S(1)}, u32[]{:S(2)}) copy-start(f32[264,256]{1,0:T(8,128)S(1)} %collective-permute-done.7.refs_1_) | copy-start | bytes 811012
  61.8 2.5 %copy-start.2 = (f32[264,256]{1,0:T(8,128)}, f32[264,256]{1,0:T(8,128)S(1)}, u32[]{:S(2)}) copy-start(f32[264,256]{1,0:T(8,128)S(1)} %collective-permute-done.9.refs_3_) | copy-start | bytes 811012
  64.3 0.7 copy-start.3
  67.6 1.6 %collective-permute-start.10 = (f32[128,256]{1,0:T(8,128)}, f32[128,256]{1,0:T(8,128)S(1)}, u32[]{:S(2)}, u32[]{:S(2)}) collective-permute-start(f32[128,256]{1,0:T(8,128)} %get-tuple-element.33), channel_id=1, source_target_pairs={{0,4},{1,5},{2,6},{3,7},{4,0},{5,1},{6,2},{7,3},{8,12},{9,13},{10,... | collective-permute-start | bytes 393224 | tf_op jit(solution)/shard_map/ppermute | solution.py:193
  69.2 0.6 copy-start.4

commit v2 on v1

v2 whole, which is shorter than its diff:
```python
import functools
import math

import jax
import jax.numpy as jnp
from jax import lax
from jax.experimental import pallas as pl
from jax.experimental.pallas import tpu as pltpu
from jax.sharding import PartitionSpec as P

DH = 128
LOG2E = 1.4426950408889634
STAT_ROWS = 8
AXES = ("pb", "kv")


def params(mib):
    return pltpu.CompilerParams(vmem_limit_bytes=mib * 1024 * 1024)


def split2(x):
    high = x.astype(jnp.bfloat16)
    return high, (x - high.astype(jnp.float32)).astype(jnp.bfloat16)


def split3(x):
    high = x.astype(jnp.bfloat16)
    rest = x - high.astype(jnp.float32)
    mid = rest.astype(jnp.bfloat16)
    return high, mid, (rest - mid.astype(jnp.float32)).astype(jnp.bfloat16)


def dot_nt(left, right):
    return lax.dot_general(
        left, right, (((1,), (1,)), ((), ())), preferred_element_type=jnp.float32
    )


def dot_nn(left, right):
    return jnp.dot(left, right, preferred_element_type=jnp.float32)


def f32(*shape):
    return jax.ShapeDtypeStruct(shape, jnp.float32)


def pack_kernel(core_ref, *refs):
    *ins, own_q, own_k, give, give_k = refs
    own = pl.multiple_of(core_ref[0] * DH, DH)
    other = pl.multiple_of((1 - core_ref[0]) * DH, DH)
    for i, ref in enumerate(ins):
        out, at = (own_q, i) if i < 2 else (own_k, i - 2)
        out[:, at * DH : (at + 1) * DH] = ref[:, pl.ds(own, DH)]
        far = ref[:, pl.ds(other, DH)]
        give[:, i * DH : (i + 1) * DH] = far
        if i >= 2:
            give_k[:, at * DH : (at + 1) * DH] = far


def join_kernel(own_q, own_k, got, out_q, out_k):
    rows = got.shape[0]
    out_q[0:rows, :] = own_q[...]
    out_q[rows:, :] = got[:, 0 : 2 * DH]
    out_k[0:rows, :] = own_k[...]
    out_k[rows:, :] = got[:, 2 * DH :]


def attend_kernel(n_q, n_k, rows, has_prev, last, *refs):
    refs = list(refs)

    def take(count):
        head, refs[:] = refs[:count], refs[count:]
        return head

    q_refs, k_refs = take(n_q), take(n_k)
    prev = take(2 * n_q) if has_prev else None
    outs = take(2 * n_q)
    ka, kb, va, vb, vc = refs
    scale = 1.0 / math.sqrt(DH)
    end = 0
    for ref in k_refs:
        at = slice(end, end + ref.shape[0])
        end += ref.shape[0]
        k1, k2, k3 = split3(ref[:, 0:DH])
        d1, d2 = split2(ref[:, DH : 2 * DH])
        v1, v2 = split2(ref[:, 2 * DH : 3 * DH])
        w1, w2 = split2(ref[:, 3 * DH : 4 * DH])
        ka[at, :] = jnp.concatenate([k1, k2, k1, k3, k1, k2], axis=1)
        kb[at, :] = jnp.concatenate([k1, d1, k2, d2, k1, d1], axis=1)
        va[at, :] = jnp.concatenate([v1, w1], axis=1)
        vb[at, :] = jnp.concatenate([v2, w2], axis=1)
        vc[at, :] = jnp.concatenate([v1, v2], axis=1)
    lane = lax.broadcasted_iota(jnp.int32, (rows, DH), 1)
    for b, ref in enumerate(q_refs):
        q = ref[:, 0:DH]
        a1, a2, a3 = split3(q * (scale * LOG2E))
        q1, q2 = split2(q * scale)
        d1, d2 = split2(ref[:, DH : 2 * DH] * scale)
        s = dot_nt(jnp.concatenate([a1, a1, a2, a1, a3, a2], axis=1), ka[...])
        st = dot_nt(jnp.concatenate([d1, q1, d1, q1, d2, q2], axis=1), kb[...])
        peak = jnp.max(s, axis=1, keepdims=True)
        if has_prev:
            old = prev[2 * b + 1][:, 0:3]
            peak = jnp.maximum(peak, old[:, 0:1])
        e = jnp.exp2(s - peak)
        w = e * st
        total = jnp.sum(e, axis=1, keepdims=True)
        total_t = jnp.sum(w, axis=1, keepdims=True)
        e1, e2 = split2(e)
        w1, w2 = split2(w)
        both = dot_nn(e1, va[...]) + dot_nn(e1, vb[...]) + dot_nn(e2, va[...])
        first = dot_nn(w1, vc[...])
        numer = both[:, :DH]
        numer_t = both[:, DH:] + first[:, :DH] + first[:, DH:] + dot_nn(w2, vc[:, :DH])
        if has_prev:
            factor = jnp.exp2(old[:, 0:1] - peak)
            total += factor * old[:, 1:2]
            total_t += factor * old[:, 2:3]
            numer += factor * prev[2 * b][:, :DH]
            numer_t += factor * prev[2 * b][:, DH:]
        stats = jnp.where(lane == 0, peak, jnp.where(lane == 1, total, total_t))
        if last:
            half = rows // 2
            for i in range(2):
                at = slice(i * half, (i + 1) * half)
                outs[2 * b + i][0:half, :DH] = numer[at]
                outs[2 * b + i][0:half, DH:] = numer_t[at]
                flat = stats[at].T[0:STAT_ROWS, :]
                outs[2 * b + i][half:, :] = jnp.concatenate([flat, jnp.zeros_like(flat)], axis=1)
        else:
            outs[2 * b][:, :DH] = numer
            outs[2 * b][:, DH:] = numer_t
            outs[2 * b + 1][...] = stats


def attend(q_blocks, k_blocks, prev, last):
    n_q, n_k, rows = len(q_blocks), len(k_blocks), q_blocks[0].shape[0]
    assert rows == 2 * DH
    keys = sum(x.shape[0] for x in k_blocks)
    shape = [f32(rows // 2 + STAT_ROWS, 2 * DH)] * 2 if last else [f32(rows, 2 * DH), f32(rows, DH)]
    work = n_q * rows * keys
    outs = pl.pallas_call(
        functools.partial(attend_kernel, n_q, n_k, rows, bool(prev), last),
        out_shape=shape * n_q,
        scratch_shapes=[pltpu.VMEM((keys, w * DH), jnp.bfloat16) for w in (6, 6, 2, 2, 2)],
        compiler_params=params(8 + keys * 16 // 1024),
        cost_estimate=pl.CostEstimate(
            flops=work * 2 * 256 * 18, transcendentals=work, bytes_accessed=n_q * rows * 4096 + keys * 2048
        ),
    )(*q_blocks, *k_blocks, *(x for pair in prev for x in pair))
    return [tuple(outs[i : i + 2]) for i in range(0, 2 * n_q, 2)]


def finish_kernel(n_q, core_ref, *refs):
    part_refs = refs[: 2 * n_q]
    out, tan = refs[2 * n_q :]
    rows = out.shape[0]
    for group, head in ((part_refs[0::2], core_ref[0]), (part_refs[1::2], 1 - core_ref[0])):
        wides = [
            jnp.concatenate(
                [ref[rows:, :DH], jnp.zeros((DH - STAT_ROWS, DH), jnp.float32)], axis=0
            ).T
            for ref in group
        ]
        peaks = [wide[:, 0:1] for wide in wides]
        top = functools.reduce(jnp.maximum, peaks)
        total = total_t = numer = numer_t = 0.0
        for ref, wide, peak in zip(group, wides, peaks):
            factor = jnp.exp2(peak - top)
            total += factor * wide[:, 1:2]
            total_t += factor * wide[:, 2:3]
            numer += factor * ref[0:rows, :DH]
            numer_t += factor * ref[0:rows, DH:]
        attended = numer / total
        column = pl.multiple_of(head * DH, DH)
        out[:, pl.ds(column, DH)] = attended
        tan[:, pl.ds(column, DH)] = (numer_t - attended * total_t) / total


def bits_of(n_pb, n_kv):
    low = n_kv.bit_length() - 1
    far = [1 << i for i in range(low)]
    near = [1 << (low + i) for i in range(1, n_pb.bit_length() - 1)]
    one = far[0::2] + near[1::2]
    two = far[1::2] + near[0::2]
    return ((one, two), (two, one)) if len(one) == len(two) else ((one, one), (two, two))


def per_device(n_pb, n_kv, *arrays):
    rows, width = arrays[0].shape
    assert width == 2 * DH and n_pb & (n_pb - 1) == 0 and n_kv & (n_kv - 1) == 0
    q_bits, k_bits = bits_of(n_pb, n_kv)
    core = (lax.axis_index("pb") % 2).astype(jnp.int32).reshape(1)

    def swap(x, masks, cross=False):
        flip = n_kv if cross else 0
        return lax.ppermute(
            x, AXES, [(i, i ^ flip ^ masks[i // n_kv % 2]) for i in range(n_pb * n_kv)]
        )

    smem = pl.BlockSpec(memory_space=pltpu.SMEM)
    vmem = pl.BlockSpec(memory_space=pltpu.VMEM)
    arrays = [arrays[i] for i in (0, 3, 1, 4, 2, 5)]
    own_q, own_k, give, give_k = pl.pallas_call(
        pack_kernel,
        out_shape=[f32(rows, w * DH) for w in (2, 4, 6, 4)],
        in_specs=[smem] + [vmem] * 6,
        compiler_params=params(8),
    )(core, *arrays)
    far = (k_bits[0][0], k_bits[1][0])
    got = swap(give, (0, 0), True)
    late_k = [swap(own_k, far), swap(give_k, far[::-1], True)]
    mine_q, mine_k = pl.pallas_call(
        join_kernel,
        out_shape=[f32(2 * rows, 2 * DH), f32(2 * rows, 4 * DH)],
        compiler_params=params(8),
    )(own_q, own_k, got)

    q_blocks = [mine_q]
    for masks in zip(*q_bits):
        q_blocks += [swap(x, masks) for x in q_blocks]
    early_k, forwarded = [mine_k] + late_k, []
    for masks in list(zip(*k_bits))[1:]:
        forwarded += [swap(x, masks) for x in late_k + forwarded]
        early_k += [swap(x, masks) for x in early_k if x is not late_k[0] and x is not late_k[1]]
    n_q = len(q_blocks)
    early_q = [i for i in range(n_q) if i & 1 == 0 or i == 1]
    states = dict(zip(early_q, attend([q_blocks[i] for i in early_q], early_k, [], False)))
    parts = {}
    for i in range(n_q - 1, -1, -1):
        if i not in states:
            parts[i] = attend([q_blocks[i]], early_k + forwarded, [], True)[0]
    for group in ([1], [i for i in early_q if i != 1]):
        prev = [states[i] for i in group]
        parts.update(zip(group, attend([q_blocks[i] for i in group], forwarded, prev, True)))

    def mask(bits, index):
        return sum(bit for i, bit in enumerate(bits) if index >> i & 1)

    back = []
    for i in range(n_q):
        masks = (mask(q_bits[0], i), mask(q_bits[1], i))
        back += [swap(parts[i][0], masks) if i else parts[i][0], swap(parts[i][1], masks, True)]
    return tuple(
        pl.pallas_call(
            functools.partial(finish_kernel, n_q),
            out_shape=[f32(rows, width)] * 2,
            in_specs=[smem] + [vmem] * (2 * n_q),
            compiler_params=params(8),
        )(core, *back)
    )


def solution(mesh):
    spec = P(AXES, None)
    body = functools.partial(per_device, mesh.shape["pb"], mesh.shape["kv"])
    return jax.shard_map(body, mesh=mesh, in_specs=(spec,) * 6, out_specs=(spec,) * 2, check_vma=False)
```

time: 71.8 us -> 63.1 us (0.88); the launches traced: 71.5 us -> 62.1 us
  Pallas kernels: 23.6 us -> 9.62 us
  starting transfers between devices: 15.9 us -> 29.7 us
  waiting for transfers between devices: 27 us -> 16.7 us
  local copies, waits for them, and re-layouts: 4.36 us -> 5.42 us
    ppermute x11 -> x16, starting transfers between devices: 15.9 us -> 29.7 us  [swap(): lax.ppermute(x, AXES, [(i, i ^ flip ^ masks[i // n_kv % 2]) for i in rang...]
    ppermute x11 -> x16, waiting for transfers between devices: 27 us -> 16.7 us  [swap(): lax.ppermute(x, AXES, [(i, i ^ flip ^ masks[i // n_kv % 2]) for i in rang...]
    pallas_call x3 -> x4, Pallas kernels: 15 us -> 7.86 us  [attend(): pl.pallas_call(functools.partial(attend_kernel, n_q, n_k, rows, bool(prev...]
    pallas_call x3 -> x2, Pallas kernels: 6.26 us -> 1.7 us  [the longest x1 1.61 us: per_device(): pl.pallas_call(functools.partial(finish_kernel, n_q), out_shape=[f32(rows...]
    pallas_call x1, Pallas kernels: 2.27 us -> 0.05 us  [per_device(): pl.pallas_call(join_kernel, out_shape=[f32(2 * rows, 2 * DH), f32(2 * row...]
    unnamed x22 -> x12, local copies, waits for them, and re-layouts: 4.36 us -> 5.42 us
  transfers between devices with their start and end apart: 11 -> 16, of which waited for: 8 -> 7; matrix products, arithmetic and copies ran while one was open for 0% -> 0% of each run, Pallas kernels for 14% -> 13%
where the time goes in v2:
time: 63.1 us; the launch traced here: 62.1 us
  starting transfers between devices  29.7 us (47%)
  waiting for transfers between devices  16.7 us (26%)
  Pallas kernels  9.62 us (15%)
  local copies, waits for them, and re-layouts  5.42 us (9%)
  between operations  0.7 us (1%)
    ppermute x16, starting transfers between devices, swap(): lax.ppermute(x, AXES, [(i, i ^ flip ^ masks[i // n_kv % 2]) for i in rang...  29.7 us
    ppermute x16, waiting for transfers between devices, swap(): lax.ppermute(x, AXES, [(i, i ^ flip ^ masks[i // n_kv % 2]) for i in rang...  16.7 us
    pallas_call x4, Pallas kernels, attend(): pl.pallas_call(functools.partial(attend_kernel, n_q, n_k, rows, bool(prev...  7.86 us
    unnamed x12, local copies, waits for them, and re-layouts  5.42 us
    pallas_call x1, Pallas kernels, per_device(): pl.pallas_call(functools.partial(finish_kernel, n_q), out_shape=[f32(rows...  1.61 us
  transfers between devices with their start and end apart: 16, of which 7 were waited for; matrix products, arithmetic and copies ran while one was open for 0% of the time, Pallas kernels for 13%

profile of v2, /device:TPU:0, one launch (start us, length us, event | category | flops | bytes accessed | tf_op | source)
XLA Modules:
  0.0 62.1 jit_solution(11145791620284465924)
XLA Ops:
  0.7 0.9 %copy-done = f32[128,256]{1,0:T(8,128)S(1)} copy-done((f32[128,256]{1,0:T(8,128)S(1)}, f32[128,256]{1,0:T(8,128)}, u32[]{:S(2)}) %copy-start) | copy-done | bytes 131096
  1.6 0.9 %copy-done.1 = f32[128,256]{1,0:T(8,128)S(1)} copy-done((f32[128,256]{1,0:T(8,128)S(1)}, f32[128,256]{1,0:T(8,128)}, u32[]{:S(2)}) %copy-start.1) | copy-done | bytes 131096
  2.5 0.9 %copy-done.2 = f32[128,256]{1,0:T(8,128)S(1)} copy-done((f32[128,256]{1,0:T(8,128)S(1)}, f32[128,256]{1,0:T(8,128)}, u32[]{:S(2)}) %copy-start.2) | copy-done | bytes 131096
  3.4 0.9 %copy-done.3 = f32[128,256]{1,0:T(8,128)S(1)} copy-done((f32[128,256]{1,0:T(8,128)S(1)}, f32[128,256]{1,0:T(8,128)}, u32[]{:S(2)}) %copy-start.3) | copy-done | bytes 131096
  4.3 0.9 %copy-done.4 = f32[128,256]{1,0:T(8,128)S(1)} copy-done((f32[128,256]{1,0:T(8,128)S(1)}, f32[128,256]{1,0:T(8,128)}, u32[]{:S(2)}) %copy-start.4) | copy-done | bytes 131096
  5.2 0.9 %copy-done.5 = f32[128,256]{1,0:T(8,128)S(1)} copy-done((f32[128,256]{1,0:T(8,128)S(1)}, f32[128,256]{1,0:T(8,128)}, u32[]{:S(2)}) %copy-start.5) | copy-done | bytes 131096
  6.2 0.5 collective-permute-start
  6.7 3.7 %collective-permute-start.2 = (f32[128,512]{1,0:T(8,128)S(1)}, f32[128,512]{1,0:T(8,128)S(1)}, u32[]{:S(2)}, u32[]{:S(2)}) collective-permute-start(f32[128,512]{1,0:T(8,128)S(1)} %get-tuple-element.23.own_k), channel_id=1, source_target_pairs={{0,2},{1,3},{2,0},{3,1},{4,5},{5,4},{6,7},{7,6},{8,10},{9,11},{10,... | collective-permute-start | bytes 786440 | tf_op jit(solution)/shard_map/ppermute | solution.py:197
  10.4 1.6 %collective-permute-start.6 = (f32[256,256]{1,0:T(8,128)S(1)}, f32[256,256]{1,0:T(8,128)S(1)}, u32[]{:S(2)}, u32[]{:S(2)}) collective-permute-start(f32[256,256]{1,0:T(8,128)S(1)} %get-tuple-element.25.refs_0_), channel_id=1, source_target_pairs={{0,1},{1,0},{2,3},{3,2},{4,6},{5,7},{6,4},{7,5},{8,9},{9,8},{10,11... | collective-permute-start | bytes 786440 | tf_op jit(solution)/shard_map/ppermute | solution.py:197
  12.1 1.5 %collective-permute-start.7 = (f32[256,512]{1,0:T(8,128)S(1)}, f32[256,512]{1,0:T(8,128)S(1)}, u32[]{:S(2)}, u32[]{:S(2)}) collective-permute-start(f32[256,512]{1,0:T(8,128)S(1)} %get-tuple-element.27.refs_3_.refs_1_), channel_id=1, source_target_pairs={{0,8},{1,9},{2,10},{3,11},{4,20},{5,21},{6,22},{7,23},{8,0},{9,1},... | collective-permute-start | bytes 1572872 | tf_op jit(solution)/shard_map/ppermute | solution.py:197
  13.6 5.5 %collective-permute-done.2.refs_4_.refs_2_ = f32[128,512]{1,0:T(8,128)S(1)} collective-permute-done((f32[128,512]{1,0:T(8,128)S(1)}, f32[128,512]{1,0:T(8,128)S(1)}, u32[]{:S(2)}, u32[]{:S(2)}) %collective-permute-start.2) | collective-permute-done | bytes 262176 | tf_op jit(solution)/shard_map/ppermute | solution.py:197
  19.0 2.8 %collective-permute-start.3 = (f32[128,512]{1,0:T(8,128)S(1)}, f32[128,512]{1,0:T(8,128)S(1)}, u32[]{:S(2)}, u32[]{:S(2)}) collective-permute-start(f32[128,512]{1,0:T(8,128)S(1)} %collective-permute-done.2.refs_4_.refs_2_), channel_id=1, source_target_pairs={{0,8},{1,9},{2,10},{3,11},{4,20},{5,21},{6,22},{7,23},{8,0},{9,1},... | collective-permute-start | bytes 786440 | tf_op jit(solution)/shard_map/ppermute | solution.py:197
  21.8 1.0 %collective-permute-done.4.refs_5_.refs_3_ = f32[128,512]{1,0:T(8,128)S(1)} collective-permute-done((f32[128,512]{1,0:T(8,128)S(1)}, f32[128,512]{1,0:T(8,128)S(1)}, u32[]{:S(2)}, u32[]{:S(2)}) %collective-permute-start.4) | collective-permute-done | bytes 262176 | tf_op jit(solution)/shard_map/ppermute | solution.py:197
  22.8 2.0 %collective-permute-start.5 = (f32[128,512]{1,0:T(8,128)S(1)}, f32[128,512]{1,0:T(8,128)S(1)}, u32[]{:S(2)}, u32[]{:S(2)}) collective-permute-start(f32[128,512]{1,0:T(8,128)S(1)} %collective-permute-done.4.refs_5_.refs_3_), channel_id=1, source_target_pairs={{0,8},{1,9},{2,10},{3,11},{4,20},{5,21},{6,22},{7,23},{8,0},{9,1},... | collective-permute-start | bytes 786440 | tf_op jit(solution)/shard_map/ppermute | solution.py:197
  24.8 2.0 %collective-permute-done.6.refs_1_.refs_0_ = f32[256,256]{1,0:T(8,128)S(1)} collective-permute-done((f32[256,256]{1,0:T(8,128)S(1)}, f32[256,256]{1,0:T(8,128)S(1)}, u32[]{:S(2)}, u32[]{:S(2)}) %collective-permute-start.6) | collective-permute-done | bytes 262176 | tf_op jit(solution)/shard_map/ppermute | solution.py:197
  26.8 1.5 %collective-permute-start.13 = (f32[256,256]{1,0:T(8,128)S(1)}, f32[256,256]{1,0:T(8,128)S(1)}, u32[]{:S(2)}, u32[]{:S(2)}) collective-permute-start(f32[256,256]{1,0:T(8,128)S(1)} %collective-permute-done.6.refs_1_.refs_0_), channel_id=1, source_target_pairs={{0,16},{1,17},{2,18},{3,19},{4,12},{5,13},{6,14},{7,15},{8,24},{9,... | collective-permute-start | bytes 786440 | tf_op jit(solution)/shard_map/ppermute | solution.py:197
  28.3 0.5 collective-permute-start.1
  28.8 0.3 collective-permute-done.5.refs_3_.refs_2_.refs_6_
  29.2 4.0 %collective-permute-done.13.refs_0_ = f32[256,256]{1,0:T(8,128)S(1)} collective-permute-done((f32[256,256]{1,0:T(8,128)S(1)}, f32[256,256]{1,0:T(8,128)S(1)}, u32[]{:S(2)}, u32[]{:S(2)}) %collective-permute-start.13) | collective-permute-done | bytes 262176 | tf_op jit(solution)/shard_map/ppermute | solution.py:197
  33.2 1.8 %shard_map.82 = (f32[136,256]{1,0:T(8,128)S(1)}, f32[136,256]{1,0:T(8,128)S(1)}) custom-call(f32[256,256]{1,0:T(8,128)S(1)} %collective-permute-done.13.refs_0_, f32[256,512]{1,0:T(8,128)S(1)} %get-tuple-element.27.refs_3_.refs_1_, f32[128,512]{1,0:T(8,128)S(1)} %collective-permute-done.2.refs_4_.refs_2_, ...), custom_call_target="tpu_custom_call" | custom-call | flops 2415919104 | bytes 3145728 | tf_op jit(solution)/shard_map/pallas_call | solution.py:142
  35.0 7.6 %collective-permute-start.14 = (f32[136,256]{1,0:T(8,128)S(1)}, f32[136,256]{1,0:T(8,128)S(1)}, u32[]{:S(2)}, u32[]{:S(2)}) collective-permute-start(f32[136,256]{1,0:T(8,128)S(1)} %get-tuple-element.40), channel_id=1, source_target_pairs={{0,17},{1,16},{2,19},{3,18},{4,14},{5,15},{6,12},{7,13},{8,25},{9,... | collective-permute-start | bytes 417800 | tf_op jit(solution)/shard_map/ppermute | solution.py:197
  42.6 1.7 %collective-permute-start.15 = (f32[136,256]{1,0:T(8,128)S(1)}, f32[136,256]{1,0:T(8,128)S(1)}, u32[]{:S(2)}, u32[]{:S(2)}) collective-permute-start(f32[136,256]{1,0:T(8,128)S(1)} %get-tuple-element.41), channel_id=1, source_target_pairs={{0,21},{1,20},{2,23},{3,22},{4,10},{5,11},{6,8},{7,9},{8,29},{9,28... | collective-permute-start | bytes 417800 | tf_op jit(solution)/shard_map/ppermute | solution.py:197
  44.3 3.8 %shard_map.79 = (f32[256,256]{1,0:T(8,128)S(1)}, f32[256,128]{1,0:T(8,128)S(1)}, f32[256,256]{1,0:T(8,128)S(1)}, f32[256,128]{1,0:T(8,128)S(1)}, f32[256,256]{1,0:T(8,128)S(1)}, /*index=5*/f32[256,128]{1,0:T(8,128)S(1)}) custom-call(f32[256,256]{1,0:T(8,128)S(1)} %get-tuple-element.25.refs_0_, f32[256,256]{1,0:T(8,128)S(1)} %collective-permute-done.6.refs_1_.refs_0_, ...), custom_call_target="tpu_custom_call" | custom-call | flops 5435817984 | bytes 4718592 | tf_op jit(solution)/shard_map/pallas_call | solution.py:142
  48.1 0.8 %shard_map.81 = (f32[136,256]{1,0:T(8,128)S(1)}, f32[136,256]{1,0:T(8,128)S(1)}) custom-call(f32[256,256]{1,0:T(8,128)S(1)} %collective-permute-done.6.refs_1_.refs_0_, f32[128,512]{1,0:T(8,128)S(1)} %collective-permute-done.3.refs_2_.refs_1_.refs_5_, f32[128,512]{1,0:T(8,128)S(1)} %collective-permute-done.5.refs_3_.refs_2_.refs_6_, ...), custom_call_target="tpu_custom_call" | custom-call | flops 603979776 | bytes 1572864 | tf_op jit(solution)/shard_map/pallas_call | solution.py:142
  48.9 2.1 %collective-permute-start.10 = (f32[136,256]{1,0:T(8,128)S(1)}, f32[136,256]{1,0:T(8,128)S(1)}, u32[]{:S(2)}, u32[]{:S(2)}) collective-permute-start(f32[136,256]{1,0:T(8,128)S(1)} %get-tuple-element.37), channel_id=1, source_target_pairs={{0,5},{1,4},{2,7},{3,6},{4,2},{5,3},{6,0},{7,1},{8,13},{9,12},{10,... | collective-permute-start | bytes 417800 | tf_op jit(solution)/shard_map/ppermute | solution.py:197
  51.0 2.9 %collective-permute-start.9 = (f32[136,256]{1,0:T(8,128)S(1)}, f32[136,256]{1,0:T(8,128)S(1)}, u32[]{:S(2)}, u32[]{:S(2)}) collective-permute-start(f32[136,256]{1,0:T(8,128)S(1)} %get-tuple-element.36), channel_id=1, source_target_pairs={{0,1},{1,0},{2,3},{3,2},{4,6},{5,7},{6,4},{7,5},{8,9},{9,8},{10,11... | collective-permute-start | bytes 417800 | tf_op jit(solution)/shard_map/ppermute | solution.py:197
  53.9 1.4 %shard_map.80 = (f32[136,256]{1,0:T(8,128)S(1)}, f32[136,256]{1,0:T(8,128)S(1)}, f32[136,256]{1,0:T(8,128)S(1)}, f32[136,256]{1,0:T(8,128)S(1)}) custom-call(f32[256,256]{1,0:T(8,128)S(1)} %get-tuple-element.25.refs_0_, f32[256,256]{1,0:T(8,128)S(1)} %collective-permute-done.1.refs_2_.refs_1_, f32[128,512]{1,0:T(8,128)S(1)} %collective-permute-done.3.refs_2_.refs_1_.refs_5_, ...), custom_call_target="tpu_custom_call" | custom-call | flops 1207959552 | bytes 2621440 | tf_op jit(solution)/shard_map/pallas_call | solution.py:142
  55.3 0.6 collective-permute-start.11
  55.9 0.6 %collective-permute-start.8 = (f32[136,256]{1,0:T(8,128)S(1)}, f32[136,256]{1,0:T(8,128)S(1)}, u32[]{:S(2)}, u32[]{:S(2)}) collective-permute-start(f32[136,256]{1,0:T(8,128)S(1)} %get-tuple-element.33), channel_id=1, source_target_pairs={{0,4},{1,5},{2,6},{3,7},{4,0},{5,1},{6,2},{7,3},{8,12},{9,13},{10,... | collective-permute-start | bytes 417800 | tf_op jit(solution)/shard_map/ppermute | solution.py:197
  56.6 3.3 %collective-permute-done.9.refs_2_ = f32[136,256]{1,0:T(8,128)S(1)} collective-permute-done((f32[136,256]{1,0:T(8,128)S(1)}, f32[136,256]{1,0:T(8,128)S(1)}, u32[]{:S(2)}, u32[]{:S(2)}) %collective-permute-start.9) | collective-permute-done | bytes 139296 | tf_op jit(solution)/shard_map/ppermute | solution.py:197
  59.9 0.5 collective-permute-done.11.refs_4_
  60.5 1.6 %shard_map.83 = (f32[128,256]{1,0:T(8,128)}, f32[128,256]{1,0:T(8,128)}) custom-call(s32[1]{0:T(128)} %bitcast.core_ref, f32[136,256]{1,0:T(8,128)S(1)} %get-tuple-element.32.refs_0_, f32[136,256]{1,0:T(8,128)S(1)} %collective-permute-done.8.refs_1_, f32[136,256]{1,0:T(8,128)S(1)} %collective-permute-done.9.refs_2_, ...), custom_call_target="tpu_custom_call" | custom-call | tf_op jit(solution)/shard_map/pallas_call | solution.py:245
  (19 shorter events, 0.2 us)
Async XLA Ops:
  0.6 0.9 %copy-start = (f32[128,256]{1,0:T(8,128)S(1)}, f32[128,256]{1,0:T(8,128)}, u32[]{:S(2)}) copy-start(f32[128,256]{1,0:T(8,128)} %refs_0_.1) | copy-start | bytes 393220
  1.5 0.9 %copy-start.1 = (f32[128,256]{1,0:T(8,128)S(1)}, f32[128,256]{1,0:T(8,128)}, u32[]{:S(2)}) copy-start(f32[128,256]{1,0:T(8,128)} %refs_1_.1) | copy-start | bytes 393220
  2.5 0.9 %copy-start.2 = (f32[128,256]{1,0:T(8,128)S(1)}, f32[128,256]{1,0:T(8,128)}, u32[]{:S(2)}) copy-start(f32[128,256]{1,0:T(8,128)} %refs_2_.1) | copy-start | bytes 393220
  3.4 0.9 %copy-start.3 = (f32[128,256]{1,0:T(8,128)S(1)}, f32[128,256]{1,0:T(8,128)}, u32[]{:S(2)}) copy-start(f32[128,256]{1,0:T(8,128)} %refs_3_.1) | copy-start | bytes 393220
  4.3 0.9 %copy-start.4 = (f32[128,256]{1,0:T(8,128)S(1)}, f32[128,256]{1,0:T(8,128)}, u32[]{:S(2)}) copy-start(f32[128,256]{1,0:T(8,128)} %refs_4_.1) | copy-start | bytes 393220
  5.2 0.9 %copy-start.5 = (f32[128,256]{1,0:T(8,128)S(1)}, f32[128,256]{1,0:T(8,128)}, u32[]{:S(2)}) copy-start(f32[128,256]{1,0:T(8,128)} %refs_5_.1) | copy-start | bytes 393220
  6.2 4.2 %collective-permute-start = (f32[128,768]{1,0:T(8,128)S(1)}, f32[128,768]{1,0:T(8,128)S(1)}, u32[]{:S(2)}, u32[]{:S(2)}) collective-permute-start(f32[128,768]{1,0:T(8,128)S(1)} %get-tuple-element.24), channel_id=1, source_target_pairs={{0,4},{1,5},{2,6},{3,7},{4,0},{5,1},{6,2},{7,3},{8,12},{9,13},{10,... | collective-permute-start | bytes 1179656 | tf_op jit(solution)/shard_map/ppermute | solution.py:197
  6.7 12.3 %collective-permute-start.2 = (f32[128,512]{1,0:T(8,128)S(1)}, f32[128,512]{1,0:T(8,128)S(1)}, u32[]{:S(2)}, u32[]{:S(2)}) collective-permute-start(f32[128,512]{1,0:T(8,128)S(1)} %get-tuple-element.23.own_k), channel_id=1, source_target_pairs={{0,2},{1,3},{2,0},{3,1},{4,5},{5,4},{6,7},{7,6},{8,10},{9,11},{10,... | collective-permute-start | bytes 786440 | tf_op jit(solution)/shard_map/ppermute | solution.py:197
  10.4 12.4 %collective-permute-start.4 = (f32[128,512]{1,0:T(8,128)S(1)}, f32[128,512]{1,0:T(8,128)S(1)}, u32[]{:S(2)}, u32[]{:S(2)}) collective-permute-start(f32[128,512]{1,0:T(8,128)S(1)} %get-tuple-element.26), channel_id=1, source_target_pairs={{0,5},{1,4},{2,7},{3,6},{4,2},{5,3},{6,0},{7,1},{8,13},{9,12},{10,... | collective-permute-start | bytes 786440 | tf_op jit(solution)/shard_map/ppermute | solution.py:197
  10.4 16.4 %collective-permute-start.6 = (f32[256,256]{1,0:T(8,128)S(1)}, f32[256,256]{1,0:T(8,128)S(1)}, u32[]{:S(2)}, u32[]{:S(2)}) collective-permute-start(f32[256,256]{1,0:T(8,128)S(1)} %get-tuple-element.25.refs_0_), channel_id=1, source_target_pairs={{0,1},{1,0},{2,3},{3,2},{4,6},{5,7},{6,4},{7,5},{8,9},{9,8},{10,11... | collective-permute-start | bytes 786440 | tf_op jit(solution)/shard_map/ppermute | solution.py:197
  12.1 21.1 %collective-permute-start.7 = (f32[256,512]{1,0:T(8,128)S(1)}, f32[256,512]{1,0:T(8,128)S(1)}, u32[]{:S(2)}, u32[]{:S(2)}) collective-permute-start(f32[256,512]{1,0:T(8,128)S(1)} %get-tuple-element.27.refs_3_.refs_1_), channel_id=1, source_target_pairs={{0,8},{1,9},{2,10},{3,11},{4,20},{5,21},{6,22},{7,23},{8,0},{9,1},... | collective-permute-start | bytes 1572872 | tf_op jit(solution)/shard_map/ppermute | solution.py:197
  19.0 9.8 %collective-permute-start.3 = (f32[128,512]{1,0:T(8,128)S(1)}, f32[128,512]{1,0:T(8,128)S(1)}, u32[]{:S(2)}, u32[]{:S(2)}) collective-permute-start(f32[128,512]{1,0:T(8,128)S(1)} %collective-permute-done.2.refs_4_.refs_2_), channel_id=1, source_target_pairs={{0,8},{1,9},{2,10},{3,11},{4,20},{5,21},{6,22},{7,23},{8,0},{9,1},... | collective-permute-start | bytes 786440 | tf_op jit(solution)/shard_map/ppermute | solution.py:197
  22.8 6.4 %collective-permute-start.5 = (f32[128,512]{1,0:T(8,128)S(1)}, f32[128,512]{1,0:T(8,128)S(1)}, u32[]{:S(2)}, u32[]{:S(2)}) collective-permute-start(f32[128,512]{1,0:T(8,128)S(1)} %collective-permute-done.4.refs_5_.refs_3_), channel_id=1, source_target_pairs={{0,8},{1,9},{2,10},{3,11},{4,20},{5,21},{6,22},{7,23},{8,0},{9,1},... | collective-permute-start | bytes 786440 | tf_op jit(solution)/shard_map/ppermute | solution.py:197
  26.8 6.4 %collective-permute-start.13 = (f32[256,256]{1,0:T(8,128)S(1)}, f32[256,256]{1,0:T(8,128)S(1)}, u32[]{:S(2)}, u32[]{:S(2)}) collective-permute-start(f32[256,256]{1,0:T(8,128)S(1)} %collective-permute-done.6.refs_1_.refs_0_), channel_id=1, source_target_pairs={{0,16},{1,17},{2,18},{3,19},{4,12},{5,13},{6,14},{7,15},{8,24},{9,... | collective-permute-start | bytes 786440 | tf_op jit(solution)/shard_map/ppermute | solution.py:197
  28.3 16.0 %collective-permute-start.1 = (f32[256,256]{1,0:T(8,128)S(1)}, f32[256,256]{1,0:T(8,128)S(1)}, u32[]{:S(2)}, u32[]{:S(2)}) collective-permute-start(f32[256,256]{1,0:T(8,128)S(1)} %get-tuple-element.25.refs_0_), channel_id=1, source_target_pairs={{0,16},{1,17},{2,18},{3,19},{4,12},{5,13},{6,14},{7,15},{8,24},{9,... | collective-permute-start | bytes 786440 | tf_op jit(solution)/shard_map/ppermute | solution.py:197
  35.0 20.9 %collective-permute-start.14 = (f32[136,256]{1,0:T(8,128)S(1)}, f32[136,256]{1,0:T(8,128)S(1)}, u32[]{:S(2)}, u32[]{:S(2)}) collective-permute-start(f32[136,256]{1,0:T(8,128)S(1)} %get-tuple-element.40), channel_id=1, source_target_pairs={{0,17},{1,16},{2,19},{3,18},{4,14},{5,15},{6,12},{7,13},{8,25},{9,... | collective-permute-start | bytes 417800 | tf_op jit(solution)/shard_map/ppermute | solution.py:197
  42.6 13.3 %collective-permute-start.15 = (f32[136,256]{1,0:T(8,128)S(1)}, f32[136,256]{1,0:T(8,128)S(1)}, u32[]{:S(2)}, u32[]{:S(2)}) collective-permute-start(f32[136,256]{1,0:T(8,128)S(1)} %get-tuple-element.41), channel_id=1, source_target_pairs={{0,21},{1,20},{2,23},{3,22},{4,10},{5,11},{6,8},{7,9},{8,29},{9,28... | collective-permute-start | bytes 417800 | tf_op jit(solution)/shard_map/ppermute | solution.py:197
  48.9 7.6 %collective-permute-start.10 = (f32[136,256]{1,0:T(8,128)S(1)}, f32[136,256]{1,0:T(8,128)S(1)}, u32[]{:S(2)}, u32[]{:S(2)}) collective-permute-start(f32[136,256]{1,0:T(8,128)S(1)} %get-tuple-element.37), channel_id=1, source_target_pairs={{0,5},{1,4},{2,7},{3,6},{4,2},{5,3},{6,0},{7,1},{8,13},{9,12},{10,... | collective-permute-start | bytes 417800 | tf_op jit(solution)/shard_map/ppermute | solution.py:197
  51.0 8.9 %collective-permute-start.9 = (f32[136,256]{1,0:T(8,128)S(1)}, f32[136,256]{1,0:T(8,128)S(1)}, u32[]{:S(2)}, u32[]{:S(2)}) collective-permute-start(f32[136,256]{1,0:T(8,128)S(1)} %get-tuple-element.36), channel_id=1, source_target_pairs={{0,1},{1,0},{2,3},{3,2},{4,6},{5,7},{6,4},{7,5},{8,9},{9,8},{10,11... | collective-permute-start | bytes 417800 | tf_op jit(solution)/shard_map/ppermute | solution.py:197
  55.3 5.1 %collective-permute-start.11 = (f32[136,256]{1,0:T(8,128)S(1)}, f32[136,256]{1,0:T(8,128)S(1)}, u32[]{:S(2)}, u32[]{:S(2)}) collective-permute-start(f32[136,256]{1,0:T(8,128)S(1)} %get-tuple-element.38), channel_id=1, source_target_pairs={{0,16},{1,17},{2,18},{3,19},{4,12},{5,13},{6,14},{7,15},{8,24},{9,... | collective-permute-start | bytes 417800 | tf_op jit(solution)/shard_map/ppermute | solution.py:197
  55.9 4.5 %collective-permute-start.12 = (f32[136,256]{1,0:T(8,128)S(1)}, f32[136,256]{1,0:T(8,128)S(1)}, u32[]{:S(2)}, u32[]{:S(2)}) collective-permute-start(f32[136,256]{1,0:T(8,128)S(1)} %get-tuple-element.39), channel_id=1, source_target_pairs={{0,20},{1,21},{2,22},{3,23},{4,8},{5,9},{6,10},{7,11},{8,28},{9,29... | collective-permute-start | bytes 417800 | tf_op jit(solution)/shard_map/ppermute | solution.py:197
  55.9 4.5 %collective-permute-start.8 = (f32[136,256]{1,0:T(8,128)S(1)}, f32[136,256]{1,0:T(8,128)S(1)}, u32[]{:S(2)}, u32[]{:S(2)}) collective-permute-start(f32[136,256]{1,0:T(8,128)S(1)} %get-tuple-element.33), channel_id=1, source_target_pairs={{0,4},{1,5},{2,6},{3,7},{4,0},{5,1},{6,2},{7,3},{8,12},{9,13},{10,... | collective-permute-start | bytes 417800 | tf_op jit(solution)/shard_map/ppermute | solution.py:197

commit v3 on v2

--- a/solution.py
+++ b/solution.py
@@ -15,7 +15,7 @@
 
 
 def params(mib):
-    return pltpu.CompilerParams(vmem_limit_bytes=mib * 1024 * 1024)
+    return pltpu.CompilerParams(vmem_limit_bytes=int(mib * 1024 * 1024))
 
 
 def split2(x):
@@ -44,28 +44,33 @@
     return jax.ShapeDtypeStruct(shape, jnp.float32)
 
 
-def pack_kernel(core_ref, *refs):
-    *ins, own_q, own_k, give, give_k = refs
-    own = pl.multiple_of(core_ref[0] * DH, DH)
-    other = pl.multiple_of((1 - core_ref[0]) * DH, DH)
+def pack_kernel(*refs):
+    ins, owns, (give, sems) = refs[:6], refs[6:12], refs[12:]
+    core = lax.axis_index("pb") % 2
+    own = pl.multiple_of(core * DH, DH)
+    other = pl.multiple_of((1 - core) * DH, DH)
+    moves = []
     for i, ref in enumerate(ins):
-        out, at = (own_q, i) if i < 2 else (own_k, i - 2)
-        out[:, at * DH : (at + 1) * DH] = ref[:, pl.ds(own, DH)]
-        far = ref[:, pl.ds(other, DH)]
-        give[:, i * DH : (i + 1) * DH] = far
-        if i >= 2:
-            give_k[:, at * DH : (at + 1) * DH] = far
-
-
-def join_kernel(own_q, own_k, got, out_q, out_k):
+        moves.append((ref.at[:, pl.ds(own, DH)], owns[i]))
+        moves.append((ref.at[:, pl.ds(other, DH)], give.at[:, i * DH : (i + 1) * DH]))
+    copies = [pltpu.make_async_copy(src, dst, sems.at[i]) for i, (src, dst) in enumerate(moves)]
+    for copy in copies:
+        copy.start()
+    for copy in copies:
+        copy.wait()
+
+
+def join_kernel(*refs):
+    *owns, got, out_q, out_k = refs
     rows = got.shape[0]
-    out_q[0:rows, :] = own_q[...]
+    for i, ref in enumerate(owns):
+        out, at = (out_q, i) if i < 2 else (out_k, i - 2)
+        out[0:rows, at * DH : (at + 1) * DH] = ref[...]
     out_q[rows:, :] = got[:, 0 : 2 * DH]
-    out_k[0:rows, :] = own_k[...]
     out_k[rows:, :] = got[:, 2 * DH :]
 
 
-def attend_kernel(n_q, n_k, rows, has_prev, last, *refs):
+def attend_kernel(n_q, n_k, rows, has_prev, last, n_after, *refs):
     refs = list(refs)
 
     def take(count):
@@ -74,6 +79,7 @@
 
     q_refs, k_refs = take(n_q), take(n_k)
     prev = take(2 * n_q) if has_prev else None
+    take(n_after)
     outs = take(2 * n_q)
     ka, kb, va, vb, vc = refs
     scale = 1.0 / math.sqrt(DH)
@@ -133,21 +139,21 @@
             outs[2 * b + 1][...] = stats
 
 
-def attend(q_blocks, k_blocks, prev, last):
+def attend(q_blocks, k_blocks, prev, last, after=()):
     n_q, n_k, rows = len(q_blocks), len(k_blocks), q_blocks[0].shape[0]
     assert rows == 2 * DH
     keys = sum(x.shape[0] for x in k_blocks)
     shape = [f32(rows // 2 + STAT_ROWS, 2 * DH)] * 2 if last else [f32(rows, 2 * DH), f32(rows, DH)]
     work = n_q * rows * keys
     outs = pl.pallas_call(
-        functools.partial(attend_kernel, n_q, n_k, rows, bool(prev), last),
+        functools.partial(attend_kernel, n_q, n_k, rows, bool(prev), last, len(after)),
         out_shape=shape * n_q,
         scratch_shapes=[pltpu.VMEM((keys, w * DH), jnp.bfloat16) for w in (6, 6, 2, 2, 2)],
         compiler_params=params(8 + keys * 16 // 1024),
         cost_estimate=pl.CostEstimate(
             flops=work * 2 * 256 * 18, transcendentals=work, bytes_accessed=n_q * rows * 4096 + keys * 2048
         ),
-    )(*q_blocks, *k_blocks, *(x for pair in prev for x in pair))
+    )(*q_blocks, *k_blocks, *(x for pair in prev for x in pair), *after)
     return [tuple(outs[i : i + 2]) for i in range(0, 2 * n_q, 2)]
 
 
@@ -201,35 +207,36 @@
     smem = pl.BlockSpec(memory_space=pltpu.SMEM)
     vmem = pl.BlockSpec(memory_space=pltpu.VMEM)
     arrays = [arrays[i] for i in (0, 3, 1, 4, 2, 5)]
-    own_q, own_k, give, give_k = pl.pallas_call(
+    *owns, give = pl.pallas_call(
         pack_kernel,
-        out_shape=[f32(rows, w * DH) for w in (2, 4, 6, 4)],
-        in_specs=[smem] + [vmem] * 6,
-        compiler_params=params(8),
-    )(core, *arrays)
-    far = (k_bits[0][0], k_bits[1][0])
+        out_shape=[f32(rows, w * DH) for w in (1, 1, 1, 1, 1, 1, 6)],
+        in_specs=[pl.BlockSpec(memory_space=pl.ANY)] * 6,
+        out_specs=[vmem] * 6 + [pl.BlockSpec(memory_space=pl.ANY)],
+        scratch_shapes=[pltpu.SemaphoreType.DMA((12,))],
+        compiler_params=params(53.5),
+    )(*arrays)
     got = swap(give, (0, 0), True)
-    late_k = [swap(own_k, far), swap(give_k, far[::-1], True)]
     mine_q, mine_k = pl.pallas_call(
         join_kernel,
         out_shape=[f32(2 * rows, 2 * DH), f32(2 * rows, 4 * DH)],
         compiler_params=params(8),
-    )(own_q, own_k, got)
+    )(*owns, got)
 
     q_blocks = [mine_q]
     for masks in zip(*q_bits):
         q_blocks += [swap(x, masks) for x in q_blocks]
-    early_k, forwarded = [mine_k] + late_k, []
-    for masks in list(zip(*k_bits))[1:]:
-        forwarded += [swap(x, masks) for x in late_k + forwarded]
-        early_k += [swap(x, masks) for x in early_k if x is not late_k[0] and x is not late_k[1]]
+    k_blocks = [mine_k]
+    for masks in zip(*k_bits):
+        k_blocks += [swap(x, masks) for x in k_blocks]
+    early_k = k_blocks[:1] + k_blocks[1:2] + k_blocks[2::2]
+    forwarded = k_blocks[3::2]
     n_q = len(q_blocks)
     early_q = [i for i in range(n_q) if i & 1 == 0 or i == 1]
     states = dict(zip(early_q, attend([q_blocks[i] for i in early_q], early_k, [], False)))
     parts = {}
     for i in range(n_q - 1, -1, -1):
         if i not in states:
-            parts[i] = attend([q_blocks[i]], early_k + forwarded, [], True)[0]
+            parts[i] = attend([q_blocks[i]], early_k + forwarded, [], True, [states[0][1]])[0]
     for group in ([1], [i for i in early_q if i != 1]):
         prev = [states[i] for i in group]
         parts.update(zip(group, attend([q_blocks[i] for i in group], forwarded, prev, True)))

time: 63.1 us -> 67.9 us (1.076); the launches traced: 62.1 us -> 67.8 us
  Pallas kernels: 9.62 us -> 22.7 us
  starting transfers between devices: 29.7 us -> 20.4 us
  waiting for transfers between devices: 16.7 us -> 24.1 us
  local copies, waits for them, and re-layouts: 5.42 us -> 0 us
    pallas_call x1, Pallas kernels: 0.09 us -> 13.1 us  [per_device(): pl.pallas_call(pack_kernel, out_shape=[f32(rows, w * DH) for w in (1, 1,...]
    ppermute x16 -> x14, starting transfers between devices: 29.7 us -> 20.4 us  [swap(): lax.ppermute(x, AXES, [(i, i ^ flip ^ masks[i // n_kv % 2]) for i in rang...]
    ppermute x16 -> x14, waiting for transfers between devices: 16.7 us -> 24.1 us  [swap(): lax.ppermute(x, AXES, [(i, i ^ flip ^ masks[i // n_kv % 2]) for i in rang...]
    unnamed x12 -> x0, local copies, waits for them, and re-layouts: 5.42 us -> none
  transfers between devices with their start and end apart: 16 -> 14, of which waited for: 7 -> 6; matrix products, arithmetic and copies ran while one was open for 0% -> 0% of each run, Pallas kernels for 13% -> 9%
where the time goes in v3:
time: 67.9 us; the launch traced here: 67.8 us
  waiting for transfers between devices  24.1 us (35%)
  Pallas kernels  22.7 us (33%)
  starting transfers between devices  20.4 us (30%)
    ppermute x14, waiting for transfers between devices, swap(): lax.ppermute(x, AXES, [(i, i ^ flip ^ masks[i // n_kv % 2]) for i in rang...  24.1 us
    ppermute x14, starting transfers between devices, swap(): lax.ppermute(x, AXES, [(i, i ^ flip ^ masks[i // n_kv % 2]) for i in rang...  20.4 us
    pallas_call x1, Pallas kernels, per_device(): pl.pallas_call(pack_kernel, out_shape=[f32(rows, w * DH) for w in (1, 1,...  13.1 us
    pallas_call x4, Pallas kernels, attend(): pl.pallas_call(functools.partial(attend_kernel, n_q, n_k, rows, bool(prev...  7.86 us
    pallas_call x1, Pallas kernels, per_device(): pl.pallas_call(functools.partial(finish_kernel, n_q), out_shape=[f32(rows...  1.6 us
  transfers between devices with their start and end apart: 14, of which 6 were waited for; matrix products, arithmetic and copies ran while one was open for 0% of the time, Pallas kernels for 9%

profile of v3, /device:TPU:0, one launch (start us, length us, event | category | flops | bytes accessed | tf_op | source)
XLA Modules:
  0.0 67.8 jit_solution(966675099963114411)
XLA Ops:
  0.6 13.1 %shard_map.77 = (f32[128,128]{1,0:T(8,128)S(1)}, f32[128,128]{1,0:T(8,128)S(1)}, f32[128,128]{1,0:T(8,128)S(1)}, f32[128,128]{1,0:T(8,128)S(1)}, f32[128,128]{1,...) custom-call(f32[128,256]{1,0:T(8,128)} %refs_0_.1, f32[128,256]{1,0:T(8,128)} %refs_1_.1, f32[128,256]{1,0:T(8,128)} %refs_2_.1, ...), custom_call_target="tpu_custom_call" | custom-call | tf_op jit(solution)/shard_map/pallas_call | solution.py:210
  13.8 0.5 collective-permute-start
  14.3 1.6 %collective-permute-done.refs_6_ = f32[128,768]{1,0:T(8,128)S(1)} collective-permute-done((f32[128,768]{1,0:T(8,128)}, f32[128,768]{1,0:T(8,128)S(1)}, u32[]{:S(2)}, u32[]{:S(2)}) %collective-permute-start) | collective-permute-done | bytes 393248 | tf_op jit(solution)/shard_map/ppermute | solution.py:203
  15.9 0.1 shard_map.78
  15.9 4.0 %collective-permute-start.2 = (f32[256,512]{1,0:T(8,128)S(1)}, f32[256,512]{1,0:T(8,128)S(1)}, u32[]{:S(2)}, u32[]{:S(2)}) collective-permute-start(f32[256,512]{1,0:T(8,128)S(1)} %get-tuple-element.33.refs_3_.refs_1_), channel_id=1, source_target_pairs={{0,2},{1,3},{2,0},{3,1},{4,5},{5,4},{6,7},{7,6},{8,10},{9,11},{10,... | collective-permute-start | bytes 1572872 | tf_op jit(solution)/shard_map/ppermute | solution.py:203
  19.9 1.5 %collective-permute-start.5 = (f32[256,512]{1,0:T(8,128)S(1)}, f32[256,512]{1,0:T(8,128)S(1)}, u32[]{:S(2)}, u32[]{:S(2)}) collective-permute-start(f32[256,512]{1,0:T(8,128)S(1)} %get-tuple-element.33.refs_3_.refs_1_), channel_id=1, source_target_pairs={{0,8},{1,9},{2,10},{3,11},{4,20},{5,21},{6,22},{7,23},{8,0},{9,1},... | collective-permute-start | bytes 1572872 | tf_op jit(solution)/shard_map/ppermute | solution.py:203
  21.4 1.6 %collective-permute-start.4 = (f32[256,256]{1,0:T(8,128)S(1)}, f32[256,256]{1,0:T(8,128)S(1)}, u32[]{:S(2)}, u32[]{:S(2)}) collective-permute-start(f32[256,256]{1,0:T(8,128)S(1)} %get-tuple-element.32.refs_0_), channel_id=1, source_target_pairs={{0,1},{1,0},{2,3},{3,2},{4,6},{5,7},{6,4},{7,5},{8,9},{9,8},{10,11... | collective-permute-start | bytes 786440 | tf_op jit(solution)/shard_map/ppermute | solution.py:203
  23.0 1.5 %collective-permute-start.1 = (f32[256,256]{1,0:T(8,128)S(1)}, f32[256,256]{1,0:T(8,128)S(1)}, u32[]{:S(2)}, u32[]{:S(2)}) collective-permute-start(f32[256,256]{1,0:T(8,128)S(1)} %get-tuple-element.32.refs_0_), channel_id=1, source_target_pairs={{0,16},{1,17},{2,18},{3,19},{4,12},{5,13},{6,14},{7,15},{8,24},{9,... | collective-permute-start | bytes 786440 | tf_op jit(solution)/shard_map/ppermute | solution.py:203
  24.5 13.9 %collective-permute-done.2.refs_4_.refs_2_ = f32[256,512]{1,0:T(8,128)S(1)} collective-permute-done((f32[256,512]{1,0:T(8,128)S(1)}, f32[256,512]{1,0:T(8,128)S(1)}, u32[]{:S(2)}, u32[]{:S(2)}) %collective-permute-start.2) | collective-permute-done | bytes 524320 | tf_op jit(solution)/shard_map/ppermute | solution.py:203
  38.4 1.8 %collective-permute-start.3 = (f32[256,512]{1,0:T(8,128)S(1)}, f32[256,512]{1,0:T(8,128)S(1)}, u32[]{:S(2)}, u32[]{:S(2)}) collective-permute-start(f32[256,512]{1,0:T(8,128)S(1)} %collective-permute-done.2.refs_4_.refs_2_), channel_id=1, source_target_pairs={{0,8},{1,9},{2,10},{3,11},{4,20},{5,21},{6,22},{7,23},{8,0},{9,1},... | collective-permute-start | bytes 1572872 | tf_op jit(solution)/shard_map/ppermute | solution.py:203
  40.2 0.0 collective-permute-done.4.refs_1_.refs_0_
  40.2 1.5 %collective-permute-start.11 = (f32[256,256]{1,0:T(8,128)S(1)}, f32[256,256]{1,0:T(8,128)S(1)}, u32[]{:S(2)}, u32[]{:S(2)}) collective-permute-start(f32[256,256]{1,0:T(8,128)S(1)} %collective-permute-done.4.refs_1_.refs_0_), channel_id=1, source_target_pairs={{0,16},{1,17},{2,18},{3,19},{4,12},{5,13},{6,14},{7,15},{8,24},{9,... | collective-permute-start | bytes 786440 | tf_op jit(solution)/shard_map/ppermute | solution.py:203
  41.7 0.0 collective-permute-done.1.refs_2_.refs_1_
  41.7 0.0 collective-permute-done.5.refs_5_.refs_3_
  41.7 3.8 %shard_map.79 = (f32[256,256]{1,0:T(8,128)S(1)}, f32[256,128]{1,0:T(8,128)S(1)}, f32[256,256]{1,0:T(8,128)S(1)}, f32[256,128]{1,0:T(8,128)S(1)}, f32[256,256]{1,0:T(8,128)S(1)}, /*index=5*/f32[256,128]{1,0:T(8,128)S(1)}) custom-call(f32[256,256]{1,0:T(8,128)S(1)} %get-tuple-element.32.refs_0_, f32[256,256]{1,0:T(8,128)S(1)} %collective-permute-done.4.refs_1_.refs_0_, ...), custom_call_target="tpu_custom_call" | custom-call | flops 5435817984 | bytes 4718592 | tf_op jit(solution)/shard_map/pallas_call | solution.py:148
  45.5 1.1 %collective-permute-done.11.refs_0_ = f32[256,256]{1,0:T(8,128)S(1)} collective-permute-done((f32[256,256]{1,0:T(8,128)S(1)}, f32[256,256]{1,0:T(8,128)S(1)}, u32[]{:S(2)}, u32[]{:S(2)}) %collective-permute-start.11) | collective-permute-done | bytes 262176 | tf_op jit(solution)/shard_map/ppermute | solution.py:203
  46.6 1.0 %collective-permute-done.3.refs_2_.refs_1_.refs_4_ = f32[256,512]{1,0:T(8,128)S(1)} collective-permute-done((f32[256,512]{1,0:T(8,128)S(1)}, f32[256,512]{1,0:T(8,128)S(1)}, u32[]{:S(2)}, u32[]{:S(2)}) %collective-permute-start.3) | collective-permute-done | bytes 524320 | tf_op jit(solution)/shard_map/ppermute | solution.py:203
  47.6 1.8 %shard_map.82 = (f32[136,256]{1,0:T(8,128)S(1)}, f32[136,256]{1,0:T(8,128)S(1)}) custom-call(f32[256,256]{1,0:T(8,128)S(1)} %collective-permute-done.11.refs_0_, f32[256,512]{1,0:T(8,128)S(1)} %get-tuple-element.33.refs_3_.refs_1_, f32[256,512]{1,0:T(8,128)S(1)} %collective-permute-done.2.refs_4_.refs_2_, ...), custom_call_target="tpu_custom_call" | custom-call | flops 2415919104 | bytes 3145728 | tf_op jit(solution)/shard_map/pallas_call | solution.py:148
  49.4 3.1 %collective-permute-start.12 = (f32[136,256]{1,0:T(8,128)S(1)}, f32[136,256]{1,0:T(8,128)S(1)}, u32[]{:S(2)}, u32[]{:S(2)}) collective-permute-start(f32[136,256]{1,0:T(8,128)S(1)} %get-tuple-element.46), channel_id=1, source_target_pairs={{0,17},{1,16},{2,19},{3,18},{4,14},{5,15},{6,12},{7,13},{8,25},{9,... | collective-permute-start | bytes 417800 | tf_op jit(solution)/shard_map/ppermute | solution.py:203
  52.5 0.0 collective-permute-start.13
  52.5 0.8 %shard_map.81 = (f32[136,256]{1,0:T(8,128)S(1)}, f32[136,256]{1,0:T(8,128)S(1)}) custom-call(f32[256,256]{1,0:T(8,128)S(1)} %collective-permute-done.4.refs_1_.refs_0_, f32[256,512]{1,0:T(8,128)S(1)} %collective-permute-done.3.refs_2_.refs_1_.refs_4_, f32[256,256]{1,0:T(8,128)S(1)} %get-tuple-element.40.refs_2_, f32[256,128]{1,0:T(8,128)S(1)} %get-tuple-element.41.refs_3_), custom_call_target="tpu_custom_call" | custom-call | flops 603979776 | bytes 1572864 | tf_op jit(solution)/shard_map/pallas_call | solution.py:148
  53.4 0.3 collective-permute-start.7
  53.7 3.3 %collective-permute-start.8 = (f32[136,256]{1,0:T(8,128)S(1)}, f32[136,256]{1,0:T(8,128)S(1)}, u32[]{:S(2)}, u32[]{:S(2)}) collective-permute-start(f32[136,256]{1,0:T(8,128)S(1)} %get-tuple-element.43), channel_id=1, source_target_pairs={{0,5},{1,4},{2,7},{3,6},{4,2},{5,3},{6,0},{7,1},{8,13},{9,12},{10,... | collective-permute-start | bytes 417800 | tf_op jit(solution)/shard_map/ppermute | solution.py:203
  56.9 1.4 %shard_map.80 = (f32[136,256]{1,0:T(8,128)S(1)}, f32[136,256]{1,0:T(8,128)S(1)}, f32[136,256]{1,0:T(8,128)S(1)}, f32[136,256]{1,0:T(8,128)S(1)}) custom-call(f32[256,256]{1,0:T(8,128)S(1)} %get-tuple-element.32.refs_0_, f32[256,256]{1,0:T(8,128)S(1)} %collective-permute-done.1.refs_2_.refs_1_, f32[256,512]{1,0:T(8,128)S(1)} %collective-permute-done.3.refs_2_.refs_1_.refs_4_, ...), custom_call_target="tpu_custom_call" | custom-call | flops 1207959552 | bytes 2621440 | tf_op jit(solution)/shard_map/pallas_call | solution.py:148
  58.4 0.3 collective-permute-start.10
  58.7 0.0 collective-permute-done.12.refs_6_
  58.7 0.4 collective-permute-start.6
  59.1 1.2 %collective-permute-done.13.refs_7_ = f32[136,256]{1,0:T(8,128)S(1)} collective-permute-done((f32[136,256]{1,0:T(8,128)S(1)}, f32[136,256]{1,0:T(8,128)S(1)}, u32[]{:S(2)}, u32[]{:S(2)}) %collective-permute-start.13) | collective-permute-done | bytes 139296 | tf_op jit(solution)/shard_map/ppermute | solution.py:203
  60.3 0.5 collective-permute-start.9
  60.8 0.0 collective-permute-done.7.refs_2_
  60.8 5.4 %collective-permute-done.8.refs_3_ = f32[136,256]{1,0:T(8,128)S(1)} collective-permute-done((f32[136,256]{1,0:T(8,128)S(1)}, f32[136,256]{1,0:T(8,128)S(1)}, u32[]{:S(2)}, u32[]{:S(2)}) %collective-permute-start.8) | collective-permute-done | bytes 139296 | tf_op jit(solution)/shard_map/ppermute | solution.py:203
  66.2 1.6 %shard_map.83 = (f32[128,256]{1,0:T(8,128)}, f32[128,256]{1,0:T(8,128)}) custom-call(s32[1]{0:T(128)} %bitcast.core_ref, f32[136,256]{1,0:T(8,128)S(1)} %get-tuple-element.38.refs_0_, f32[136,256]{1,0:T(8,128)S(1)} %collective-permute-done.6.refs_1_, f32[136,256]{1,0:T(8,128)S(1)} %collective-permute-done.7.refs_2_, ...), custom_call_target="tpu_custom_call" | custom-call | tf_op jit(solution)/shard_map/pallas_call | solution.py:252
  (3 shorter events, 0.0 us)
Async XLA Ops:
  13.8 2.1 %collective-permute-start = (f32[128,768]{1,0:T(8,128)}, f32[128,768]{1,0:T(8,128)S(1)}, u32[]{:S(2)}, u32[]{:S(2)}) collective-permute-start(f32[128,768]{1,0:T(8,128)} %get-tuple-element.31), channel_id=1, source_target_pairs={{0,4},{1,5},{2,6},{3,7},{4,0},{5,1},{6,2},{7,3},{8,12},{9,13},{10,... | collective-permute-start | bytes 1179656 | tf_op jit(solution)/shard_map/ppermute | solution.py:203
  15.9 22.5 %collective-permute-start.2 = (f32[256,512]{1,0:T(8,128)S(1)}, f32[256,512]{1,0:T(8,128)S(1)}, u32[]{:S(2)}, u32[]{:S(2)}) collective-permute-start(f32[256,512]{1,0:T(8,128)S(1)} %get-tuple-element.33.refs_3_.refs_1_), channel_id=1, source_target_pairs={{0,2},{1,3},{2,0},{3,1},{4,5},{5,4},{6,7},{7,6},{8,10},{9,11},{10,... | collective-permute-start | bytes 1572872 | tf_op jit(solution)/shard_map/ppermute | solution.py:203
  19.9 21.8 %collective-permute-start.5 = (f32[256,512]{1,0:T(8,128)S(1)}, f32[256,512]{1,0:T(8,128)S(1)}, u32[]{:S(2)}, u32[]{:S(2)}) collective-permute-start(f32[256,512]{1,0:T(8,128)S(1)} %get-tuple-element.33.refs_3_.refs_1_), channel_id=1, source_target_pairs={{0,8},{1,9},{2,10},{3,11},{4,20},{5,21},{6,22},{7,23},{8,0},{9,1},... | collective-permute-start | bytes 1572872 | tf_op jit(solution)/shard_map/ppermute | solution.py:203
  21.4 18.8 %collective-permute-start.4 = (f32[256,256]{1,0:T(8,128)S(1)}, f32[256,256]{1,0:T(8,128)S(1)}, u32[]{:S(2)}, u32[]{:S(2)}) collective-permute-start(f32[256,256]{1,0:T(8,128)S(1)} %get-tuple-element.32.refs_0_), channel_id=1, source_target_pairs={{0,1},{1,0},{2,3},{3,2},{4,6},{5,7},{6,4},{7,5},{8,9},{9,8},{10,11... | collective-permute-start | bytes 786440 | tf_op jit(solution)/shard_map/ppermute | solution.py:203
  23.0 18.7 %collective-permute-start.1 = (f32[256,256]{1,0:T(8,128)S(1)}, f32[256,256]{1,0:T(8,128)S(1)}, u32[]{:S(2)}, u32[]{:S(2)}) collective-permute-start(f32[256,256]{1,0:T(8,128)S(1)} %get-tuple-element.32.refs_0_), channel_id=1, source_target_pairs={{0,16},{1,17},{2,18},{3,19},{4,12},{5,13},{6,14},{7,15},{8,24},{9,... | collective-permute-start | bytes 786440 | tf_op jit(solution)/shard_map/ppermute | solution.py:203
  38.4 9.2 %collective-permute-start.3 = (f32[256,512]{1,0:T(8,128)S(1)}, f32[256,512]{1,0:T(8,128)S(1)}, u32[]{:S(2)}, u32[]{:S(2)}) collective-permute-start(f32[256,512]{1,0:T(8,128)S(1)} %collective-permute-done.2.refs_4_.refs_2_), channel_id=1, source_target_pairs={{0,8},{1,9},{2,10},{3,11},{4,20},{5,21},{6,22},{7,23},{8,0},{9,1},... | collective-permute-start | bytes 1572872 | tf_op jit(solution)/shard_map/ppermute | solution.py:203
  40.2 6.4 %collective-permute-start.11 = (f32[256,256]{1,0:T(8,128)S(1)}, f32[256,256]{1,0:T(8,128)S(1)}, u32[]{:S(2)}, u32[]{:S(2)}) collective-permute-start(f32[256,256]{1,0:T(8,128)S(1)} %collective-permute-done.4.refs_1_.refs_0_), channel_id=1, source_target_pairs={{0,16},{1,17},{2,18},{3,19},{4,12},{5,13},{6,14},{7,15},{8,24},{9,... | collective-permute-start | bytes 786440 | tf_op jit(solution)/shard_map/ppermute | solution.py:203
  49.4 9.3 %collective-permute-start.12 = (f32[136,256]{1,0:T(8,128)S(1)}, f32[136,256]{1,0:T(8,128)S(1)}, u32[]{:S(2)}, u32[]{:S(2)}) collective-permute-start(f32[136,256]{1,0:T(8,128)S(1)} %get-tuple-element.46), channel_id=1, source_target_pairs={{0,17},{1,16},{2,19},{3,18},{4,14},{5,15},{6,12},{7,13},{8,25},{9,... | collective-permute-start | bytes 417800 | tf_op jit(solution)/shard_map/ppermute | solution.py:203
  52.5 7.8 %collective-permute-start.13 = (f32[136,256]{1,0:T(8,128)S(1)}, f32[136,256]{1,0:T(8,128)S(1)}, u32[]{:S(2)}, u32[]{:S(2)}) collective-permute-start(f32[136,256]{1,0:T(8,128)S(1)} %get-tuple-element.47), channel_id=1, source_target_pairs={{0,21},{1,20},{2,23},{3,22},{4,10},{5,11},{6,8},{7,9},{8,29},{9,28... | collective-permute-start | bytes 417800 | tf_op jit(solution)/shard_map/ppermute | solution.py:203
  53.4 7.4 %collective-permute-start.7 = (f32[136,256]{1,0:T(8,128)S(1)}, f32[136,256]{1,0:T(8,128)S(1)}, u32[]{:S(2)}, u32[]{:S(2)}) collective-permute-start(f32[136,256]{1,0:T(8,128)S(1)} %get-tuple-element.42), channel_id=1, source_target_pairs={{0,1},{1,0},{2,3},{3,2},{4,6},{5,7},{6,4},{7,5},{8,9},{9,8},{10,11... | collective-permute-start | bytes 417800 | tf_op jit(solution)/shard_map/ppermute | solution.py:203
  53.7 12.5 %collective-permute-start.8 = (f32[136,256]{1,0:T(8,128)S(1)}, f32[136,256]{1,0:T(8,128)S(1)}, u32[]{:S(2)}, u32[]{:S(2)}) collective-permute-start(f32[136,256]{1,0:T(8,128)S(1)} %get-tuple-element.43), channel_id=1, source_target_pairs={{0,5},{1,4},{2,7},{3,6},{4,2},{5,3},{6,0},{7,1},{8,13},{9,12},{10,... | collective-permute-start | bytes 417800 | tf_op jit(solution)/shard_map/ppermute | solution.py:203
  58.4 7.8 %collective-permute-start.10 = (f32[136,256]{1,0:T(8,128)S(1)}, f32[136,256]{1,0:T(8,128)S(1)}, u32[]{:S(2)}, u32[]{:S(2)}) collective-permute-start(f32[136,256]{1,0:T(8,128)S(1)} %get-tuple-element.45), channel_id=1, source_target_pairs={{0,20},{1,21},{2,22},{3,23},{4,8},{5,9},{6,10},{7,11},{8,28},{9,29... | collective-permute-start | bytes 417800 | tf_op jit(solution)/shard_map/ppermute | solution.py:203
  58.7 7.4 %collective-permute-start.6 = (f32[136,256]{1,0:T(8,128)S(1)}, f32[136,256]{1,0:T(8,128)S(1)}, u32[]{:S(2)}, u32[]{:S(2)}) collective-permute-start(f32[136,256]{1,0:T(8,128)S(1)} %get-tuple-element.39), channel_id=1, source_target_pairs={{0,4},{1,5},{2,6},{3,7},{4,0},{5,1},{6,2},{7,3},{8,12},{9,13},{10,... | collective-permute-start | bytes 417800 | tf_op jit(solution)/shard_map/ppermute | solution.py:203
  60.3 5.9 %collective-permute-start.9 = (f32[136,256]{1,0:T(8,128)S(1)}, f32[136,256]{1,0:T(8,128)S(1)}, u32[]{:S(2)}, u32[]{:S(2)}) collective-permute-start(f32[136,256]{1,0:T(8,128)S(1)} %get-tuple-element.44), channel_id=1, source_target_pairs={{0,16},{1,17},{2,18},{3,19},{4,12},{5,13},{6,14},{7,15},{8,24},{9,... | collective-permute-start | bytes 417800 | tf_op jit(solution)/shard_map/ppermute | solution.py:203

commit v4 on v3

--- a/solution.py
+++ b/solution.py
@@ -45,52 +45,63 @@
 
 
 def pack_kernel(*refs):
-    ins, owns, (give, sems) = refs[:6], refs[6:12], refs[12:]
+    ins, owns, (give, held, sems) = refs[:6], refs[6:12], refs[12:]
     core = lax.axis_index("pb") % 2
     own = pl.multiple_of(core * DH, DH)
     other = pl.multiple_of((1 - core) * DH, DH)
-    moves = []
-    for i, ref in enumerate(ins):
-        moves.append((ref.at[:, pl.ds(own, DH)], owns[i]))
-        moves.append((ref.at[:, pl.ds(other, DH)], give.at[:, i * DH : (i + 1) * DH]))
-    copies = [pltpu.make_async_copy(src, dst, sems.at[i]) for i, (src, dst) in enumerate(moves)]
+    copies = [pltpu.make_async_copy(ref, held.at[i], sems.at[i]) for i, ref in enumerate(ins)]
     for copy in copies:
         copy.start()
-    for copy in copies:
+    for i, copy in enumerate(copies):
         copy.wait()
+        owns[i][...] = held[i, :, pl.ds(own, DH)]
+        give[:, i * DH : (i + 1) * DH] = held[i, :, pl.ds(other, DH)]
 
 
 def join_kernel(*refs):
-    *owns, got, out_q, out_k = refs
+    *owns, got, out_q, out_k, out_kv = refs
     rows = got.shape[0]
     for i, ref in enumerate(owns):
-        out, at = (out_q, i) if i < 2 else (out_k, i - 2)
-        out[0:rows, at * DH : (at + 1) * DH] = ref[...]
-    out_q[rows:, :] = got[:, 0 : 2 * DH]
-    out_k[rows:, :] = got[:, 2 * DH :]
-
-
-def attend_kernel(n_q, n_k, rows, has_prev, last, n_after, *refs):
+        both = (ref[...], got[:, i * DH : (i + 1) * DH])
+        for j, x in enumerate(both):
+            at = slice(j * rows, (j + 1) * rows)
+            if i < 2:
+                out_q[at, i * DH : (i + 1) * DH] = x
+            else:
+                out_kv[at, (i - 2) * DH : (i - 1) * DH] = x
+            if i in (2, 3):
+                out_k[at, (i - 2) * DH : (i - 1) * DH] = x
+
+
+def later_kernel(x, after, out):
+    out[...] = x[:, x.shape[1] - out.shape[1] :]
+
+
+def later(x, columns, after):
+    return pl.pallas_call(
+        later_kernel, out_shape=f32(x.shape[0], columns), compiler_params=params(8)
+    )(x, after)
+
+
+def attend_kernel(n_q, n_k, rows, has_prev, last, *refs):
     refs = list(refs)
 
     def take(count):
         head, refs[:] = refs[:count], refs[count:]
         return head
 
-    q_refs, k_refs = take(n_q), take(n_k)
+    q_refs, k_refs = take(n_q), [take(count) for count in n_k]
     prev = take(2 * n_q) if has_prev else None
-    take(n_after)
     outs = take(2 * n_q)
     ka, kb, va, vb, vc = refs
     scale = 1.0 / math.sqrt(DH)
-    end = 0
-    for ref in k_refs:
-        at = slice(end, end + ref.shape[0])
-        end += ref.shape[0]
-        k1, k2, k3 = split3(ref[:, 0:DH])
-        d1, d2 = split2(ref[:, DH : 2 * DH])
-        v1, v2 = split2(ref[:, 2 * DH : 3 * DH])
-        w1, w2 = split2(ref[:, 3 * DH : 4 * DH])
+    for b, block in enumerate(k_refs):
+        at = slice(b * rows, (b + 1) * rows)
+        k, d, v, w = [ref[:, i : i + DH] for ref in block for i in range(0, ref.shape[1], DH)]
+        k1, k2, k3 = split3(k)
+        d1, d2 = split2(d)
+        v1, v2 = split2(v)
+        w1, w2 = split2(w)
         ka[at, :] = jnp.concatenate([k1, k2, k1, k3, k1, k2], axis=1)
         kb[at, :] = jnp.concatenate([k1, d1, k2, d2, k1, d1], axis=1)
         va[at, :] = jnp.concatenate([v1, w1], axis=1)
@@ -139,21 +150,21 @@
             outs[2 * b + 1][...] = stats
 
 
-def attend(q_blocks, k_blocks, prev, last, after=()):
-    n_q, n_k, rows = len(q_blocks), len(k_blocks), q_blocks[0].shape[0]
+def attend(q_blocks, k_blocks, prev, last):
+    n_q, n_k, rows = len(q_blocks), [len(block) for block in k_blocks], q_blocks[0].shape[0]
     assert rows == 2 * DH
-    keys = sum(x.shape[0] for x in k_blocks)
+    keys = rows * len(k_blocks)
     shape = [f32(rows // 2 + STAT_ROWS, 2 * DH)] * 2 if last else [f32(rows, 2 * DH), f32(rows, DH)]
     work = n_q * rows * keys
     outs = pl.pallas_call(
-        functools.partial(attend_kernel, n_q, n_k, rows, bool(prev), last, len(after)),
+        functools.partial(attend_kernel, n_q, n_k, rows, bool(prev), last),
         out_shape=shape * n_q,
         scratch_shapes=[pltpu.VMEM((keys, w * DH), jnp.bfloat16) for w in (6, 6, 2, 2, 2)],
         compiler_params=params(8 + keys * 16 // 1024),
         cost_estimate=pl.CostEstimate(
             flops=work * 2 * 256 * 18, transcendentals=work, bytes_accessed=n_q * rows * 4096 + keys * 2048
         ),
-    )(*q_blocks, *k_blocks, *(x for pair in prev for x in pair), *after)
+    )(*q_blocks, *(x for block in k_blocks for x in block), *(x for pair in prev for x in pair))
     return [tuple(outs[i : i + 2]) for i in range(0, 2 * n_q, 2)]
 
 
@@ -211,35 +222,37 @@
         pack_kernel,
         out_shape=[f32(rows, w * DH) for w in (1, 1, 1, 1, 1, 1, 6)],
         in_specs=[pl.BlockSpec(memory_space=pl.ANY)] * 6,
-        out_specs=[vmem] * 6 + [pl.BlockSpec(memory_space=pl.ANY)],
-        scratch_shapes=[pltpu.SemaphoreType.DMA((12,))],
+        out_specs=[vmem] * 7,
+        scratch_shapes=[pltpu.VMEM((6, rows, width), jnp.float32), pltpu.SemaphoreType.DMA((6,))],
         compiler_params=params(53.5),
     )(*arrays)
     got = swap(give, (0, 0), True)
-    mine_q, mine_k = pl.pallas_call(
+    mine_q, mine_k, mine_kv = pl.pallas_call(
         join_kernel,
-        out_shape=[f32(2 * rows, 2 * DH), f32(2 * rows, 4 * DH)],
+        out_shape=[f32(2 * rows, w * DH) for w in (2, 2, 4)],
         compiler_params=params(8),
     )(*owns, got)
 
-    q_blocks = [mine_q]
+    q_blocks, near_k = [mine_q], [(mine_kv,)]
     for masks in zip(*q_bits):
         q_blocks += [swap(x, masks) for x in q_blocks]
-    k_blocks = [mine_k]
-    for masks in zip(*k_bits):
-        k_blocks += [swap(x, masks) for x in k_blocks]
-    early_k = k_blocks[:1] + k_blocks[1:2] + k_blocks[2::2]
-    forwarded = k_blocks[3::2]
+    (far, *near) = zip(*k_bits)
+    for masks in near:
+        near_k += [tuple(swap(x, masks) for x in block) for block in near_k]
+    far_k = swap(mine_k, far)
+    far_v = swap(later(mine_kv, 2 * DH, far_k), far)
     n_q = len(q_blocks)
-    early_q = [i for i in range(n_q) if i & 1 == 0 or i == 1]
-    states = dict(zip(early_q, attend([q_blocks[i] for i in early_q], early_k, [], False)))
-    parts = {}
-    for i in range(n_q - 1, -1, -1):
-        if i not in states:
-            parts[i] = attend([q_blocks[i]], early_k + forwarded, [], True, [states[0][1]])[0]
-    for group in ([1], [i for i in early_q if i != 1]):
-        prev = [states[i] for i in group]
-        parts.update(zip(group, attend([q_blocks[i] for i in group], forwarded, prev, True)))
+    groups = [list(range(1, n_q, 2)), list(range(0, n_q, 2))]
+    states, parts = {}, {}
+    states.update(zip(groups[1], attend([q_blocks[i] for i in groups[1]], near_k, [], False)))
+    last_k = [(far_k, later(far_v, 2 * DH, states[0][1]))]
+    for masks in near:
+        last_k += [tuple(swap(x, masks) for x in block) for block in last_k]
+    states.update(zip(groups[0], attend([q_blocks[i] for i in groups[0]], near_k, [], False)))
+    states = attend(q_blocks, [(far_k, far_v)], [states[i] for i in range(n_q)], False)
+    for group in groups:
+        done = attend([q_blocks[i] for i in group], last_k[1:], [states[i] for i in group], True)
+        parts.update(zip(group, done))
 
     def mask(bits, index):
         return sum(bit for i, bit in enumerate(bits) if index >> i & 1)

time: 67.9 us -> 58.7 us (0.86)
  Pallas kernels: 22.7 us -> 12.8 us
  starting transfers between devices: 20.4 us -> 19.4 us
  waiting for transfers between devices: 24.1 us -> 25 us
    pallas_call x1, Pallas kernels: 13.1 us -> 2.02 us  [per_device(): pl.pallas_call(pack_kernel, out_shape=[f32(rows, w * DH) for w in (1, 1,...]
    pallas_call x4 -> x5, Pallas kernels: 7.86 us -> 9.07 us  [attend(): pl.pallas_call(functools.partial(attend_kernel, n_q, n_k, rows, bool(prev...]
    ppermute x14 -> x16, starting transfers between devices: 20.4 us -> 19.4 us  [swap(): lax.ppermute(x, AXES, [(i, i ^ flip ^ masks[i // n_kv % 2]) for i in rang...]
    ppermute x14 -> x16, waiting for transfers between devices: 24.1 us -> 25 us  [swap(): lax.ppermute(x, AXES, [(i, i ^ flip ^ masks[i // n_kv % 2]) for i in rang...]
  transfers between devices with their start and end apart: 14 -> 16, of which waited for: 6 -> 7; matrix products, arithmetic and copies ran while one was open for 0% -> 0% of each run, Pallas kernels for 9% -> 13%
where the time goes in v4:
time: 58.7 us; the launch traced here: 57.9 us
  waiting for transfers between devices  25 us (43%)
  starting transfers between devices  19.4 us (33%)
  Pallas kernels  12.8 us (22%)
  between operations  0.73 us (1%)
    ppermute x16, waiting for transfers between devices, swap(): lax.ppermute(x, AXES, [(i, i ^ flip ^ masks[i // n_kv % 2]) for i in rang...  25 us
    ppermute x16, starting transfers between devices, swap(): lax.ppermute(x, AXES, [(i, i ^ flip ^ masks[i // n_kv % 2]) for i in rang...  19.4 us
    pallas_call x5, Pallas kernels, attend(): pl.pallas_call(functools.partial(attend_kernel, n_q, n_k, rows, bool(prev...  9.07 us
    pallas_call x1, Pallas kernels, per_device(): pl.pallas_call(pack_kernel, out_shape=[f32(rows, w * DH) for w in (1, 1,...  2.02 us
    pallas_call x1, Pallas kernels, per_device(): pl.pallas_call(functools.partial(finish_kernel, n_q), out_shape=[f32(rows...  1.6 us
  transfers between devices with their start and end apart: 16, of which 7 were waited for; matrix products, arithmetic and copies ran while one was open for 0% of the time, Pallas kernels for 13%

profile of v4, /device:TPU:0, one launch (start us, length us, event | category | flops | bytes accessed | tf_op | source)
XLA Modules:
  0.0 57.9 jit_solution(8257599338479810662)
XLA Ops:
  0.6 2.0 %shard_map.77 = (f32[128,128]{1,0:T(8,128)S(1)}, f32[128,128]{1,0:T(8,128)S(1)}, f32[128,128]{1,0:T(8,128)S(1)}, f32[128,128]{1,0:T(8,128)S(1)}, f32[128,128]{1,...) custom-call(f32[128,256]{1,0:T(8,128)} %refs_0_.1, f32[128,256]{1,0:T(8,128)} %refs_1_.1, f32[128,256]{1,0:T(8,128)} %refs_2_.1, ...), custom_call_target="tpu_custom_call" | custom-call | tf_op jit(solution)/shard_map/pallas_call | solution.py:221
  2.7 0.5 collective-permute-start
  3.2 1.6 %collective-permute-done.refs_6_ = f32[128,768]{1,0:T(8,128)S(1)} collective-permute-done((f32[128,768]{1,0:T(8,128)}, f32[128,768]{1,0:T(8,128)S(1)}, u32[]{:S(2)}, u32[]{:S(2)}) %collective-permute-start) | collective-permute-done | bytes 393248 | tf_op jit(solution)/shard_map/ppermute | solution.py:214
  4.7 0.1 shard_map.78
  4.8 2.9 %collective-permute-start.5 = (f32[256,512]{1,0:T(8,128)S(1)}, f32[256,512]{1,0:T(8,128)S(1)}, u32[]{:S(2)}, u32[]{:S(2)}) collective-permute-start(f32[256,512]{1,0:T(8,128)S(1)} %get-tuple-element.45.x.refs_2_), channel_id=1, source_target_pairs={{0,8},{1,9},{2,10},{3,11},{4,20},{5,21},{6,22},{7,23},{8,0},{9,1},... | collective-permute-start | bytes 1572872 | tf_op jit(solution)/shard_map/ppermute | solution.py:214
  7.8 2.6 %collective-permute-start.2 = (f32[256,256]{1,0:T(8,128)S(1)}, f32[256,256]{1,0:T(8,128)S(1)}, u32[]{:S(2)}, u32[]{:S(2)}) collective-permute-start(f32[256,256]{1,0:T(8,128)S(1)} %get-tuple-element.44), channel_id=1, source_target_pairs={{0,2},{1,3},{2,0},{3,1},{4,5},{5,4},{6,7},{7,6},{8,10},{9,11},{10,... | collective-permute-start | bytes 786440 | tf_op jit(solution)/shard_map/ppermute | solution.py:214
  10.4 1.6 %collective-permute-start.7 = (f32[256,256]{1,0:T(8,128)S(1)}, f32[256,256]{1,0:T(8,128)S(1)}, u32[]{:S(2)}, u32[]{:S(2)}) collective-permute-start(f32[256,256]{1,0:T(8,128)S(1)} %get-tuple-element.43.refs_0_), channel_id=1, source_target_pairs={{0,1},{1,0},{2,3},{3,2},{4,6},{5,7},{6,4},{7,5},{8,9},{9,8},{10,11... | collective-permute-start | bytes 786440 | tf_op jit(solution)/shard_map/ppermute | solution.py:214
  11.9 1.5 %collective-permute-start.1 = (f32[256,256]{1,0:T(8,128)S(1)}, f32[256,256]{1,0:T(8,128)S(1)}, u32[]{:S(2)}, u32[]{:S(2)}) collective-permute-start(f32[256,256]{1,0:T(8,128)S(1)} %get-tuple-element.43.refs_0_), channel_id=1, source_target_pairs={{0,16},{1,17},{2,18},{3,19},{4,12},{5,13},{6,14},{7,15},{8,24},{9,... | collective-permute-start | bytes 786440 | tf_op jit(solution)/shard_map/ppermute | solution.py:214
  13.5 9.9 %collective-permute-done.2.after.refs_4_ = f32[256,256]{1,0:T(8,128)S(1)} collective-permute-done((f32[256,256]{1,0:T(8,128)S(1)}, f32[256,256]{1,0:T(8,128)S(1)}, u32[]{:S(2)}, u32[]{:S(2)}) %collective-permute-start.2) | collective-permute-done | bytes 262176 | tf_op jit(solution)/shard_map/ppermute | solution.py:214
  23.4 0.1 collective-permute-start.4
  23.5 0.0 collective-permute-done.7.refs_0_.refs_1_
  23.5 1.0 %collective-permute-start.8 = (f32[256,256]{1,0:T(8,128)S(1)}, f32[256,256]{1,0:T(8,128)S(1)}, u32[]{:S(2)}, u32[]{:S(2)}) collective-permute-start(f32[256,256]{1,0:T(8,128)S(1)} %collective-permute-done.7.refs_0_.refs_1_), channel_id=1, source_target_pairs={{0,16},{1,17},{2,18},{3,19},{4,12},{5,13},{6,14},{7,15},{8,24},{9,... | collective-permute-start | bytes 786440 | tf_op jit(solution)/shard_map/ppermute | solution.py:214
  24.5 1.2 %collective-permute-start.3 = (f32[256,256]{1,0:T(8,128)S(1)}, f32[256,256]{1,0:T(8,128)S(1)}, u32[]{:S(2)}, u32[]{:S(2)}) collective-permute-start(f32[256,256]{1,0:T(8,128)S(1)} %collective-permute-done.2.after.refs_4_), channel_id=1, source_target_pairs={{0,8},{1,9},{2,10},{3,11},{4,20},{5,21},{6,22},{7,23},{8,0},{9,1},... | collective-permute-start | bytes 786440 | tf_op jit(solution)/shard_map/ppermute | solution.py:214
  25.7 0.0 collective-permute-done.1.refs_1_.refs_2_
  25.7 0.0 collective-permute-done.5.refs_3_
  25.7 1.8 %shard_map.80 = (f32[256,256]{1,0:T(8,128)S(1)}, f32[256,128]{1,0:T(8,128)S(1)}, f32[256,256]{1,0:T(8,128)S(1)}, f32[256,128]{1,0:T(8,128)S(1)}) custom-call(f32[256,256]{1,0:T(8,128)S(1)} %get-tuple-element.43.refs_0_, f32[256,256]{1,0:T(8,128)S(1)} %collective-permute-done.1.refs_1_.refs_2_, f32[256,512]{1,0:T(8,128)S(1)} %get-tuple-element.45.x.refs_2_, ...), custom_call_target="tpu_custom_call" | custom-call | flops 2415919104 | bytes 3145728 | tf_op jit(solution)/shard_map/pallas_call | solution.py:159
  27.5 6.0 %collective-permute-done.4.x.refs_5_ = f32[256,256]{1,0:T(8,128)S(1)} collective-permute-done((f32[256,256]{1,0:T(8,128)S(1)}, f32[256,256]{1,0:T(8,128)S(1)}, u32[]{:S(2)}, u32[]{:S(2)}) %collective-permute-start.4) | collective-permute-done | bytes 262176 | tf_op jit(solution)/shard_map/ppermute | solution.py:214
  33.5 0.1 collective-permute-start.6
  33.6 1.8 %shard_map.82 = (f32[256,256]{1,0:T(8,128)S(1)}, f32[256,128]{1,0:T(8,128)S(1)}, f32[256,256]{1,0:T(8,128)S(1)}, f32[256,128]{1,0:T(8,128)S(1)}) custom-call(f32[256,256]{1,0:T(8,128)S(1)} %collective-permute-done.7.refs_0_.refs_1_, f32[256,256]{1,0:T(8,128)S(1)} %collective-permute-done.8.refs_1_.refs_3_, f32[256,512]{1,0:T(8,128)S(1)} %get-tuple-element.45.x.refs_2_, ...), custom_call_target="tpu_custom_call" | custom-call | flops 2415919104 | bytes 3145728 | tf_op jit(solution)/shard_map/pallas_call | solution.py:159
  35.4 2.6 %shard_map.83 = (f32[256,256]{1,0:T(8,128)S(1)}, f32[256,128]{1,0:T(8,128)S(1)}, f32[256,256]{1,0:T(8,128)S(1)}, f32[256,128]{1,0:T(8,128)S(1)}, f32[256,256]{1,...) custom-call(f32[256,256]{1,0:T(8,128)S(1)} %get-tuple-element.43.refs_0_, ...), custom_call_target="tpu_custom_call" | custom-call | flops 2415919104 | bytes 4718592 | tf_op jit(solution)/shard_map/pallas_call | solution.py:159
  38.0 1.9 %collective-permute-done.6.refs_3_ = f32[256,256]{1,0:T(8,128)S(1)} collective-permute-done((f32[256,256]{1,0:T(8,128)S(1)}, f32[256,256]{1,0:T(8,128)S(1)}, u32[]{:S(2)}, u32[]{:S(2)}) %collective-permute-start.6) | collective-permute-done | bytes 262176 | tf_op jit(solution)/shard_map/ppermute | solution.py:214
  40.0 1.4 %shard_map.85 = (f32[136,256]{1,0:T(8,128)S(1)}, f32[136,256]{1,0:T(8,128)S(1)}, f32[136,256]{1,0:T(8,128)S(1)}, f32[136,256]{1,0:T(8,128)S(1)}) custom-call(f32[256,256]{1,0:T(8,128)S(1)} %collective-permute-done.7.refs_0_.refs_1_, f32[256,256]{1,0:T(8,128)S(1)} %collective-permute-done.8.refs_1_.refs_3_, f32[256,256]{1,0:T(8,128)S(1)} %collective-permute-done.3.refs_2_, ...), custom_call_target="tpu_custom_call" | custom-call | flops 1207959552 | bytes 2621440 | tf_op jit(solution)/shard_map/pallas_call | solution.py:159
  41.4 0.7 %collective-permute-start.10 = (f32[136,256]{1,0:T(8,128)S(1)}, f32[136,256]{1,0:T(8,128)S(1)}, u32[]{:S(2)}, u32[]{:S(2)}) collective-permute-start(f32[136,256]{1,0:T(8,128)S(1)} %get-tuple-element.64), channel_id=1, source_target_pairs={{0,1},{1,0},{2,3},{3,2},{4,6},{5,7},{6,4},{7,5},{8,9},{9,8},{10,11... | collective-permute-start | bytes 417800 | tf_op jit(solution)/shard_map/ppermute | solution.py:214
  42.1 1.4 %collective-permute-start.14 = (f32[136,256]{1,0:T(8,128)S(1)}, f32[136,256]{1,0:T(8,128)S(1)}, u32[]{:S(2)}, u32[]{:S(2)}) collective-permute-start(f32[136,256]{1,0:T(8,128)S(1)} %get-tuple-element.68), channel_id=1, source_target_pairs={{0,17},{1,16},{2,19},{3,18},{4,14},{5,15},{6,12},{7,13},{8,25},{9,... | collective-permute-start | bytes 417800 | tf_op jit(solution)/shard_map/ppermute | solution.py:214
  43.5 3.2 %collective-permute-start.15 = (f32[136,256]{1,0:T(8,128)S(1)}, f32[136,256]{1,0:T(8,128)S(1)}, u32[]{:S(2)}, u32[]{:S(2)}) collective-permute-start(f32[136,256]{1,0:T(8,128)S(1)} %get-tuple-element.69), channel_id=1, source_target_pairs={{0,21},{1,20},{2,23},{3,22},{4,10},{5,11},{6,8},{7,9},{8,29},{9,28... | collective-permute-start | bytes 417800 | tf_op jit(solution)/shard_map/ppermute | solution.py:214
  46.7 1.4 %shard_map.84 = (f32[136,256]{1,0:T(8,128)S(1)}, f32[136,256]{1,0:T(8,128)S(1)}, f32[136,256]{1,0:T(8,128)S(1)}, f32[136,256]{1,0:T(8,128)S(1)}) custom-call(f32[256,256]{1,0:T(8,128)S(1)} %get-tuple-element.43.refs_0_, f32[256,256]{1,0:T(8,128)S(1)} %collective-permute-done.1.refs_1_.refs_2_, f32[256,256]{1,0:T(8,128)S(1)} %collective-permute-done.3.refs_2_, ...), custom_call_target="tpu_custom_call" | custom-call | flops 1207959552 | bytes 2621440 | tf_op jit(solution)/shard_map/pallas_call | solution.py:159
  48.2 0.7 %collective-permute-start.12 = (f32[136,256]{1,0:T(8,128)S(1)}, f32[136,256]{1,0:T(8,128)S(1)}, u32[]{:S(2)}, u32[]{:S(2)}) collective-permute-start(f32[136,256]{1,0:T(8,128)S(1)} %get-tuple-element.66), channel_id=1, source_target_pairs={{0,16},{1,17},{2,18},{3,19},{4,12},{5,13},{6,14},{7,15},{8,24},{9,... | collective-permute-start | bytes 417800 | tf_op jit(solution)/shard_map/ppermute | solution.py:214
  48.9 1.9 %collective-permute-start.9 = (f32[136,256]{1,0:T(8,128)S(1)}, f32[136,256]{1,0:T(8,128)S(1)}, u32[]{:S(2)}, u32[]{:S(2)}) collective-permute-start(f32[136,256]{1,0:T(8,128)S(1)} %get-tuple-element.59), channel_id=1, source_target_pairs={{0,4},{1,5},{2,6},{3,7},{4,0},{5,1},{6,2},{7,3},{8,12},{9,13},{10,... | collective-permute-start | bytes 417800 | tf_op jit(solution)/shard_map/ppermute | solution.py:214
  50.8 3.3 %collective-permute-done.14.refs_6_ = f32[136,256]{1,0:T(8,128)S(1)} collective-permute-done((f32[136,256]{1,0:T(8,128)S(1)}, f32[136,256]{1,0:T(8,128)S(1)}, u32[]{:S(2)}, u32[]{:S(2)}) %collective-permute-start.14) | collective-permute-done | bytes 139296 | tf_op jit(solution)/shard_map/ppermute | solution.py:214
  54.1 2.1 %collective-permute-done.15.refs_7_ = f32[136,256]{1,0:T(8,128)S(1)} collective-permute-done((f32[136,256]{1,0:T(8,128)S(1)}, f32[136,256]{1,0:T(8,128)S(1)}, u32[]{:S(2)}, u32[]{:S(2)}) %collective-permute-start.15) | collective-permute-done | bytes 139296 | tf_op jit(solution)/shard_map/ppermute | solution.py:214
  56.2 0.1 collective-permute-done.13.refs_5_
  56.3 1.6 %shard_map.86 = (f32[128,256]{1,0:T(8,128)}, f32[128,256]{1,0:T(8,128)}) custom-call(s32[1]{0:T(128)} %bitcast.core_ref, f32[136,256]{1,0:T(8,128)S(1)} %get-tuple-element.58.refs_0_, f32[136,256]{1,0:T(8,128)S(1)} %collective-permute-done.9.refs_1_, f32[136,256]{1,0:T(8,128)S(1)} %collective-permute-done.10.refs_2_, ...), custom_call_target="tpu_custom_call" | custom-call | tf_op jit(solution)/shard_map/pallas_call | solution.py:265
  (10 shorter events, 0.1 us)
Async XLA Ops:
  2.7 2.1 %collective-permute-start = (f32[128,768]{1,0:T(8,128)}, f32[128,768]{1,0:T(8,128)S(1)}, u32[]{:S(2)}, u32[]{:S(2)}) collective-permute-start(f32[128,768]{1,0:T(8,128)} %get-tuple-element.42), channel_id=1, source_target_pairs={{0,4},{1,5},{2,6},{3,7},{4,0},{5,1},{6,2},{7,3},{8,12},{9,13},{10,... | collective-permute-start | bytes 1179656 | tf_op jit(solution)/shard_map/ppermute | solution.py:214
  4.8 20.8 %collective-permute-start.5 = (f32[256,512]{1,0:T(8,128)S(1)}, f32[256,512]{1,0:T(8,128)S(1)}, u32[]{:S(2)}, u32[]{:S(2)}) collective-permute-start(f32[256,512]{1,0:T(8,128)S(1)} %get-tuple-element.45.x.refs_2_), channel_id=1, source_target_pairs={{0,8},{1,9},{2,10},{3,11},{4,20},{5,21},{6,22},{7,23},{8,0},{9,1},... | collective-permute-start | bytes 1572872 | tf_op jit(solution)/shard_map/ppermute | solution.py:214
  7.8 15.6 %collective-permute-start.2 = (f32[256,256]{1,0:T(8,128)S(1)}, f32[256,256]{1,0:T(8,128)S(1)}, u32[]{:S(2)}, u32[]{:S(2)}) collective-permute-start(f32[256,256]{1,0:T(8,128)S(1)} %get-tuple-element.44), channel_id=1, source_target_pairs={{0,2},{1,3},{2,0},{3,1},{4,5},{5,4},{6,7},{7,6},{8,10},{9,11},{10,... | collective-permute-start | bytes 786440 | tf_op jit(solution)/shard_map/ppermute | solution.py:214
  10.4 13.1 %collective-permute-start.7 = (f32[256,256]{1,0:T(8,128)S(1)}, f32[256,256]{1,0:T(8,128)S(1)}, u32[]{:S(2)}, u32[]{:S(2)}) collective-permute-start(f32[256,256]{1,0:T(8,128)S(1)} %get-tuple-element.43.refs_0_), channel_id=1, source_target_pairs={{0,1},{1,0},{2,3},{3,2},{4,6},{5,7},{6,4},{7,5},{8,9},{9,8},{10,11... | collective-permute-start | bytes 786440 | tf_op jit(solution)/shard_map/ppermute | solution.py:214
  11.9 13.8 %collective-permute-start.1 = (f32[256,256]{1,0:T(8,128)S(1)}, f32[256,256]{1,0:T(8,128)S(1)}, u32[]{:S(2)}, u32[]{:S(2)}) collective-permute-start(f32[256,256]{1,0:T(8,128)S(1)} %get-tuple-element.43.refs_0_), channel_id=1, source_target_pairs={{0,16},{1,17},{2,18},{3,19},{4,12},{5,13},{6,14},{7,15},{8,24},{9,... | collective-permute-start | bytes 786440 | tf_op jit(solution)/shard_map/ppermute | solution.py:214
  23.4 10.1 %collective-permute-start.4 = (f32[256,256]{1,0:T(8,128)S(1)}, f32[256,256]{1,0:T(8,128)S(1)}, u32[]{:S(2)}, u32[]{:S(2)}) collective-permute-start(f32[256,256]{1,0:T(8,128)S(1)} %shard_map.79), channel_id=1, source_target_pairs={{0,2},{1,3},{2,0},{3,1},{4,5},{5,4},{6,7},{7,6},{8,10},{9,11},{10,... | collective-permute-start | bytes 786440 | tf_op jit(solution)/shard_map/ppermute | solution.py:214
  23.5 10.1 %collective-permute-start.8 = (f32[256,256]{1,0:T(8,128)S(1)}, f32[256,256]{1,0:T(8,128)S(1)}, u32[]{:S(2)}, u32[]{:S(2)}) collective-permute-start(f32[256,256]{1,0:T(8,128)S(1)} %collective-permute-done.7.refs_0_.refs_1_), channel_id=1, source_target_pairs={{0,16},{1,17},{2,18},{3,19},{4,12},{5,13},{6,14},{7,15},{8,24},{9,... | collective-permute-start | bytes 786440 | tf_op jit(solution)/shard_map/ppermute | solution.py:214
  24.5 13.5 %collective-permute-start.3 = (f32[256,256]{1,0:T(8,128)S(1)}, f32[256,256]{1,0:T(8,128)S(1)}, u32[]{:S(2)}, u32[]{:S(2)}) collective-permute-start(f32[256,256]{1,0:T(8,128)S(1)} %collective-permute-done.2.after.refs_4_), channel_id=1, source_target_pairs={{0,8},{1,9},{2,10},{3,11},{4,20},{5,21},{6,22},{7,23},{8,0},{9,1},... | collective-permute-start | bytes 786440 | tf_op jit(solution)/shard_map/ppermute | solution.py:214
  33.5 6.4 %collective-permute-start.6 = (f32[256,256]{1,0:T(8,128)S(1)}, f32[256,256]{1,0:T(8,128)S(1)}, u32[]{:S(2)}, u32[]{:S(2)}) collective-permute-start(f32[256,256]{1,0:T(8,128)S(1)} %shard_map.81), channel_id=1, source_target_pairs={{0,8},{1,9},{2,10},{3,11},{4,20},{5,21},{6,22},{7,23},{8,0},{9,1},... | collective-permute-start | bytes 786440 | tf_op jit(solution)/shard_map/ppermute | solution.py:214
  41.4 7.5 %collective-permute-start.10 = (f32[136,256]{1,0:T(8,128)S(1)}, f32[136,256]{1,0:T(8,128)S(1)}, u32[]{:S(2)}, u32[]{:S(2)}) collective-permute-start(f32[136,256]{1,0:T(8,128)S(1)} %get-tuple-element.64), channel_id=1, source_target_pairs={{0,1},{1,0},{2,3},{3,2},{4,6},{5,7},{6,4},{7,5},{8,9},{9,8},{10,11... | collective-permute-start | bytes 417800 | tf_op jit(solution)/shard_map/ppermute | solution.py:214
  42.1 6.8 %collective-permute-start.11 = (f32[136,256]{1,0:T(8,128)S(1)}, f32[136,256]{1,0:T(8,128)S(1)}, u32[]{:S(2)}, u32[]{:S(2)}) collective-permute-start(f32[136,256]{1,0:T(8,128)S(1)} %get-tuple-element.65), channel_id=1, source_target_pairs={{0,5},{1,4},{2,7},{3,6},{4,2},{5,3},{6,0},{7,1},{8,13},{9,12},{10,... | collective-permute-start | bytes 417800 | tf_op jit(solution)/shard_map/ppermute | solution.py:214
  42.1 12.0 %collective-permute-start.14 = (f32[136,256]{1,0:T(8,128)S(1)}, f32[136,256]{1,0:T(8,128)S(1)}, u32[]{:S(2)}, u32[]{:S(2)}) collective-permute-start(f32[136,256]{1,0:T(8,128)S(1)} %get-tuple-element.68), channel_id=1, source_target_pairs={{0,17},{1,16},{2,19},{3,18},{4,14},{5,15},{6,12},{7,13},{8,25},{9,... | collective-permute-start | bytes 417800 | tf_op jit(solution)/shard_map/ppermute | solution.py:214
  43.5 12.7 %collective-permute-start.15 = (f32[136,256]{1,0:T(8,128)S(1)}, f32[136,256]{1,0:T(8,128)S(1)}, u32[]{:S(2)}, u32[]{:S(2)}) collective-permute-start(f32[136,256]{1,0:T(8,128)S(1)} %get-tuple-element.69), channel_id=1, source_target_pairs={{0,21},{1,20},{2,23},{3,22},{4,10},{5,11},{6,8},{7,9},{8,29},{9,28... | collective-permute-start | bytes 417800 | tf_op jit(solution)/shard_map/ppermute | solution.py:214
  48.2 8.0 %collective-permute-start.12 = (f32[136,256]{1,0:T(8,128)S(1)}, f32[136,256]{1,0:T(8,128)S(1)}, u32[]{:S(2)}, u32[]{:S(2)}) collective-permute-start(f32[136,256]{1,0:T(8,128)S(1)} %get-tuple-element.66), channel_id=1, source_target_pairs={{0,16},{1,17},{2,18},{3,19},{4,12},{5,13},{6,14},{7,15},{8,24},{9,... | collective-permute-start | bytes 417800 | tf_op jit(solution)/shard_map/ppermute | solution.py:214
  48.9 7.4 %collective-permute-start.13 = (f32[136,256]{1,0:T(8,128)S(1)}, f32[136,256]{1,0:T(8,128)S(1)}, u32[]{:S(2)}, u32[]{:S(2)}) collective-permute-start(f32[136,256]{1,0:T(8,128)S(1)} %get-tuple-element.67), channel_id=1, source_target_pairs={{0,20},{1,21},{2,22},{3,23},{4,8},{5,9},{6,10},{7,11},{8,28},{9,29... | collective-permute-start | bytes 417800 | tf_op jit(solution)/shard_map/ppermute | solution.py:214
  48.9 7.4 %collective-permute-start.9 = (f32[136,256]{1,0:T(8,128)S(1)}, f32[136,256]{1,0:T(8,128)S(1)}, u32[]{:S(2)}, u32[]{:S(2)}) collective-permute-start(f32[136,256]{1,0:T(8,128)S(1)} %get-tuple-element.59), channel_id=1, source_target_pairs={{0,4},{1,5},{2,6},{3,7},{4,0},{5,1},{6,2},{7,3},{8,12},{9,13},{10,... | collective-permute-start | bytes 417800 | tf_op jit(solution)/shard_map/ppermute | solution.py:214

commit v5 on v4

--- a/solution.py
+++ b/solution.py
@@ -135,19 +135,15 @@
             total_t += factor * old[:, 2:3]
             numer += factor * prev[2 * b][:, :DH]
             numer_t += factor * prev[2 * b][:, DH:]
-        stats = jnp.where(lane == 0, peak, jnp.where(lane == 1, total, total_t))
         if last:
             half = rows // 2
             for i in range(2):
                 at = slice(i * half, (i + 1) * half)
-                outs[2 * b + i][0:half, :DH] = numer[at]
-                outs[2 * b + i][0:half, DH:] = numer_t[at]
-                flat = stats[at].T[0:STAT_ROWS, :]
-                outs[2 * b + i][half:, :] = jnp.concatenate([flat, jnp.zeros_like(flat)], axis=1)
+                store_part(outs[2 * b + i], *(x[at] for x in (peak, total, total_t, numer, numer_t)))
         else:
             outs[2 * b][:, :DH] = numer
             outs[2 * b][:, DH:] = numer_t
-            outs[2 * b + 1][...] = stats
+            outs[2 * b + 1][...] = jnp.where(lane == 0, peak, jnp.where(lane == 1, total, total_t))
 
 
 def attend(q_blocks, k_blocks, prev, last):
@@ -168,26 +164,44 @@
     return [tuple(outs[i : i + 2]) for i in range(0, 2 * n_q, 2)]
 
 
-def finish_kernel(n_q, core_ref, *refs):
-    part_refs = refs[: 2 * n_q]
-    out, tan = refs[2 * n_q :]
-    rows = out.shape[0]
-    for group, head in ((part_refs[0::2], core_ref[0]), (part_refs[1::2], 1 - core_ref[0])):
-        wides = [
-            jnp.concatenate(
-                [ref[rows:, :DH], jnp.zeros((DH - STAT_ROWS, DH), jnp.float32)], axis=0
-            ).T
-            for ref in group
-        ]
-        peaks = [wide[:, 0:1] for wide in wides]
-        top = functools.reduce(jnp.maximum, peaks)
-        total = total_t = numer = numer_t = 0.0
-        for ref, wide, peak in zip(group, wides, peaks):
-            factor = jnp.exp2(peak - top)
-            total += factor * wide[:, 1:2]
-            total_t += factor * wide[:, 2:3]
-            numer += factor * ref[0:rows, :DH]
-            numer_t += factor * ref[0:rows, DH:]
+def merge(refs):
+    rows = refs[0].shape[0] - STAT_ROWS
+    wides = [
+        jnp.concatenate(
+            [ref[rows:, :DH], jnp.zeros((DH - STAT_ROWS, DH), jnp.float32)], axis=0
+        ).T
+        for ref in refs
+    ]
+    peaks = [wide[:, 0:1] for wide in wides]
+    top = functools.reduce(jnp.maximum, peaks)
+    total = total_t = numer = numer_t = 0.0
+    for ref, wide, peak in zip(refs, wides, peaks):
+        factor = jnp.exp2(peak - top)
+        total += factor * wide[:, 1:2]
+        total_t += factor * wide[:, 2:3]
+        numer += factor * ref[0:rows, :DH]
+        numer_t += factor * ref[0:rows, DH:]
+    return top, total, total_t, numer, numer_t
+
+
+def store_part(out, peak, total, total_t, numer, numer_t):
+    rows = out.shape[0] - STAT_ROWS
+    lane = lax.broadcasted_iota(jnp.int32, (rows, DH), 1)
+    stats = jnp.where(lane == 0, peak, jnp.where(lane == 1, total, total_t))
+    flat = stats.T[0:STAT_ROWS, :]
+    out[0:rows, :DH] = numer
+    out[0:rows, DH:] = numer_t
+    out[rows:, :] = jnp.concatenate([flat, jnp.zeros_like(flat)], axis=1)
+
+
+def merge_kernel(one, two, out):
+    store_part(out, *merge([one, two]))
+
+
+def finish_kernel(n_own, core_ref, *refs):
+    *part_refs, out, tan = refs
+    for group, head in ((part_refs[:n_own], core_ref[0]), (part_refs[n_own:], 1 - core_ref[0])):
+        _, total, total_t, numer, numer_t = merge(group)
         attended = numer / total
         column = pl.multiple_of(head * DH, DH)
         out[:, pl.ds(column, DH)] = attended
@@ -240,34 +254,41 @@
     for masks in near:
         near_k += [tuple(swap(x, masks) for x in block) for block in near_k]
     far_k = swap(mine_k, far)
-    far_v = swap(later(mine_kv, 2 * DH, far_k), far)
+    far_v = swap(later(mine_kv, 2 * DH, near_k[-1][0]), far)
     n_q = len(q_blocks)
-    groups = [list(range(1, n_q, 2)), list(range(0, n_q, 2))]
-    states, parts = {}, {}
-    states.update(zip(groups[1], attend([q_blocks[i] for i in groups[1]], near_k, [], False)))
+    top_bit = n_q // 2
+    far_q, near_q = list(range(1, n_q, 2)), list(range(0, n_q, 2))
+    states = dict(zip(near_q, attend([q_blocks[i] for i in near_q], near_k, [], False)))
     last_k = [(far_k, later(far_v, 2 * DH, states[0][1]))]
     for masks in near:
         last_k += [tuple(swap(x, masks) for x in block) for block in last_k]
-    states.update(zip(groups[0], attend([q_blocks[i] for i in groups[0]], near_k, [], False)))
+    states.update(zip(far_q, attend([q_blocks[i] for i in far_q], near_k, [], False)))
     states = attend(q_blocks, [(far_k, far_v)], [states[i] for i in range(n_q)], False)
-    for group in groups:
+    parts = {}
+    for group in (
+        [i for i in far_q if i & top_bit], [i for i in far_q if not i & top_bit], near_q
+    ):
         done = attend([q_blocks[i] for i in group], last_k[1:], [states[i] for i in group], True)
         parts.update(zip(group, done))
 
-    def mask(bits, index):
-        return sum(bit for i, bit in enumerate(bits) if index >> i & 1)
-
-    back = []
-    for i in range(n_q):
-        masks = (mask(q_bits[0], i), mask(q_bits[1], i))
-        back += [swap(parts[i][0], masks) if i else parts[i][0], swap(parts[i][1], masks, True)]
+    def masks_of(index):
+        return tuple(sum(bit for i, bit in enumerate(bits) if index >> i & 1) for bits in q_bits)
+
+    own = [parts[0][0]] + [swap(parts[i][0], masks_of(i)) for i in range(1, n_q)]
+    cross = [swap(parts[0][1], masks_of(0), True), swap(parts[top_bit][1], masks_of(top_bit), True)]
+    for i in range(1, top_bit):
+        beside = swap(parts[i | top_bit][1], masks_of(top_bit))
+        merged = pl.pallas_call(
+            merge_kernel, out_shape=f32(rows + STAT_ROWS, 2 * DH), compiler_params=params(8)
+        )(parts[i][1], beside)
+        cross.append(swap(merged, masks_of(i), True))
     return tuple(
         pl.pallas_call(
             functools.partial(finish_kernel, n_q),
             out_shape=[f32(rows, width)] * 2,
-            in_specs=[smem] + [vmem] * (2 * n_q),
+            in_specs=[smem] + [vmem] * (n_q + len(cross)),
             compiler_params=params(8),
-        )(core, *back)
+        )(core, *own, *cross)
     )
 
 

time: 58.7 us -> 53.8 us (0.917); the launches traced: 57.9 us -> 53.7 us
  waiting for transfers between devices: 25 us -> 16.5 us
  starting transfers between devices: 19.4 us -> 22.9 us
  Pallas kernels: 12.8 us -> 13.6 us
    ppermute x16, waiting for transfers between devices: 25 us -> 16.5 us  [swap(): lax.ppermute(x, AXES, [(i, i ^ flip ^ masks[i // n_kv % 2]) for i in rang...]
    ppermute x16, starting transfers between devices: 19.4 us -> 22.9 us  [swap(): lax.ppermute(x, AXES, [(i, i ^ flip ^ masks[i // n_kv % 2]) for i in rang...]
    pallas_call x5 -> x6, Pallas kernels: 9.07 us -> 9.5 us  [attend(): pl.pallas_call(functools.partial(attend_kernel, n_q, n_k, rows, bool(prev...]
  transfers between devices with their start and end apart: 16 -> 16, of which waited for: 7 -> 11; matrix products, arithmetic and copies ran while one was open for 0% -> 0% of each run, Pallas kernels for 13% -> 17%
where the time goes in v5:
time: 53.8 us; the launch traced here: 53.7 us
  starting transfers between devices  22.9 us (43%)
  waiting for transfers between devices  16.5 us (31%)
  Pallas kernels  13.6 us (25%)
  between operations  0.7 us (1%)
    ppermute x16, starting transfers between devices, swap(): lax.ppermute(x, AXES, [(i, i ^ flip ^ masks[i // n_kv % 2]) for i in rang...  22.9 us
    ppermute x16, waiting for transfers between devices, swap(): lax.ppermute(x, AXES, [(i, i ^ flip ^ masks[i // n_kv % 2]) for i in rang...  16.5 us
    pallas_call x6, Pallas kernels, attend(): pl.pallas_call(functools.partial(attend_kernel, n_q, n_k, rows, bool(prev...  9.5 us
    pallas_call x1, Pallas kernels, per_device(): pl.pallas_call(pack_kernel, out_shape=[f32(rows, w * DH) for w in (1, 1,...  2.01 us
    pallas_call x1, Pallas kernels, per_device(): pl.pallas_call(functools.partial(finish_kernel, n_q), out_shape=[f32(rows...  1.51 us
  transfers between devices with their start and end apart: 16, of which 11 were waited for; matrix products, arithmetic and copies ran while one was open for 0% of the time, Pallas kernels for 17%

profile of v5, /device:TPU:0, one launch (start us, length us, event | category | flops | bytes accessed | tf_op | source)
XLA Modules:
  0.0 53.7 jit_solution(17375431918352110840)
XLA Ops:
  0.6 2.0 %shard_map.77 = (f32[128,128]{1,0:T(8,128)S(1)}, f32[128,128]{1,0:T(8,128)S(1)}, f32[128,128]{1,0:T(8,128)S(1)}, f32[128,128]{1,0:T(8,128)S(1)}, f32[128,128]{1,...) custom-call(f32[128,256]{1,0:T(8,128)} %refs_0_.1, f32[128,256]{1,0:T(8,128)} %refs_1_.1, f32[128,256]{1,0:T(8,128)} %refs_2_.1, ...), custom_call_target="tpu_custom_call" | custom-call | tf_op jit(solution)/shard_map/pallas_call | solution.py:235
  2.7 0.5 collective-permute-start
  3.2 1.6 %collective-permute-done.refs_6_ = f32[128,768]{1,0:T(8,128)S(1)} collective-permute-done((f32[128,768]{1,0:T(8,128)}, f32[128,768]{1,0:T(8,128)S(1)}, u32[]{:S(2)}, u32[]{:S(2)}) %collective-permute-start) | collective-permute-done | bytes 393248 | tf_op jit(solution)/shard_map/ppermute | solution.py:228
  4.8 2.9 %collective-permute-start.4 = (f32[256,512]{1,0:T(8,128)S(1)}, f32[256,512]{1,0:T(8,128)S(1)}, u32[]{:S(2)}, u32[]{:S(2)}) collective-permute-start(f32[256,512]{1,0:T(8,128)S(1)} %get-tuple-element.45.x.refs_2_), channel_id=1, source_target_pairs={{0,8},{1,9},{2,10},{3,11},{4,20},{5,21},{6,22},{7,23},{8,0},{9,1},... | collective-permute-start | bytes 1572872 | tf_op jit(solution)/shard_map/ppermute | solution.py:228
  7.8 1.6 %collective-permute-start.7 = (f32[256,256]{1,0:T(8,128)S(1)}, f32[256,256]{1,0:T(8,128)S(1)}, u32[]{:S(2)}, u32[]{:S(2)}) collective-permute-start(f32[256,256]{1,0:T(8,128)S(1)} %get-tuple-element.43.refs_0_), channel_id=1, source_target_pairs={{0,1},{1,0},{2,3},{3,2},{4,6},{5,7},{6,4},{7,5},{8,9},{9,8},{10,11... | collective-permute-start | bytes 786440 | tf_op jit(solution)/shard_map/ppermute | solution.py:228
  9.3 2.6 %collective-permute-start.2 = (f32[256,256]{1,0:T(8,128)S(1)}, f32[256,256]{1,0:T(8,128)S(1)}, u32[]{:S(2)}, u32[]{:S(2)}) collective-permute-start(f32[256,256]{1,0:T(8,128)S(1)} %get-tuple-element.44), channel_id=1, source_target_pairs={{0,2},{1,3},{2,0},{3,1},{4,5},{5,4},{6,7},{7,6},{8,10},{9,11},{10,... | collective-permute-start | bytes 786440 | tf_op jit(solution)/shard_map/ppermute | solution.py:228
  11.9 1.5 %collective-permute-start.1 = (f32[256,256]{1,0:T(8,128)S(1)}, f32[256,256]{1,0:T(8,128)S(1)}, u32[]{:S(2)}, u32[]{:S(2)}) collective-permute-start(f32[256,256]{1,0:T(8,128)S(1)} %get-tuple-element.43.refs_0_), channel_id=1, source_target_pairs={{0,16},{1,17},{2,18},{3,19},{4,12},{5,13},{6,14},{7,15},{8,24},{9,... | collective-permute-start | bytes 786440 | tf_op jit(solution)/shard_map/ppermute | solution.py:228
  13.4 2.5 %collective-permute-done.4.after.refs_3_ = f32[256,512]{1,0:T(8,128)S(1)} collective-permute-done((f32[256,512]{1,0:T(8,128)S(1)}, f32[256,512]{1,0:T(8,128)S(1)}, u32[]{:S(2)}, u32[]{:S(2)}) %collective-permute-start.4) | collective-permute-done | bytes 524320 | tf_op jit(solution)/shard_map/ppermute | solution.py:228
  16.0 4.9 %collective-permute-start.5 = (f32[256,256]{1,0:T(8,128)S(1)}, f32[256,256]{1,0:T(8,128)S(1)}, u32[]{:S(2)}, u32[]{:S(2)}) collective-permute-start(f32[256,256]{1,0:T(8,128)S(1)} %shard_map.79), channel_id=1, source_target_pairs={{0,2},{1,3},{2,0},{3,1},{4,5},{5,4},{6,7},{7,6},{8,10},{9,11},{10,... | collective-permute-start | bytes 786440 | tf_op jit(solution)/shard_map/ppermute | solution.py:228
  20.9 1.1 %collective-permute-done.7.refs_0_.refs_1_ = f32[256,256]{1,0:T(8,128)S(1)} collective-permute-done((f32[256,256]{1,0:T(8,128)S(1)}, f32[256,256]{1,0:T(8,128)S(1)}, u32[]{:S(2)}, u32[]{:S(2)}) %collective-permute-start.7) | collective-permute-done | bytes 262176 | tf_op jit(solution)/shard_map/ppermute | solution.py:228
  22.1 0.6 %collective-permute-start.8 = (f32[256,256]{1,0:T(8,128)S(1)}, f32[256,256]{1,0:T(8,128)S(1)}, u32[]{:S(2)}, u32[]{:S(2)}) collective-permute-start(f32[256,256]{1,0:T(8,128)S(1)} %collective-permute-done.7.refs_0_.refs_1_), channel_id=1, source_target_pairs={{0,16},{1,17},{2,18},{3,19},{4,12},{5,13},{6,14},{7,15},{8,24},{9,... | collective-permute-start | bytes 786440 | tf_op jit(solution)/shard_map/ppermute | solution.py:228
  22.7 1.4 %collective-permute-start.3 = (f32[256,256]{1,0:T(8,128)S(1)}, f32[256,256]{1,0:T(8,128)S(1)}, u32[]{:S(2)}, u32[]{:S(2)}) collective-permute-start(f32[256,256]{1,0:T(8,128)S(1)} %collective-permute-done.2.refs_4_), channel_id=1, source_target_pairs={{0,8},{1,9},{2,10},{3,11},{4,20},{5,21},{6,22},{7,23},{8,0},{9,1},... | collective-permute-start | bytes 786440 | tf_op jit(solution)/shard_map/ppermute | solution.py:228
  24.1 1.8 %shard_map.80 = (f32[256,256]{1,0:T(8,128)S(1)}, f32[256,128]{1,0:T(8,128)S(1)}, f32[256,256]{1,0:T(8,128)S(1)}, f32[256,128]{1,0:T(8,128)S(1)}) custom-call(f32[256,256]{1,0:T(8,128)S(1)} %get-tuple-element.43.refs_0_, f32[256,256]{1,0:T(8,128)S(1)} %collective-permute-done.1.refs_1_.refs_2_, f32[256,512]{1,0:T(8,128)S(1)} %get-tuple-element.45.x.refs_2_, ...), custom_call_target="tpu_custom_call" | custom-call | flops 2415919104 | bytes 3145728 | tf_op jit(solution)/shard_map/pallas_call | solution.py:155
  25.9 3.3 %collective-permute-done.5.x.refs_5_ = f32[256,256]{1,0:T(8,128)S(1)} collective-permute-done((f32[256,256]{1,0:T(8,128)S(1)}, f32[256,256]{1,0:T(8,128)S(1)}, u32[]{:S(2)}, u32[]{:S(2)}) %collective-permute-start.5) | collective-permute-done | bytes 262176 | tf_op jit(solution)/shard_map/ppermute | solution.py:228
  29.6 0.8 %collective-permute-done.8.refs_1_.refs_3_.refs_0_ = f32[256,256]{1,0:T(8,128)S(1)} collective-permute-done((f32[256,256]{1,0:T(8,128)S(1)}, f32[256,256]{1,0:T(8,128)S(1)}, u32[]{:S(2)}, u32[]{:S(2)}) %collective-permute-start.8) | collective-permute-done | bytes 262176 | tf_op jit(solution)/shard_map/ppermute | solution.py:228
  30.4 1.8 %shard_map.82 = (f32[256,256]{1,0:T(8,128)S(1)}, f32[256,128]{1,0:T(8,128)S(1)}, f32[256,256]{1,0:T(8,128)S(1)}, f32[256,128]{1,0:T(8,128)S(1)}) custom-call(f32[256,256]{1,0:T(8,128)S(1)} %collective-permute-done.7.refs_0_.refs_1_, f32[256,256]{1,0:T(8,128)S(1)} %collective-permute-done.8.refs_1_.refs_3_.refs_0_, ...), custom_call_target="tpu_custom_call" | custom-call | flops 2415919104 | bytes 3145728 | tf_op jit(solution)/shard_map/pallas_call | solution.py:155
  32.2 2.6 %shard_map.83 = (f32[256,256]{1,0:T(8,128)S(1)}, f32[256,128]{1,0:T(8,128)S(1)}, f32[256,256]{1,0:T(8,128)S(1)}, f32[256,128]{1,0:T(8,128)S(1)}, f32[256,256]{1,...) custom-call(f32[256,256]{1,0:T(8,128)S(1)} %get-tuple-element.43.refs_0_, ...), custom_call_target="tpu_custom_call" | custom-call | flops 2415919104 | bytes 4718592 | tf_op jit(solution)/shard_map/pallas_call | solution.py:155
  34.8 0.8 %collective-permute-done.6.refs_3_.refs_2_ = f32[256,256]{1,0:T(8,128)S(1)} collective-permute-done((f32[256,256]{1,0:T(8,128)S(1)}, f32[256,256]{1,0:T(8,128)S(1)}, u32[]{:S(2)}, u32[]{:S(2)}) %collective-permute-start.6) | collective-permute-done | bytes 262176 | tf_op jit(solution)/shard_map/ppermute | solution.py:228
  35.6 0.9 %shard_map.86 = (f32[136,256]{1,0:T(8,128)S(1)}, f32[136,256]{1,0:T(8,128)S(1)}) custom-call(f32[256,256]{1,0:T(8,128)S(1)} %collective-permute-done.8.refs_1_.refs_3_.refs_0_, f32[256,256]{1,0:T(8,128)S(1)} %collective-permute-done.3.refs_2_.refs_1_, f32[256,256]{1,0:T(8,128)S(1)} %collective-permute-done.6.refs_3_.refs_2_, ...), custom_call_target="tpu_custom_call" | custom-call | flops 603979776 | bytes 1572864 | tf_op jit(solution)/shard_map/pallas_call | solution.py:155
  36.5 0.8 %collective-permute-start.14 = (f32[136,256]{1,0:T(8,128)S(1)}, f32[136,256]{1,0:T(8,128)S(1)}, u32[]{:S(2)}, u32[]{:S(2)}) collective-permute-start(f32[136,256]{1,0:T(8,128)S(1)} %get-tuple-element.69), channel_id=1, source_target_pairs={{0,16},{1,17},{2,18},{3,19},{4,12},{5,13},{6,14},{7,15},{8,24},{9,... | collective-permute-start | bytes 417800 | tf_op jit(solution)/shard_map/ppermute | solution.py:228
  37.4 1.2 %collective-permute-start.11 = (f32[136,256]{1,0:T(8,128)S(1)}, f32[136,256]{1,0:T(8,128)S(1)}, u32[]{:S(2)}, u32[]{:S(2)}) collective-permute-start(f32[136,256]{1,0:T(8,128)S(1)} %get-tuple-element.65), channel_id=1, source_target_pairs={{0,17},{1,16},{2,19},{3,18},{4,14},{5,15},{6,12},{7,13},{8,25},{9,... | collective-permute-start | bytes 417800 | tf_op jit(solution)/shard_map/ppermute | solution.py:228
  38.6 0.9 %shard_map.85 = (f32[136,256]{1,0:T(8,128)S(1)}, f32[136,256]{1,0:T(8,128)S(1)}) custom-call(f32[256,256]{1,0:T(8,128)S(1)} %collective-permute-done.7.refs_0_.refs_1_, f32[256,256]{1,0:T(8,128)S(1)} %collective-permute-done.3.refs_2_.refs_1_, f32[256,256]{1,0:T(8,128)S(1)} %collective-permute-done.6.refs_3_.refs_2_, ...), custom_call_target="tpu_custom_call" | custom-call | flops 603979776 | bytes 1572864 | tf_op jit(solution)/shard_map/pallas_call | solution.py:155
  39.5 1.5 %collective-permute-start.9 = (f32[136,256]{1,0:T(8,128)S(1)}, f32[136,256]{1,0:T(8,128)S(1)}, u32[]{:S(2)}, u32[]{:S(2)}) collective-permute-start(f32[136,256]{1,0:T(8,128)S(1)} %get-tuple-element.61), channel_id=1, source_target_pairs={{0,1},{1,0},{2,3},{3,2},{4,6},{5,7},{6,4},{7,5},{8,9},{9,8},{10,11... | collective-permute-start | bytes 417800 | tf_op jit(solution)/shard_map/ppermute | solution.py:228
  41.0 1.5 %shard_map.84 = (f32[136,256]{1,0:T(8,128)S(1)}, f32[136,256]{1,0:T(8,128)S(1)}, f32[136,256]{1,0:T(8,128)S(1)}, f32[136,256]{1,0:T(8,128)S(1)}) custom-call(f32[256,256]{1,0:T(8,128)S(1)} %get-tuple-element.43.refs_0_, f32[256,256]{1,0:T(8,128)S(1)} %collective-permute-done.1.refs_1_.refs_2_, f32[256,256]{1,0:T(8,128)S(1)} %collective-permute-done.3.refs_2_.refs_1_, ...), custom_call_target="tpu_custom_call" | custom-call | flops 1207959552 | bytes 2621440 | tf_op jit(solution)/shard_map/pallas_call | solution.py:155
  42.5 0.8 %collective-permute-start.10 = (f32[136,256]{1,0:T(8,128)S(1)}, f32[136,256]{1,0:T(8,128)S(1)}, u32[]{:S(2)}, u32[]{:S(2)}) collective-permute-start(f32[136,256]{1,0:T(8,128)S(1)} %get-tuple-element.62), channel_id=1, source_target_pairs={{0,16},{1,17},{2,18},{3,19},{4,12},{5,13},{6,14},{7,15},{8,24},{9,... | collective-permute-start | bytes 417800 | tf_op jit(solution)/shard_map/ppermute | solution.py:228
  43.4 1.4 %collective-permute-start.13 = (f32[136,256]{1,0:T(8,128)S(1)}, f32[136,256]{1,0:T(8,128)S(1)}, u32[]{:S(2)}, u32[]{:S(2)}) collective-permute-start(f32[136,256]{1,0:T(8,128)S(1)} %get-tuple-element.67), channel_id=1, source_target_pairs={{0,20},{1,21},{2,22},{3,23},{4,8},{5,9},{6,10},{7,11},{8,28},{9,29... | collective-permute-start | bytes 417800 | tf_op jit(solution)/shard_map/ppermute | solution.py:228
  44.7 0.4 shard_map.87
  45.3 0.6 %collective-permute-start.15 = (f32[136,256]{1,0:T(8,128)S(1)}, f32[136,256]{1,0:T(8,128)S(1)}, u32[]{:S(2)}, u32[]{:S(2)}) collective-permute-start(f32[136,256]{1,0:T(8,128)S(1)} %shard_map.87), channel_id=1, source_target_pairs={{0,5},{1,4},{2,7},{3,6},{4,2},{5,3},{6,0},{7,1},{8,13},{9,12},{10,... | collective-permute-start | bytes 417800 | tf_op jit(solution)/shard_map/ppermute | solution.py:228
  45.9 0.5 collective-permute-done.9.refs_1_
  46.4 1.2 %collective-permute-done.10.refs_2_ = f32[136,256]{1,0:T(8,128)S(1)} collective-permute-done((f32[136,256]{1,0:T(8,128)S(1)}, f32[136,256]{1,0:T(8,128)S(1)}, u32[]{:S(2)}, u32[]{:S(2)}) %collective-permute-start.10) | collective-permute-done | bytes 139296 | tf_op jit(solution)/shard_map/ppermute | solution.py:228
  47.9 4.3 %collective-permute-done.15.refs_6_ = f32[136,256]{1,0:T(8,128)S(1)} collective-permute-done((f32[136,256]{1,0:T(8,128)S(1)}, f32[136,256]{1,0:T(8,128)S(1)}, u32[]{:S(2)}, u32[]{:S(2)}) %collective-permute-start.15) | collective-permute-done | bytes 139296 | tf_op jit(solution)/shard_map/ppermute | solution.py:228
  52.2 1.5 %shard_map.88 = (f32[128,256]{1,0:T(8,128)}, f32[128,256]{1,0:T(8,128)}) custom-call(s32[1]{0:T(128)} %bitcast.core_ref, f32[136,256]{1,0:T(8,128)S(1)} %get-tuple-element.58.refs_0_, f32[136,256]{1,0:T(8,128)S(1)} %collective-permute-done.9.refs_1_, f32[136,256]{1,0:T(8,128)S(1)} %collective-permute-done.10.refs_2_, ...), custom_call_target="tpu_custom_call" | custom-call | tf_op jit(solution)/shard_map/pallas_call | solution.py:286
  (12 shorter events, 0.9 us)
Async XLA Ops:
  2.7 2.1 %collective-permute-start = (f32[128,768]{1,0:T(8,128)}, f32[128,768]{1,0:T(8,128)S(1)}, u32[]{:S(2)}, u32[]{:S(2)}) collective-permute-start(f32[128,768]{1,0:T(8,128)} %get-tuple-element.42), channel_id=1, source_target_pairs={{0,4},{1,5},{2,6},{3,7},{4,0},{5,1},{6,2},{7,3},{8,12},{9,13},{10,... | collective-permute-start | bytes 1179656 | tf_op jit(solution)/shard_map/ppermute | solution.py:228
  4.8 11.2 %collective-permute-start.4 = (f32[256,512]{1,0:T(8,128)S(1)}, f32[256,512]{1,0:T(8,128)S(1)}, u32[]{:S(2)}, u32[]{:S(2)}) collective-permute-start(f32[256,512]{1,0:T(8,128)S(1)} %get-tuple-element.45.x.refs_2_), channel_id=1, source_target_pairs={{0,8},{1,9},{2,10},{3,11},{4,20},{5,21},{6,22},{7,23},{8,0},{9,1},... | collective-permute-start | bytes 1572872 | tf_op jit(solution)/shard_map/ppermute | solution.py:228
  7.8 14.3 %collective-permute-start.7 = (f32[256,256]{1,0:T(8,128)S(1)}, f32[256,256]{1,0:T(8,128)S(1)}, u32[]{:S(2)}, u32[]{:S(2)}) collective-permute-start(f32[256,256]{1,0:T(8,128)S(1)} %get-tuple-element.43.refs_0_), channel_id=1, source_target_pairs={{0,1},{1,0},{2,3},{3,2},{4,6},{5,7},{6,4},{7,5},{8,9},{9,8},{10,11... | collective-permute-start | bytes 786440 | tf_op jit(solution)/shard_map/ppermute | solution.py:228
  9.3 13.4 %collective-permute-start.2 = (f32[256,256]{1,0:T(8,128)S(1)}, f32[256,256]{1,0:T(8,128)S(1)}, u32[]{:S(2)}, u32[]{:S(2)}) collective-permute-start(f32[256,256]{1,0:T(8,128)S(1)} %get-tuple-element.44), channel_id=1, source_target_pairs={{0,2},{1,3},{2,0},{3,1},{4,5},{5,4},{6,7},{7,6},{8,10},{9,11},{10,... | collective-permute-start | bytes 786440 | tf_op jit(solution)/shard_map/ppermute | solution.py:228
  11.9 12.1 %collective-permute-start.1 = (f32[256,256]{1,0:T(8,128)S(1)}, f32[256,256]{1,0:T(8,128)S(1)}, u32[]{:S(2)}, u32[]{:S(2)}) collective-permute-start(f32[256,256]{1,0:T(8,128)S(1)} %get-tuple-element.43.refs_0_), channel_id=1, source_target_pairs={{0,16},{1,17},{2,18},{3,19},{4,12},{5,13},{6,14},{7,15},{8,24},{9,... | collective-permute-start | bytes 786440 | tf_op jit(solution)/shard_map/ppermute | solution.py:228
  16.0 13.1 %collective-permute-start.5 = (f32[256,256]{1,0:T(8,128)S(1)}, f32[256,256]{1,0:T(8,128)S(1)}, u32[]{:S(2)}, u32[]{:S(2)}) collective-permute-start(f32[256,256]{1,0:T(8,128)S(1)} %shard_map.79), channel_id=1, source_target_pairs={{0,2},{1,3},{2,0},{3,1},{4,5},{5,4},{6,7},{7,6},{8,10},{9,11},{10,... | collective-permute-start | bytes 786440 | tf_op jit(solution)/shard_map/ppermute | solution.py:228
  22.1 8.3 %collective-permute-start.8 = (f32[256,256]{1,0:T(8,128)S(1)}, f32[256,256]{1,0:T(8,128)S(1)}, u32[]{:S(2)}, u32[]{:S(2)}) collective-permute-start(f32[256,256]{1,0:T(8,128)S(1)} %collective-permute-done.7.refs_0_.refs_1_), channel_id=1, source_target_pairs={{0,16},{1,17},{2,18},{3,19},{4,12},{5,13},{6,14},{7,15},{8,24},{9,... | collective-permute-start | bytes 786440 | tf_op jit(solution)/shard_map/ppermute | solution.py:228
  22.7 12.1 %collective-permute-start.3 = (f32[256,256]{1,0:T(8,128)S(1)}, f32[256,256]{1,0:T(8,128)S(1)}, u32[]{:S(2)}, u32[]{:S(2)}) collective-permute-start(f32[256,256]{1,0:T(8,128)S(1)} %collective-permute-done.2.refs_4_), channel_id=1, source_target_pairs={{0,8},{1,9},{2,10},{3,11},{4,20},{5,21},{6,22},{7,23},{8,0},{9,1},... | collective-permute-start | bytes 786440 | tf_op jit(solution)/shard_map/ppermute | solution.py:228
  29.2 6.4 %collective-permute-start.6 = (f32[256,256]{1,0:T(8,128)S(1)}, f32[256,256]{1,0:T(8,128)S(1)}, u32[]{:S(2)}, u32[]{:S(2)}) collective-permute-start(f32[256,256]{1,0:T(8,128)S(1)} %shard_map.81), channel_id=1, source_target_pairs={{0,8},{1,9},{2,10},{3,11},{4,20},{5,21},{6,22},{7,23},{8,0},{9,1},... | collective-permute-start | bytes 786440 | tf_op jit(solution)/shard_map/ppermute | solution.py:228
  36.5 6.9 %collective-permute-start.14 = (f32[136,256]{1,0:T(8,128)S(1)}, f32[136,256]{1,0:T(8,128)S(1)}, u32[]{:S(2)}, u32[]{:S(2)}) collective-permute-start(f32[136,256]{1,0:T(8,128)S(1)} %get-tuple-element.69), channel_id=1, source_target_pairs={{0,16},{1,17},{2,18},{3,19},{4,12},{5,13},{6,14},{7,15},{8,24},{9,... | collective-permute-start | bytes 417800 | tf_op jit(solution)/shard_map/ppermute | solution.py:228
  37.4 7.9 %collective-permute-start.11 = (f32[136,256]{1,0:T(8,128)S(1)}, f32[136,256]{1,0:T(8,128)S(1)}, u32[]{:S(2)}, u32[]{:S(2)}) collective-permute-start(f32[136,256]{1,0:T(8,128)S(1)} %get-tuple-element.65), channel_id=1, source_target_pairs={{0,17},{1,16},{2,19},{3,18},{4,14},{5,15},{6,12},{7,13},{8,25},{9,... | collective-permute-start | bytes 417800 | tf_op jit(solution)/shard_map/ppermute | solution.py:228
  39.5 6.9 %collective-permute-start.9 = (f32[136,256]{1,0:T(8,128)S(1)}, f32[136,256]{1,0:T(8,128)S(1)}, u32[]{:S(2)}, u32[]{:S(2)}) collective-permute-start(f32[136,256]{1,0:T(8,128)S(1)} %get-tuple-element.61), channel_id=1, source_target_pairs={{0,1},{1,0},{2,3},{3,2},{4,6},{5,7},{6,4},{7,5},{8,9},{9,8},{10,11... | collective-permute-start | bytes 417800 | tf_op jit(solution)/shard_map/ppermute | solution.py:228
  42.5 5.1 %collective-permute-start.10 = (f32[136,256]{1,0:T(8,128)S(1)}, f32[136,256]{1,0:T(8,128)S(1)}, u32[]{:S(2)}, u32[]{:S(2)}) collective-permute-start(f32[136,256]{1,0:T(8,128)S(1)} %get-tuple-element.62), channel_id=1, source_target_pairs={{0,16},{1,17},{2,18},{3,19},{4,12},{5,13},{6,14},{7,15},{8,24},{9,... | collective-permute-start | bytes 417800 | tf_op jit(solution)/shard_map/ppermute | solution.py:228
  43.4 4.3 %collective-permute-start.12 = (f32[136,256]{1,0:T(8,128)S(1)}, f32[136,256]{1,0:T(8,128)S(1)}, u32[]{:S(2)}, u32[]{:S(2)}) collective-permute-start(f32[136,256]{1,0:T(8,128)S(1)} %get-tuple-element.66), channel_id=1, source_target_pairs={{0,4},{1,5},{2,6},{3,7},{4,0},{5,1},{6,2},{7,3},{8,12},{9,13},{10,... | collective-permute-start | bytes 417800 | tf_op jit(solution)/shard_map/ppermute | solution.py:228
  43.4 4.5 %collective-permute-start.13 = (f32[136,256]{1,0:T(8,128)S(1)}, f32[136,256]{1,0:T(8,128)S(1)}, u32[]{:S(2)}, u32[]{:S(2)}) collective-permute-start(f32[136,256]{1,0:T(8,128)S(1)} %get-tuple-element.67), channel_id=1, source_target_pairs={{0,20},{1,21},{2,22},{3,23},{4,8},{5,9},{6,10},{7,11},{8,28},{9,29... | collective-permute-start | bytes 417800 | tf_op jit(solution)/shard_map/ppermute | solution.py:228
  45.3 6.9 %collective-permute-start.15 = (f32[136,256]{1,0:T(8,128)S(1)}, f32[136,256]{1,0:T(8,128)S(1)}, u32[]{:S(2)}, u32[]{:S(2)}) collective-permute-start(f32[136,256]{1,0:T(8,128)S(1)} %shard_map.87), channel_id=1, source_target_pairs={{0,5},{1,4},{2,7},{3,6},{4,2},{5,3},{6,0},{7,1},{8,13},{9,12},{10,... | collective-permute-start | bytes 417800 | tf_op jit(solution)/shard_map/ppermute | solution.py:228

commit v6 on v5

--- a/solution.py
+++ b/solution.py
@@ -247,41 +247,47 @@
         compiler_params=params(8),
     )(*owns, got)
 
-    q_blocks, near_k = [mine_q], [(mine_kv,)]
-    for masks in zip(*q_bits):
-        q_blocks += [swap(x, masks) for x in q_blocks]
+    near_k = [(mine_kv,)]
     (far, *near) = zip(*k_bits)
     for masks in near:
         near_k += [tuple(swap(x, masks) for x in block) for block in near_k]
     far_k = swap(mine_k, far)
-    far_v = swap(later(mine_kv, 2 * DH, near_k[-1][0]), far)
+    mine_v = later(mine_kv, 2 * DH, near_k[-1][0])
+    far_v = swap(mine_v, far)
+    q_blocks = [mine_q]
+    for masks in zip(*q_bits):
+        sent = [later(x, 2 * DH, mine_v) if i == 1 else x for i, x in enumerate(q_blocks)]
+        q_blocks += [swap(x, masks) for x in sent]
     n_q = len(q_blocks)
     top_bit = n_q // 2
     far_q, near_q = list(range(1, n_q, 2)), list(range(0, n_q, 2))
     states = dict(zip(near_q, attend([q_blocks[i] for i in near_q], near_k, [], False)))
-    last_k = [(far_k, later(far_v, 2 * DH, states[0][1]))]
+    last_k = [(later(far_k, 2 * DH, mine_v), later(far_v, 2 * DH, states[0][1]))]
     for masks in near:
         last_k += [tuple(swap(x, masks) for x in block) for block in last_k]
-    states.update(zip(far_q, attend([q_blocks[i] for i in far_q], near_k, [], False)))
-    states = attend(q_blocks, [(far_k, far_v)], [states[i] for i in range(n_q)], False)
-    parts = {}
-    for group in (
-        [i for i in far_q if i & top_bit], [i for i in far_q if not i & top_bit], near_q
-    ):
-        done = attend([q_blocks[i] for i in group], last_k[1:], [states[i] for i in group], True)
-        parts.update(zip(group, done))
+    far_kv = [(far_k, far_v)]
+    first = [1] + near_q
+    states[1] = attend([q_blocks[1]], near_k, [], False)[0]
+    states.update(zip(first, attend([q_blocks[i] for i in first], far_kv, [states[i] for i in first], False)))
+    rest = far_q[1:]
+    if rest:
+        blocks = [later(q_blocks[i], 2 * DH, states[1][1]) for i in rest]
+        states.update(zip(rest, attend(blocks, near_k + far_kv, [], False)))
+    parts = attend(q_blocks, last_k[1:], [states[i] for i in range(n_q)], True)
 
     def masks_of(index):
         return tuple(sum(bit for i, bit in enumerate(bits) if index >> i & 1) for bits in q_bits)
 
     own = [parts[0][0]] + [swap(parts[i][0], masks_of(i)) for i in range(1, n_q)]
-    cross = [swap(parts[0][1], masks_of(0), True), swap(parts[top_bit][1], masks_of(top_bit), True)]
+    cross, merged = [], parts[0][1]
     for i in range(1, top_bit):
         beside = swap(parts[i | top_bit][1], masks_of(top_bit))
         merged = pl.pallas_call(
             merge_kernel, out_shape=f32(rows + STAT_ROWS, 2 * DH), compiler_params=params(8)
         )(parts[i][1], beside)
         cross.append(swap(merged, masks_of(i), True))
+    for i in (top_bit, 0):
+        cross.append(swap(later(parts[i][1], 2 * DH, merged), masks_of(i), True))
     return tuple(
         pl.pallas_call(
             functools.partial(finish_kernel, n_q),

time: 53.8 us -> 53.2 us (0.989)
    pallas_call x6 -> x5, Pallas kernels: 9.5 us -> 8.96 us  [attend(): pl.pallas_call(functools.partial(attend_kernel, n_q, n_k, rows, bool(prev...]
  transfers between devices with their start and end apart: 16 -> 16, of which waited for: 11 -> 9; matrix products, arithmetic and copies ran while one was open for 0% -> 0% of each run, Pallas kernels for 17% -> 13%
where the time goes in v6:
time: 53.2 us; the launch traced here: 53 us
  starting transfers between devices  22.6 us (42%)
  waiting for transfers between devices  16.6 us (31%)
  Pallas kernels  13.1 us (25%)
  between operations  0.75 us (1%)
    ppermute x16, starting transfers between devices, swap(): lax.ppermute(x, AXES, [(i, i ^ flip ^ masks[i // n_kv % 2]) for i in rang...  22.6 us
    ppermute x16, waiting for transfers between devices, swap(): lax.ppermute(x, AXES, [(i, i ^ flip ^ masks[i // n_kv % 2]) for i in rang...  16.6 us
    pallas_call x5, Pallas kernels, attend(): pl.pallas_call(functools.partial(attend_kernel, n_q, n_k, rows, bool(prev...  8.96 us
    pallas_call x1, Pallas kernels, per_device(): pl.pallas_call(pack_kernel, out_shape=[f32(rows, w * DH) for w in (1, 1,...  2.02 us
    pallas_call x1, Pallas kernels, per_device(): pl.pallas_call(functools.partial(finish_kernel, n_q), out_shape=[f32(rows...  1.51 us
  transfers between devices with their start and end apart: 16, of which 9 were waited for; matrix products, arithmetic and copies ran while one was open for 0% of the time, Pallas kernels for 13%

profile of v6, /device:TPU:0, one launch (start us, length us, event | category | flops | bytes accessed | tf_op | source)
XLA Modules:
  0.0 53.0 jit_solution(1559089913706760229)
XLA Ops:
  0.6 2.0 %shard_map.77 = (f32[128,128]{1,0:T(8,128)S(1)}, f32[128,128]{1,0:T(8,128)S(1)}, f32[128,128]{1,0:T(8,128)S(1)}, f32[128,128]{1,0:T(8,128)S(1)}, f32[128,128]{1,...) custom-call(f32[128,256]{1,0:T(8,128)} %refs_0_.1, f32[128,256]{1,0:T(8,128)} %refs_1_.1, f32[128,256]{1,0:T(8,128)} %refs_2_.1, ...), custom_call_target="tpu_custom_call" | custom-call | tf_op jit(solution)/shard_map/pallas_call | solution.py:235
  2.7 0.5 collective-permute-start
  3.2 1.6 %collective-permute-done.refs_6_ = f32[128,768]{1,0:T(8,128)S(1)} collective-permute-done((f32[128,768]{1,0:T(8,128)}, f32[128,768]{1,0:T(8,128)S(1)}, u32[]{:S(2)}, u32[]{:S(2)}) %collective-permute-start) | collective-permute-done | bytes 393248 | tf_op jit(solution)/shard_map/ppermute | solution.py:228
  4.8 2.9 %collective-permute-start.3 = (f32[256,512]{1,0:T(8,128)S(1)}, f32[256,512]{1,0:T(8,128)S(1)}, u32[]{:S(2)}, u32[]{:S(2)}) collective-permute-start(f32[256,512]{1,0:T(8,128)S(1)} %get-tuple-element.42.x.refs_2_.refs_1_), channel_id=1, source_target_pairs={{0,8},{1,9},{2,10},{3,11},{4,20},{5,21},{6,22},{7,23},{8,0},{9,1},... | collective-permute-start | bytes 1572872 | tf_op jit(solution)/shard_map/ppermute | solution.py:228
  7.8 1.6 %collective-permute-start.1 = (f32[256,256]{1,0:T(8,128)S(1)}, f32[256,256]{1,0:T(8,128)S(1)}, u32[]{:S(2)}, u32[]{:S(2)}) collective-permute-start(f32[256,256]{1,0:T(8,128)S(1)} %get-tuple-element.41.refs_0_.refs_1_), channel_id=1, source_target_pairs={{0,1},{1,0},{2,3},{3,2},{4,6},{5,7},{6,4},{7,5},{8,9},{9,8},{10,11... | collective-permute-start | bytes 786440 | tf_op jit(solution)/shard_map/ppermute | solution.py:228
  9.3 2.6 %collective-permute-start.5 = (f32[256,256]{1,0:T(8,128)S(1)}, f32[256,256]{1,0:T(8,128)S(1)}, u32[]{:S(2)}, u32[]{:S(2)}) collective-permute-start(f32[256,256]{1,0:T(8,128)S(1)} %get-tuple-element.43), channel_id=1, source_target_pairs={{0,2},{1,3},{2,0},{3,1},{4,5},{5,4},{6,7},{7,6},{8,10},{9,11},{10,... | collective-permute-start | bytes 786440 | tf_op jit(solution)/shard_map/ppermute | solution.py:228
  11.9 1.5 %collective-permute-start.2 = (f32[256,256]{1,0:T(8,128)S(1)}, f32[256,256]{1,0:T(8,128)S(1)}, u32[]{:S(2)}, u32[]{:S(2)}) collective-permute-start(f32[256,256]{1,0:T(8,128)S(1)} %get-tuple-element.41.refs_0_.refs_1_), channel_id=1, source_target_pairs={{0,16},{1,17},{2,18},{3,19},{4,12},{5,13},{6,14},{7,15},{8,24},{9,... | collective-permute-start | bytes 786440 | tf_op jit(solution)/shard_map/ppermute | solution.py:228
  13.5 2.5 %collective-permute-done.3.after.refs_3_.refs_2_ = f32[256,512]{1,0:T(8,128)S(1)} collective-permute-done((f32[256,512]{1,0:T(8,128)S(1)}, f32[256,512]{1,0:T(8,128)S(1)}, u32[]{:S(2)}, u32[]{:S(2)}) %collective-permute-start.3) | collective-permute-done | bytes 524320 | tf_op jit(solution)/shard_map/ppermute | solution.py:228
  16.0 4.9 %collective-permute-start.7 = (f32[256,256]{1,0:T(8,128)S(1)}, f32[256,256]{1,0:T(8,128)S(1)}, u32[]{:S(2)}, u32[]{:S(2)}) collective-permute-start(f32[256,256]{1,0:T(8,128)S(1)} %shard_map.79.after), channel_id=1, source_target_pairs={{0,2},{1,3},{2,0},{3,1},{4,5},{5,4},{6,7},{7,6},{8,10},{9,11},{10,... | collective-permute-start | bytes 786440 | tf_op jit(solution)/shard_map/ppermute | solution.py:228
  20.9 1.1 %collective-permute-done.1.x.refs_0_.refs_1_ = f32[256,256]{1,0:T(8,128)S(1)} collective-permute-done((f32[256,256]{1,0:T(8,128)S(1)}, f32[256,256]{1,0:T(8,128)S(1)}, u32[]{:S(2)}, u32[]{:S(2)}) %collective-permute-start.1) | collective-permute-done | bytes 262176 | tf_op jit(solution)/shard_map/ppermute | solution.py:228
  22.1 0.7 %collective-permute-start.4 = (f32[256,256]{1,0:T(8,128)S(1)}, f32[256,256]{1,0:T(8,128)S(1)}, u32[]{:S(2)}, u32[]{:S(2)}) collective-permute-start(f32[256,256]{1,0:T(8,128)S(1)} %shard_map.80), channel_id=1, source_target_pairs={{0,16},{1,17},{2,18},{3,19},{4,12},{5,13},{6,14},{7,15},{8,24},{9,... | collective-permute-start | bytes 786440 | tf_op jit(solution)/shard_map/ppermute | solution.py:228
  22.8 1.4 %collective-permute-start.6 = (f32[256,256]{1,0:T(8,128)S(1)}, f32[256,256]{1,0:T(8,128)S(1)}, u32[]{:S(2)}, u32[]{:S(2)}) collective-permute-start(f32[256,256]{1,0:T(8,128)S(1)} %shard_map.81), channel_id=1, source_target_pairs={{0,8},{1,9},{2,10},{3,11},{4,20},{5,21},{6,22},{7,23},{8,0},{9,1},... | collective-permute-start | bytes 786440 | tf_op jit(solution)/shard_map/ppermute | solution.py:228
  24.3 1.8 %shard_map.82 = (f32[256,256]{1,0:T(8,128)S(1)}, f32[256,128]{1,0:T(8,128)S(1)}, f32[256,256]{1,0:T(8,128)S(1)}, f32[256,128]{1,0:T(8,128)S(1)}) custom-call(f32[256,256]{1,0:T(8,128)S(1)} %get-tuple-element.41.refs_0_.refs_1_, f32[256,256]{1,0:T(8,128)S(1)} %collective-permute-done.2.refs_1_.refs_2_, f32[256,512]{1,0:T(8,128)S(1)} %get-tuple-element.42.x.refs_2_.refs_1_, ...), custom_call_target="tpu_custom_call" | custom-call | flops 2415919104 | bytes 3145728 | tf_op jit(solution)/shard_map/pallas_call | solution.py:155
  26.1 1.0 %shard_map.84 = (f32[256,256]{1,0:T(8,128)S(1)}, f32[256,128]{1,0:T(8,128)S(1)}) custom-call(f32[256,256]{1,0:T(8,128)S(1)} %collective-permute-done.1.x.refs_0_.refs_1_, f32[256,512]{1,0:T(8,128)S(1)} %get-tuple-element.42.x.refs_2_.refs_1_, f32[256,512]{1,0:T(8,128)S(1)} %collective-permute-done.3.after.refs_3_.refs_2_), custom_call_target="tpu_custom_call" | custom-call | flops 1207959552 | bytes 2097152 | tf_op jit(solution)/shard_map/pallas_call | solution.py:155
  27.1 2.1 %collective-permute-done.7.x.refs_4_ = f32[256,256]{1,0:T(8,128)S(1)} collective-permute-done((f32[256,256]{1,0:T(8,128)S(1)}, f32[256,256]{1,0:T(8,128)S(1)}, u32[]{:S(2)}, u32[]{:S(2)}) %collective-permute-start.7) | collective-permute-done | bytes 262176 | tf_op jit(solution)/shard_map/ppermute | solution.py:228
  29.2 0.4 collective-permute-start.8
  29.6 2.1 %shard_map.85 = (f32[256,256]{1,0:T(8,128)S(1)}, f32[256,128]{1,0:T(8,128)S(1)}, f32[256,256]{1,0:T(8,128)S(1)}, f32[256,128]{1,0:T(8,128)S(1)}, f32[256,256]{1,0:T(8,128)S(1)}, /*index=5*/f32[256,128]{1,0:T(8,128)S(1)}) custom-call(f32[256,256]{1,0:T(8,128)S(1)} %collective-permute-done.1.x.refs_0_.refs_1_, ...), custom_call_target="tpu_custom_call" | custom-call | flops 1811939328 | bytes 3670016 | tf_op jit(solution)/shard_map/pallas_call | solution.py:155
  31.7 1.4 %shard_map.87 = (f32[256,256]{1,0:T(8,128)S(1)}, f32[256,128]{1,0:T(8,128)S(1)}) custom-call(f32[256,256]{1,0:T(8,128)S(1)} %shard_map.86.refs_0_, f32[256,512]{1,0:T(8,128)S(1)} %get-tuple-element.42.x.refs_2_.refs_1_, f32[256,512]{1,0:T(8,128)S(1)} %collective-permute-done.3.after.refs_3_.refs_2_, f32[256,256]{1,0:T(8,128)S(1)} %collective-permute-done.5.x.refs_3_, ...), custom_call_target="tpu_custom_call" | custom-call | flops 1811939328 | bytes 2621440 | tf_op jit(solution)/shard_map/pallas_call | solution.py:155
  33.1 2.5 %collective-permute-done.8.refs_5_ = f32[256,256]{1,0:T(8,128)S(1)} collective-permute-done((f32[256,256]{1,0:T(8,128)S(1)}, f32[256,256]{1,0:T(8,128)S(1)}, u32[]{:S(2)}, u32[]{:S(2)}) %collective-permute-start.8) | collective-permute-done | bytes 262176 | tf_op jit(solution)/shard_map/ppermute | solution.py:228
  35.6 2.6 %shard_map.88 = (f32[136,256]{1,0:T(8,128)S(1)}, f32[136,256]{1,0:T(8,128)S(1)}, f32[136,256]{1,0:T(8,128)S(1)}, f32[136,256]{1,0:T(8,128)S(1)}, f32[136,256]{1,...) custom-call(f32[256,256]{1,0:T(8,128)S(1)} %get-tuple-element.41.refs_0_.refs_1_, ...), custom_call_target="tpu_custom_call" | custom-call | flops 2415919104 | bytes 4718592 | tf_op jit(solution)/shard_map/pallas_call | solution.py:155
  38.3 0.8 %collective-permute-start.12 = (f32[136,256]{1,0:T(8,128)S(1)}, f32[136,256]{1,0:T(8,128)S(1)}, u32[]{:S(2)}, u32[]{:S(2)}) collective-permute-start(f32[136,256]{1,0:T(8,128)S(1)} %get-tuple-element.63), channel_id=1, source_target_pairs={{0,16},{1,17},{2,18},{3,19},{4,12},{5,13},{6,14},{7,15},{8,24},{9,... | collective-permute-start | bytes 417800 | tf_op jit(solution)/shard_map/ppermute | solution.py:228
  39.1 1.2 %collective-permute-start.10 = (f32[136,256]{1,0:T(8,128)S(1)}, f32[136,256]{1,0:T(8,128)S(1)}, u32[]{:S(2)}, u32[]{:S(2)}) collective-permute-start(f32[136,256]{1,0:T(8,128)S(1)} %get-tuple-element.60), channel_id=1, source_target_pairs={{0,16},{1,17},{2,18},{3,19},{4,12},{5,13},{6,14},{7,15},{8,24},{9,... | collective-permute-start | bytes 417800 | tf_op jit(solution)/shard_map/ppermute | solution.py:228
  40.4 0.6 %collective-permute-start.11 = (f32[136,256]{1,0:T(8,128)S(1)}, f32[136,256]{1,0:T(8,128)S(1)}, u32[]{:S(2)}, u32[]{:S(2)}) collective-permute-start(f32[136,256]{1,0:T(8,128)S(1)} %get-tuple-element.61), channel_id=1, source_target_pairs={{0,17},{1,16},{2,19},{3,18},{4,14},{5,15},{6,12},{7,13},{8,25},{9,... | collective-permute-start | bytes 417800 | tf_op jit(solution)/shard_map/ppermute | solution.py:228
  40.9 1.7 %collective-permute-start.9 = (f32[136,256]{1,0:T(8,128)S(1)}, f32[136,256]{1,0:T(8,128)S(1)}, u32[]{:S(2)}, u32[]{:S(2)}) collective-permute-start(f32[136,256]{1,0:T(8,128)S(1)} %get-tuple-element.59), channel_id=1, source_target_pairs={{0,1},{1,0},{2,3},{3,2},{4,6},{5,7},{6,4},{7,5},{8,9},{9,8},{10,11... | collective-permute-start | bytes 417800 | tf_op jit(solution)/shard_map/ppermute | solution.py:228
  42.6 0.8 %collective-permute-done.12.two = f32[136,256]{1,0:T(8,128)S(1)} collective-permute-done((f32[136,256]{1,0:T(8,128)S(1)}, f32[136,256]{1,0:T(8,128)S(1)}, u32[]{:S(2)}, u32[]{:S(2)}) %collective-permute-start.12) | collective-permute-done | bytes 139296 | tf_op jit(solution)/shard_map/ppermute | solution.py:228
  43.4 0.4 shard_map.89.after
  44.0 0.9 %collective-permute-start.14 = (f32[136,256]{1,0:T(8,128)S(1)}, f32[136,256]{1,0:T(8,128)S(1)}, u32[]{:S(2)}, u32[]{:S(2)}) collective-permute-start(f32[136,256]{1,0:T(8,128)S(1)} %shard_map.90), channel_id=1, source_target_pairs={{0,20},{1,21},{2,22},{3,23},{4,8},{5,9},{6,10},{7,11},{8,28},{9,29... | collective-permute-start | bytes 417800 | tf_op jit(solution)/shard_map/ppermute | solution.py:228
  44.9 0.7 %collective-permute-start.13 = (f32[136,256]{1,0:T(8,128)S(1)}, f32[136,256]{1,0:T(8,128)S(1)}, u32[]{:S(2)}, u32[]{:S(2)}) collective-permute-start(f32[136,256]{1,0:T(8,128)S(1)} %shard_map.89.after), channel_id=1, source_target_pairs={{0,5},{1,4},{2,7},{3,6},{4,2},{5,3},{6,0},{7,1},{8,13},{9,12},{10,... | collective-permute-start | bytes 417800 | tf_op jit(solution)/shard_map/ppermute | solution.py:228
  45.6 1.6 %collective-permute-done.11.refs_3_ = f32[136,256]{1,0:T(8,128)S(1)} collective-permute-done((f32[136,256]{1,0:T(8,128)S(1)}, f32[136,256]{1,0:T(8,128)S(1)}, u32[]{:S(2)}, u32[]{:S(2)}) %collective-permute-start.11) | collective-permute-done | bytes 139296 | tf_op jit(solution)/shard_map/ppermute | solution.py:228
  47.2 1.3 %collective-permute-done.9.refs_1_ = f32[136,256]{1,0:T(8,128)S(1)} collective-permute-done((f32[136,256]{1,0:T(8,128)S(1)}, f32[136,256]{1,0:T(8,128)S(1)}, u32[]{:S(2)}, u32[]{:S(2)}) %collective-permute-start.9) | collective-permute-done | bytes 139296 | tf_op jit(solution)/shard_map/ppermute | solution.py:228
  48.5 3.0 %collective-permute-done.13.refs_4_ = f32[136,256]{1,0:T(8,128)S(1)} collective-permute-done((f32[136,256]{1,0:T(8,128)S(1)}, f32[136,256]{1,0:T(8,128)S(1)}, u32[]{:S(2)}, u32[]{:S(2)}) %collective-permute-start.13) | collective-permute-done | bytes 139296 | tf_op jit(solution)/shard_map/ppermute | solution.py:228
  51.5 1.5 %shard_map.92 = (f32[128,256]{1,0:T(8,128)}, f32[128,256]{1,0:T(8,128)}) custom-call(s32[1]{0:T(128)} %bitcast.core_ref, f32[136,256]{1,0:T(8,128)S(1)} %get-tuple-element.58.refs_0_, f32[136,256]{1,0:T(8,128)S(1)} %collective-permute-done.9.refs_1_, f32[136,256]{1,0:T(8,128)S(1)} %collective-permute-done.10.refs_2_, ...), custom_call_target="tpu_custom_call" | custom-call | tf_op jit(solution)/shard_map/pallas_call | solution.py:292
  (16 shorter events, 0.3 us)
Async XLA Ops:
  2.7 2.1 %collective-permute-start = (f32[128,768]{1,0:T(8,128)}, f32[128,768]{1,0:T(8,128)S(1)}, u32[]{:S(2)}, u32[]{:S(2)}) collective-permute-start(f32[128,768]{1,0:T(8,128)} %get-tuple-element.40), channel_id=1, source_target_pairs={{0,4},{1,5},{2,6},{3,7},{4,0},{5,1},{6,2},{7,3},{8,12},{9,13},{10,... | collective-permute-start | bytes 1179656 | tf_op jit(solution)/shard_map/ppermute | solution.py:228
  4.8 11.2 %collective-permute-start.3 = (f32[256,512]{1,0:T(8,128)S(1)}, f32[256,512]{1,0:T(8,128)S(1)}, u32[]{:S(2)}, u32[]{:S(2)}) collective-permute-start(f32[256,512]{1,0:T(8,128)S(1)} %get-tuple-element.42.x.refs_2_.refs_1_), channel_id=1, source_target_pairs={{0,8},{1,9},{2,10},{3,11},{4,20},{5,21},{6,22},{7,23},{8,0},{9,1},... | collective-permute-start | bytes 1572872 | tf_op jit(solution)/shard_map/ppermute | solution.py:228
  7.8 14.3 %collective-permute-start.1 = (f32[256,256]{1,0:T(8,128)S(1)}, f32[256,256]{1,0:T(8,128)S(1)}, u32[]{:S(2)}, u32[]{:S(2)}) collective-permute-start(f32[256,256]{1,0:T(8,128)S(1)} %get-tuple-element.41.refs_0_.refs_1_), channel_id=1, source_target_pairs={{0,1},{1,0},{2,3},{3,2},{4,6},{5,7},{6,4},{7,5},{8,9},{9,8},{10,11... | collective-permute-start | bytes 786440 | tf_op jit(solution)/shard_map/ppermute | solution.py:228
  9.3 13.4 %collective-permute-start.5 = (f32[256,256]{1,0:T(8,128)S(1)}, f32[256,256]{1,0:T(8,128)S(1)}, u32[]{:S(2)}, u32[]{:S(2)}) collective-permute-start(f32[256,256]{1,0:T(8,128)S(1)} %get-tuple-element.43), channel_id=1, source_target_pairs={{0,2},{1,3},{2,0},{3,1},{4,5},{5,4},{6,7},{7,6},{8,10},{9,11},{10,... | collective-permute-start | bytes 786440 | tf_op jit(solution)/shard_map/ppermute | solution.py:228
  11.9 12.3 %collective-permute-start.2 = (f32[256,256]{1,0:T(8,128)S(1)}, f32[256,256]{1,0:T(8,128)S(1)}, u32[]{:S(2)}, u32[]{:S(2)}) collective-permute-start(f32[256,256]{1,0:T(8,128)S(1)} %get-tuple-element.41.refs_0_.refs_1_), channel_id=1, source_target_pairs={{0,16},{1,17},{2,18},{3,19},{4,12},{5,13},{6,14},{7,15},{8,24},{9,... | collective-permute-start | bytes 786440 | tf_op jit(solution)/shard_map/ppermute | solution.py:228
  16.0 13.1 %collective-permute-start.7 = (f32[256,256]{1,0:T(8,128)S(1)}, f32[256,256]{1,0:T(8,128)S(1)}, u32[]{:S(2)}, u32[]{:S(2)}) collective-permute-start(f32[256,256]{1,0:T(8,128)S(1)} %shard_map.79.after), channel_id=1, source_target_pairs={{0,2},{1,3},{2,0},{3,1},{4,5},{5,4},{6,7},{7,6},{8,10},{9,11},{10,... | collective-permute-start | bytes 786440 | tf_op jit(solution)/shard_map/ppermute | solution.py:228
  22.1 9.5 %collective-permute-start.4 = (f32[256,256]{1,0:T(8,128)S(1)}, f32[256,256]{1,0:T(8,128)S(1)}, u32[]{:S(2)}, u32[]{:S(2)}) collective-permute-start(f32[256,256]{1,0:T(8,128)S(1)} %shard_map.80), channel_id=1, source_target_pairs={{0,16},{1,17},{2,18},{3,19},{4,12},{5,13},{6,14},{7,15},{8,24},{9,... | collective-permute-start | bytes 786440 | tf_op jit(solution)/shard_map/ppermute | solution.py:228
  22.8 10.3 %collective-permute-start.6 = (f32[256,256]{1,0:T(8,128)S(1)}, f32[256,256]{1,0:T(8,128)S(1)}, u32[]{:S(2)}, u32[]{:S(2)}) collective-permute-start(f32[256,256]{1,0:T(8,128)S(1)} %shard_map.81), channel_id=1, source_target_pairs={{0,8},{1,9},{2,10},{3,11},{4,20},{5,21},{6,22},{7,23},{8,0},{9,1},... | collective-permute-start | bytes 786440 | tf_op jit(solution)/shard_map/ppermute | solution.py:228
  29.2 6.4 %collective-permute-start.8 = (f32[256,256]{1,0:T(8,128)S(1)}, f32[256,256]{1,0:T(8,128)S(1)}, u32[]{:S(2)}, u32[]{:S(2)}) collective-permute-start(f32[256,256]{1,0:T(8,128)S(1)} %shard_map.83), channel_id=1, source_target_pairs={{0,8},{1,9},{2,10},{3,11},{4,20},{5,21},{6,22},{7,23},{8,0},{9,1},... | collective-permute-start | bytes 786440 | tf_op jit(solution)/shard_map/ppermute | solution.py:228
  38.3 5.1 %collective-permute-start.12 = (f32[136,256]{1,0:T(8,128)S(1)}, f32[136,256]{1,0:T(8,128)S(1)}, u32[]{:S(2)}, u32[]{:S(2)}) collective-permute-start(f32[136,256]{1,0:T(8,128)S(1)} %get-tuple-element.63), channel_id=1, source_target_pairs={{0,16},{1,17},{2,18},{3,19},{4,12},{5,13},{6,14},{7,15},{8,24},{9,... | collective-permute-start | bytes 417800 | tf_op jit(solution)/shard_map/ppermute | solution.py:228
  39.1 5.8 %collective-permute-start.10 = (f32[136,256]{1,0:T(8,128)S(1)}, f32[136,256]{1,0:T(8,128)S(1)}, u32[]{:S(2)}, u32[]{:S(2)}) collective-permute-start(f32[136,256]{1,0:T(8,128)S(1)} %get-tuple-element.60), channel_id=1, source_target_pairs={{0,16},{1,17},{2,18},{3,19},{4,12},{5,13},{6,14},{7,15},{8,24},{9,... | collective-permute-start | bytes 417800 | tf_op jit(solution)/shard_map/ppermute | solution.py:228
  40.4 6.8 %collective-permute-start.11 = (f32[136,256]{1,0:T(8,128)S(1)}, f32[136,256]{1,0:T(8,128)S(1)}, u32[]{:S(2)}, u32[]{:S(2)}) collective-permute-start(f32[136,256]{1,0:T(8,128)S(1)} %get-tuple-element.61), channel_id=1, source_target_pairs={{0,17},{1,16},{2,19},{3,18},{4,14},{5,15},{6,12},{7,13},{8,25},{9,... | collective-permute-start | bytes 417800 | tf_op jit(solution)/shard_map/ppermute | solution.py:228
  40.9 7.6 %collective-permute-start.9 = (f32[136,256]{1,0:T(8,128)S(1)}, f32[136,256]{1,0:T(8,128)S(1)}, u32[]{:S(2)}, u32[]{:S(2)}) collective-permute-start(f32[136,256]{1,0:T(8,128)S(1)} %get-tuple-element.59), channel_id=1, source_target_pairs={{0,1},{1,0},{2,3},{3,2},{4,6},{5,7},{6,4},{7,5},{8,9},{9,8},{10,11... | collective-permute-start | bytes 417800 | tf_op jit(solution)/shard_map/ppermute | solution.py:228
  43.9 4.7 %collective-permute-start.15 = (f32[136,256]{1,0:T(8,128)S(1)}, f32[136,256]{1,0:T(8,128)S(1)}, u32[]{:S(2)}, u32[]{:S(2)}) collective-permute-start(f32[136,256]{1,0:T(8,128)S(1)} %shard_map.91), channel_id=1, source_target_pairs={{0,4},{1,5},{2,6},{3,7},{4,0},{5,1},{6,2},{7,3},{8,12},{9,13},{10,... | collective-permute-start | bytes 417800 | tf_op jit(solution)/shard_map/ppermute | solution.py:228
  44.0 4.6 %collective-permute-start.14 = (f32[136,256]{1,0:T(8,128)S(1)}, f32[136,256]{1,0:T(8,128)S(1)}, u32[]{:S(2)}, u32[]{:S(2)}) collective-permute-start(f32[136,256]{1,0:T(8,128)S(1)} %shard_map.90), channel_id=1, source_target_pairs={{0,20},{1,21},{2,22},{3,23},{4,8},{5,9},{6,10},{7,11},{8,28},{9,29... | collective-permute-start | bytes 417800 | tf_op jit(solution)/shard_map/ppermute | solution.py:228
  44.9 6.6 %collective-permute-start.13 = (f32[136,256]{1,0:T(8,128)S(1)}, f32[136,256]{1,0:T(8,128)S(1)}, u32[]{:S(2)}, u32[]{:S(2)}) collective-permute-start(f32[136,256]{1,0:T(8,128)S(1)} %shard_map.89.after), channel_id=1, source_target_pairs={{0,5},{1,4},{2,7},{3,6},{4,2},{5,3},{6,0},{7,1},{8,13},{9,12},{10,... | collective-permute-start | bytes 417800 | tf_op jit(solution)/shard_map/ppermute | solution.py:228

commit v7 on v6

--- a/solution.py
+++ b/solution.py
@@ -83,7 +83,29 @@
     )(x, after)
 
 
-def attend_kernel(n_q, n_k, rows, has_prev, last, *refs):
+def same_kernel(*refs):
+    for ref, out in zip(refs[: len(refs) // 2], refs[len(refs) // 2 :]):
+        out[...] = ref[...]
+
+
+def landed(arrays):
+    return pl.pallas_call(
+        same_kernel, out_shape=[f32(*x.shape) for x in arrays], compiler_params=params(8)
+    )(*arrays)
+
+
+def halves_kernel(x, after, one, two):
+    one[...] = x[:, :DH]
+    two[...] = x[:, DH:]
+
+
+def halves(x, after):
+    return pl.pallas_call(
+        halves_kernel, out_shape=[f32(x.shape[0], DH)] * 2, compiler_params=params(8)
+    )(x, after)
+
+
+def attend_kernel(n_q, n_k, rows, has_prev, last, split, *refs):
     refs = list(refs)
 
     def take(count):
@@ -92,7 +114,7 @@
 
     q_refs, k_refs = take(n_q), [take(count) for count in n_k]
     prev = take(2 * n_q) if has_prev else None
-    outs = take(2 * n_q)
+    outs = parts_of(take((3 if split else 2) * n_q), ([1, 2] if split else [1, 1]) * n_q)
     ka, kb, va, vb, vc = refs
     scale = 1.0 / math.sqrt(DH)
     for b, block in enumerate(k_refs):
@@ -141,19 +163,22 @@
                 at = slice(i * half, (i + 1) * half)
                 store_part(outs[2 * b + i], *(x[at] for x in (peak, total, total_t, numer, numer_t)))
         else:
-            outs[2 * b][:, :DH] = numer
-            outs[2 * b][:, DH:] = numer_t
-            outs[2 * b + 1][...] = jnp.where(lane == 0, peak, jnp.where(lane == 1, total, total_t))
-
-
-def attend(q_blocks, k_blocks, prev, last):
+            outs[2 * b][0][:, :DH] = numer
+            outs[2 * b][0][:, DH:] = numer_t
+            outs[2 * b + 1][0][...] = jnp.where(lane == 0, peak, jnp.where(lane == 1, total, total_t))
+
+
+def attend(q_blocks, k_blocks, prev, last, split=False):
     n_q, n_k, rows = len(q_blocks), [len(block) for block in k_blocks], q_blocks[0].shape[0]
     assert rows == 2 * DH
     keys = rows * len(k_blocks)
-    shape = [f32(rows // 2 + STAT_ROWS, 2 * DH)] * 2 if last else [f32(rows, 2 * DH), f32(rows, DH)]
+    if last:
+        shape = part_shapes(rows // 2, 1) + part_shapes(rows // 2, 2 if split else 1)
+    else:
+        shape = [f32(rows, 2 * DH), f32(rows, DH)]
     work = n_q * rows * keys
     outs = pl.pallas_call(
-        functools.partial(attend_kernel, n_q, n_k, rows, bool(prev), last),
+        functools.partial(attend_kernel, n_q, n_k, rows, bool(prev), last, split),
         out_shape=shape * n_q,
         scratch_shapes=[pltpu.VMEM((keys, w * DH), jnp.bfloat16) for w in (6, 6, 2, 2, 2)],
         compiler_params=params(8 + keys * 16 // 1024),
@@ -161,46 +186,62 @@
             flops=work * 2 * 256 * 18, transcendentals=work, bytes_accessed=n_q * rows * 4096 + keys * 2048
         ),
     )(*q_blocks, *(x for block in k_blocks for x in block), *(x for pair in prev for x in pair))
-    return [tuple(outs[i : i + 2]) for i in range(0, 2 * n_q, 2)]
-
-
-def merge(refs):
-    rows = refs[0].shape[0] - STAT_ROWS
+    return [tuple(outs[i : i + len(shape)]) for i in range(0, len(outs), len(shape))]
+
+
+def parts_of(refs, counts):
+    refs = iter(refs)
+    return [tuple(next(refs) for _ in range(count)) for count in counts]
+
+
+def merge(parts):
+    rows = parts[0][0].shape[0] - STAT_ROWS
     wides = [
         jnp.concatenate(
-            [ref[rows:, :DH], jnp.zeros((DH - STAT_ROWS, DH), jnp.float32)], axis=0
+            [part[0][rows:, :DH], jnp.zeros((DH - STAT_ROWS, DH), jnp.float32)], axis=0
         ).T
-        for ref in refs
+        for part in parts
     ]
     peaks = [wide[:, 0:1] for wide in wides]
     top = functools.reduce(jnp.maximum, peaks)
     total = total_t = numer = numer_t = 0.0
-    for ref, wide, peak in zip(refs, wides, peaks):
+    for part, wide, peak in zip(parts, wides, peaks):
         factor = jnp.exp2(peak - top)
         total += factor * wide[:, 1:2]
         total_t += factor * wide[:, 2:3]
-        numer += factor * ref[0:rows, :DH]
-        numer_t += factor * ref[0:rows, DH:]
+        numer += factor * part[0][0:rows, :DH]
+        numer_t += factor * (part[1][...] if len(part) == 2 else part[0][0:rows, DH:])
     return top, total, total_t, numer, numer_t
 
 
-def store_part(out, peak, total, total_t, numer, numer_t):
-    rows = out.shape[0] - STAT_ROWS
+def store_part(part, peak, total, total_t, numer, numer_t):
+    rows = part[0].shape[0] - STAT_ROWS
     lane = lax.broadcasted_iota(jnp.int32, (rows, DH), 1)
     stats = jnp.where(lane == 0, peak, jnp.where(lane == 1, total, total_t))
     flat = stats.T[0:STAT_ROWS, :]
-    out[0:rows, :DH] = numer
-    out[0:rows, DH:] = numer_t
-    out[rows:, :] = jnp.concatenate([flat, jnp.zeros_like(flat)], axis=1)
+    part[0][0:rows, :DH] = numer
+    part[0][rows:, :DH] = flat
+    if len(part) == 2:
+        part[1][...] = numer_t
+    else:
+        part[0][0:rows, DH:] = numer_t
+        part[0][rows:, DH:] = jnp.zeros_like(flat)
+
+
+def part_shapes(rows, count):
+    if count == 2:
+        return [f32(rows + STAT_ROWS, DH), f32(rows, DH)]
+    return [f32(rows + STAT_ROWS, 2 * DH)]
 
 
 def merge_kernel(one, two, out):
-    store_part(out, *merge([one, two]))
-
-
-def finish_kernel(n_own, core_ref, *refs):
+    store_part((out,), *merge([(one,), (two,)]))
+
+
+def finish_kernel(n_own, counts, core_ref, *refs):
     *part_refs, out, tan = refs
-    for group, head in ((part_refs[:n_own], core_ref[0]), (part_refs[n_own:], 1 - core_ref[0])):
+    parts = parts_of(part_refs, counts)
+    for group, head in ((parts[:n_own], core_ref[0]), (parts[n_own:], 1 - core_ref[0])):
         _, total, total_t, numer, numer_t = merge(group)
         attended = numer / total
         column = pl.multiple_of(head * DH, DH)
@@ -262,7 +303,7 @@
     top_bit = n_q // 2
     far_q, near_q = list(range(1, n_q, 2)), list(range(0, n_q, 2))
     states = dict(zip(near_q, attend([q_blocks[i] for i in near_q], near_k, [], False)))
-    last_k = [(later(far_k, 2 * DH, mine_v), later(far_v, 2 * DH, states[0][1]))]
+    last_k = [(later(far_k, 2 * DH, mine_v), *halves(far_v, states[0][1]))]
     for masks in near:
         last_k += [tuple(swap(x, masks) for x in block) for block in last_k]
     far_kv = [(far_k, far_v)]
@@ -273,28 +314,39 @@
     if rest:
         blocks = [later(q_blocks[i], 2 * DH, states[1][1]) for i in rest]
         states.update(zip(rest, attend(blocks, near_k + far_kv, [], False)))
-    parts = attend(q_blocks, last_k[1:], [states[i] for i in range(n_q)], True)
+    aside = [i for i in far_q if i & top_bit]
+    parts = {}
+    for group, split in ((aside, False), ([i for i in range(n_q) if i not in aside], False)):
+        if group:
+            done = attend(
+                [q_blocks[i] for i in group], last_k[1:], [states[i] for i in group], True, split
+            )
+            parts.update(zip(group, done))
 
     def masks_of(index):
         return tuple(sum(bit for i, bit in enumerate(bits) if index >> i & 1) for bits in q_bits)
 
     own = [parts[0][0]] + [swap(parts[i][0], masks_of(i)) for i in range(1, n_q)]
-    cross, merged = [], parts[0][1]
+    cross = []
     for i in range(1, top_bit):
-        beside = swap(parts[i | top_bit][1], masks_of(top_bit))
+        beside = [swap(x, masks_of(top_bit)) for x in parts[i | top_bit][1:]]
         merged = pl.pallas_call(
-            merge_kernel, out_shape=f32(rows + STAT_ROWS, 2 * DH), compiler_params=params(8)
-        )(parts[i][1], beside)
-        cross.append(swap(merged, masks_of(i), True))
+            merge_kernel, out_shape=part_shapes(rows, 1), compiler_params=params(8)
+        )(parts[i][1], *beside)
+        cross.append([swap(x, masks_of(i), True) for x in merged])
     for i in (top_bit, 0):
-        cross.append(swap(later(parts[i][1], 2 * DH, merged), masks_of(i), True))
+        cross.append((swap(parts[i][1], masks_of(i), True),))
+    got = iter(landed([own[i] for i in far_q] + [x for part in cross[:-2] for x in part]))
+    own = [next(got) if i in far_q else x for i, x in enumerate(own)]
+    cross = [[next(got) for _ in part] for part in cross[:-2]] + cross[-2:]
+    counts = [1] * n_q + [len(part) for part in cross]
     return tuple(
         pl.pallas_call(
-            functools.partial(finish_kernel, n_q),
+            functools.partial(finish_kernel, n_q, counts),
             out_shape=[f32(rows, width)] * 2,
-            in_specs=[smem] + [vmem] * (n_q + len(cross)),
+            in_specs=[smem] + [vmem] * sum(counts),
             compiler_params=params(8),
-        )(core, *own, *cross)
+        )(core, *own, *(x for part in cross for x in part))
     )
 
 

time: 53.2 us -> 52.1 us (0.979)
  waiting for transfers between devices: 16.6 us -> 12.4 us
  starting transfers between devices: 22.6 us -> 25.2 us
    ppermute x16 -> x17, waiting for transfers between devices: 16.6 us -> 12.4 us  [swap(): lax.ppermute(x, AXES, [(i, i ^ flip ^ masks[i // n_kv % 2]) for i in rang...]
    ppermute x16 -> x17, starting transfers between devices: 22.6 us -> 25.2 us  [swap(): lax.ppermute(x, AXES, [(i, i ^ flip ^ masks[i // n_kv % 2]) for i in rang...]
    pallas_call x5 -> x6, Pallas kernels: 8.96 us -> 9.39 us  [attend(): pl.pallas_call(functools.partial(attend_kernel, n_q, n_k, rows, bool(prev...]
    pallas_call x2 -> x4, Pallas kernels: 1.94 us -> 1.99 us  [the longest x1 1.51 us: per_device(): pl.pallas_call(functools.partial(finish_kernel, n_q, counts), out_shape=[...]
  transfers between devices with their start and end apart: 16 -> 17, of which waited for: 9 -> 7; matrix products, arithmetic and copies ran while one was open for 0% -> 0% of each run, Pallas kernels for 13% -> 17%
where the time goes in v7:
time: 52.1 us; the launch traced here: 51.9 us
  starting transfers between devices  25.2 us (48%)
  Pallas kernels  13.6 us (26%)
  waiting for transfers between devices  12.4 us (24%)
  between operations  0.77 us (1%)
    ppermute x17, starting transfers between devices, swap(): lax.ppermute(x, AXES, [(i, i ^ flip ^ masks[i // n_kv % 2]) for i in rang...  25.2 us
    ppermute x17, waiting for transfers between devices, swap(): lax.ppermute(x, AXES, [(i, i ^ flip ^ masks[i // n_kv % 2]) for i in rang...  12.4 us
    pallas_call x6, Pallas kernels, attend(): pl.pallas_call(functools.partial(attend_kernel, n_q, n_k, rows, bool(prev...  9.39 us
    pallas_call x1, Pallas kernels, per_device(): pl.pallas_call(pack_kernel, out_shape=[f32(rows, w * DH) for w in (1, 1,...  2.02 us
    pallas_call x1, Pallas kernels, per_device(): pl.pallas_call(functools.partial(finish_kernel, n_q, counts), out_shape=[...  1.51 us
  transfers between devices with their start and end apart: 17, of which 7 were waited for; matrix products, arithmetic and copies ran while one was open for 0% of the time, Pallas kernels for 17%

profile of v7, /device:TPU:0, one launch (start us, length us, event | category | flops | bytes accessed | tf_op | source)
XLA Modules:
  0.0 51.9 jit_solution(7069510637997338529)
XLA Ops:
  0.6 2.0 %shard_map.77 = (f32[128,128]{1,0:T(8,128)S(1)}, f32[128,128]{1,0:T(8,128)S(1)}, f32[128,128]{1,0:T(8,128)S(1)}, f32[128,128]{1,0:T(8,128)S(1)}, f32[128,128]{1,...) custom-call(f32[128,256]{1,0:T(8,128)} %refs_0_.1, f32[128,256]{1,0:T(8,128)} %refs_1_.1, f32[128,256]{1,0:T(8,128)} %refs_2_.1, ...), custom_call_target="tpu_custom_call" | custom-call | tf_op jit(solution)/shard_map/pallas_call | solution.py:276
  2.7 0.5 collective-permute-start
  3.2 1.6 %collective-permute-done.refs_6_ = f32[128,768]{1,0:T(8,128)S(1)} collective-permute-done((f32[128,768]{1,0:T(8,128)}, f32[128,768]{1,0:T(8,128)S(1)}, u32[]{:S(2)}, u32[]{:S(2)}) %collective-permute-start) | collective-permute-done | bytes 393248 | tf_op jit(solution)/shard_map/ppermute | solution.py:269
  4.7 0.1 shard_map.78
  4.8 2.9 %collective-permute-start.4 = (f32[256,512]{1,0:T(8,128)S(1)}, f32[256,512]{1,0:T(8,128)S(1)}, u32[]{:S(2)}, u32[]{:S(2)}) collective-permute-start(f32[256,512]{1,0:T(8,128)S(1)} %get-tuple-element.48.x.refs_2_.refs_1_), channel_id=1, source_target_pairs={{0,8},{1,9},{2,10},{3,11},{4,20},{5,21},{6,22},{7,23},{8,0},{9,1},... | collective-permute-start | bytes 1572872 | tf_op jit(solution)/shard_map/ppermute | solution.py:269
  7.8 1.6 %collective-permute-start.1 = (f32[256,256]{1,0:T(8,128)S(1)}, f32[256,256]{1,0:T(8,128)S(1)}, u32[]{:S(2)}, u32[]{:S(2)}) collective-permute-start(f32[256,256]{1,0:T(8,128)S(1)} %get-tuple-element.46.refs_0_.refs_1_), channel_id=1, source_target_pairs={{0,1},{1,0},{2,3},{3,2},{4,6},{5,7},{6,4},{7,5},{8,9},{9,8},{10,11... | collective-permute-start | bytes 786440 | tf_op jit(solution)/shard_map/ppermute | solution.py:269
  9.3 2.6 %collective-permute-start.3 = (f32[256,256]{1,0:T(8,128)S(1)}, f32[256,256]{1,0:T(8,128)S(1)}, u32[]{:S(2)}, u32[]{:S(2)}) collective-permute-start(f32[256,256]{1,0:T(8,128)S(1)} %get-tuple-element.47), channel_id=1, source_target_pairs={{0,2},{1,3},{2,0},{3,1},{4,5},{5,4},{6,7},{7,6},{8,10},{9,11},{10,... | collective-permute-start | bytes 786440 | tf_op jit(solution)/shard_map/ppermute | solution.py:269
  11.9 1.5 %collective-permute-start.2 = (f32[256,256]{1,0:T(8,128)S(1)}, f32[256,256]{1,0:T(8,128)S(1)}, u32[]{:S(2)}, u32[]{:S(2)}) collective-permute-start(f32[256,256]{1,0:T(8,128)S(1)} %get-tuple-element.46.refs_0_.refs_1_), channel_id=1, source_target_pairs={{0,16},{1,17},{2,18},{3,19},{4,12},{5,13},{6,14},{7,15},{8,24},{9,... | collective-permute-start | bytes 786440 | tf_op jit(solution)/shard_map/ppermute | solution.py:269
  13.4 2.5 %collective-permute-done.4.after.refs_3_.refs_2_ = f32[256,512]{1,0:T(8,128)S(1)} collective-permute-done((f32[256,512]{1,0:T(8,128)S(1)}, f32[256,512]{1,0:T(8,128)S(1)}, u32[]{:S(2)}, u32[]{:S(2)}) %collective-permute-start.4) | collective-permute-done | bytes 524320 | tf_op jit(solution)/shard_map/ppermute | solution.py:269
  16.0 4.9 %collective-permute-start.6 = (f32[256,256]{1,0:T(8,128)S(1)}, f32[256,256]{1,0:T(8,128)S(1)}, u32[]{:S(2)}, u32[]{:S(2)}) collective-permute-start(f32[256,256]{1,0:T(8,128)S(1)} %shard_map.79.after), channel_id=1, source_target_pairs={{0,2},{1,3},{2,0},{3,1},{4,5},{5,4},{6,7},{7,6},{8,10},{9,11},{10,... | collective-permute-start | bytes 786440 | tf_op jit(solution)/shard_map/ppermute | solution.py:269
  20.9 1.1 %collective-permute-done.1.refs_0_.refs_1_.x = f32[256,256]{1,0:T(8,128)S(1)} collective-permute-done((f32[256,256]{1,0:T(8,128)S(1)}, f32[256,256]{1,0:T(8,128)S(1)}, u32[]{:S(2)}, u32[]{:S(2)}) %collective-permute-start.1) | collective-permute-done | bytes 262176 | tf_op jit(solution)/shard_map/ppermute | solution.py:269
  22.1 0.7 %collective-permute-start.10 = (f32[256,256]{1,0:T(8,128)S(1)}, f32[256,256]{1,0:T(8,128)S(1)}, u32[]{:S(2)}, u32[]{:S(2)}) collective-permute-start(f32[256,256]{1,0:T(8,128)S(1)} %shard_map.86), channel_id=1, source_target_pairs={{0,16},{1,17},{2,18},{3,19},{4,12},{5,13},{6,14},{7,15},{8,24},{9,... | collective-permute-start | bytes 786440 | tf_op jit(solution)/shard_map/ppermute | solution.py:269
  22.8 1.4 %collective-permute-start.5 = (f32[256,256]{1,0:T(8,128)S(1)}, f32[256,256]{1,0:T(8,128)S(1)}, u32[]{:S(2)}, u32[]{:S(2)}) collective-permute-start(f32[256,256]{1,0:T(8,128)S(1)} %shard_map.80), channel_id=1, source_target_pairs={{0,8},{1,9},{2,10},{3,11},{4,20},{5,21},{6,22},{7,23},{8,0},{9,1},... | collective-permute-start | bytes 786440 | tf_op jit(solution)/shard_map/ppermute | solution.py:269
  24.3 1.8 %shard_map.81 = (f32[256,256]{1,0:T(8,128)S(1)}, f32[256,128]{1,0:T(8,128)S(1)}, f32[256,256]{1,0:T(8,128)S(1)}, f32[256,128]{1,0:T(8,128)S(1)}) custom-call(f32[256,256]{1,0:T(8,128)S(1)} %get-tuple-element.46.refs_0_.refs_1_, f32[256,256]{1,0:T(8,128)S(1)} %collective-permute-done.2.refs_1_.refs_2_, f32[256,512]{1,0:T(8,128)S(1)} %get-tuple-element.48.x.refs_2_.refs_1_, ...), custom_call_target="tpu_custom_call" | custom-call | flops 2415919104 | bytes 3145728 | tf_op jit(solution)/shard_map/pallas_call | solution.py:180
  26.1 1.1 %shard_map.83 = (f32[256,256]{1,0:T(8,128)S(1)}, f32[256,128]{1,0:T(8,128)S(1)}) custom-call(f32[256,256]{1,0:T(8,128)S(1)} %collective-permute-done.1.refs_0_.refs_1_.x, f32[256,512]{1,0:T(8,128)S(1)} %get-tuple-element.48.x.refs_2_.refs_1_, f32[256,512]{1,0:T(8,128)S(1)} %collective-permute-done.4.after.refs_3_.refs_2_), custom_call_target="tpu_custom_call" | custom-call | flops 1207959552 | bytes 2097152 | tf_op jit(solution)/shard_map/pallas_call | solution.py:180
  27.1 2.0 %collective-permute-done.6.x.refs_4_ = f32[256,256]{1,0:T(8,128)S(1)} collective-permute-done((f32[256,256]{1,0:T(8,128)S(1)}, f32[256,256]{1,0:T(8,128)S(1)}, u32[]{:S(2)}, u32[]{:S(2)}) %collective-permute-start.6) | collective-permute-done | bytes 262176 | tf_op jit(solution)/shard_map/ppermute | solution.py:269
  29.2 0.4 collective-permute-start.7
  29.6 1.7 %collective-permute-start.8 = (f32[256,128]{1,0:T(8,128)S(1)}, f32[256,128]{1,0:T(8,128)S(1)}, u32[]{:S(2)}, u32[]{:S(2)}) collective-permute-start(f32[256,128]{1,0:T(8,128)S(1)} %get-tuple-element.51), channel_id=1, source_target_pairs={{0,8},{1,9},{2,10},{3,11},{4,20},{5,21},{6,22},{7,23},{8,0},{9,1},... | collective-permute-start | bytes 393224 | tf_op jit(solution)/shard_map/ppermute | solution.py:269
  31.3 2.1 %shard_map.84 = (f32[256,256]{1,0:T(8,128)S(1)}, f32[256,128]{1,0:T(8,128)S(1)}, f32[256,256]{1,0:T(8,128)S(1)}, f32[256,128]{1,0:T(8,128)S(1)}, f32[256,256]{1,0:T(8,128)S(1)}, /*index=5*/f32[256,128]{1,0:T(8,128)S(1)}) custom-call(f32[256,256]{1,0:T(8,128)S(1)} %collective-permute-done.1.refs_0_.refs_1_.x, ...), custom_call_target="tpu_custom_call" | custom-call | flops 1811939328 | bytes 3670016 | tf_op jit(solution)/shard_map/pallas_call | solution.py:180
  33.4 1.4 %shard_map.88 = (f32[256,256]{1,0:T(8,128)S(1)}, f32[256,128]{1,0:T(8,128)S(1)}) custom-call(f32[256,256]{1,0:T(8,128)S(1)} %shard_map.87.refs_0_, f32[256,512]{1,0:T(8,128)S(1)} %get-tuple-element.48.x.refs_2_.refs_1_, f32[256,512]{1,0:T(8,128)S(1)} %collective-permute-done.4.after.refs_3_.refs_2_, f32[256,256]{1,0:T(8,128)S(1)} %collective-permute-done.3.x.refs_3_, ...), custom_call_target="tpu_custom_call" | custom-call | flops 1811939328 | bytes 2621440 | tf_op jit(solution)/shard_map/pallas_call | solution.py:180
  34.8 0.8 %collective-permute-done.8.refs_5_.refs_3_ = f32[256,128]{1,0:T(8,128)S(1)} collective-permute-done((f32[256,128]{1,0:T(8,128)S(1)}, f32[256,128]{1,0:T(8,128)S(1)}, u32[]{:S(2)}, u32[]{:S(2)}) %collective-permute-start.8) | collective-permute-done | bytes 131104 | tf_op jit(solution)/shard_map/ppermute | solution.py:269
  35.6 0.9 %shard_map.89 = (f32[136,256]{1,0:T(8,128)S(1)}, f32[136,256]{1,0:T(8,128)S(1)}) custom-call(f32[256,256]{1,0:T(8,128)S(1)} %collective-permute-done.10.x.refs_0_, f32[256,256]{1,0:T(8,128)S(1)} %collective-permute-done.5.refs_3_.refs_1_, f32[256,128]{1,0:T(8,128)S(1)} %collective-permute-done.7.refs_4_.refs_2_, ...), custom_call_target="tpu_custom_call" | custom-call | flops 603979776 | bytes 1572864 | tf_op jit(solution)/shard_map/pallas_call | solution.py:180
  36.5 0.8 %collective-permute-start.12 = (f32[136,256]{1,0:T(8,128)S(1)}, f32[136,256]{1,0:T(8,128)S(1)}, u32[]{:S(2)}, u32[]{:S(2)}) collective-permute-start(f32[136,256]{1,0:T(8,128)S(1)} %get-tuple-element.69), channel_id=1, source_target_pairs={{0,16},{1,17},{2,18},{3,19},{4,12},{5,13},{6,14},{7,15},{8,24},{9,... | collective-permute-start | bytes 417800 | tf_op jit(solution)/shard_map/ppermute | solution.py:269
  37.4 1.2 %collective-permute-start.11 = (f32[136,256]{1,0:T(8,128)S(1)}, f32[136,256]{1,0:T(8,128)S(1)}, u32[]{:S(2)}, u32[]{:S(2)}) collective-permute-start(f32[136,256]{1,0:T(8,128)S(1)} %get-tuple-element.67), channel_id=1, source_target_pairs={{0,17},{1,16},{2,19},{3,18},{4,14},{5,15},{6,12},{7,13},{8,25},{9,... | collective-permute-start | bytes 417800 | tf_op jit(solution)/shard_map/ppermute | solution.py:269
  38.6 2.2 %shard_map.85 = (f32[136,256]{1,0:T(8,128)S(1)}, f32[136,256]{1,0:T(8,128)S(1)}, f32[136,256]{1,0:T(8,128)S(1)}, f32[136,256]{1,0:T(8,128)S(1)}, f32[136,256]{1,0:T(8,128)S(1)}, /*index=5*/f32[136,256]{1,0:T(8,128)S(1)}) custom-call(f32[256,256]{1,0:T(8,128)S(1)} %get-tuple-element.46.refs_0_.refs_1_, ...), custom_call_target="tpu_custom_call" | custom-call | flops 1811939328 | bytes 3670016 | tf_op jit(solution)/shard_map/pallas_call | solution.py:180
  40.7 1.6 %collective-permute-start.9 = (f32[136,256]{1,0:T(8,128)S(1)}, f32[136,256]{1,0:T(8,128)S(1)}, u32[]{:S(2)}, u32[]{:S(2)}) collective-permute-start(f32[136,256]{1,0:T(8,128)S(1)} %get-tuple-element.64), channel_id=1, source_target_pairs={{0,1},{1,0},{2,3},{3,2},{4,6},{5,7},{6,4},{7,5},{8,9},{9,8},{10,11... | collective-permute-start | bytes 417800 | tf_op jit(solution)/shard_map/ppermute | solution.py:269
  42.3 0.8 %collective-permute-start.14 = (f32[136,256]{1,0:T(8,128)S(1)}, f32[136,256]{1,0:T(8,128)S(1)}, u32[]{:S(2)}, u32[]{:S(2)}) collective-permute-start(f32[136,256]{1,0:T(8,128)S(1)} %get-tuple-element.71), channel_id=1, source_target_pairs={{0,16},{1,17},{2,18},{3,19},{4,12},{5,13},{6,14},{7,15},{8,24},{9,... | collective-permute-start | bytes 417800 | tf_op jit(solution)/shard_map/ppermute | solution.py:269
  43.1 0.4 shard_map.90
  43.5 2.5 %collective-permute-start.15 = (f32[136,256]{1,0:T(8,128)S(1)}, f32[136,256]{1,0:T(8,128)S(1)}, u32[]{:S(2)}, u32[]{:S(2)}) collective-permute-start(f32[136,256]{1,0:T(8,128)S(1)} %get-tuple-element.74), channel_id=1, source_target_pairs={{0,20},{1,21},{2,22},{3,23},{4,8},{5,9},{6,10},{7,11},{8,28},{9,29... | collective-permute-start | bytes 417800 | tf_op jit(solution)/shard_map/ppermute | solution.py:269
  46.0 0.6 %collective-permute-done.9.refs_0_ = f32[136,256]{1,0:T(8,128)S(1)} collective-permute-done((f32[136,256]{1,0:T(8,128)S(1)}, f32[136,256]{1,0:T(8,128)S(1)}, u32[]{:S(2)}, u32[]{:S(2)}) %collective-permute-start.9) | collective-permute-done | bytes 139296 | tf_op jit(solution)/shard_map/ppermute | solution.py:269
  46.7 3.7 %collective-permute-done.13.refs_2_ = f32[136,256]{1,0:T(8,128)S(1)} collective-permute-done((f32[136,256]{1,0:T(8,128)S(1)}, f32[136,256]{1,0:T(8,128)S(1)}, u32[]{:S(2)}, u32[]{:S(2)}) %collective-permute-start.13) | collective-permute-done | bytes 139296 | tf_op jit(solution)/shard_map/ppermute | solution.py:269
  50.4 1.5 %shard_map.92 = (f32[128,256]{1,0:T(8,128)}, f32[128,256]{1,0:T(8,128)}) custom-call(s32[1]{0:T(128)} %bitcast.core_ref, f32[136,256]{1,0:T(8,128)S(1)} %get-tuple-element.63.refs_0_, f32[136,256]{1,0:T(8,128)S(1)} %get-tuple-element.70.refs_1_, f32[136,256]{1,0:T(8,128)S(1)} %collective-permute-done.14.refs_2_, f32[136,256]{1,0:T(8,128)S(1)} %get-tuple-element.72.refs_3_, ...), custom_call_target="tpu_custom_call" | custom-call | tf_op jit(solution)/shard_map/pallas_call | solution.py:344
  (18 shorter events, 0.2 us)
Async XLA Ops:
  2.7 2.1 %collective-permute-start = (f32[128,768]{1,0:T(8,128)}, f32[128,768]{1,0:T(8,128)S(1)}, u32[]{:S(2)}, u32[]{:S(2)}) collective-permute-start(f32[128,768]{1,0:T(8,128)} %get-tuple-element.45), channel_id=1, source_target_pairs={{0,4},{1,5},{2,6},{3,7},{4,0},{5,1},{6,2},{7,3},{8,12},{9,13},{10,... | collective-permute-start | bytes 1179656 | tf_op jit(solution)/shard_map/ppermute | solution.py:269
  4.8 11.2 %collective-permute-start.4 = (f32[256,512]{1,0:T(8,128)S(1)}, f32[256,512]{1,0:T(8,128)S(1)}, u32[]{:S(2)}, u32[]{:S(2)}) collective-permute-start(f32[256,512]{1,0:T(8,128)S(1)} %get-tuple-element.48.x.refs_2_.refs_1_), channel_id=1, source_target_pairs={{0,8},{1,9},{2,10},{3,11},{4,20},{5,21},{6,22},{7,23},{8,0},{9,1},... | collective-permute-start | bytes 1572872 | tf_op jit(solution)/shard_map/ppermute | solution.py:269
  7.8 14.3 %collective-permute-start.1 = (f32[256,256]{1,0:T(8,128)S(1)}, f32[256,256]{1,0:T(8,128)S(1)}, u32[]{:S(2)}, u32[]{:S(2)}) collective-permute-start(f32[256,256]{1,0:T(8,128)S(1)} %get-tuple-element.46.refs_0_.refs_1_), channel_id=1, source_target_pairs={{0,1},{1,0},{2,3},{3,2},{4,6},{5,7},{6,4},{7,5},{8,9},{9,8},{10,11... | collective-permute-start | bytes 786440 | tf_op jit(solution)/shard_map/ppermute | solution.py:269
  9.3 13.4 %collective-permute-start.3 = (f32[256,256]{1,0:T(8,128)S(1)}, f32[256,256]{1,0:T(8,128)S(1)}, u32[]{:S(2)}, u32[]{:S(2)}) collective-permute-start(f32[256,256]{1,0:T(8,128)S(1)} %get-tuple-element.47), channel_id=1, source_target_pairs={{0,2},{1,3},{2,0},{3,1},{4,5},{5,4},{6,7},{7,6},{8,10},{9,11},{10,... | collective-permute-start | bytes 786440 | tf_op jit(solution)/shard_map/ppermute | solution.py:269
  11.9 12.3 %collective-permute-start.2 = (f32[256,256]{1,0:T(8,128)S(1)}, f32[256,256]{1,0:T(8,128)S(1)}, u32[]{:S(2)}, u32[]{:S(2)}) collective-permute-start(f32[256,256]{1,0:T(8,128)S(1)} %get-tuple-element.46.refs_0_.refs_1_), channel_id=1, source_target_pairs={{0,16},{1,17},{2,18},{3,19},{4,12},{5,13},{6,14},{7,15},{8,24},{9,... | collective-permute-start | bytes 786440 | tf_op jit(solution)/shard_map/ppermute | solution.py:269
  16.0 13.1 %collective-permute-start.6 = (f32[256,256]{1,0:T(8,128)S(1)}, f32[256,256]{1,0:T(8,128)S(1)}, u32[]{:S(2)}, u32[]{:S(2)}) collective-permute-start(f32[256,256]{1,0:T(8,128)S(1)} %shard_map.79.after), channel_id=1, source_target_pairs={{0,2},{1,3},{2,0},{3,1},{4,5},{5,4},{6,7},{7,6},{8,10},{9,11},{10,... | collective-permute-start | bytes 786440 | tf_op jit(solution)/shard_map/ppermute | solution.py:269
  22.1 11.3 %collective-permute-start.10 = (f32[256,256]{1,0:T(8,128)S(1)}, f32[256,256]{1,0:T(8,128)S(1)}, u32[]{:S(2)}, u32[]{:S(2)}) collective-permute-start(f32[256,256]{1,0:T(8,128)S(1)} %shard_map.86), channel_id=1, source_target_pairs={{0,16},{1,17},{2,18},{3,19},{4,12},{5,13},{6,14},{7,15},{8,24},{9,... | collective-permute-start | bytes 786440 | tf_op jit(solution)/shard_map/ppermute | solution.py:269
  22.8 12.0 %collective-permute-start.5 = (f32[256,256]{1,0:T(8,128)S(1)}, f32[256,256]{1,0:T(8,128)S(1)}, u32[]{:S(2)}, u32[]{:S(2)}) collective-permute-start(f32[256,256]{1,0:T(8,128)S(1)} %shard_map.80), channel_id=1, source_target_pairs={{0,8},{1,9},{2,10},{3,11},{4,20},{5,21},{6,22},{7,23},{8,0},{9,1},... | collective-permute-start | bytes 786440 | tf_op jit(solution)/shard_map/ppermute | solution.py:269
  29.2 5.6 %collective-permute-start.7 = (f32[256,128]{1,0:T(8,128)S(1)}, f32[256,128]{1,0:T(8,128)S(1)}, u32[]{:S(2)}, u32[]{:S(2)}) collective-permute-start(f32[256,128]{1,0:T(8,128)S(1)} %get-tuple-element.50), channel_id=1, source_target_pairs={{0,8},{1,9},{2,10},{3,11},{4,20},{5,21},{6,22},{7,23},{8,0},{9,1},... | collective-permute-start | bytes 393224 | tf_op jit(solution)/shard_map/ppermute | solution.py:269
  29.6 6.1 %collective-permute-start.8 = (f32[256,128]{1,0:T(8,128)S(1)}, f32[256,128]{1,0:T(8,128)S(1)}, u32[]{:S(2)}, u32[]{:S(2)}) collective-permute-start(f32[256,128]{1,0:T(8,128)S(1)} %get-tuple-element.51), channel_id=1, source_target_pairs={{0,8},{1,9},{2,10},{3,11},{4,20},{5,21},{6,22},{7,23},{8,0},{9,1},... | collective-permute-start | bytes 393224 | tf_op jit(solution)/shard_map/ppermute | solution.py:269
  36.5 6.6 %collective-permute-start.12 = (f32[136,256]{1,0:T(8,128)S(1)}, f32[136,256]{1,0:T(8,128)S(1)}, u32[]{:S(2)}, u32[]{:S(2)}) collective-permute-start(f32[136,256]{1,0:T(8,128)S(1)} %get-tuple-element.69), channel_id=1, source_target_pairs={{0,16},{1,17},{2,18},{3,19},{4,12},{5,13},{6,14},{7,15},{8,24},{9,... | collective-permute-start | bytes 417800 | tf_op jit(solution)/shard_map/ppermute | solution.py:269
  37.4 8.7 %collective-permute-start.11 = (f32[136,256]{1,0:T(8,128)S(1)}, f32[136,256]{1,0:T(8,128)S(1)}, u32[]{:S(2)}, u32[]{:S(2)}) collective-permute-start(f32[136,256]{1,0:T(8,128)S(1)} %get-tuple-element.67), channel_id=1, source_target_pairs={{0,17},{1,16},{2,19},{3,18},{4,14},{5,15},{6,12},{7,13},{8,25},{9,... | collective-permute-start | bytes 417800 | tf_op jit(solution)/shard_map/ppermute | solution.py:269
  40.7 5.9 %collective-permute-start.9 = (f32[136,256]{1,0:T(8,128)S(1)}, f32[136,256]{1,0:T(8,128)S(1)}, u32[]{:S(2)}, u32[]{:S(2)}) collective-permute-start(f32[136,256]{1,0:T(8,128)S(1)} %get-tuple-element.64), channel_id=1, source_target_pairs={{0,1},{1,0},{2,3},{3,2},{4,6},{5,7},{6,4},{7,5},{8,9},{9,8},{10,11... | collective-permute-start | bytes 417800 | tf_op jit(solution)/shard_map/ppermute | solution.py:269
  42.3 8.1 %collective-permute-start.14 = (f32[136,256]{1,0:T(8,128)S(1)}, f32[136,256]{1,0:T(8,128)S(1)}, u32[]{:S(2)}, u32[]{:S(2)}) collective-permute-start(f32[136,256]{1,0:T(8,128)S(1)} %get-tuple-element.71), channel_id=1, source_target_pairs={{0,16},{1,17},{2,18},{3,19},{4,12},{5,13},{6,14},{7,15},{8,24},{9,... | collective-permute-start | bytes 417800 | tf_op jit(solution)/shard_map/ppermute | solution.py:269
  43.5 6.8 %collective-permute-start.13 = (f32[136,256]{1,0:T(8,128)S(1)}, f32[136,256]{1,0:T(8,128)S(1)}, u32[]{:S(2)}, u32[]{:S(2)}) collective-permute-start(f32[136,256]{1,0:T(8,128)S(1)} %shard_map.90), channel_id=1, source_target_pairs={{0,5},{1,4},{2,7},{3,6},{4,2},{5,3},{6,0},{7,1},{8,13},{9,12},{10,... | collective-permute-start | bytes 417800 | tf_op jit(solution)/shard_map/ppermute | solution.py:269
  43.5 6.8 %collective-permute-start.15 = (f32[136,256]{1,0:T(8,128)S(1)}, f32[136,256]{1,0:T(8,128)S(1)}, u32[]{:S(2)}, u32[]{:S(2)}) collective-permute-start(f32[136,256]{1,0:T(8,128)S(1)} %get-tuple-element.74), channel_id=1, source_target_pairs={{0,20},{1,21},{2,22},{3,23},{4,8},{5,9},{6,10},{7,11},{8,28},{9,29... | collective-permute-start | bytes 417800 | tf_op jit(solution)/shard_map/ppermute | solution.py:269
  46.0 4.4 %collective-permute-start.16 = (f32[136,256]{1,0:T(8,128)S(1)}, f32[136,256]{1,0:T(8,128)S(1)}, u32[]{:S(2)}, u32[]{:S(2)}) collective-permute-start(f32[136,256]{1,0:T(8,128)S(1)} %get-tuple-element.75), channel_id=1, source_target_pairs={{0,4},{1,5},{2,6},{3,7},{4,0},{5,1},{6,2},{7,3},{8,12},{9,13},{10,... | collective-permute-start | bytes 417800 | tf_op jit(solution)/shard_map/ppermute | solution.py:269

commit v8 on v7

--- a/solution.py
+++ b/solution.py
@@ -81,6 +81,17 @@
     return pl.pallas_call(
         later_kernel, out_shape=f32(x.shape[0], columns), compiler_params=params(8)
     )(x, after)
+
+
+def same_kernel(*refs):
+    for ref, out in zip(refs[: len(refs) // 2], refs[len(refs) // 2 :]):
+        out[...] = ref[...]
+
+
+def landed(arrays):
+    return pl.pallas_call(
+        same_kernel, out_shape=[f32(*x.shape) for x in arrays], compiler_params=params(8)
+    )(*arrays)
 
 
 def same_kernel(*refs):
@@ -303,7 +314,7 @@
     top_bit = n_q // 2
     far_q, near_q = list(range(1, n_q, 2)), list(range(0, n_q, 2))
     states = dict(zip(near_q, attend([q_blocks[i] for i in near_q], near_k, [], False)))
-    last_k = [(later(far_k, 2 * DH, mine_v), *halves(far_v, states[0][1]))]
+    last_k = [(later(far_k, 2 * DH, mine_v), later(far_v, 2 * DH, states[0][1]))]
     for masks in near:
         last_k += [tuple(swap(x, masks) for x in block) for block in last_k]
     far_kv = [(far_k, far_v)]
@@ -335,7 +346,7 @@
         )(parts[i][1], *beside)
         cross.append([swap(x, masks_of(i), True) for x in merged])
     for i in (top_bit, 0):
-        cross.append((swap(parts[i][1], masks_of(i), True),))
+        cross.append((swap(later(parts[i][1], 2 * DH, own[-1]), masks_of(i), True),))
     got = iter(landed([own[i] for i in far_q] + [x for part in cross[:-2] for x in part]))
     own = [next(got) if i in far_q else x for i, x in enumerate(own)]
     cross = [[next(got) for _ in part] for part in cross[:-2]] + cross[-2:]

time: 52.1 us -> 52.4 us (level)
  waiting for transfers between devices: 12.4 us -> 14.5 us
  starting transfers between devices: 25.2 us -> 23.5 us
    ppermute x17 -> x16, waiting for transfers between devices: 12.4 us -> 14.5 us  [swap(): lax.ppermute(x, AXES, [(i, i ^ flip ^ masks[i // n_kv % 2]) for i in rang...]
    ppermute x17 -> x16, starting transfers between devices: 25.2 us -> 23.5 us  [swap(): lax.ppermute(x, AXES, [(i, i ^ flip ^ masks[i // n_kv % 2]) for i in rang...]
  transfers between devices with their start and end apart: 17 -> 16, of which waited for: 7 -> 9; matrix products, arithmetic and copies ran while one was open for 0% -> 0% of each run, Pallas kernels for 17% -> 17%
where the time goes in v8:
time: 52.4 us; the launch traced here: 52.3 us
  starting transfers between devices  23.5 us (45%)
  waiting for transfers between devices  14.5 us (28%)
  Pallas kernels  13.5 us (26%)
  between operations  0.76 us (1%)
    ppermute x16, starting transfers between devices, swap(): lax.ppermute(x, AXES, [(i, i ^ flip ^ masks[i // n_kv % 2]) for i in rang...  23.5 us
    ppermute x16, waiting for transfers between devices, swap(): lax.ppermute(x, AXES, [(i, i ^ flip ^ masks[i // n_kv % 2]) for i in rang...  14.5 us
    pallas_call x6, Pallas kernels, attend(): pl.pallas_call(functools.partial(attend_kernel, n_q, n_k, rows, bool(prev...  9.35 us
    pallas_call x1, Pallas kernels, per_device(): pl.pallas_call(pack_kernel, out_shape=[f32(rows, w * DH) for w in (1, 1,...  2.02 us
    pallas_call x1, Pallas kernels, per_device(): pl.pallas_call(functools.partial(finish_kernel, n_q, counts), out_shape=[...  1.51 us
  transfers between devices with their start and end apart: 16, of which 9 were waited for; matrix products, arithmetic and copies ran while one was open for 0% of the time, Pallas kernels for 17%

profile of v8, /device:TPU:0, one launch (start us, length us, event | category | flops | bytes accessed | tf_op | source)
XLA Modules:
  0.0 52.3 jit_solution(7226948573087238918)
XLA Ops:
  0.6 2.0 %shard_map.77 = (f32[128,128]{1,0:T(8,128)S(1)}, f32[128,128]{1,0:T(8,128)S(1)}, f32[128,128]{1,0:T(8,128)S(1)}, f32[128,128]{1,0:T(8,128)S(1)}, f32[128,128]{1,...) custom-call(f32[128,256]{1,0:T(8,128)} %refs_0_.1, f32[128,256]{1,0:T(8,128)} %refs_1_.1, f32[128,256]{1,0:T(8,128)} %refs_2_.1, ...), custom_call_target="tpu_custom_call" | custom-call | tf_op jit(solution)/shard_map/pallas_call | solution.py:287
  2.7 0.5 collective-permute-start
  3.2 1.6 %collective-permute-done.refs_6_ = f32[128,768]{1,0:T(8,128)S(1)} collective-permute-done((f32[128,768]{1,0:T(8,128)}, f32[128,768]{1,0:T(8,128)S(1)}, u32[]{:S(2)}, u32[]{:S(2)}) %collective-permute-start) | collective-permute-done | bytes 393248 | tf_op jit(solution)/shard_map/ppermute | solution.py:280
  4.8 2.9 %collective-permute-start.4 = (f32[256,512]{1,0:T(8,128)S(1)}, f32[256,512]{1,0:T(8,128)S(1)}, u32[]{:S(2)}, u32[]{:S(2)}) collective-permute-start(f32[256,512]{1,0:T(8,128)S(1)} %get-tuple-element.46.x.refs_2_.refs_1_), channel_id=1, source_target_pairs={{0,8},{1,9},{2,10},{3,11},{4,20},{5,21},{6,22},{7,23},{8,0},{9,1},... | collective-permute-start | bytes 1572872 | tf_op jit(solution)/shard_map/ppermute | solution.py:280
  7.8 1.6 %collective-permute-start.1 = (f32[256,256]{1,0:T(8,128)S(1)}, f32[256,256]{1,0:T(8,128)S(1)}, u32[]{:S(2)}, u32[]{:S(2)}) collective-permute-start(f32[256,256]{1,0:T(8,128)S(1)} %get-tuple-element.44.refs_0_.refs_1_), channel_id=1, source_target_pairs={{0,1},{1,0},{2,3},{3,2},{4,6},{5,7},{6,4},{7,5},{8,9},{9,8},{10,11... | collective-permute-start | bytes 786440 | tf_op jit(solution)/shard_map/ppermute | solution.py:280
  9.3 2.6 %collective-permute-start.3 = (f32[256,256]{1,0:T(8,128)S(1)}, f32[256,256]{1,0:T(8,128)S(1)}, u32[]{:S(2)}, u32[]{:S(2)}) collective-permute-start(f32[256,256]{1,0:T(8,128)S(1)} %get-tuple-element.45), channel_id=1, source_target_pairs={{0,2},{1,3},{2,0},{3,1},{4,5},{5,4},{6,7},{7,6},{8,10},{9,11},{10,... | collective-permute-start | bytes 786440 | tf_op jit(solution)/shard_map/ppermute | solution.py:280
  11.9 1.5 %collective-permute-start.2 = (f32[256,256]{1,0:T(8,128)S(1)}, f32[256,256]{1,0:T(8,128)S(1)}, u32[]{:S(2)}, u32[]{:S(2)}) collective-permute-start(f32[256,256]{1,0:T(8,128)S(1)} %get-tuple-element.44.refs_0_.refs_1_), channel_id=1, source_target_pairs={{0,16},{1,17},{2,18},{3,19},{4,12},{5,13},{6,14},{7,15},{8,24},{9,... | collective-permute-start | bytes 786440 | tf_op jit(solution)/shard_map/ppermute | solution.py:280
  13.4 2.5 %collective-permute-done.4.after.refs_3_.refs_2_ = f32[256,512]{1,0:T(8,128)S(1)} collective-permute-done((f32[256,512]{1,0:T(8,128)S(1)}, f32[256,512]{1,0:T(8,128)S(1)}, u32[]{:S(2)}, u32[]{:S(2)}) %collective-permute-start.4) | collective-permute-done | bytes 524320 | tf_op jit(solution)/shard_map/ppermute | solution.py:280
  16.0 4.9 %collective-permute-start.6 = (f32[256,256]{1,0:T(8,128)S(1)}, f32[256,256]{1,0:T(8,128)S(1)}, u32[]{:S(2)}, u32[]{:S(2)}) collective-permute-start(f32[256,256]{1,0:T(8,128)S(1)} %shard_map.79.after), channel_id=1, source_target_pairs={{0,2},{1,3},{2,0},{3,1},{4,5},{5,4},{6,7},{7,6},{8,10},{9,11},{10,... | collective-permute-start | bytes 786440 | tf_op jit(solution)/shard_map/ppermute | solution.py:280
  20.9 1.1 %collective-permute-done.1.refs_0_.refs_1_.x = f32[256,256]{1,0:T(8,128)S(1)} collective-permute-done((f32[256,256]{1,0:T(8,128)S(1)}, f32[256,256]{1,0:T(8,128)S(1)}, u32[]{:S(2)}, u32[]{:S(2)}) %collective-permute-start.1) | collective-permute-done | bytes 262176 | tf_op jit(solution)/shard_map/ppermute | solution.py:280
  22.1 0.7 %collective-permute-start.9 = (f32[256,256]{1,0:T(8,128)S(1)}, f32[256,256]{1,0:T(8,128)S(1)}, u32[]{:S(2)}, u32[]{:S(2)}) collective-permute-start(f32[256,256]{1,0:T(8,128)S(1)} %shard_map.86), channel_id=1, source_target_pairs={{0,16},{1,17},{2,18},{3,19},{4,12},{5,13},{6,14},{7,15},{8,24},{9,... | collective-permute-start | bytes 786440 | tf_op jit(solution)/shard_map/ppermute | solution.py:280
  22.8 1.4 %collective-permute-start.5 = (f32[256,256]{1,0:T(8,128)S(1)}, f32[256,256]{1,0:T(8,128)S(1)}, u32[]{:S(2)}, u32[]{:S(2)}) collective-permute-start(f32[256,256]{1,0:T(8,128)S(1)} %shard_map.80), channel_id=1, source_target_pairs={{0,8},{1,9},{2,10},{3,11},{4,20},{5,21},{6,22},{7,23},{8,0},{9,1},... | collective-permute-start | bytes 786440 | tf_op jit(solution)/shard_map/ppermute | solution.py:280
  24.3 1.8 %shard_map.81 = (f32[256,256]{1,0:T(8,128)S(1)}, f32[256,128]{1,0:T(8,128)S(1)}, f32[256,256]{1,0:T(8,128)S(1)}, f32[256,128]{1,0:T(8,128)S(1)}) custom-call(f32[256,256]{1,0:T(8,128)S(1)} %get-tuple-element.44.refs_0_.refs_1_, f32[256,256]{1,0:T(8,128)S(1)} %collective-permute-done.2.refs_1_.refs_2_, f32[256,512]{1,0:T(8,128)S(1)} %get-tuple-element.46.x.refs_2_.refs_1_, ...), custom_call_target="tpu_custom_call" | custom-call | flops 2415919104 | bytes 3145728 | tf_op jit(solution)/shard_map/pallas_call | solution.py:191
  26.1 1.0 %shard_map.83 = (f32[256,256]{1,0:T(8,128)S(1)}, f32[256,128]{1,0:T(8,128)S(1)}) custom-call(f32[256,256]{1,0:T(8,128)S(1)} %collective-permute-done.1.refs_0_.refs_1_.x, f32[256,512]{1,0:T(8,128)S(1)} %get-tuple-element.46.x.refs_2_.refs_1_, f32[256,512]{1,0:T(8,128)S(1)} %collective-permute-done.4.after.refs_3_.refs_2_), custom_call_target="tpu_custom_call" | custom-call | flops 1207959552 | bytes 2097152 | tf_op jit(solution)/shard_map/pallas_call | solution.py:191
  27.1 2.1 %collective-permute-done.6.x.refs_4_ = f32[256,256]{1,0:T(8,128)S(1)} collective-permute-done((f32[256,256]{1,0:T(8,128)S(1)}, f32[256,256]{1,0:T(8,128)S(1)}, u32[]{:S(2)}, u32[]{:S(2)}) %collective-permute-start.6) | collective-permute-done | bytes 262176 | tf_op jit(solution)/shard_map/ppermute | solution.py:280
  29.2 0.4 collective-permute-start.7
  29.6 2.1 %shard_map.84 = (f32[256,256]{1,0:T(8,128)S(1)}, f32[256,128]{1,0:T(8,128)S(1)}, f32[256,256]{1,0:T(8,128)S(1)}, f32[256,128]{1,0:T(8,128)S(1)}, f32[256,256]{1,0:T(8,128)S(1)}, /*index=5*/f32[256,128]{1,0:T(8,128)S(1)}) custom-call(f32[256,256]{1,0:T(8,128)S(1)} %collective-permute-done.1.refs_0_.refs_1_.x, ...), custom_call_target="tpu_custom_call" | custom-call | flops 1811939328 | bytes 3670016 | tf_op jit(solution)/shard_map/pallas_call | solution.py:191
  31.7 1.4 %shard_map.88 = (f32[256,256]{1,0:T(8,128)S(1)}, f32[256,128]{1,0:T(8,128)S(1)}) custom-call(f32[256,256]{1,0:T(8,128)S(1)} %shard_map.87.refs_0_, f32[256,512]{1,0:T(8,128)S(1)} %get-tuple-element.46.x.refs_2_.refs_1_, f32[256,512]{1,0:T(8,128)S(1)} %collective-permute-done.4.after.refs_3_.refs_2_, f32[256,256]{1,0:T(8,128)S(1)} %collective-permute-done.3.x.refs_3_, ...), custom_call_target="tpu_custom_call" | custom-call | flops 1811939328 | bytes 2621440 | tf_op jit(solution)/shard_map/pallas_call | solution.py:191
  33.1 2.5 %collective-permute-done.7.refs_4_.refs_2_ = f32[256,256]{1,0:T(8,128)S(1)} collective-permute-done((f32[256,256]{1,0:T(8,128)S(1)}, f32[256,256]{1,0:T(8,128)S(1)}, u32[]{:S(2)}, u32[]{:S(2)}) %collective-permute-start.7) | collective-permute-done | bytes 262176 | tf_op jit(solution)/shard_map/ppermute | solution.py:280
  35.6 0.9 %shard_map.89 = (f32[136,256]{1,0:T(8,128)S(1)}, f32[136,256]{1,0:T(8,128)S(1)}) custom-call(f32[256,256]{1,0:T(8,128)S(1)} %collective-permute-done.9.x.refs_0_, f32[256,256]{1,0:T(8,128)S(1)} %collective-permute-done.5.refs_3_.refs_1_, f32[256,256]{1,0:T(8,128)S(1)} %collective-permute-done.7.refs_4_.refs_2_, f32[256,256]{1,0:T(8,128)S(1)} %get-tuple-element.61.refs_3_, ...), custom_call_target="tpu_custom_call" | custom-call | flops 603979776 | bytes 1572864 | tf_op jit(solution)/shard_map/pallas_call | solution.py:191
  36.5 0.6 %collective-permute-start.10 = (f32[136,256]{1,0:T(8,128)S(1)}, f32[136,256]{1,0:T(8,128)S(1)}, u32[]{:S(2)}, u32[]{:S(2)}) collective-permute-start(f32[136,256]{1,0:T(8,128)S(1)} %get-tuple-element.63), channel_id=1, source_target_pairs={{0,17},{1,16},{2,19},{3,18},{4,14},{5,15},{6,12},{7,13},{8,25},{9,... | collective-permute-start | bytes 417800 | tf_op jit(solution)/shard_map/ppermute | solution.py:280
  37.1 1.4 %collective-permute-start.11 = (f32[136,256]{1,0:T(8,128)S(1)}, f32[136,256]{1,0:T(8,128)S(1)}, u32[]{:S(2)}, u32[]{:S(2)}) collective-permute-start(f32[136,256]{1,0:T(8,128)S(1)} %get-tuple-element.65), channel_id=1, source_target_pairs={{0,16},{1,17},{2,18},{3,19},{4,12},{5,13},{6,14},{7,15},{8,24},{9,... | collective-permute-start | bytes 417800 | tf_op jit(solution)/shard_map/ppermute | solution.py:280
  38.6 2.1 %shard_map.85 = (f32[136,256]{1,0:T(8,128)S(1)}, f32[136,256]{1,0:T(8,128)S(1)}, f32[136,256]{1,0:T(8,128)S(1)}, f32[136,256]{1,0:T(8,128)S(1)}, f32[136,256]{1,0:T(8,128)S(1)}, /*index=5*/f32[136,256]{1,0:T(8,128)S(1)}) custom-call(f32[256,256]{1,0:T(8,128)S(1)} %get-tuple-element.44.refs_0_.refs_1_, ...), custom_call_target="tpu_custom_call" | custom-call | flops 1811939328 | bytes 3670016 | tf_op jit(solution)/shard_map/pallas_call | solution.py:191
  40.7 1.6 %collective-permute-start.8 = (f32[136,256]{1,0:T(8,128)S(1)}, f32[136,256]{1,0:T(8,128)S(1)}, u32[]{:S(2)}, u32[]{:S(2)}) collective-permute-start(f32[136,256]{1,0:T(8,128)S(1)} %get-tuple-element.60), channel_id=1, source_target_pairs={{0,1},{1,0},{2,3},{3,2},{4,6},{5,7},{6,4},{7,5},{8,9},{9,8},{10,11... | collective-permute-start | bytes 417800 | tf_op jit(solution)/shard_map/ppermute | solution.py:280
  42.3 0.8 %collective-permute-start.13 = (f32[136,256]{1,0:T(8,128)S(1)}, f32[136,256]{1,0:T(8,128)S(1)}, u32[]{:S(2)}, u32[]{:S(2)}) collective-permute-start(f32[136,256]{1,0:T(8,128)S(1)} %get-tuple-element.67), channel_id=1, source_target_pairs={{0,16},{1,17},{2,18},{3,19},{4,12},{5,13},{6,14},{7,15},{8,24},{9,... | collective-permute-start | bytes 417800 | tf_op jit(solution)/shard_map/ppermute | solution.py:280
  43.1 0.5 collective-permute-done.11.two
  43.6 0.4 shard_map.90
  44.3 1.9 %collective-permute-start.15 = (f32[136,256]{1,0:T(8,128)S(1)}, f32[136,256]{1,0:T(8,128)S(1)}, u32[]{:S(2)}, u32[]{:S(2)}) collective-permute-start(f32[136,256]{1,0:T(8,128)S(1)} %shard_map.93), channel_id=1, source_target_pairs={{0,4},{1,5},{2,6},{3,7},{4,0},{5,1},{6,2},{7,3},{8,12},{9,13},{10,... | collective-permute-start | bytes 417800 | tf_op jit(solution)/shard_map/ppermute | solution.py:280
  46.2 0.6 %collective-permute-start.14 = (f32[136,256]{1,0:T(8,128)S(1)}, f32[136,256]{1,0:T(8,128)S(1)}, u32[]{:S(2)}, u32[]{:S(2)}) collective-permute-start(f32[136,256]{1,0:T(8,128)S(1)} %shard_map.92), channel_id=1, source_target_pairs={{0,20},{1,21},{2,22},{3,23},{4,8},{5,9},{6,10},{7,11},{8,28},{9,29... | collective-permute-start | bytes 417800 | tf_op jit(solution)/shard_map/ppermute | solution.py:280
  46.8 3.6 %collective-permute-done.12.refs_2_ = f32[136,256]{1,0:T(8,128)S(1)} collective-permute-done((f32[136,256]{1,0:T(8,128)S(1)}, f32[136,256]{1,0:T(8,128)S(1)}, u32[]{:S(2)}, u32[]{:S(2)}) %collective-permute-start.12) | collective-permute-done | bytes 139296 | tf_op jit(solution)/shard_map/ppermute | solution.py:280
  50.5 0.2 collective-permute-done.14.refs_5_
  50.8 1.5 %shard_map.94 = (f32[128,256]{1,0:T(8,128)}, f32[128,256]{1,0:T(8,128)}) custom-call(s32[1]{0:T(128)} %bitcast.core_ref, f32[136,256]{1,0:T(8,128)S(1)} %get-tuple-element.59.refs_0_, f32[136,256]{1,0:T(8,128)S(1)} %get-tuple-element.66.refs_1_, f32[136,256]{1,0:T(8,128)S(1)} %collective-permute-done.13.refs_2_, f32[136,256]{1,0:T(8,128)S(1)} %get-tuple-element.68.refs_3_, ...), custom_call_target="tpu_custom_call" | custom-call | tf_op jit(solution)/shard_map/pallas_call | solution.py:355
  (18 shorter events, 0.5 us)
Async XLA Ops:
  2.7 2.1 %collective-permute-start = (f32[128,768]{1,0:T(8,128)}, f32[128,768]{1,0:T(8,128)S(1)}, u32[]{:S(2)}, u32[]{:S(2)}) collective-permute-start(f32[128,768]{1,0:T(8,128)} %get-tuple-element.43), channel_id=1, source_target_pairs={{0,4},{1,5},{2,6},{3,7},{4,0},{5,1},{6,2},{7,3},{8,12},{9,13},{10,... | collective-permute-start | bytes 1179656 | tf_op jit(solution)/shard_map/ppermute | solution.py:280
  4.8 11.2 %collective-permute-start.4 = (f32[256,512]{1,0:T(8,128)S(1)}, f32[256,512]{1,0:T(8,128)S(1)}, u32[]{:S(2)}, u32[]{:S(2)}) collective-permute-start(f32[256,512]{1,0:T(8,128)S(1)} %get-tuple-element.46.x.refs_2_.refs_1_), channel_id=1, source_target_pairs={{0,8},{1,9},{2,10},{3,11},{4,20},{5,21},{6,22},{7,23},{8,0},{9,1},... | collective-permute-start | bytes 1572872 | tf_op jit(solution)/shard_map/ppermute | solution.py:280
  7.8 14.3 %collective-permute-start.1 = (f32[256,256]{1,0:T(8,128)S(1)}, f32[256,256]{1,0:T(8,128)S(1)}, u32[]{:S(2)}, u32[]{:S(2)}) collective-permute-start(f32[256,256]{1,0:T(8,128)S(1)} %get-tuple-element.44.refs_0_.refs_1_), channel_id=1, source_target_pairs={{0,1},{1,0},{2,3},{3,2},{4,6},{5,7},{6,4},{7,5},{8,9},{9,8},{10,11... | collective-permute-start | bytes 786440 | tf_op jit(solution)/shard_map/ppermute | solution.py:280
  9.3 13.4 %collective-permute-start.3 = (f32[256,256]{1,0:T(8,128)S(1)}, f32[256,256]{1,0:T(8,128)S(1)}, u32[]{:S(2)}, u32[]{:S(2)}) collective-permute-start(f32[256,256]{1,0:T(8,128)S(1)} %get-tuple-element.45), channel_id=1, source_target_pairs={{0,2},{1,3},{2,0},{3,1},{4,5},{5,4},{6,7},{7,6},{8,10},{9,11},{10,... | collective-permute-start | bytes 786440 | tf_op jit(solution)/shard_map/ppermute | solution.py:280
  11.9 12.3 %collective-permute-start.2 = (f32[256,256]{1,0:T(8,128)S(1)}, f32[256,256]{1,0:T(8,128)S(1)}, u32[]{:S(2)}, u32[]{:S(2)}) collective-permute-start(f32[256,256]{1,0:T(8,128)S(1)} %get-tuple-element.44.refs_0_.refs_1_), channel_id=1, source_target_pairs={{0,16},{1,17},{2,18},{3,19},{4,12},{5,13},{6,14},{7,15},{8,24},{9,... | collective-permute-start | bytes 786440 | tf_op jit(solution)/shard_map/ppermute | solution.py:280
  16.0 13.1 %collective-permute-start.6 = (f32[256,256]{1,0:T(8,128)S(1)}, f32[256,256]{1,0:T(8,128)S(1)}, u32[]{:S(2)}, u32[]{:S(2)}) collective-permute-start(f32[256,256]{1,0:T(8,128)S(1)} %shard_map.79.after), channel_id=1, source_target_pairs={{0,2},{1,3},{2,0},{3,1},{4,5},{5,4},{6,7},{7,6},{8,10},{9,11},{10,... | collective-permute-start | bytes 786440 | tf_op jit(solution)/shard_map/ppermute | solution.py:280
  22.1 9.5 %collective-permute-start.9 = (f32[256,256]{1,0:T(8,128)S(1)}, f32[256,256]{1,0:T(8,128)S(1)}, u32[]{:S(2)}, u32[]{:S(2)}) collective-permute-start(f32[256,256]{1,0:T(8,128)S(1)} %shard_map.86), channel_id=1, source_target_pairs={{0,16},{1,17},{2,18},{3,19},{4,12},{5,13},{6,14},{7,15},{8,24},{9,... | collective-permute-start | bytes 786440 | tf_op jit(solution)/shard_map/ppermute | solution.py:280
  22.8 10.3 %collective-permute-start.5 = (f32[256,256]{1,0:T(8,128)S(1)}, f32[256,256]{1,0:T(8,128)S(1)}, u32[]{:S(2)}, u32[]{:S(2)}) collective-permute-start(f32[256,256]{1,0:T(8,128)S(1)} %shard_map.80), channel_id=1, source_target_pairs={{0,8},{1,9},{2,10},{3,11},{4,20},{5,21},{6,22},{7,23},{8,0},{9,1},... | collective-permute-start | bytes 786440 | tf_op jit(solution)/shard_map/ppermute | solution.py:280
  29.2 6.4 %collective-permute-start.7 = (f32[256,256]{1,0:T(8,128)S(1)}, f32[256,256]{1,0:T(8,128)S(1)}, u32[]{:S(2)}, u32[]{:S(2)}) collective-permute-start(f32[256,256]{1,0:T(8,128)S(1)} %shard_map.82), channel_id=1, source_target_pairs={{0,8},{1,9},{2,10},{3,11},{4,20},{5,21},{6,22},{7,23},{8,0},{9,1},... | collective-permute-start | bytes 786440 | tf_op jit(solution)/shard_map/ppermute | solution.py:280
  36.5 7.8 %collective-permute-start.10 = (f32[136,256]{1,0:T(8,128)S(1)}, f32[136,256]{1,0:T(8,128)S(1)}, u32[]{:S(2)}, u32[]{:S(2)}) collective-permute-start(f32[136,256]{1,0:T(8,128)S(1)} %get-tuple-element.63), channel_id=1, source_target_pairs={{0,17},{1,16},{2,19},{3,18},{4,14},{5,15},{6,12},{7,13},{8,25},{9,... | collective-permute-start | bytes 417800 | tf_op jit(solution)/shard_map/ppermute | solution.py:280
  37.1 6.4 %collective-permute-start.11 = (f32[136,256]{1,0:T(8,128)S(1)}, f32[136,256]{1,0:T(8,128)S(1)}, u32[]{:S(2)}, u32[]{:S(2)}) collective-permute-start(f32[136,256]{1,0:T(8,128)S(1)} %get-tuple-element.65), channel_id=1, source_target_pairs={{0,16},{1,17},{2,18},{3,19},{4,12},{5,13},{6,14},{7,15},{8,24},{9,... | collective-permute-start | bytes 417800 | tf_op jit(solution)/shard_map/ppermute | solution.py:280
  40.7 6.1 %collective-permute-start.8 = (f32[136,256]{1,0:T(8,128)S(1)}, f32[136,256]{1,0:T(8,128)S(1)}, u32[]{:S(2)}, u32[]{:S(2)}) collective-permute-start(f32[136,256]{1,0:T(8,128)S(1)} %get-tuple-element.60), channel_id=1, source_target_pairs={{0,1},{1,0},{2,3},{3,2},{4,6},{5,7},{6,4},{7,5},{8,9},{9,8},{10,11... | collective-permute-start | bytes 417800 | tf_op jit(solution)/shard_map/ppermute | solution.py:280
  42.3 8.2 %collective-permute-start.13 = (f32[136,256]{1,0:T(8,128)S(1)}, f32[136,256]{1,0:T(8,128)S(1)}, u32[]{:S(2)}, u32[]{:S(2)}) collective-permute-start(f32[136,256]{1,0:T(8,128)S(1)} %get-tuple-element.67), channel_id=1, source_target_pairs={{0,16},{1,17},{2,18},{3,19},{4,12},{5,13},{6,14},{7,15},{8,24},{9,... | collective-permute-start | bytes 417800 | tf_op jit(solution)/shard_map/ppermute | solution.py:280
  44.0 6.5 %collective-permute-start.12 = (f32[136,256]{1,0:T(8,128)S(1)}, f32[136,256]{1,0:T(8,128)S(1)}, u32[]{:S(2)}, u32[]{:S(2)}) collective-permute-start(f32[136,256]{1,0:T(8,128)S(1)} %shard_map.90), channel_id=1, source_target_pairs={{0,5},{1,4},{2,7},{3,6},{4,2},{5,3},{6,0},{7,1},{8,13},{9,12},{10,... | collective-permute-start | bytes 417800 | tf_op jit(solution)/shard_map/ppermute | solution.py:280
  44.3 6.2 %collective-permute-start.15 = (f32[136,256]{1,0:T(8,128)S(1)}, f32[136,256]{1,0:T(8,128)S(1)}, u32[]{:S(2)}, u32[]{:S(2)}) collective-permute-start(f32[136,256]{1,0:T(8,128)S(1)} %shard_map.93), channel_id=1, source_target_pairs={{0,4},{1,5},{2,6},{3,7},{4,0},{5,1},{6,2},{7,3},{8,12},{9,13},{10,... | collective-permute-start | bytes 417800 | tf_op jit(solution)/shard_map/ppermute | solution.py:280
  46.2 4.5 %collective-permute-start.14 = (f32[136,256]{1,0:T(8,128)S(1)}, f32[136,256]{1,0:T(8,128)S(1)}, u32[]{:S(2)}, u32[]{:S(2)}) collective-permute-start(f32[136,256]{1,0:T(8,128)S(1)} %shard_map.92), channel_id=1, source_target_pairs={{0,20},{1,21},{2,22},{3,23},{4,8},{5,9},{6,10},{7,11},{8,28},{9,29... | collective-permute-start | bytes 417800 | tf_op jit(solution)/shard_map/ppermute | solution.py:280

commit v9 on v8

--- a/solution.py
+++ b/solution.py
@@ -327,29 +327,37 @@
         states.update(zip(rest, attend(blocks, near_k + far_kv, [], False)))
     aside = [i for i in far_q if i & top_bit]
     parts = {}
-    for group, split in ((aside, False), ([i for i in range(n_q) if i not in aside], False)):
-        if group:
-            done = attend(
-                [q_blocks[i] for i in group], last_k[1:], [states[i] for i in group], True, split
-            )
-            parts.update(zip(group, done))
+
+    def last_stage(group, after=None):
+        prev = [states[i] for i in group]
+        if after is not None:
+            prev[0] = (prev[0][0], later(prev[0][1], DH, after))
+        done = attend([q_blocks[i] for i in group], last_k[1:], prev, True)
+        parts.update(zip(group, done))
+
+    last_stage([i for i in far_q if i & top_bit])
+    last_stage([i for i in far_q if not i & top_bit])
 
     def masks_of(index):
         return tuple(sum(bit for i, bit in enumerate(bits) if index >> i & 1) for bits in q_bits)
 
-    own = [parts[0][0]] + [swap(parts[i][0], masks_of(i)) for i in range(1, n_q)]
-    cross = []
-    for i in range(1, top_bit):
-        beside = [swap(x, masks_of(top_bit)) for x in parts[i | top_bit][1:]]
-        merged = pl.pallas_call(
-            merge_kernel, out_shape=part_shapes(rows, 1), compiler_params=params(8)
-        )(parts[i][1], *beside)
-        cross.append([swap(x, masks_of(i), True) for x in merged])
-    for i in (top_bit, 0):
-        cross.append((swap(later(parts[i][1], 2 * DH, own[-1]), masks_of(i), True),))
-    got = iter(landed([own[i] for i in far_q] + [x for part in cross[:-2] for x in part]))
-    own = [next(got) if i in far_q else x for i, x in enumerate(own)]
-    cross = [[next(got) for _ in part] for part in cross[:-2]] + cross[-2:]
+    own = {i: swap(parts[i][0], masks_of(i)) for i in far_q}
+    cross, merged = [], None
+    for i in far_q:
+        if not i & top_bit:
+            beside = swap(parts[i | top_bit][1], masks_of(top_bit))
+            merged = pl.pallas_call(
+                merge_kernel, out_shape=f32(rows + STAT_ROWS, 2 * DH), compiler_params=params(8)
+            )(parts[i][1], beside)
+            cross.append((swap(merged, masks_of(i), True),))
+    last_stage(near_q, merged)
+    own.update({i: swap(parts[i][0], masks_of(i)) if i else parts[i][0] for i in near_q})
+    for i in [i for i in near_q if i & top_bit] + [i for i in near_q if not i & top_bit]:
+        cross.append((swap(parts[i][1], masks_of(i), True),))
+    far_cross = cross[: -len(near_q)]
+    got = iter(landed([own[i] for i in far_q] + [x for part in far_cross for x in part]))
+    own = [next(got) if i in far_q else own[i] for i in range(n_q)]
+    cross = [(next(got),) for _ in far_cross] + cross[-len(near_q) :]
     counts = [1] * n_q + [len(part) for part in cross]
     return tuple(
         pl.pallas_call(

time: 52.4 us -> 52.5 us (level)
    pallas_call x6 -> x7, Pallas kernels: 9.35 us -> 9.61 us  [attend(): pl.pallas_call(functools.partial(attend_kernel, n_q, n_k, rows, bool(prev...]
  transfers between devices with their start and end apart: 16 -> 16, of which waited for: 9 -> 9; matrix products, arithmetic and copies ran while one was open for 0% -> 0% of each run, Pallas kernels for 17% -> 18%
where the time goes in v9:
time: 52.5 us; the launch traced here: 52.4 us
  starting transfers between devices  23.4 us (45%)
  waiting for transfers between devices  14.5 us (28%)
  Pallas kernels  13.8 us (26%)
  between operations  0.75 us (1%)
    ppermute x16, starting transfers between devices, swap(): lax.ppermute(x, AXES, [(i, i ^ flip ^ masks[i // n_kv % 2]) for i in rang...  23.4 us
    ppermute x16, waiting for transfers between devices, swap(): lax.ppermute(x, AXES, [(i, i ^ flip ^ masks[i // n_kv % 2]) for i in rang...  14.5 us
    pallas_call x7, Pallas kernels, attend(): pl.pallas_call(functools.partial(attend_kernel, n_q, n_k, rows, bool(prev...  9.61 us
    pallas_call x1, Pallas kernels, per_device(): pl.pallas_call(pack_kernel, out_shape=[f32(rows, w * DH) for w in (1, 1,...  2 us
    pallas_call x1, Pallas kernels, per_device(): pl.pallas_call(functools.partial(finish_kernel, n_q, counts), out_shape=[...  1.51 us
  transfers between devices with their start and end apart: 16, of which 9 were waited for; matrix products, arithmetic and copies ran while one was open for 0% of the time, Pallas kernels for 18%

profile of v9, /device:TPU:0, one launch (start us, length us, event | category | flops | bytes accessed | tf_op | source)
XLA Modules:
  0.0 52.4 jit_solution(1194141859926633296)
XLA Ops:
  0.6 2.0 %shard_map.77 = (f32[128,128]{1,0:T(8,128)S(1)}, f32[128,128]{1,0:T(8,128)S(1)}, f32[128,128]{1,0:T(8,128)S(1)}, f32[128,128]{1,0:T(8,128)S(1)}, f32[128,128]{1,...) custom-call(f32[128,256]{1,0:T(8,128)} %refs_0_.1, f32[128,256]{1,0:T(8,128)} %refs_1_.1, f32[128,256]{1,0:T(8,128)} %refs_2_.1, ...), custom_call_target="tpu_custom_call" | custom-call | tf_op jit(solution)/shard_map/pallas_call | solution.py:287
  2.6 0.5 collective-permute-start
  3.2 1.6 %collective-permute-done.refs_6_ = f32[128,768]{1,0:T(8,128)S(1)} collective-permute-done((f32[128,768]{1,0:T(8,128)}, f32[128,768]{1,0:T(8,128)S(1)}, u32[]{:S(2)}, u32[]{:S(2)}) %collective-permute-start) | collective-permute-done | bytes 393248 | tf_op jit(solution)/shard_map/ppermute | solution.py:280
  4.8 2.9 %collective-permute-start.3 = (f32[256,512]{1,0:T(8,128)S(1)}, f32[256,512]{1,0:T(8,128)S(1)}, u32[]{:S(2)}, u32[]{:S(2)}) collective-permute-start(f32[256,512]{1,0:T(8,128)S(1)} %get-tuple-element.46.x.refs_2_.refs_1_), channel_id=1, source_target_pairs={{0,8},{1,9},{2,10},{3,11},{4,20},{5,21},{6,22},{7,23},{8,0},{9,1},... | collective-permute-start | bytes 1572872 | tf_op jit(solution)/shard_map/ppermute | solution.py:280
  7.7 1.6 %collective-permute-start.7 = (f32[256,256]{1,0:T(8,128)S(1)}, f32[256,256]{1,0:T(8,128)S(1)}, u32[]{:S(2)}, u32[]{:S(2)}) collective-permute-start(f32[256,256]{1,0:T(8,128)S(1)} %get-tuple-element.44.refs_0_.refs_1_), channel_id=1, source_target_pairs={{0,1},{1,0},{2,3},{3,2},{4,6},{5,7},{6,4},{7,5},{8,9},{9,8},{10,11... | collective-permute-start | bytes 786440 | tf_op jit(solution)/shard_map/ppermute | solution.py:280
  9.3 2.6 %collective-permute-start.2 = (f32[256,256]{1,0:T(8,128)S(1)}, f32[256,256]{1,0:T(8,128)S(1)}, u32[]{:S(2)}, u32[]{:S(2)}) collective-permute-start(f32[256,256]{1,0:T(8,128)S(1)} %get-tuple-element.45), channel_id=1, source_target_pairs={{0,2},{1,3},{2,0},{3,1},{4,5},{5,4},{6,7},{7,6},{8,10},{9,11},{10,... | collective-permute-start | bytes 786440 | tf_op jit(solution)/shard_map/ppermute | solution.py:280
  11.9 1.5 %collective-permute-start.1 = (f32[256,256]{1,0:T(8,128)S(1)}, f32[256,256]{1,0:T(8,128)S(1)}, u32[]{:S(2)}, u32[]{:S(2)}) collective-permute-start(f32[256,256]{1,0:T(8,128)S(1)} %get-tuple-element.44.refs_0_.refs_1_), channel_id=1, source_target_pairs={{0,16},{1,17},{2,18},{3,19},{4,12},{5,13},{6,14},{7,15},{8,24},{9,... | collective-permute-start | bytes 786440 | tf_op jit(solution)/shard_map/ppermute | solution.py:280
  13.4 2.5 %collective-permute-done.3.after.refs_3_.refs_2_ = f32[256,512]{1,0:T(8,128)S(1)} collective-permute-done((f32[256,512]{1,0:T(8,128)S(1)}, f32[256,512]{1,0:T(8,128)S(1)}, u32[]{:S(2)}, u32[]{:S(2)}) %collective-permute-start.3) | collective-permute-done | bytes 524320 | tf_op jit(solution)/shard_map/ppermute | solution.py:280
  16.0 4.9 %collective-permute-start.5 = (f32[256,256]{1,0:T(8,128)S(1)}, f32[256,256]{1,0:T(8,128)S(1)}, u32[]{:S(2)}, u32[]{:S(2)}) collective-permute-start(f32[256,256]{1,0:T(8,128)S(1)} %shard_map.79.after), channel_id=1, source_target_pairs={{0,2},{1,3},{2,0},{3,1},{4,5},{5,4},{6,7},{7,6},{8,10},{9,11},{10,... | collective-permute-start | bytes 786440 | tf_op jit(solution)/shard_map/ppermute | solution.py:280
  20.9 1.1 %collective-permute-done.7.refs_0_.x = f32[256,256]{1,0:T(8,128)S(1)} collective-permute-done((f32[256,256]{1,0:T(8,128)S(1)}, f32[256,256]{1,0:T(8,128)S(1)}, u32[]{:S(2)}, u32[]{:S(2)}) %collective-permute-start.7) | collective-permute-done | bytes 262176 | tf_op jit(solution)/shard_map/ppermute | solution.py:280
  22.1 0.7 %collective-permute-start.8 = (f32[256,256]{1,0:T(8,128)S(1)}, f32[256,256]{1,0:T(8,128)S(1)}, u32[]{:S(2)}, u32[]{:S(2)}) collective-permute-start(f32[256,256]{1,0:T(8,128)S(1)} %shard_map.86), channel_id=1, source_target_pairs={{0,16},{1,17},{2,18},{3,19},{4,12},{5,13},{6,14},{7,15},{8,24},{9,... | collective-permute-start | bytes 786440 | tf_op jit(solution)/shard_map/ppermute | solution.py:280
  22.8 1.4 %collective-permute-start.4 = (f32[256,256]{1,0:T(8,128)S(1)}, f32[256,256]{1,0:T(8,128)S(1)}, u32[]{:S(2)}, u32[]{:S(2)}) collective-permute-start(f32[256,256]{1,0:T(8,128)S(1)} %shard_map.80), channel_id=1, source_target_pairs={{0,8},{1,9},{2,10},{3,11},{4,20},{5,21},{6,22},{7,23},{8,0},{9,1},... | collective-permute-start | bytes 786440 | tf_op jit(solution)/shard_map/ppermute | solution.py:280
  24.2 1.8 %shard_map.81 = (f32[256,256]{1,0:T(8,128)S(1)}, f32[256,128]{1,0:T(8,128)S(1)}, f32[256,256]{1,0:T(8,128)S(1)}, f32[256,128]{1,0:T(8,128)S(1)}) custom-call(f32[256,256]{1,0:T(8,128)S(1)} %get-tuple-element.44.refs_0_.refs_1_, f32[256,256]{1,0:T(8,128)S(1)} %collective-permute-done.1.refs_1_.refs_2_, f32[256,512]{1,0:T(8,128)S(1)} %get-tuple-element.46.x.refs_2_.refs_1_, ...), custom_call_target="tpu_custom_call" | custom-call | flops 2415919104 | bytes 3145728 | tf_op jit(solution)/shard_map/pallas_call | solution.py:191
  26.0 1.1 %shard_map.83 = (f32[256,256]{1,0:T(8,128)S(1)}, f32[256,128]{1,0:T(8,128)S(1)}) custom-call(f32[256,256]{1,0:T(8,128)S(1)} %collective-permute-done.7.refs_0_.x, f32[256,512]{1,0:T(8,128)S(1)} %get-tuple-element.46.x.refs_2_.refs_1_, f32[256,512]{1,0:T(8,128)S(1)} %collective-permute-done.3.after.refs_3_.refs_2_), custom_call_target="tpu_custom_call" | custom-call | flops 1207959552 | bytes 2097152 | tf_op jit(solution)/shard_map/pallas_call | solution.py:191
  27.1 2.1 %collective-permute-done.5.x.refs_4_ = f32[256,256]{1,0:T(8,128)S(1)} collective-permute-done((f32[256,256]{1,0:T(8,128)S(1)}, f32[256,256]{1,0:T(8,128)S(1)}, u32[]{:S(2)}, u32[]{:S(2)}) %collective-permute-start.5) | collective-permute-done | bytes 262176 | tf_op jit(solution)/shard_map/ppermute | solution.py:280
  29.5 2.1 %shard_map.84 = (f32[256,256]{1,0:T(8,128)S(1)}, f32[256,128]{1,0:T(8,128)S(1)}, f32[256,256]{1,0:T(8,128)S(1)}, f32[256,128]{1,0:T(8,128)S(1)}, f32[256,256]{1,0:T(8,128)S(1)}, /*index=5*/f32[256,128]{1,0:T(8,128)S(1)}) custom-call(f32[256,256]{1,0:T(8,128)S(1)} %collective-permute-done.7.refs_0_.x, f32[256,256]{1,0:T(8,128)S(1)} %get-tuple-element.44.refs_0_.refs_1_, ...), custom_call_target="tpu_custom_call" | custom-call | flops 1811939328 | bytes 3670016 | tf_op jit(solution)/shard_map/pallas_call | solution.py:191
  31.7 1.4 %shard_map.88 = (f32[256,256]{1,0:T(8,128)S(1)}, f32[256,128]{1,0:T(8,128)S(1)}) custom-call(f32[256,256]{1,0:T(8,128)S(1)} %shard_map.87.refs_0_, f32[256,512]{1,0:T(8,128)S(1)} %get-tuple-element.46.x.refs_2_.refs_1_, f32[256,512]{1,0:T(8,128)S(1)} %collective-permute-done.3.after.refs_3_.refs_2_, f32[256,256]{1,0:T(8,128)S(1)} %collective-permute-done.2.x.refs_3_, ...), custom_call_target="tpu_custom_call" | custom-call | flops 1811939328 | bytes 2621440 | tf_op jit(solution)/shard_map/pallas_call | solution.py:191
  33.1 2.5 %collective-permute-done.6.refs_2_.refs_3_ = f32[256,256]{1,0:T(8,128)S(1)} collective-permute-done((f32[256,256]{1,0:T(8,128)S(1)}, f32[256,256]{1,0:T(8,128)S(1)}, u32[]{:S(2)}, u32[]{:S(2)}) %collective-permute-start.6) | collective-permute-done | bytes 262176 | tf_op jit(solution)/shard_map/ppermute | solution.py:280
  35.6 0.9 %shard_map.89 = (f32[136,256]{1,0:T(8,128)S(1)}, f32[136,256]{1,0:T(8,128)S(1)}) custom-call(f32[256,256]{1,0:T(8,128)S(1)} %collective-permute-done.8.x.refs_0_, f32[256,256]{1,0:T(8,128)S(1)} %collective-permute-done.4.refs_1_.refs_2_, f32[256,256]{1,0:T(8,128)S(1)} %collective-permute-done.6.refs_2_.refs_3_, f32[256,256]{1,0:T(8,128)S(1)} %get-tuple-element.58.refs_3_, ...), custom_call_target="tpu_custom_call" | custom-call | flops 603979776 | bytes 1572864 | tf_op jit(solution)/shard_map/pallas_call | solution.py:191
  36.5 0.8 %collective-permute-start.9 = (f32[136,256]{1,0:T(8,128)S(1)}, f32[136,256]{1,0:T(8,128)S(1)}, u32[]{:S(2)}, u32[]{:S(2)}) collective-permute-start(f32[136,256]{1,0:T(8,128)S(1)} %get-tuple-element.60), channel_id=1, source_target_pairs={{0,16},{1,17},{2,18},{3,19},{4,12},{5,13},{6,14},{7,15},{8,24},{9,... | collective-permute-start | bytes 417800 | tf_op jit(solution)/shard_map/ppermute | solution.py:280
  37.3 1.2 %collective-permute-start.11 = (f32[136,256]{1,0:T(8,128)S(1)}, f32[136,256]{1,0:T(8,128)S(1)}, u32[]{:S(2)}, u32[]{:S(2)}) collective-permute-start(f32[136,256]{1,0:T(8,128)S(1)} %get-tuple-element.65), channel_id=1, source_target_pairs={{0,17},{1,16},{2,19},{3,18},{4,14},{5,15},{6,12},{7,13},{8,25},{9,... | collective-permute-start | bytes 417800 | tf_op jit(solution)/shard_map/ppermute | solution.py:280
  38.6 0.9 %shard_map.85 = (f32[136,256]{1,0:T(8,128)S(1)}, f32[136,256]{1,0:T(8,128)S(1)}) custom-call(f32[256,256]{1,0:T(8,128)S(1)} %collective-permute-done.7.refs_0_.x, f32[256,256]{1,0:T(8,128)S(1)} %collective-permute-done.4.refs_1_.refs_2_, f32[256,256]{1,0:T(8,128)S(1)} %collective-permute-done.6.refs_2_.refs_3_, f32[256,256]{1,0:T(8,128)S(1)} %get-tuple-element.55.refs_3_, ...), custom_call_target="tpu_custom_call" | custom-call | flops 603979776 | bytes 1572864 | tf_op jit(solution)/shard_map/pallas_call | solution.py:191
  39.5 1.5 %collective-permute-start.10 = (f32[136,256]{1,0:T(8,128)S(1)}, f32[136,256]{1,0:T(8,128)S(1)}, u32[]{:S(2)}, u32[]{:S(2)}) collective-permute-start(f32[136,256]{1,0:T(8,128)S(1)} %get-tuple-element.64), channel_id=1, source_target_pairs={{0,1},{1,0},{2,3},{3,2},{4,6},{5,7},{6,4},{7,5},{8,9},{9,8},{10,11... | collective-permute-start | bytes 417800 | tf_op jit(solution)/shard_map/ppermute | solution.py:280
  41.0 0.6 %collective-permute-done.9.two = f32[136,256]{1,0:T(8,128)S(1)} collective-permute-done((f32[136,256]{1,0:T(8,128)S(1)}, f32[136,256]{1,0:T(8,128)S(1)}, u32[]{:S(2)}, u32[]{:S(2)}) %collective-permute-start.9) | collective-permute-done | bytes 139296 | tf_op jit(solution)/shard_map/ppermute | solution.py:280
  41.6 0.4 shard_map.90.after
  42.1 1.5 %shard_map.92 = (f32[136,256]{1,0:T(8,128)S(1)}, f32[136,256]{1,0:T(8,128)S(1)}, f32[136,256]{1,0:T(8,128)S(1)}, f32[136,256]{1,0:T(8,128)S(1)}) custom-call(f32[256,256]{1,0:T(8,128)S(1)} %get-tuple-element.44.refs_0_.refs_1_, f32[256,256]{1,0:T(8,128)S(1)} %collective-permute-done.1.refs_1_.refs_2_, f32[256,256]{1,0:T(8,128)S(1)} %collective-permute-done.4.refs_1_.refs_2_, ...), custom_call_target="tpu_custom_call" | custom-call | flops 1207959552 | bytes 2621440 | tf_op jit(solution)/shard_map/pallas_call | solution.py:191
  43.6 0.9 %collective-permute-start.13 = (f32[136,256]{1,0:T(8,128)S(1)}, f32[136,256]{1,0:T(8,128)S(1)}, u32[]{:S(2)}, u32[]{:S(2)}) collective-permute-start(f32[136,256]{1,0:T(8,128)S(1)} %get-tuple-element.67), channel_id=1, source_target_pairs={{0,16},{1,17},{2,18},{3,19},{4,12},{5,13},{6,14},{7,15},{8,24},{9,... | collective-permute-start | bytes 417800 | tf_op jit(solution)/shard_map/ppermute | solution.py:280
  44.5 2.2 %collective-permute-start.14 = (f32[136,256]{1,0:T(8,128)S(1)}, f32[136,256]{1,0:T(8,128)S(1)}, u32[]{:S(2)}, u32[]{:S(2)}) collective-permute-start(f32[136,256]{1,0:T(8,128)S(1)} %get-tuple-element.70), channel_id=1, source_target_pairs={{0,20},{1,21},{2,22},{3,23},{4,8},{5,9},{6,10},{7,11},{8,28},{9,29... | collective-permute-start | bytes 417800 | tf_op jit(solution)/shard_map/ppermute | solution.py:280
  46.8 0.5 collective-permute-done.10.refs_0_
  47.3 1.7 %collective-permute-done.12.refs_2_ = f32[136,256]{1,0:T(8,128)S(1)} collective-permute-done((f32[136,256]{1,0:T(8,128)S(1)}, f32[136,256]{1,0:T(8,128)S(1)}, u32[]{:S(2)}, u32[]{:S(2)}) %collective-permute-start.12) | collective-permute-done | bytes 139296 | tf_op jit(solution)/shard_map/ppermute | solution.py:280
  49.1 1.8 %collective-permute-done.14.refs_5_ = f32[136,256]{1,0:T(8,128)S(1)} collective-permute-done((f32[136,256]{1,0:T(8,128)S(1)}, f32[136,256]{1,0:T(8,128)S(1)}, u32[]{:S(2)}, u32[]{:S(2)}) %collective-permute-start.14) | collective-permute-done | bytes 139296 | tf_op jit(solution)/shard_map/ppermute | solution.py:280
  50.9 1.5 %shard_map.94 = (f32[128,256]{1,0:T(8,128)}, f32[128,256]{1,0:T(8,128)}) custom-call(s32[1]{0:T(128)} %bitcast.core_ref, f32[136,256]{1,0:T(8,128)S(1)} %get-tuple-element.63.refs_0_, f32[136,256]{1,0:T(8,128)S(1)} %get-tuple-element.66.refs_1_, f32[136,256]{1,0:T(8,128)S(1)} %collective-permute-done.13.refs_2_, f32[136,256]{1,0:T(8,128)S(1)} %get-tuple-element.68.refs_3_, ...), custom_call_target="tpu_custom_call" | custom-call | tf_op jit(solution)/shard_map/pallas_call | solution.py:363
  (18 shorter events, 0.9 us)
Async XLA Ops:
  2.6 2.1 %collective-permute-start = (f32[128,768]{1,0:T(8,128)}, f32[128,768]{1,0:T(8,128)S(1)}, u32[]{:S(2)}, u32[]{:S(2)}) collective-permute-start(f32[128,768]{1,0:T(8,128)} %get-tuple-element.43), channel_id=1, source_target_pairs={{0,4},{1,5},{2,6},{3,7},{4,0},{5,1},{6,2},{7,3},{8,12},{9,13},{10,... | collective-permute-start | bytes 1179656 | tf_op jit(solution)/shard_map/ppermute | solution.py:280
  4.8 11.2 %collective-permute-start.3 = (f32[256,512]{1,0:T(8,128)S(1)}, f32[256,512]{1,0:T(8,128)S(1)}, u32[]{:S(2)}, u32[]{:S(2)}) collective-permute-start(f32[256,512]{1,0:T(8,128)S(1)} %get-tuple-element.46.x.refs_2_.refs_1_), channel_id=1, source_target_pairs={{0,8},{1,9},{2,10},{3,11},{4,20},{5,21},{6,22},{7,23},{8,0},{9,1},... | collective-permute-start | bytes 1572872 | tf_op jit(solution)/shard_map/ppermute | solution.py:280
  7.7 14.3 %collective-permute-start.7 = (f32[256,256]{1,0:T(8,128)S(1)}, f32[256,256]{1,0:T(8,128)S(1)}, u32[]{:S(2)}, u32[]{:S(2)}) collective-permute-start(f32[256,256]{1,0:T(8,128)S(1)} %get-tuple-element.44.refs_0_.refs_1_), channel_id=1, source_target_pairs={{0,1},{1,0},{2,3},{3,2},{4,6},{5,7},{6,4},{7,5},{8,9},{9,8},{10,11... | collective-permute-start | bytes 786440 | tf_op jit(solution)/shard_map/ppermute | solution.py:280
  9.3 13.4 %collective-permute-start.2 = (f32[256,256]{1,0:T(8,128)S(1)}, f32[256,256]{1,0:T(8,128)S(1)}, u32[]{:S(2)}, u32[]{:S(2)}) collective-permute-start(f32[256,256]{1,0:T(8,128)S(1)} %get-tuple-element.45), channel_id=1, source_target_pairs={{0,2},{1,3},{2,0},{3,1},{4,5},{5,4},{6,7},{7,6},{8,10},{9,11},{10,... | collective-permute-start | bytes 786440 | tf_op jit(solution)/shard_map/ppermute | solution.py:280
  11.9 12.3 %collective-permute-start.1 = (f32[256,256]{1,0:T(8,128)S(1)}, f32[256,256]{1,0:T(8,128)S(1)}, u32[]{:S(2)}, u32[]{:S(2)}) collective-permute-start(f32[256,256]{1,0:T(8,128)S(1)} %get-tuple-element.44.refs_0_.refs_1_), channel_id=1, source_target_pairs={{0,16},{1,17},{2,18},{3,19},{4,12},{5,13},{6,14},{7,15},{8,24},{9,... | collective-permute-start | bytes 786440 | tf_op jit(solution)/shard_map/ppermute | solution.py:280
  16.0 13.1 %collective-permute-start.5 = (f32[256,256]{1,0:T(8,128)S(1)}, f32[256,256]{1,0:T(8,128)S(1)}, u32[]{:S(2)}, u32[]{:S(2)}) collective-permute-start(f32[256,256]{1,0:T(8,128)S(1)} %shard_map.79.after), channel_id=1, source_target_pairs={{0,2},{1,3},{2,0},{3,1},{4,5},{5,4},{6,7},{7,6},{8,10},{9,11},{10,... | collective-permute-start | bytes 786440 | tf_op jit(solution)/shard_map/ppermute | solution.py:280
  22.1 9.5 %collective-permute-start.8 = (f32[256,256]{1,0:T(8,128)S(1)}, f32[256,256]{1,0:T(8,128)S(1)}, u32[]{:S(2)}, u32[]{:S(2)}) collective-permute-start(f32[256,256]{1,0:T(8,128)S(1)} %shard_map.86), channel_id=1, source_target_pairs={{0,16},{1,17},{2,18},{3,19},{4,12},{5,13},{6,14},{7,15},{8,24},{9,... | collective-permute-start | bytes 786440 | tf_op jit(solution)/shard_map/ppermute | solution.py:280
  22.8 10.3 %collective-permute-start.4 = (f32[256,256]{1,0:T(8,128)S(1)}, f32[256,256]{1,0:T(8,128)S(1)}, u32[]{:S(2)}, u32[]{:S(2)}) collective-permute-start(f32[256,256]{1,0:T(8,128)S(1)} %shard_map.80), channel_id=1, source_target_pairs={{0,8},{1,9},{2,10},{3,11},{4,20},{5,21},{6,22},{7,23},{8,0},{9,1},... | collective-permute-start | bytes 786440 | tf_op jit(solution)/shard_map/ppermute | solution.py:280
  29.2 6.4 %collective-permute-start.6 = (f32[256,256]{1,0:T(8,128)S(1)}, f32[256,256]{1,0:T(8,128)S(1)}, u32[]{:S(2)}, u32[]{:S(2)}) collective-permute-start(f32[256,256]{1,0:T(8,128)S(1)} %shard_map.82), channel_id=1, source_target_pairs={{0,8},{1,9},{2,10},{3,11},{4,20},{5,21},{6,22},{7,23},{8,0},{9,1},... | collective-permute-start | bytes 786440 | tf_op jit(solution)/shard_map/ppermute | solution.py:280
  36.5 5.1 %collective-permute-start.9 = (f32[136,256]{1,0:T(8,128)S(1)}, f32[136,256]{1,0:T(8,128)S(1)}, u32[]{:S(2)}, u32[]{:S(2)}) collective-permute-start(f32[136,256]{1,0:T(8,128)S(1)} %get-tuple-element.60), channel_id=1, source_target_pairs={{0,16},{1,17},{2,18},{3,19},{4,12},{5,13},{6,14},{7,15},{8,24},{9,... | collective-permute-start | bytes 417800 | tf_op jit(solution)/shard_map/ppermute | solution.py:280
  37.3 9.3 %collective-permute-start.11 = (f32[136,256]{1,0:T(8,128)S(1)}, f32[136,256]{1,0:T(8,128)S(1)}, u32[]{:S(2)}, u32[]{:S(2)}) collective-permute-start(f32[136,256]{1,0:T(8,128)S(1)} %get-tuple-element.65), channel_id=1, source_target_pairs={{0,17},{1,16},{2,19},{3,18},{4,14},{5,15},{6,12},{7,13},{8,25},{9,... | collective-permute-start | bytes 417800 | tf_op jit(solution)/shard_map/ppermute | solution.py:280
  39.5 7.9 %collective-permute-start.10 = (f32[136,256]{1,0:T(8,128)S(1)}, f32[136,256]{1,0:T(8,128)S(1)}, u32[]{:S(2)}, u32[]{:S(2)}) collective-permute-start(f32[136,256]{1,0:T(8,128)S(1)} %get-tuple-element.64), channel_id=1, source_target_pairs={{0,1},{1,0},{2,3},{3,2},{4,6},{5,7},{6,4},{7,5},{8,9},{9,8},{10,11... | collective-permute-start | bytes 417800 | tf_op jit(solution)/shard_map/ppermute | solution.py:280
  42.0 7.0 %collective-permute-start.12 = (f32[136,256]{1,0:T(8,128)S(1)}, f32[136,256]{1,0:T(8,128)S(1)}, u32[]{:S(2)}, u32[]{:S(2)}) collective-permute-start(f32[136,256]{1,0:T(8,128)S(1)} %shard_map.90.after), channel_id=1, source_target_pairs={{0,5},{1,4},{2,7},{3,6},{4,2},{5,3},{6,0},{7,1},{8,13},{9,12},{10,... | collective-permute-start | bytes 417800 | tf_op jit(solution)/shard_map/ppermute | solution.py:280
  43.6 5.5 %collective-permute-start.13 = (f32[136,256]{1,0:T(8,128)S(1)}, f32[136,256]{1,0:T(8,128)S(1)}, u32[]{:S(2)}, u32[]{:S(2)}) collective-permute-start(f32[136,256]{1,0:T(8,128)S(1)} %get-tuple-element.67), channel_id=1, source_target_pairs={{0,16},{1,17},{2,18},{3,19},{4,12},{5,13},{6,14},{7,15},{8,24},{9,... | collective-permute-start | bytes 417800 | tf_op jit(solution)/shard_map/ppermute | solution.py:280
  44.5 6.4 %collective-permute-start.14 = (f32[136,256]{1,0:T(8,128)S(1)}, f32[136,256]{1,0:T(8,128)S(1)}, u32[]{:S(2)}, u32[]{:S(2)}) collective-permute-start(f32[136,256]{1,0:T(8,128)S(1)} %get-tuple-element.70), channel_id=1, source_target_pairs={{0,20},{1,21},{2,22},{3,23},{4,8},{5,9},{6,10},{7,11},{8,28},{9,29... | collective-permute-start | bytes 417800 | tf_op jit(solution)/shard_map/ppermute | solution.py:280
  46.6 4.2 %collective-permute-start.15 = (f32[136,256]{1,0:T(8,128)S(1)}, f32[136,256]{1,0:T(8,128)S(1)}, u32[]{:S(2)}, u32[]{:S(2)}) collective-permute-start(f32[136,256]{1,0:T(8,128)S(1)} %get-tuple-element.71), channel_id=1, source_target_pairs={{0,4},{1,5},{2,6},{3,7},{4,0},{5,1},{6,2},{7,3},{8,12},{9,13},{10,... | collective-permute-start | bytes 417800 | tf_op jit(solution)/shard_map/ppermute | solution.py:280

commit v10 on v7

--- a/solution.py
+++ b/solution.py
@@ -73,13 +73,15 @@
                 out_k[at, (i - 2) * DH : (i - 1) * DH] = x
 
 
-def later_kernel(x, after, out):
-    out[...] = x[:, x.shape[1] - out.shape[1] :]
-
-
-def later(x, columns, after):
+def later_kernel(start, x, after, out):
+    out[...] = x[:, start : start + out.shape[1]]
+
+
+def later(x, columns, after, start=0):
     return pl.pallas_call(
-        later_kernel, out_shape=f32(x.shape[0], columns), compiler_params=params(8)
+        functools.partial(later_kernel, start),
+        out_shape=f32(x.shape[0], columns),
+        compiler_params=params(8),
     )(x, after)
 
 
@@ -92,17 +94,6 @@
     return pl.pallas_call(
         same_kernel, out_shape=[f32(*x.shape) for x in arrays], compiler_params=params(8)
     )(*arrays)
-
-
-def halves_kernel(x, after, one, two):
-    one[...] = x[:, :DH]
-    two[...] = x[:, DH:]
-
-
-def halves(x, after):
-    return pl.pallas_call(
-        halves_kernel, out_shape=[f32(x.shape[0], DH)] * 2, compiler_params=params(8)
-    )(x, after)
 
 
 def attend_kernel(n_q, n_k, rows, has_prev, last, split, *refs):
@@ -293,8 +284,9 @@
     for masks in near:
         near_k += [tuple(swap(x, masks) for x in block) for block in near_k]
     far_k = swap(mine_k, far)
-    mine_v = later(mine_kv, 2 * DH, near_k[-1][0])
-    far_v = swap(mine_v, far)
+    mine_v = later(mine_kv, DH, near_k[-1][0], 2 * DH)
+    sent_k = later(far_k, 2 * DH, mine_v)
+    far_v = (swap(mine_v, far), swap(later(mine_kv, DH, sent_k, 3 * DH), far))
     q_blocks = [mine_q]
     for masks in zip(*q_bits):
         sent = [later(x, 2 * DH, mine_v) if i == 1 else x for i, x in enumerate(q_blocks)]
@@ -303,10 +295,10 @@
     top_bit = n_q // 2
     far_q, near_q = list(range(1, n_q, 2)), list(range(0, n_q, 2))
     states = dict(zip(near_q, attend([q_blocks[i] for i in near_q], near_k, [], False)))
-    last_k = [(later(far_k, 2 * DH, mine_v), *halves(far_v, states[0][1]))]
+    last_k = [(sent_k, *(later(x, DH, states[0][1]) for x in far_v))]
     for masks in near:
         last_k += [tuple(swap(x, masks) for x in block) for block in last_k]
-    far_kv = [(far_k, far_v)]
+    far_kv = [(far_k, *far_v)]
     first = [1] + near_q
     states[1] = attend([q_blocks[1]], near_k, [], False)[0]
     states.update(zip(first, attend([q_blocks[i] for i in first], far_kv, [states[i] for i in first], False)))

time: 52.1 us -> 55.7 us (1.069)
  waiting for transfers between devices: 12.4 us -> 17.6 us
  starting transfers between devices: 25.2 us -> 23.6 us
    ppermute x17 -> x18, waiting for transfers between devices: 12.4 us -> 17.6 us  [swap(): lax.ppermute(x, AXES, [(i, i ^ flip ^ masks[i // n_kv % 2]) for i in rang...]
    ppermute x17 -> x18, starting transfers between devices: 25.2 us -> 23.6 us  [swap(): lax.ppermute(x, AXES, [(i, i ^ flip ^ masks[i // n_kv % 2]) for i in rang...]
  transfers between devices with their start and end apart: 17 -> 18, of which waited for: 7 -> 8; matrix products, arithmetic and copies ran while one was open for 0% -> 0% of each run, Pallas kernels for 17% -> 16%
where the time goes in v10:
time: 55.7 us; the launch traced here: 55.6 us
  starting transfers between devices  23.6 us (42%)
  waiting for transfers between devices  17.6 us (32%)
  Pallas kernels  13.6 us (24%)
  between operations  0.8 us (1%)
    ppermute x18, starting transfers between devices, swap(): lax.ppermute(x, AXES, [(i, i ^ flip ^ masks[i // n_kv % 2]) for i in rang...  23.6 us
    ppermute x18, waiting for transfers between devices, swap(): lax.ppermute(x, AXES, [(i, i ^ flip ^ masks[i // n_kv % 2]) for i in rang...  17.6 us
    pallas_call x6, Pallas kernels, attend(): pl.pallas_call(functools.partial(attend_kernel, n_q, n_k, rows, bool(prev...  9.38 us
    pallas_call x1, Pallas kernels, per_device(): pl.pallas_call(pack_kernel, out_shape=[f32(rows, w * DH) for w in (1, 1,...  2.02 us
    pallas_call x1, Pallas kernels, per_device(): pl.pallas_call(functools.partial(finish_kernel, n_q, counts), out_shape=[...  1.51 us
  transfers between devices with their start and end apart: 18, of which 8 were waited for; matrix products, arithmetic and copies ran while one was open for 0% of the time, Pallas kernels for 16%

profile of v10, /device:TPU:0, one launch (start us, length us, event | category | flops | bytes accessed | tf_op | source)
XLA Modules:
  0.0 55.6 jit_solution(6782326269283558801)
XLA Ops:
  0.6 2.0 %shard_map.77 = (f32[128,128]{1,0:T(8,128)S(1)}, f32[128,128]{1,0:T(8,128)S(1)}, f32[128,128]{1,0:T(8,128)S(1)}, f32[128,128]{1,0:T(8,128)S(1)}, f32[128,128]{1,...) custom-call(f32[128,256]{1,0:T(8,128)} %refs_0_.1, f32[128,256]{1,0:T(8,128)} %refs_1_.1, f32[128,256]{1,0:T(8,128)} %refs_2_.1, ...), custom_call_target="tpu_custom_call" | custom-call | tf_op jit(solution)/shard_map/pallas_call | solution.py:267
  2.7 0.5 collective-permute-start
  3.2 1.6 %collective-permute-done.refs_6_ = f32[128,768]{1,0:T(8,128)S(1)} collective-permute-done((f32[128,768]{1,0:T(8,128)}, f32[128,768]{1,0:T(8,128)S(1)}, u32[]{:S(2)}, u32[]{:S(2)}) %collective-permute-start) | collective-permute-done | bytes 393248 | tf_op jit(solution)/shard_map/ppermute | solution.py:260
  4.7 0.1 shard_map.78
  4.8 2.9 %collective-permute-start.4 = (f32[256,512]{1,0:T(8,128)S(1)}, f32[256,512]{1,0:T(8,128)S(1)}, u32[]{:S(2)}, u32[]{:S(2)}) collective-permute-start(f32[256,512]{1,0:T(8,128)S(1)} %get-tuple-element.46.x.refs_2_.refs_1_), channel_id=1, source_target_pairs={{0,8},{1,9},{2,10},{3,11},{4,20},{5,21},{6,22},{7,23},{8,0},{9,1},... | collective-permute-start | bytes 1572872 | tf_op jit(solution)/shard_map/ppermute | solution.py:260
  7.8 2.6 %collective-permute-start.3 = (f32[256,256]{1,0:T(8,128)S(1)}, f32[256,256]{1,0:T(8,128)S(1)}, u32[]{:S(2)}, u32[]{:S(2)}) collective-permute-start(f32[256,256]{1,0:T(8,128)S(1)} %get-tuple-element.45), channel_id=1, source_target_pairs={{0,2},{1,3},{2,0},{3,1},{4,5},{5,4},{6,7},{7,6},{8,10},{9,11},{10,... | collective-permute-start | bytes 786440 | tf_op jit(solution)/shard_map/ppermute | solution.py:260
  10.3 1.6 %collective-permute-start.1 = (f32[256,256]{1,0:T(8,128)S(1)}, f32[256,256]{1,0:T(8,128)S(1)}, u32[]{:S(2)}, u32[]{:S(2)}) collective-permute-start(f32[256,256]{1,0:T(8,128)S(1)} %get-tuple-element.44.refs_0_.refs_1_), channel_id=1, source_target_pairs={{0,1},{1,0},{2,3},{3,2},{4,6},{5,7},{6,4},{7,5},{8,9},{9,8},{10,11... | collective-permute-start | bytes 786440 | tf_op jit(solution)/shard_map/ppermute | solution.py:260
  11.9 1.5 %collective-permute-start.2 = (f32[256,256]{1,0:T(8,128)S(1)}, f32[256,256]{1,0:T(8,128)S(1)}, u32[]{:S(2)}, u32[]{:S(2)}) collective-permute-start(f32[256,256]{1,0:T(8,128)S(1)} %get-tuple-element.44.refs_0_.refs_1_), channel_id=1, source_target_pairs={{0,16},{1,17},{2,18},{3,19},{4,12},{5,13},{6,14},{7,15},{8,24},{9,... | collective-permute-start | bytes 786440 | tf_op jit(solution)/shard_map/ppermute | solution.py:260
  13.4 2.5 %collective-permute-done.4.after.refs_3_.refs_2_ = f32[256,512]{1,0:T(8,128)S(1)} collective-permute-done((f32[256,512]{1,0:T(8,128)S(1)}, f32[256,512]{1,0:T(8,128)S(1)}, u32[]{:S(2)}, u32[]{:S(2)}) %collective-permute-start.4) | collective-permute-done | bytes 524320 | tf_op jit(solution)/shard_map/ppermute | solution.py:260
  16.0 4.9 %collective-permute-start.6 = (f32[256,128]{1,0:T(8,128)S(1)}, f32[256,128]{1,0:T(8,128)S(1)}, u32[]{:S(2)}, u32[]{:S(2)}) collective-permute-start(f32[256,128]{1,0:T(8,128)S(1)} %shard_map.79.after), channel_id=1, source_target_pairs={{0,2},{1,3},{2,0},{3,1},{4,5},{5,4},{6,7},{7,6},{8,10},{9,11},{10,... | collective-permute-start | bytes 393224 | tf_op jit(solution)/shard_map/ppermute | solution.py:260
  20.9 2.5 %collective-permute-done.3.x.refs_3_ = f32[256,256]{1,0:T(8,128)S(1)} collective-permute-done((f32[256,256]{1,0:T(8,128)S(1)}, f32[256,256]{1,0:T(8,128)S(1)}, u32[]{:S(2)}, u32[]{:S(2)}) %collective-permute-start.3) | collective-permute-done | bytes 262176 | tf_op jit(solution)/shard_map/ppermute | solution.py:260
  23.6 2.0 %collective-permute-start.11 = (f32[256,256]{1,0:T(8,128)S(1)}, f32[256,256]{1,0:T(8,128)S(1)}, u32[]{:S(2)}, u32[]{:S(2)}) collective-permute-start(f32[256,256]{1,0:T(8,128)S(1)} %shard_map.88), channel_id=1, source_target_pairs={{0,16},{1,17},{2,18},{3,19},{4,12},{5,13},{6,14},{7,15},{8,24},{9,... | collective-permute-start | bytes 786440 | tf_op jit(solution)/shard_map/ppermute | solution.py:260
  25.6 1.8 %shard_map.81 = (f32[256,256]{1,0:T(8,128)S(1)}, f32[256,128]{1,0:T(8,128)S(1)}, f32[256,256]{1,0:T(8,128)S(1)}, f32[256,128]{1,0:T(8,128)S(1)}) custom-call(f32[256,256]{1,0:T(8,128)S(1)} %get-tuple-element.44.refs_0_.refs_1_, f32[256,256]{1,0:T(8,128)S(1)} %collective-permute-done.2.refs_1_.refs_2_, f32[256,512]{1,0:T(8,128)S(1)} %get-tuple-element.46.x.refs_2_.refs_1_, ...), custom_call_target="tpu_custom_call" | custom-call | flops 2415919104 | bytes 3145728 | tf_op jit(solution)/shard_map/pallas_call | solution.py:171
  27.4 1.1 %shard_map.85 = (f32[256,256]{1,0:T(8,128)S(1)}, f32[256,128]{1,0:T(8,128)S(1)}) custom-call(f32[256,256]{1,0:T(8,128)S(1)} %collective-permute-done.1.refs_0_.refs_1_.x, f32[256,512]{1,0:T(8,128)S(1)} %get-tuple-element.46.x.refs_2_.refs_1_, f32[256,512]{1,0:T(8,128)S(1)} %collective-permute-done.4.after.refs_3_.refs_2_), custom_call_target="tpu_custom_call" | custom-call | flops 1207959552 | bytes 2097152 | tf_op jit(solution)/shard_map/pallas_call | solution.py:171
  28.5 2.4 %collective-permute-done.8.x.refs_5_ = f32[256,128]{1,0:T(8,128)S(1)} collective-permute-done((f32[256,128]{1,0:T(8,128)S(1)}, f32[256,128]{1,0:T(8,128)S(1)}, u32[]{:S(2)}, u32[]{:S(2)}) %collective-permute-start.8) | collective-permute-done | bytes 131104 | tf_op jit(solution)/shard_map/ppermute | solution.py:260
  30.9 2.0 %collective-permute-start.9 = (f32[256,128]{1,0:T(8,128)S(1)}, f32[256,128]{1,0:T(8,128)S(1)}, u32[]{:S(2)}, u32[]{:S(2)}) collective-permute-start(f32[256,128]{1,0:T(8,128)S(1)} %shard_map.84), channel_id=1, source_target_pairs={{0,8},{1,9},{2,10},{3,11},{4,20},{5,21},{6,22},{7,23},{8,0},{9,1},... | collective-permute-start | bytes 393224 | tf_op jit(solution)/shard_map/ppermute | solution.py:260
  32.8 0.2 collective-permute-start.7
  33.0 2.1 %shard_map.86 = (f32[256,256]{1,0:T(8,128)S(1)}, f32[256,128]{1,0:T(8,128)S(1)}, f32[256,256]{1,0:T(8,128)S(1)}, f32[256,128]{1,0:T(8,128)S(1)}, f32[256,256]{1,0:T(8,128)S(1)}, /*index=5*/f32[256,128]{1,0:T(8,128)S(1)}) custom-call(f32[256,256]{1,0:T(8,128)S(1)} %collective-permute-done.1.refs_0_.refs_1_.x, ...), custom_call_target="tpu_custom_call" | custom-call | flops 1811939328 | bytes 3670016 | tf_op jit(solution)/shard_map/pallas_call | solution.py:171
  35.2 1.4 %shard_map.90 = (f32[256,256]{1,0:T(8,128)S(1)}, f32[256,128]{1,0:T(8,128)S(1)}) custom-call(f32[256,256]{1,0:T(8,128)S(1)} %shard_map.89.refs_0_, f32[256,512]{1,0:T(8,128)S(1)} %get-tuple-element.46.x.refs_2_.refs_1_, f32[256,512]{1,0:T(8,128)S(1)} %collective-permute-done.4.after.refs_3_.refs_2_, f32[256,256]{1,0:T(8,128)S(1)} %collective-permute-done.3.x.refs_3_, ...), custom_call_target="tpu_custom_call" | custom-call | flops 1811939328 | bytes 2621440 | tf_op jit(solution)/shard_map/pallas_call | solution.py:171
  36.6 2.4 %collective-permute-done.7.refs_4_.refs_2_ = f32[256,128]{1,0:T(8,128)S(1)} collective-permute-done((f32[256,128]{1,0:T(8,128)S(1)}, f32[256,128]{1,0:T(8,128)S(1)}, u32[]{:S(2)}, u32[]{:S(2)}) %collective-permute-start.7) | collective-permute-done | bytes 131104 | tf_op jit(solution)/shard_map/ppermute | solution.py:260
  39.0 0.9 %shard_map.91 = (f32[136,256]{1,0:T(8,128)S(1)}, f32[136,256]{1,0:T(8,128)S(1)}) custom-call(f32[256,256]{1,0:T(8,128)S(1)} %collective-permute-done.11.x.refs_0_, f32[256,256]{1,0:T(8,128)S(1)} %collective-permute-done.5.refs_3_.refs_1_, f32[256,128]{1,0:T(8,128)S(1)} %collective-permute-done.7.refs_4_.refs_2_, ...), custom_call_target="tpu_custom_call" | custom-call | flops 603979776 | bytes 1572864 | tf_op jit(solution)/shard_map/pallas_call | solution.py:171
  39.9 1.2 %collective-permute-start.13 = (f32[136,256]{1,0:T(8,128)S(1)}, f32[136,256]{1,0:T(8,128)S(1)}, u32[]{:S(2)}, u32[]{:S(2)}) collective-permute-start(f32[136,256]{1,0:T(8,128)S(1)} %get-tuple-element.65), channel_id=1, source_target_pairs={{0,16},{1,17},{2,18},{3,19},{4,12},{5,13},{6,14},{7,15},{8,24},{9,... | collective-permute-start | bytes 417800 | tf_op jit(solution)/shard_map/ppermute | solution.py:260
  41.1 2.1 %shard_map.87 = (f32[136,256]{1,0:T(8,128)S(1)}, f32[136,256]{1,0:T(8,128)S(1)}, f32[136,256]{1,0:T(8,128)S(1)}, f32[136,256]{1,0:T(8,128)S(1)}, f32[136,256]{1,0:T(8,128)S(1)}, /*index=5*/f32[136,256]{1,0:T(8,128)S(1)}) custom-call(f32[256,256]{1,0:T(8,128)S(1)} %get-tuple-element.44.refs_0_.refs_1_, ...), custom_call_target="tpu_custom_call" | custom-call | flops 1811939328 | bytes 3670016 | tf_op jit(solution)/shard_map/pallas_call | solution.py:171
  43.2 2.4 %collective-permute-start.10 = (f32[136,256]{1,0:T(8,128)S(1)}, f32[136,256]{1,0:T(8,128)S(1)}, u32[]{:S(2)}, u32[]{:S(2)}) collective-permute-start(f32[136,256]{1,0:T(8,128)S(1)} %get-tuple-element.60), channel_id=1, source_target_pairs={{0,1},{1,0},{2,3},{3,2},{4,6},{5,7},{6,4},{7,5},{8,9},{9,8},{10,11... | collective-permute-start | bytes 417800 | tf_op jit(solution)/shard_map/ppermute | solution.py:260
  45.6 1.1 %collective-permute-start.15 = (f32[136,256]{1,0:T(8,128)S(1)}, f32[136,256]{1,0:T(8,128)S(1)}, u32[]{:S(2)}, u32[]{:S(2)}) collective-permute-start(f32[136,256]{1,0:T(8,128)S(1)} %get-tuple-element.67), channel_id=1, source_target_pairs={{0,16},{1,17},{2,18},{3,19},{4,12},{5,13},{6,14},{7,15},{8,24},{9,... | collective-permute-start | bytes 417800 | tf_op jit(solution)/shard_map/ppermute | solution.py:260
  46.8 0.4 shard_map.92
  47.2 0.3 collective-permute-start.16
  47.5 0.2 collective-permute-done.12.refs_1_
  47.7 0.2 collective-permute-start.17
  48.0 1.5 %collective-permute-done.10.refs_0_ = f32[136,256]{1,0:T(8,128)S(1)} collective-permute-done((f32[136,256]{1,0:T(8,128)S(1)}, f32[136,256]{1,0:T(8,128)S(1)}, u32[]{:S(2)}, u32[]{:S(2)}) %collective-permute-start.10) | collective-permute-done | bytes 139296 | tf_op jit(solution)/shard_map/ppermute | solution.py:260
  49.5 4.5 %collective-permute-done.14.refs_2_ = f32[136,256]{1,0:T(8,128)S(1)} collective-permute-done((f32[136,256]{1,0:T(8,128)S(1)}, f32[136,256]{1,0:T(8,128)S(1)}, u32[]{:S(2)}, u32[]{:S(2)}) %collective-permute-start.14) | collective-permute-done | bytes 139296 | tf_op jit(solution)/shard_map/ppermute | solution.py:260
  54.1 1.5 %shard_map.94 = (f32[128,256]{1,0:T(8,128)}, f32[128,256]{1,0:T(8,128)}) custom-call(s32[1]{0:T(128)} %bitcast.core_ref, f32[136,256]{1,0:T(8,128)S(1)} %get-tuple-element.59.refs_0_, f32[136,256]{1,0:T(8,128)S(1)} %get-tuple-element.66.refs_1_, f32[136,256]{1,0:T(8,128)S(1)} %collective-permute-done.15.refs_2_, f32[136,256]{1,0:T(8,128)S(1)} %get-tuple-element.68.refs_3_, ...), custom_call_target="tpu_custom_call" | custom-call | tf_op jit(solution)/shard_map/pallas_call | solution.py:336
  (22 shorter events, 0.3 us)
Async XLA Ops:
  2.7 2.1 %collective-permute-start = (f32[128,768]{1,0:T(8,128)}, f32[128,768]{1,0:T(8,128)S(1)}, u32[]{:S(2)}, u32[]{:S(2)}) collective-permute-start(f32[128,768]{1,0:T(8,128)} %get-tuple-element.43), channel_id=1, source_target_pairs={{0,4},{1,5},{2,6},{3,7},{4,0},{5,1},{6,2},{7,3},{8,12},{9,13},{10,... | collective-permute-start | bytes 1179656 | tf_op jit(solution)/shard_map/ppermute | solution.py:260
  4.8 11.2 %collective-permute-start.4 = (f32[256,512]{1,0:T(8,128)S(1)}, f32[256,512]{1,0:T(8,128)S(1)}, u32[]{:S(2)}, u32[]{:S(2)}) collective-permute-start(f32[256,512]{1,0:T(8,128)S(1)} %get-tuple-element.46.x.refs_2_.refs_1_), channel_id=1, source_target_pairs={{0,8},{1,9},{2,10},{3,11},{4,20},{5,21},{6,22},{7,23},{8,0},{9,1},... | collective-permute-start | bytes 1572872 | tf_op jit(solution)/shard_map/ppermute | solution.py:260
  7.8 15.6 %collective-permute-start.3 = (f32[256,256]{1,0:T(8,128)S(1)}, f32[256,256]{1,0:T(8,128)S(1)}, u32[]{:S(2)}, u32[]{:S(2)}) collective-permute-start(f32[256,256]{1,0:T(8,128)S(1)} %get-tuple-element.45), channel_id=1, source_target_pairs={{0,2},{1,3},{2,0},{3,1},{4,5},{5,4},{6,7},{7,6},{8,10},{9,11},{10,... | collective-permute-start | bytes 786440 | tf_op jit(solution)/shard_map/ppermute | solution.py:260
  10.3 13.2 %collective-permute-start.1 = (f32[256,256]{1,0:T(8,128)S(1)}, f32[256,256]{1,0:T(8,128)S(1)}, u32[]{:S(2)}, u32[]{:S(2)}) collective-permute-start(f32[256,256]{1,0:T(8,128)S(1)} %get-tuple-element.44.refs_0_.refs_1_), channel_id=1, source_target_pairs={{0,1},{1,0},{2,3},{3,2},{4,6},{5,7},{6,4},{7,5},{8,9},{9,8},{10,11... | collective-permute-start | bytes 786440 | tf_op jit(solution)/shard_map/ppermute | solution.py:260
  11.9 13.7 %collective-permute-start.2 = (f32[256,256]{1,0:T(8,128)S(1)}, f32[256,256]{1,0:T(8,128)S(1)}, u32[]{:S(2)}, u32[]{:S(2)}) collective-permute-start(f32[256,256]{1,0:T(8,128)S(1)} %get-tuple-element.44.refs_0_.refs_1_), channel_id=1, source_target_pairs={{0,16},{1,17},{2,18},{3,19},{4,12},{5,13},{6,14},{7,15},{8,24},{9,... | collective-permute-start | bytes 786440 | tf_op jit(solution)/shard_map/ppermute | solution.py:260
  16.0 16.8 %collective-permute-start.6 = (f32[256,128]{1,0:T(8,128)S(1)}, f32[256,128]{1,0:T(8,128)S(1)}, u32[]{:S(2)}, u32[]{:S(2)}) collective-permute-start(f32[256,128]{1,0:T(8,128)S(1)} %shard_map.79.after), channel_id=1, source_target_pairs={{0,2},{1,3},{2,0},{3,1},{4,5},{5,4},{6,7},{7,6},{8,10},{9,11},{10,... | collective-permute-start | bytes 393224 | tf_op jit(solution)/shard_map/ppermute | solution.py:260
  23.4 15.5 %collective-permute-start.5 = (f32[256,256]{1,0:T(8,128)S(1)}, f32[256,256]{1,0:T(8,128)S(1)}, u32[]{:S(2)}, u32[]{:S(2)}) collective-permute-start(f32[256,256]{1,0:T(8,128)S(1)} %shard_map.80.after), channel_id=1, source_target_pairs={{0,8},{1,9},{2,10},{3,11},{4,20},{5,21},{6,22},{7,23},{8,0},{9,1},... | collective-permute-start | bytes 786440 | tf_op jit(solution)/shard_map/ppermute | solution.py:260
  23.5 7.3 %collective-permute-start.8 = (f32[256,128]{1,0:T(8,128)S(1)}, f32[256,128]{1,0:T(8,128)S(1)}, u32[]{:S(2)}, u32[]{:S(2)}) collective-permute-start(f32[256,128]{1,0:T(8,128)S(1)} %shard_map.83), channel_id=1, source_target_pairs={{0,2},{1,3},{2,0},{3,1},{4,5},{5,4},{6,7},{7,6},{8,10},{9,11},{10,... | collective-permute-start | bytes 393224 | tf_op jit(solution)/shard_map/ppermute | solution.py:260
  23.6 11.5 %collective-permute-start.11 = (f32[256,256]{1,0:T(8,128)S(1)}, f32[256,256]{1,0:T(8,128)S(1)}, u32[]{:S(2)}, u32[]{:S(2)}) collective-permute-start(f32[256,256]{1,0:T(8,128)S(1)} %shard_map.88), channel_id=1, source_target_pairs={{0,16},{1,17},{2,18},{3,19},{4,12},{5,13},{6,14},{7,15},{8,24},{9,... | collective-permute-start | bytes 786440 | tf_op jit(solution)/shard_map/ppermute | solution.py:260
  30.9 5.7 %collective-permute-start.9 = (f32[256,128]{1,0:T(8,128)S(1)}, f32[256,128]{1,0:T(8,128)S(1)}, u32[]{:S(2)}, u32[]{:S(2)}) collective-permute-start(f32[256,128]{1,0:T(8,128)S(1)} %shard_map.84), channel_id=1, source_target_pairs={{0,8},{1,9},{2,10},{3,11},{4,20},{5,21},{6,22},{7,23},{8,0},{9,1},... | collective-permute-start | bytes 393224 | tf_op jit(solution)/shard_map/ppermute | solution.py:260
  32.8 6.1 %collective-permute-start.7 = (f32[256,128]{1,0:T(8,128)S(1)}, f32[256,128]{1,0:T(8,128)S(1)}, u32[]{:S(2)}, u32[]{:S(2)}) collective-permute-start(f32[256,128]{1,0:T(8,128)S(1)} %shard_map.82), channel_id=1, source_target_pairs={{0,8},{1,9},{2,10},{3,11},{4,20},{5,21},{6,22},{7,23},{8,0},{9,1},... | collective-permute-start | bytes 393224 | tf_op jit(solution)/shard_map/ppermute | solution.py:260
  39.9 6.9 %collective-permute-start.13 = (f32[136,256]{1,0:T(8,128)S(1)}, f32[136,256]{1,0:T(8,128)S(1)}, u32[]{:S(2)}, u32[]{:S(2)}) collective-permute-start(f32[136,256]{1,0:T(8,128)S(1)} %get-tuple-element.65), channel_id=1, source_target_pairs={{0,16},{1,17},{2,18},{3,19},{4,12},{5,13},{6,14},{7,15},{8,24},{9,... | collective-permute-start | bytes 417800 | tf_op jit(solution)/shard_map/ppermute | solution.py:260
  41.1 6.7 %collective-permute-start.12 = (f32[136,256]{1,0:T(8,128)S(1)}, f32[136,256]{1,0:T(8,128)S(1)}, u32[]{:S(2)}, u32[]{:S(2)}) collective-permute-start(f32[136,256]{1,0:T(8,128)S(1)} %get-tuple-element.63), channel_id=1, source_target_pairs={{0,17},{1,16},{2,19},{3,18},{4,14},{5,15},{6,12},{7,13},{8,25},{9,... | collective-permute-start | bytes 417800 | tf_op jit(solution)/shard_map/ppermute | solution.py:260
  43.2 6.3 %collective-permute-start.10 = (f32[136,256]{1,0:T(8,128)S(1)}, f32[136,256]{1,0:T(8,128)S(1)}, u32[]{:S(2)}, u32[]{:S(2)}) collective-permute-start(f32[136,256]{1,0:T(8,128)S(1)} %get-tuple-element.60), channel_id=1, source_target_pairs={{0,1},{1,0},{2,3},{3,2},{4,6},{5,7},{6,4},{7,5},{8,9},{9,8},{10,11... | collective-permute-start | bytes 417800 | tf_op jit(solution)/shard_map/ppermute | solution.py:260
  45.6 8.4 %collective-permute-start.15 = (f32[136,256]{1,0:T(8,128)S(1)}, f32[136,256]{1,0:T(8,128)S(1)}, u32[]{:S(2)}, u32[]{:S(2)}) collective-permute-start(f32[136,256]{1,0:T(8,128)S(1)} %get-tuple-element.67), channel_id=1, source_target_pairs={{0,16},{1,17},{2,18},{3,19},{4,12},{5,13},{6,14},{7,15},{8,24},{9,... | collective-permute-start | bytes 417800 | tf_op jit(solution)/shard_map/ppermute | solution.py:260
  47.2 6.8 %collective-permute-start.14 = (f32[136,256]{1,0:T(8,128)S(1)}, f32[136,256]{1,0:T(8,128)S(1)}, u32[]{:S(2)}, u32[]{:S(2)}) collective-permute-start(f32[136,256]{1,0:T(8,128)S(1)} %shard_map.92), channel_id=1, source_target_pairs={{0,5},{1,4},{2,7},{3,6},{4,2},{5,3},{6,0},{7,1},{8,13},{9,12},{10,... | collective-permute-start | bytes 417800 | tf_op jit(solution)/shard_map/ppermute | solution.py:260
  47.2 6.8 %collective-permute-start.16 = (f32[136,256]{1,0:T(8,128)S(1)}, f32[136,256]{1,0:T(8,128)S(1)}, u32[]{:S(2)}, u32[]{:S(2)}) collective-permute-start(f32[136,256]{1,0:T(8,128)S(1)} %get-tuple-element.70), channel_id=1, source_target_pairs={{0,20},{1,21},{2,22},{3,23},{4,8},{5,9},{6,10},{7,11},{8,28},{9,29... | collective-permute-start | bytes 417800 | tf_op jit(solution)/shard_map/ppermute | solution.py:260
  47.7 6.3 %collective-permute-start.17 = (f32[136,256]{1,0:T(8,128)S(1)}, f32[136,256]{1,0:T(8,128)S(1)}, u32[]{:S(2)}, u32[]{:S(2)}) collective-permute-start(f32[136,256]{1,0:T(8,128)S(1)} %get-tuple-element.71), channel_id=1, source_target_pairs={{0,4},{1,5},{2,6},{3,7},{4,0},{5,1},{6,2},{7,3},{8,12},{9,13},{10,... | collective-permute-start | bytes 417800 | tf_op jit(solution)/shard_map/ppermute | solution.py:260

commit v11 on v7

--- a/solution.py
+++ b/solution.py
@@ -92,17 +92,6 @@
     return pl.pallas_call(
         same_kernel, out_shape=[f32(*x.shape) for x in arrays], compiler_params=params(8)
     )(*arrays)
-
-
-def halves_kernel(x, after, one, two):
-    one[...] = x[:, :DH]
-    two[...] = x[:, DH:]
-
-
-def halves(x, after):
-    return pl.pallas_call(
-        halves_kernel, out_shape=[f32(x.shape[0], DH)] * 2, compiler_params=params(8)
-    )(x, after)
 
 
 def attend_kernel(n_q, n_k, rows, has_prev, last, split, *refs):
@@ -303,7 +292,7 @@
     top_bit = n_q // 2
     far_q, near_q = list(range(1, n_q, 2)), list(range(0, n_q, 2))
     states = dict(zip(near_q, attend([q_blocks[i] for i in near_q], near_k, [], False)))
-    last_k = [(later(far_k, 2 * DH, mine_v), *halves(far_v, states[0][1]))]
+    last_k = [(later(far_k, 2 * DH, mine_v), later(far_v, 2 * DH, states[0][1]))]
     for masks in near:
         last_k += [tuple(swap(x, masks) for x in block) for block in last_k]
     far_kv = [(far_k, far_v)]

time: 52.1 us -> 52 us (level)
  starting transfers between devices: 25.2 us -> 23.4 us
  waiting for transfers between devices: 12.4 us -> 14.1 us
    ppermute x17 -> x16, starting transfers between devices: 25.2 us -> 23.4 us  [swap(): lax.ppermute(x, AXES, [(i, i ^ flip ^ masks[i // n_kv % 2]) for i in rang...]
    ppermute x17 -> x16, waiting for transfers between devices: 12.4 us -> 14.1 us  [swap(): lax.ppermute(x, AXES, [(i, i ^ flip ^ masks[i // n_kv % 2]) for i in rang...]
  transfers between devices with their start and end apart: 17 -> 16, of which waited for: 7 -> 7; matrix products, arithmetic and copies ran while one was open for 0% -> 0% of each run, Pallas kernels for 17% -> 17%
where the time goes in v11:
time: 52 us; the launch traced here: 51.8 us
  starting transfers between devices  23.4 us (45%)
  waiting for transfers between devices  14.1 us (27%)
  Pallas kernels  13.6 us (26%)
  between operations  0.76 us (1%)
    ppermute x16, starting transfers between devices, swap(): lax.ppermute(x, AXES, [(i, i ^ flip ^ masks[i // n_kv % 2]) for i in rang...  23.4 us
    ppermute x16, waiting for transfers between devices, swap(): lax.ppermute(x, AXES, [(i, i ^ flip ^ masks[i // n_kv % 2]) for i in rang...  14.1 us
    pallas_call x6, Pallas kernels, attend(): pl.pallas_call(functools.partial(attend_kernel, n_q, n_k, rows, bool(prev...  9.4 us
    pallas_call x1, Pallas kernels, per_device(): pl.pallas_call(pack_kernel, out_shape=[f32(rows, w * DH) for w in (1, 1,...  2.02 us
    pallas_call x1, Pallas kernels, per_device(): pl.pallas_call(functools.partial(finish_kernel, n_q, counts), out_shape=[...  1.51 us
  transfers between devices with their start and end apart: 16, of which 7 were waited for; matrix products, arithmetic and copies ran while one was open for 0% of the time, Pallas kernels for 17%

profile of v11, /device:TPU:0, one launch (start us, length us, event | category | flops | bytes accessed | tf_op | source)
XLA Modules:
  0.0 51.8 jit_solution(419228777425031828)
XLA Ops:
  0.6 2.0 %shard_map.77 = (f32[128,128]{1,0:T(8,128)S(1)}, f32[128,128]{1,0:T(8,128)S(1)}, f32[128,128]{1,0:T(8,128)S(1)}, f32[128,128]{1,0:T(8,128)S(1)}, f32[128,128]{1,...) custom-call(f32[128,256]{1,0:T(8,128)} %refs_0_.1, f32[128,256]{1,0:T(8,128)} %refs_1_.1, f32[128,256]{1,0:T(8,128)} %refs_2_.1, ...), custom_call_target="tpu_custom_call" | custom-call | tf_op jit(solution)/shard_map/pallas_call | solution.py:265
  2.7 0.5 collective-permute-start
  3.2 1.6 %collective-permute-done.refs_6_ = f32[128,768]{1,0:T(8,128)S(1)} collective-permute-done((f32[128,768]{1,0:T(8,128)}, f32[128,768]{1,0:T(8,128)S(1)}, u32[]{:S(2)}, u32[]{:S(2)}) %collective-permute-start) | collective-permute-done | bytes 393248 | tf_op jit(solution)/shard_map/ppermute | solution.py:258
  4.7 0.1 shard_map.78
  4.8 2.9 %collective-permute-start.4 = (f32[256,512]{1,0:T(8,128)S(1)}, f32[256,512]{1,0:T(8,128)S(1)}, u32[]{:S(2)}, u32[]{:S(2)}) collective-permute-start(f32[256,512]{1,0:T(8,128)S(1)} %get-tuple-element.46.x.refs_2_.refs_1_), channel_id=1, source_target_pairs={{0,8},{1,9},{2,10},{3,11},{4,20},{5,21},{6,22},{7,23},{8,0},{9,1},... | collective-permute-start | bytes 1572872 | tf_op jit(solution)/shard_map/ppermute | solution.py:258
  7.8 1.6 %collective-permute-start.1 = (f32[256,256]{1,0:T(8,128)S(1)}, f32[256,256]{1,0:T(8,128)S(1)}, u32[]{:S(2)}, u32[]{:S(2)}) collective-permute-start(f32[256,256]{1,0:T(8,128)S(1)} %get-tuple-element.44.refs_0_.refs_1_), channel_id=1, source_target_pairs={{0,1},{1,0},{2,3},{3,2},{4,6},{5,7},{6,4},{7,5},{8,9},{9,8},{10,11... | collective-permute-start | bytes 786440 | tf_op jit(solution)/shard_map/ppermute | solution.py:258
  9.3 2.6 %collective-permute-start.3 = (f32[256,256]{1,0:T(8,128)S(1)}, f32[256,256]{1,0:T(8,128)S(1)}, u32[]{:S(2)}, u32[]{:S(2)}) collective-permute-start(f32[256,256]{1,0:T(8,128)S(1)} %get-tuple-element.45), channel_id=1, source_target_pairs={{0,2},{1,3},{2,0},{3,1},{4,5},{5,4},{6,7},{7,6},{8,10},{9,11},{10,... | collective-permute-start | bytes 786440 | tf_op jit(solution)/shard_map/ppermute | solution.py:258
  11.9 1.5 %collective-permute-start.2 = (f32[256,256]{1,0:T(8,128)S(1)}, f32[256,256]{1,0:T(8,128)S(1)}, u32[]{:S(2)}, u32[]{:S(2)}) collective-permute-start(f32[256,256]{1,0:T(8,128)S(1)} %get-tuple-element.44.refs_0_.refs_1_), channel_id=1, source_target_pairs={{0,16},{1,17},{2,18},{3,19},{4,12},{5,13},{6,14},{7,15},{8,24},{9,... | collective-permute-start | bytes 786440 | tf_op jit(solution)/shard_map/ppermute | solution.py:258
  13.4 2.5 %collective-permute-done.4.after.refs_3_.refs_2_ = f32[256,512]{1,0:T(8,128)S(1)} collective-permute-done((f32[256,512]{1,0:T(8,128)S(1)}, f32[256,512]{1,0:T(8,128)S(1)}, u32[]{:S(2)}, u32[]{:S(2)}) %collective-permute-start.4) | collective-permute-done | bytes 524320 | tf_op jit(solution)/shard_map/ppermute | solution.py:258
  16.0 4.9 %collective-permute-start.6 = (f32[256,256]{1,0:T(8,128)S(1)}, f32[256,256]{1,0:T(8,128)S(1)}, u32[]{:S(2)}, u32[]{:S(2)}) collective-permute-start(f32[256,256]{1,0:T(8,128)S(1)} %shard_map.79.after), channel_id=1, source_target_pairs={{0,2},{1,3},{2,0},{3,1},{4,5},{5,4},{6,7},{7,6},{8,10},{9,11},{10,... | collective-permute-start | bytes 786440 | tf_op jit(solution)/shard_map/ppermute | solution.py:258
  20.9 1.1 %collective-permute-done.1.refs_0_.refs_1_.x = f32[256,256]{1,0:T(8,128)S(1)} collective-permute-done((f32[256,256]{1,0:T(8,128)S(1)}, f32[256,256]{1,0:T(8,128)S(1)}, u32[]{:S(2)}, u32[]{:S(2)}) %collective-permute-start.1) | collective-permute-done | bytes 262176 | tf_op jit(solution)/shard_map/ppermute | solution.py:258
  22.1 0.7 %collective-permute-start.9 = (f32[256,256]{1,0:T(8,128)S(1)}, f32[256,256]{1,0:T(8,128)S(1)}, u32[]{:S(2)}, u32[]{:S(2)}) collective-permute-start(f32[256,256]{1,0:T(8,128)S(1)} %shard_map.86), channel_id=1, source_target_pairs={{0,16},{1,17},{2,18},{3,19},{4,12},{5,13},{6,14},{7,15},{8,24},{9,... | collective-permute-start | bytes 786440 | tf_op jit(solution)/shard_map/ppermute | solution.py:258
  22.8 1.4 %collective-permute-start.5 = (f32[256,256]{1,0:T(8,128)S(1)}, f32[256,256]{1,0:T(8,128)S(1)}, u32[]{:S(2)}, u32[]{:S(2)}) collective-permute-start(f32[256,256]{1,0:T(8,128)S(1)} %shard_map.80), channel_id=1, source_target_pairs={{0,8},{1,9},{2,10},{3,11},{4,20},{5,21},{6,22},{7,23},{8,0},{9,1},... | collective-permute-start | bytes 786440 | tf_op jit(solution)/shard_map/ppermute | solution.py:258
  24.3 1.8 %shard_map.81 = (f32[256,256]{1,0:T(8,128)S(1)}, f32[256,128]{1,0:T(8,128)S(1)}, f32[256,256]{1,0:T(8,128)S(1)}, f32[256,128]{1,0:T(8,128)S(1)}) custom-call(f32[256,256]{1,0:T(8,128)S(1)} %get-tuple-element.44.refs_0_.refs_1_, f32[256,256]{1,0:T(8,128)S(1)} %collective-permute-done.2.refs_1_.refs_2_, f32[256,512]{1,0:T(8,128)S(1)} %get-tuple-element.46.x.refs_2_.refs_1_, ...), custom_call_target="tpu_custom_call" | custom-call | flops 2415919104 | bytes 3145728 | tf_op jit(solution)/shard_map/pallas_call | solution.py:169
  26.1 1.1 %shard_map.83 = (f32[256,256]{1,0:T(8,128)S(1)}, f32[256,128]{1,0:T(8,128)S(1)}) custom-call(f32[256,256]{1,0:T(8,128)S(1)} %collective-permute-done.1.refs_0_.refs_1_.x, f32[256,512]{1,0:T(8,128)S(1)} %get-tuple-element.46.x.refs_2_.refs_1_, f32[256,512]{1,0:T(8,128)S(1)} %collective-permute-done.4.after.refs_3_.refs_2_), custom_call_target="tpu_custom_call" | custom-call | flops 1207959552 | bytes 2097152 | tf_op jit(solution)/shard_map/pallas_call | solution.py:169
  27.1 2.0 %collective-permute-done.6.x.refs_4_ = f32[256,256]{1,0:T(8,128)S(1)} collective-permute-done((f32[256,256]{1,0:T(8,128)S(1)}, f32[256,256]{1,0:T(8,128)S(1)}, u32[]{:S(2)}, u32[]{:S(2)}) %collective-permute-start.6) | collective-permute-done | bytes 262176 | tf_op jit(solution)/shard_map/ppermute | solution.py:258
  29.2 0.4 collective-permute-start.7
  29.6 2.1 %shard_map.84 = (f32[256,256]{1,0:T(8,128)S(1)}, f32[256,128]{1,0:T(8,128)S(1)}, f32[256,256]{1,0:T(8,128)S(1)}, f32[256,128]{1,0:T(8,128)S(1)}, f32[256,256]{1,0:T(8,128)S(1)}, /*index=5*/f32[256,128]{1,0:T(8,128)S(1)}) custom-call(f32[256,256]{1,0:T(8,128)S(1)} %collective-permute-done.1.refs_0_.refs_1_.x, ...), custom_call_target="tpu_custom_call" | custom-call | flops 1811939328 | bytes 3670016 | tf_op jit(solution)/shard_map/pallas_call | solution.py:169
  31.7 1.4 %shard_map.88 = (f32[256,256]{1,0:T(8,128)S(1)}, f32[256,128]{1,0:T(8,128)S(1)}) custom-call(f32[256,256]{1,0:T(8,128)S(1)} %shard_map.87.refs_0_, f32[256,512]{1,0:T(8,128)S(1)} %get-tuple-element.46.x.refs_2_.refs_1_, f32[256,512]{1,0:T(8,128)S(1)} %collective-permute-done.4.after.refs_3_.refs_2_, f32[256,256]{1,0:T(8,128)S(1)} %collective-permute-done.3.x.refs_3_, ...), custom_call_target="tpu_custom_call" | custom-call | flops 1811939328 | bytes 2621440 | tf_op jit(solution)/shard_map/pallas_call | solution.py:169
  33.1 2.5 %collective-permute-done.7.refs_4_.refs_2_ = f32[256,256]{1,0:T(8,128)S(1)} collective-permute-done((f32[256,256]{1,0:T(8,128)S(1)}, f32[256,256]{1,0:T(8,128)S(1)}, u32[]{:S(2)}, u32[]{:S(2)}) %collective-permute-start.7) | collective-permute-done | bytes 262176 | tf_op jit(solution)/shard_map/ppermute | solution.py:258
  35.6 0.9 %shard_map.89 = (f32[136,256]{1,0:T(8,128)S(1)}, f32[136,256]{1,0:T(8,128)S(1)}) custom-call(f32[256,256]{1,0:T(8,128)S(1)} %collective-permute-done.9.x.refs_0_, f32[256,256]{1,0:T(8,128)S(1)} %collective-permute-done.5.refs_3_.refs_1_, f32[256,256]{1,0:T(8,128)S(1)} %collective-permute-done.7.refs_4_.refs_2_, f32[256,256]{1,0:T(8,128)S(1)} %get-tuple-element.61.refs_3_, ...), custom_call_target="tpu_custom_call" | custom-call | flops 603979776 | bytes 1572864 | tf_op jit(solution)/shard_map/pallas_call | solution.py:169
  36.5 0.8 %collective-permute-start.11 = (f32[136,256]{1,0:T(8,128)S(1)}, f32[136,256]{1,0:T(8,128)S(1)}, u32[]{:S(2)}, u32[]{:S(2)}) collective-permute-start(f32[136,256]{1,0:T(8,128)S(1)} %get-tuple-element.65), channel_id=1, source_target_pairs={{0,16},{1,17},{2,18},{3,19},{4,12},{5,13},{6,14},{7,15},{8,24},{9,... | collective-permute-start | bytes 417800 | tf_op jit(solution)/shard_map/ppermute | solution.py:258
  37.4 1.2 %collective-permute-start.10 = (f32[136,256]{1,0:T(8,128)S(1)}, f32[136,256]{1,0:T(8,128)S(1)}, u32[]{:S(2)}, u32[]{:S(2)}) collective-permute-start(f32[136,256]{1,0:T(8,128)S(1)} %get-tuple-element.63), channel_id=1, source_target_pairs={{0,17},{1,16},{2,19},{3,18},{4,14},{5,15},{6,12},{7,13},{8,25},{9,... | collective-permute-start | bytes 417800 | tf_op jit(solution)/shard_map/ppermute | solution.py:258
  38.6 2.2 %shard_map.85 = (f32[136,256]{1,0:T(8,128)S(1)}, f32[136,256]{1,0:T(8,128)S(1)}, f32[136,256]{1,0:T(8,128)S(1)}, f32[136,256]{1,0:T(8,128)S(1)}, f32[136,256]{1,0:T(8,128)S(1)}, /*index=5*/f32[136,256]{1,0:T(8,128)S(1)}) custom-call(f32[256,256]{1,0:T(8,128)S(1)} %get-tuple-element.44.refs_0_.refs_1_, ...), custom_call_target="tpu_custom_call" | custom-call | flops 1811939328 | bytes 3670016 | tf_op jit(solution)/shard_map/pallas_call | solution.py:169
  40.7 1.6 %collective-permute-start.8 = (f32[136,256]{1,0:T(8,128)S(1)}, f32[136,256]{1,0:T(8,128)S(1)}, u32[]{:S(2)}, u32[]{:S(2)}) collective-permute-start(f32[136,256]{1,0:T(8,128)S(1)} %get-tuple-element.60), channel_id=1, source_target_pairs={{0,1},{1,0},{2,3},{3,2},{4,6},{5,7},{6,4},{7,5},{8,9},{9,8},{10,11... | collective-permute-start | bytes 417800 | tf_op jit(solution)/shard_map/ppermute | solution.py:258
  42.3 0.8 %collective-permute-start.13 = (f32[136,256]{1,0:T(8,128)S(1)}, f32[136,256]{1,0:T(8,128)S(1)}, u32[]{:S(2)}, u32[]{:S(2)}) collective-permute-start(f32[136,256]{1,0:T(8,128)S(1)} %get-tuple-element.67), channel_id=1, source_target_pairs={{0,16},{1,17},{2,18},{3,19},{4,12},{5,13},{6,14},{7,15},{8,24},{9,... | collective-permute-start | bytes 417800 | tf_op jit(solution)/shard_map/ppermute | solution.py:258
  43.1 0.4 shard_map.90
  43.5 0.0 collective-permute-start.12
  43.5 2.5 %collective-permute-start.14 = (f32[136,256]{1,0:T(8,128)S(1)}, f32[136,256]{1,0:T(8,128)S(1)}, u32[]{:S(2)}, u32[]{:S(2)}) collective-permute-start(f32[136,256]{1,0:T(8,128)S(1)} %get-tuple-element.70), channel_id=1, source_target_pairs={{0,20},{1,21},{2,22},{3,23},{4,8},{5,9},{6,10},{7,11},{8,28},{9,29... | collective-permute-start | bytes 417800 | tf_op jit(solution)/shard_map/ppermute | solution.py:258
  46.0 0.7 %collective-permute-done.8.refs_0_ = f32[136,256]{1,0:T(8,128)S(1)} collective-permute-done((f32[136,256]{1,0:T(8,128)S(1)}, f32[136,256]{1,0:T(8,128)S(1)}, u32[]{:S(2)}, u32[]{:S(2)}) %collective-permute-start.8) | collective-permute-done | bytes 139296 | tf_op jit(solution)/shard_map/ppermute | solution.py:258
  46.7 3.6 %collective-permute-done.12.refs_2_ = f32[136,256]{1,0:T(8,128)S(1)} collective-permute-done((f32[136,256]{1,0:T(8,128)S(1)}, f32[136,256]{1,0:T(8,128)S(1)}, u32[]{:S(2)}, u32[]{:S(2)}) %collective-permute-start.12) | collective-permute-done | bytes 139296 | tf_op jit(solution)/shard_map/ppermute | solution.py:258
  50.3 1.5 %shard_map.92 = (f32[128,256]{1,0:T(8,128)}, f32[128,256]{1,0:T(8,128)}) custom-call(s32[1]{0:T(128)} %bitcast.core_ref, f32[136,256]{1,0:T(8,128)S(1)} %get-tuple-element.59.refs_0_, f32[136,256]{1,0:T(8,128)S(1)} %get-tuple-element.66.refs_1_, f32[136,256]{1,0:T(8,128)S(1)} %collective-permute-done.13.refs_2_, f32[136,256]{1,0:T(8,128)S(1)} %get-tuple-element.68.refs_3_, ...), custom_call_target="tpu_custom_call" | custom-call | tf_op jit(solution)/shard_map/pallas_call | solution.py:333
  (16 shorter events, 0.1 us)
Async XLA Ops:
  2.7 2.1 %collective-permute-start = (f32[128,768]{1,0:T(8,128)}, f32[128,768]{1,0:T(8,128)S(1)}, u32[]{:S(2)}, u32[]{:S(2)}) collective-permute-start(f32[128,768]{1,0:T(8,128)} %get-tuple-element.43), channel_id=1, source_target_pairs={{0,4},{1,5},{2,6},{3,7},{4,0},{5,1},{6,2},{7,3},{8,12},{9,13},{10,... | collective-permute-start | bytes 1179656 | tf_op jit(solution)/shard_map/ppermute | solution.py:258
  4.8 11.2 %collective-permute-start.4 = (f32[256,512]{1,0:T(8,128)S(1)}, f32[256,512]{1,0:T(8,128)S(1)}, u32[]{:S(2)}, u32[]{:S(2)}) collective-permute-start(f32[256,512]{1,0:T(8,128)S(1)} %get-tuple-element.46.x.refs_2_.refs_1_), channel_id=1, source_target_pairs={{0,8},{1,9},{2,10},{3,11},{4,20},{5,21},{6,22},{7,23},{8,0},{9,1},... | collective-permute-start | bytes 1572872 | tf_op jit(solution)/shard_map/ppermute | solution.py:258
  7.8 14.3 %collective-permute-start.1 = (f32[256,256]{1,0:T(8,128)S(1)}, f32[256,256]{1,0:T(8,128)S(1)}, u32[]{:S(2)}, u32[]{:S(2)}) collective-permute-start(f32[256,256]{1,0:T(8,128)S(1)} %get-tuple-element.44.refs_0_.refs_1_), channel_id=1, source_target_pairs={{0,1},{1,0},{2,3},{3,2},{4,6},{5,7},{6,4},{7,5},{8,9},{9,8},{10,11... | collective-permute-start | bytes 786440 | tf_op jit(solution)/shard_map/ppermute | solution.py:258
  9.3 13.4 %collective-permute-start.3 = (f32[256,256]{1,0:T(8,128)S(1)}, f32[256,256]{1,0:T(8,128)S(1)}, u32[]{:S(2)}, u32[]{:S(2)}) collective-permute-start(f32[256,256]{1,0:T(8,128)S(1)} %get-tuple-element.45), channel_id=1, source_target_pairs={{0,2},{1,3},{2,0},{3,1},{4,5},{5,4},{6,7},{7,6},{8,10},{9,11},{10,... | collective-permute-start | bytes 786440 | tf_op jit(solution)/shard_map/ppermute | solution.py:258
  11.9 12.3 %collective-permute-start.2 = (f32[256,256]{1,0:T(8,128)S(1)}, f32[256,256]{1,0:T(8,128)S(1)}, u32[]{:S(2)}, u32[]{:S(2)}) collective-permute-start(f32[256,256]{1,0:T(8,128)S(1)} %get-tuple-element.44.refs_0_.refs_1_), channel_id=1, source_target_pairs={{0,16},{1,17},{2,18},{3,19},{4,12},{5,13},{6,14},{7,15},{8,24},{9,... | collective-permute-start | bytes 786440 | tf_op jit(solution)/shard_map/ppermute | solution.py:258
  16.0 13.1 %collective-permute-start.6 = (f32[256,256]{1,0:T(8,128)S(1)}, f32[256,256]{1,0:T(8,128)S(1)}, u32[]{:S(2)}, u32[]{:S(2)}) collective-permute-start(f32[256,256]{1,0:T(8,128)S(1)} %shard_map.79.after), channel_id=1, source_target_pairs={{0,2},{1,3},{2,0},{3,1},{4,5},{5,4},{6,7},{7,6},{8,10},{9,11},{10,... | collective-permute-start | bytes 786440 | tf_op jit(solution)/shard_map/ppermute | solution.py:258
  22.1 9.6 %collective-permute-start.9 = (f32[256,256]{1,0:T(8,128)S(1)}, f32[256,256]{1,0:T(8,128)S(1)}, u32[]{:S(2)}, u32[]{:S(2)}) collective-permute-start(f32[256,256]{1,0:T(8,128)S(1)} %shard_map.86), channel_id=1, source_target_pairs={{0,16},{1,17},{2,18},{3,19},{4,12},{5,13},{6,14},{7,15},{8,24},{9,... | collective-permute-start | bytes 786440 | tf_op jit(solution)/shard_map/ppermute | solution.py:258
  22.8 10.3 %collective-permute-start.5 = (f32[256,256]{1,0:T(8,128)S(1)}, f32[256,256]{1,0:T(8,128)S(1)}, u32[]{:S(2)}, u32[]{:S(2)}) collective-permute-start(f32[256,256]{1,0:T(8,128)S(1)} %shard_map.80), channel_id=1, source_target_pairs={{0,8},{1,9},{2,10},{3,11},{4,20},{5,21},{6,22},{7,23},{8,0},{9,1},... | collective-permute-start | bytes 786440 | tf_op jit(solution)/shard_map/ppermute | solution.py:258
  29.2 6.4 %collective-permute-start.7 = (f32[256,256]{1,0:T(8,128)S(1)}, f32[256,256]{1,0:T(8,128)S(1)}, u32[]{:S(2)}, u32[]{:S(2)}) collective-permute-start(f32[256,256]{1,0:T(8,128)S(1)} %shard_map.82), channel_id=1, source_target_pairs={{0,8},{1,9},{2,10},{3,11},{4,20},{5,21},{6,22},{7,23},{8,0},{9,1},... | collective-permute-start | bytes 786440 | tf_op jit(solution)/shard_map/ppermute | solution.py:258
  36.5 6.6 %collective-permute-start.11 = (f32[136,256]{1,0:T(8,128)S(1)}, f32[136,256]{1,0:T(8,128)S(1)}, u32[]{:S(2)}, u32[]{:S(2)}) collective-permute-start(f32[136,256]{1,0:T(8,128)S(1)} %get-tuple-element.65), channel_id=1, source_target_pairs={{0,16},{1,17},{2,18},{3,19},{4,12},{5,13},{6,14},{7,15},{8,24},{9,... | collective-permute-start | bytes 417800 | tf_op jit(solution)/shard_map/ppermute | solution.py:258
  37.4 8.7 %collective-permute-start.10 = (f32[136,256]{1,0:T(8,128)S(1)}, f32[136,256]{1,0:T(8,128)S(1)}, u32[]{:S(2)}, u32[]{:S(2)}) collective-permute-start(f32[136,256]{1,0:T(8,128)S(1)} %get-tuple-element.63), channel_id=1, source_target_pairs={{0,17},{1,16},{2,19},{3,18},{4,14},{5,15},{6,12},{7,13},{8,25},{9,... | collective-permute-start | bytes 417800 | tf_op jit(solution)/shard_map/ppermute | solution.py:258
  40.7 5.9 %collective-permute-start.8 = (f32[136,256]{1,0:T(8,128)S(1)}, f32[136,256]{1,0:T(8,128)S(1)}, u32[]{:S(2)}, u32[]{:S(2)}) collective-permute-start(f32[136,256]{1,0:T(8,128)S(1)} %get-tuple-element.60), channel_id=1, source_target_pairs={{0,1},{1,0},{2,3},{3,2},{4,6},{5,7},{6,4},{7,5},{8,9},{9,8},{10,11... | collective-permute-start | bytes 417800 | tf_op jit(solution)/shard_map/ppermute | solution.py:258
  42.3 8.0 %collective-permute-start.13 = (f32[136,256]{1,0:T(8,128)S(1)}, f32[136,256]{1,0:T(8,128)S(1)}, u32[]{:S(2)}, u32[]{:S(2)}) collective-permute-start(f32[136,256]{1,0:T(8,128)S(1)} %get-tuple-element.67), channel_id=1, source_target_pairs={{0,16},{1,17},{2,18},{3,19},{4,12},{5,13},{6,14},{7,15},{8,24},{9,... | collective-permute-start | bytes 417800 | tf_op jit(solution)/shard_map/ppermute | solution.py:258
  43.5 6.8 %collective-permute-start.12 = (f32[136,256]{1,0:T(8,128)S(1)}, f32[136,256]{1,0:T(8,128)S(1)}, u32[]{:S(2)}, u32[]{:S(2)}) collective-permute-start(f32[136,256]{1,0:T(8,128)S(1)} %shard_map.90), channel_id=1, source_target_pairs={{0,5},{1,4},{2,7},{3,6},{4,2},{5,3},{6,0},{7,1},{8,13},{9,12},{10,... | collective-permute-start | bytes 417800 | tf_op jit(solution)/shard_map/ppermute | solution.py:258
  43.5 6.8 %collective-permute-start.14 = (f32[136,256]{1,0:T(8,128)S(1)}, f32[136,256]{1,0:T(8,128)S(1)}, u32[]{:S(2)}, u32[]{:S(2)}) collective-permute-start(f32[136,256]{1,0:T(8,128)S(1)} %get-tuple-element.70), channel_id=1, source_target_pairs={{0,20},{1,21},{2,22},{3,23},{4,8},{5,9},{6,10},{7,11},{8,28},{9,29... | collective-permute-start | bytes 417800 | tf_op jit(solution)/shard_map/ppermute | solution.py:258
  46.0 4.3 %collective-permute-start.15 = (f32[136,256]{1,0:T(8,128)S(1)}, f32[136,256]{1,0:T(8,128)S(1)}, u32[]{:S(2)}, u32[]{:S(2)}) collective-permute-start(f32[136,256]{1,0:T(8,128)S(1)} %get-tuple-element.71), channel_id=1, source_target_pairs={{0,4},{1,5},{2,6},{3,7},{4,0},{5,1},{6,2},{7,3},{8,12},{9,13},{10,... | collective-permute-start | bytes 417800 | tf_op jit(solution)/shard_map/ppermute | solution.py:258

commit v12 on v7

--- a/solution.py
+++ b/solution.py
@@ -253,8 +253,8 @@
     low = n_kv.bit_length() - 1
     far = [1 << i for i in range(low)]
     near = [1 << (low + i) for i in range(1, n_pb.bit_length() - 1)]
-    one = far[0::2] + near[1::2]
-    two = far[1::2] + near[0::2]
+    one = far[0::2] + near[0::2]
+    two = far[1::2] + near[1::2]
     return ((one, two), (two, one)) if len(one) == len(two) else ((one, one), (two, two))
 
 

time: 52.1 us -> 52.1 us (level)
  no operation moved by 1% of the time
where the time goes in v12:
time: 52.1 us; the launch traced here: 51.9 us
  starting transfers between devices  25.2 us (48%)
  Pallas kernels  13.6 us (26%)
  waiting for transfers between devices  12.4 us (24%)
  between operations  0.77 us (1%)
    ppermute x17, starting transfers between devices, swap(): lax.ppermute(x, AXES, [(i, i ^ flip ^ masks[i // n_kv % 2]) for i in rang...  25.2 us
    ppermute x17, waiting for transfers between devices, swap(): lax.ppermute(x, AXES, [(i, i ^ flip ^ masks[i // n_kv % 2]) for i in rang...  12.4 us
    pallas_call x6, Pallas kernels, attend(): pl.pallas_call(functools.partial(attend_kernel, n_q, n_k, rows, bool(prev...  9.38 us
    pallas_call x1, Pallas kernels, per_device(): pl.pallas_call(pack_kernel, out_shape=[f32(rows, w * DH) for w in (1, 1,...  2.02 us
    pallas_call x1, Pallas kernels, per_device(): pl.pallas_call(functools.partial(finish_kernel, n_q, counts), out_shape=[...  1.51 us
  transfers between devices with their start and end apart: 17, of which 7 were waited for; matrix products, arithmetic and copies ran while one was open for 0% of the time, Pallas kernels for 17%

profile of v12, /device:TPU:0, one launch (start us, length us, event | category | flops | bytes accessed | tf_op | source)
XLA Modules:
  0.0 51.9 jit_solution(2097580987554248719)
XLA Ops:
  0.6 2.0 %shard_map.77 = (f32[128,128]{1,0:T(8,128)S(1)}, f32[128,128]{1,0:T(8,128)S(1)}, f32[128,128]{1,0:T(8,128)S(1)}, f32[128,128]{1,0:T(8,128)S(1)}, f32[128,128]{1,...) custom-call(f32[128,256]{1,0:T(8,128)} %refs_0_.1, f32[128,256]{1,0:T(8,128)} %refs_1_.1, f32[128,256]{1,0:T(8,128)} %refs_2_.1, ...), custom_call_target="tpu_custom_call" | custom-call | tf_op jit(solution)/shard_map/pallas_call | solution.py:276
  2.7 0.5 collective-permute-start
  3.2 1.6 %collective-permute-done.refs_6_ = f32[128,768]{1,0:T(8,128)S(1)} collective-permute-done((f32[128,768]{1,0:T(8,128)}, f32[128,768]{1,0:T(8,128)S(1)}, u32[]{:S(2)}, u32[]{:S(2)}) %collective-permute-start) | collective-permute-done | bytes 393248 | tf_op jit(solution)/shard_map/ppermute | solution.py:269
  4.7 0.1 shard_map.78
  4.8 3.0 %collective-permute-start.4 = (f32[256,512]{1,0:T(8,128)S(1)}, f32[256,512]{1,0:T(8,128)S(1)}, u32[]{:S(2)}, u32[]{:S(2)}) collective-permute-start(f32[256,512]{1,0:T(8,128)S(1)} %get-tuple-element.48.x.refs_2_.refs_1_), channel_id=1, source_target_pairs={{0,16},{1,17},{2,18},{3,19},{4,12},{5,13},{6,14},{7,15},{8,24},{9,... | collective-permute-start | bytes 1572872 | tf_op jit(solution)/shard_map/ppermute | solution.py:269
  7.8 1.6 %collective-permute-start.1 = (f32[256,256]{1,0:T(8,128)S(1)}, f32[256,256]{1,0:T(8,128)S(1)}, u32[]{:S(2)}, u32[]{:S(2)}) collective-permute-start(f32[256,256]{1,0:T(8,128)S(1)} %get-tuple-element.46.refs_0_.refs_1_), channel_id=1, source_target_pairs={{0,1},{1,0},{2,3},{3,2},{4,6},{5,7},{6,4},{7,5},{8,9},{9,8},{10,11... | collective-permute-start | bytes 786440 | tf_op jit(solution)/shard_map/ppermute | solution.py:269
  9.4 2.6 %collective-permute-start.3 = (f32[256,256]{1,0:T(8,128)S(1)}, f32[256,256]{1,0:T(8,128)S(1)}, u32[]{:S(2)}, u32[]{:S(2)}) collective-permute-start(f32[256,256]{1,0:T(8,128)S(1)} %get-tuple-element.47), channel_id=1, source_target_pairs={{0,2},{1,3},{2,0},{3,1},{4,5},{5,4},{6,7},{7,6},{8,10},{9,11},{10,... | collective-permute-start | bytes 786440 | tf_op jit(solution)/shard_map/ppermute | solution.py:269
  12.0 1.5 %collective-permute-start.2 = (f32[256,256]{1,0:T(8,128)S(1)}, f32[256,256]{1,0:T(8,128)S(1)}, u32[]{:S(2)}, u32[]{:S(2)}) collective-permute-start(f32[256,256]{1,0:T(8,128)S(1)} %get-tuple-element.46.refs_0_.refs_1_), channel_id=1, source_target_pairs={{0,8},{1,9},{2,10},{3,11},{4,20},{5,21},{6,22},{7,23},{8,0},{9,1},... | collective-permute-start | bytes 786440 | tf_op jit(solution)/shard_map/ppermute | solution.py:269
  13.4 2.6 %collective-permute-done.4.after.refs_3_.refs_2_ = f32[256,512]{1,0:T(8,128)S(1)} collective-permute-done((f32[256,512]{1,0:T(8,128)S(1)}, f32[256,512]{1,0:T(8,128)S(1)}, u32[]{:S(2)}, u32[]{:S(2)}) %collective-permute-start.4) | collective-permute-done | bytes 524320 | tf_op jit(solution)/shard_map/ppermute | solution.py:269
  16.1 4.9 %collective-permute-start.6 = (f32[256,256]{1,0:T(8,128)S(1)}, f32[256,256]{1,0:T(8,128)S(1)}, u32[]{:S(2)}, u32[]{:S(2)}) collective-permute-start(f32[256,256]{1,0:T(8,128)S(1)} %shard_map.79.after), channel_id=1, source_target_pairs={{0,2},{1,3},{2,0},{3,1},{4,5},{5,4},{6,7},{7,6},{8,10},{9,11},{10,... | collective-permute-start | bytes 786440 | tf_op jit(solution)/shard_map/ppermute | solution.py:269
  20.9 1.1 %collective-permute-done.1.refs_0_.refs_1_.x = f32[256,256]{1,0:T(8,128)S(1)} collective-permute-done((f32[256,256]{1,0:T(8,128)S(1)}, f32[256,256]{1,0:T(8,128)S(1)}, u32[]{:S(2)}, u32[]{:S(2)}) %collective-permute-start.1) | collective-permute-done | bytes 262176 | tf_op jit(solution)/shard_map/ppermute | solution.py:269
  22.1 0.7 %collective-permute-start.10 = (f32[256,256]{1,0:T(8,128)S(1)}, f32[256,256]{1,0:T(8,128)S(1)}, u32[]{:S(2)}, u32[]{:S(2)}) collective-permute-start(f32[256,256]{1,0:T(8,128)S(1)} %shard_map.86), channel_id=1, source_target_pairs={{0,8},{1,9},{2,10},{3,11},{4,20},{5,21},{6,22},{7,23},{8,0},{9,1},... | collective-permute-start | bytes 786440 | tf_op jit(solution)/shard_map/ppermute | solution.py:269
  22.8 1.5 %collective-permute-start.5 = (f32[256,256]{1,0:T(8,128)S(1)}, f32[256,256]{1,0:T(8,128)S(1)}, u32[]{:S(2)}, u32[]{:S(2)}) collective-permute-start(f32[256,256]{1,0:T(8,128)S(1)} %shard_map.80), channel_id=1, source_target_pairs={{0,16},{1,17},{2,18},{3,19},{4,12},{5,13},{6,14},{7,15},{8,24},{9,... | collective-permute-start | bytes 786440 | tf_op jit(solution)/shard_map/ppermute | solution.py:269
  24.3 1.8 %shard_map.81 = (f32[256,256]{1,0:T(8,128)S(1)}, f32[256,128]{1,0:T(8,128)S(1)}, f32[256,256]{1,0:T(8,128)S(1)}, f32[256,128]{1,0:T(8,128)S(1)}) custom-call(f32[256,256]{1,0:T(8,128)S(1)} %get-tuple-element.46.refs_0_.refs_1_, f32[256,256]{1,0:T(8,128)S(1)} %collective-permute-done.2.refs_1_.refs_2_, f32[256,512]{1,0:T(8,128)S(1)} %get-tuple-element.48.x.refs_2_.refs_1_, ...), custom_call_target="tpu_custom_call" | custom-call | flops 2415919104 | bytes 3145728 | tf_op jit(solution)/shard_map/pallas_call | solution.py:180
  26.1 1.0 %shard_map.83 = (f32[256,256]{1,0:T(8,128)S(1)}, f32[256,128]{1,0:T(8,128)S(1)}) custom-call(f32[256,256]{1,0:T(8,128)S(1)} %collective-permute-done.1.refs_0_.refs_1_.x, f32[256,512]{1,0:T(8,128)S(1)} %get-tuple-element.48.x.refs_2_.refs_1_, f32[256,512]{1,0:T(8,128)S(1)} %collective-permute-done.4.after.refs_3_.refs_2_), custom_call_target="tpu_custom_call" | custom-call | flops 1207959552 | bytes 2097152 | tf_op jit(solution)/shard_map/pallas_call | solution.py:180
  27.1 2.0 %collective-permute-done.6.x.refs_4_ = f32[256,256]{1,0:T(8,128)S(1)} collective-permute-done((f32[256,256]{1,0:T(8,128)S(1)}, f32[256,256]{1,0:T(8,128)S(1)}, u32[]{:S(2)}, u32[]{:S(2)}) %collective-permute-start.6) | collective-permute-done | bytes 262176 | tf_op jit(solution)/shard_map/ppermute | solution.py:269
  29.2 0.3 collective-permute-start.7
  29.5 1.8 %collective-permute-start.8 = (f32[256,128]{1,0:T(8,128)S(1)}, f32[256,128]{1,0:T(8,128)S(1)}, u32[]{:S(2)}, u32[]{:S(2)}) collective-permute-start(f32[256,128]{1,0:T(8,128)S(1)} %get-tuple-element.51), channel_id=1, source_target_pairs={{0,16},{1,17},{2,18},{3,19},{4,12},{5,13},{6,14},{7,15},{8,24},{9,... | collective-permute-start | bytes 393224 | tf_op jit(solution)/shard_map/ppermute | solution.py:269
  31.3 2.1 %shard_map.84 = (f32[256,256]{1,0:T(8,128)S(1)}, f32[256,128]{1,0:T(8,128)S(1)}, f32[256,256]{1,0:T(8,128)S(1)}, f32[256,128]{1,0:T(8,128)S(1)}, f32[256,256]{1,0:T(8,128)S(1)}, /*index=5*/f32[256,128]{1,0:T(8,128)S(1)}) custom-call(f32[256,256]{1,0:T(8,128)S(1)} %collective-permute-done.1.refs_0_.refs_1_.x, ...), custom_call_target="tpu_custom_call" | custom-call | flops 1811939328 | bytes 3670016 | tf_op jit(solution)/shard_map/pallas_call | solution.py:180
  33.4 1.4 %shard_map.88 = (f32[256,256]{1,0:T(8,128)S(1)}, f32[256,128]{1,0:T(8,128)S(1)}) custom-call(f32[256,256]{1,0:T(8,128)S(1)} %shard_map.87.refs_0_, f32[256,512]{1,0:T(8,128)S(1)} %get-tuple-element.48.x.refs_2_.refs_1_, f32[256,512]{1,0:T(8,128)S(1)} %collective-permute-done.4.after.refs_3_.refs_2_, f32[256,256]{1,0:T(8,128)S(1)} %collective-permute-done.3.x.refs_3_, ...), custom_call_target="tpu_custom_call" | custom-call | flops 1811939328 | bytes 2621440 | tf_op jit(solution)/shard_map/pallas_call | solution.py:180
  34.9 0.8 %collective-permute-done.8.refs_5_.refs_3_ = f32[256,128]{1,0:T(8,128)S(1)} collective-permute-done((f32[256,128]{1,0:T(8,128)S(1)}, f32[256,128]{1,0:T(8,128)S(1)}, u32[]{:S(2)}, u32[]{:S(2)}) %collective-permute-start.8) | collective-permute-done | bytes 131104 | tf_op jit(solution)/shard_map/ppermute | solution.py:269
  35.6 0.9 %shard_map.89 = (f32[136,256]{1,0:T(8,128)S(1)}, f32[136,256]{1,0:T(8,128)S(1)}) custom-call(f32[256,256]{1,0:T(8,128)S(1)} %collective-permute-done.10.x.refs_0_, f32[256,256]{1,0:T(8,128)S(1)} %collective-permute-done.5.refs_3_.refs_1_, f32[256,128]{1,0:T(8,128)S(1)} %collective-permute-done.7.refs_4_.refs_2_, ...), custom_call_target="tpu_custom_call" | custom-call | flops 603979776 | bytes 1572864 | tf_op jit(solution)/shard_map/pallas_call | solution.py:180
  36.5 0.8 %collective-permute-start.12 = (f32[136,256]{1,0:T(8,128)S(1)}, f32[136,256]{1,0:T(8,128)S(1)}, u32[]{:S(2)}, u32[]{:S(2)}) collective-permute-start(f32[136,256]{1,0:T(8,128)S(1)} %get-tuple-element.69), channel_id=1, source_target_pairs={{0,8},{1,9},{2,10},{3,11},{4,20},{5,21},{6,22},{7,23},{8,0},{9,1},... | collective-permute-start | bytes 417800 | tf_op jit(solution)/shard_map/ppermute | solution.py:269
  37.4 1.2 %collective-permute-start.11 = (f32[136,256]{1,0:T(8,128)S(1)}, f32[136,256]{1,0:T(8,128)S(1)}, u32[]{:S(2)}, u32[]{:S(2)}) collective-permute-start(f32[136,256]{1,0:T(8,128)S(1)} %get-tuple-element.67), channel_id=1, source_target_pairs={{0,9},{1,8},{2,11},{3,10},{4,22},{5,23},{6,20},{7,21},{8,1},{9,0},... | collective-permute-start | bytes 417800 | tf_op jit(solution)/shard_map/ppermute | solution.py:269
  38.6 2.2 %shard_map.85 = (f32[136,256]{1,0:T(8,128)S(1)}, f32[136,256]{1,0:T(8,128)S(1)}, f32[136,256]{1,0:T(8,128)S(1)}, f32[136,256]{1,0:T(8,128)S(1)}, f32[136,256]{1,0:T(8,128)S(1)}, /*index=5*/f32[136,256]{1,0:T(8,128)S(1)}) custom-call(f32[256,256]{1,0:T(8,128)S(1)} %get-tuple-element.46.refs_0_.refs_1_, ...), custom_call_target="tpu_custom_call" | custom-call | flops 1811939328 | bytes 3670016 | tf_op jit(solution)/shard_map/pallas_call | solution.py:180
  40.7 1.6 %collective-permute-start.9 = (f32[136,256]{1,0:T(8,128)S(1)}, f32[136,256]{1,0:T(8,128)S(1)}, u32[]{:S(2)}, u32[]{:S(2)}) collective-permute-start(f32[136,256]{1,0:T(8,128)S(1)} %get-tuple-element.64), channel_id=1, source_target_pairs={{0,1},{1,0},{2,3},{3,2},{4,6},{5,7},{6,4},{7,5},{8,9},{9,8},{10,11... | collective-permute-start | bytes 417800 | tf_op jit(solution)/shard_map/ppermute | solution.py:269
  42.3 0.8 %collective-permute-start.14 = (f32[136,256]{1,0:T(8,128)S(1)}, f32[136,256]{1,0:T(8,128)S(1)}, u32[]{:S(2)}, u32[]{:S(2)}) collective-permute-start(f32[136,256]{1,0:T(8,128)S(1)} %get-tuple-element.71), channel_id=1, source_target_pairs={{0,8},{1,9},{2,10},{3,11},{4,20},{5,21},{6,22},{7,23},{8,0},{9,1},... | collective-permute-start | bytes 417800 | tf_op jit(solution)/shard_map/ppermute | solution.py:269
  43.1 0.4 shard_map.90
  43.5 2.5 %collective-permute-start.15 = (f32[136,256]{1,0:T(8,128)S(1)}, f32[136,256]{1,0:T(8,128)S(1)}, u32[]{:S(2)}, u32[]{:S(2)}) collective-permute-start(f32[136,256]{1,0:T(8,128)S(1)} %get-tuple-element.74), channel_id=1, source_target_pairs={{0,12},{1,13},{2,14},{3,15},{4,16},{5,17},{6,18},{7,19},{8,4},{9,5... | collective-permute-start | bytes 417800 | tf_op jit(solution)/shard_map/ppermute | solution.py:269
  46.1 0.6 %collective-permute-done.9.refs_0_ = f32[136,256]{1,0:T(8,128)S(1)} collective-permute-done((f32[136,256]{1,0:T(8,128)S(1)}, f32[136,256]{1,0:T(8,128)S(1)}, u32[]{:S(2)}, u32[]{:S(2)}) %collective-permute-start.9) | collective-permute-done | bytes 139296 | tf_op jit(solution)/shard_map/ppermute | solution.py:269
  46.6 3.7 %collective-permute-done.13.refs_2_ = f32[136,256]{1,0:T(8,128)S(1)} collective-permute-done((f32[136,256]{1,0:T(8,128)S(1)}, f32[136,256]{1,0:T(8,128)S(1)}, u32[]{:S(2)}, u32[]{:S(2)}) %collective-permute-start.13) | collective-permute-done | bytes 139296 | tf_op jit(solution)/shard_map/ppermute | solution.py:269
  50.4 1.5 %shard_map.92 = (f32[128,256]{1,0:T(8,128)}, f32[128,256]{1,0:T(8,128)}) custom-call(s32[1]{0:T(128)} %bitcast.core_ref, f32[136,256]{1,0:T(8,128)S(1)} %get-tuple-element.63.refs_0_, f32[136,256]{1,0:T(8,128)S(1)} %get-tuple-element.70.refs_1_, f32[136,256]{1,0:T(8,128)S(1)} %collective-permute-done.14.refs_2_, f32[136,256]{1,0:T(8,128)S(1)} %get-tuple-element.72.refs_3_, ...), custom_call_target="tpu_custom_call" | custom-call | tf_op jit(solution)/shard_map/pallas_call | solution.py:344
  (18 shorter events, 0.2 us)
Async XLA Ops:
  2.7 2.1 %collective-permute-start = (f32[128,768]{1,0:T(8,128)}, f32[128,768]{1,0:T(8,128)S(1)}, u32[]{:S(2)}, u32[]{:S(2)}) collective-permute-start(f32[128,768]{1,0:T(8,128)} %get-tuple-element.45), channel_id=1, source_target_pairs={{0,4},{1,5},{2,6},{3,7},{4,0},{5,1},{6,2},{7,3},{8,12},{9,13},{10,... | collective-permute-start | bytes 1179656 | tf_op jit(solution)/shard_map/ppermute | solution.py:269
  4.8 11.2 %collective-permute-start.4 = (f32[256,512]{1,0:T(8,128)S(1)}, f32[256,512]{1,0:T(8,128)S(1)}, u32[]{:S(2)}, u32[]{:S(2)}) collective-permute-start(f32[256,512]{1,0:T(8,128)S(1)} %get-tuple-element.48.x.refs_2_.refs_1_), channel_id=1, source_target_pairs={{0,16},{1,17},{2,18},{3,19},{4,12},{5,13},{6,14},{7,15},{8,24},{9,... | collective-permute-start | bytes 1572872 | tf_op jit(solution)/shard_map/ppermute | solution.py:269
  7.8 14.3 %collective-permute-start.1 = (f32[256,256]{1,0:T(8,128)S(1)}, f32[256,256]{1,0:T(8,128)S(1)}, u32[]{:S(2)}, u32[]{:S(2)}) collective-permute-start(f32[256,256]{1,0:T(8,128)S(1)} %get-tuple-element.46.refs_0_.refs_1_), channel_id=1, source_target_pairs={{0,1},{1,0},{2,3},{3,2},{4,6},{5,7},{6,4},{7,5},{8,9},{9,8},{10,11... | collective-permute-start | bytes 786440 | tf_op jit(solution)/shard_map/ppermute | solution.py:269
  9.4 13.4 %collective-permute-start.3 = (f32[256,256]{1,0:T(8,128)S(1)}, f32[256,256]{1,0:T(8,128)S(1)}, u32[]{:S(2)}, u32[]{:S(2)}) collective-permute-start(f32[256,256]{1,0:T(8,128)S(1)} %get-tuple-element.47), channel_id=1, source_target_pairs={{0,2},{1,3},{2,0},{3,1},{4,5},{5,4},{6,7},{7,6},{8,10},{9,11},{10,... | collective-permute-start | bytes 786440 | tf_op jit(solution)/shard_map/ppermute | solution.py:269
  12.0 12.3 %collective-permute-start.2 = (f32[256,256]{1,0:T(8,128)S(1)}, f32[256,256]{1,0:T(8,128)S(1)}, u32[]{:S(2)}, u32[]{:S(2)}) collective-permute-start(f32[256,256]{1,0:T(8,128)S(1)} %get-tuple-element.46.refs_0_.refs_1_), channel_id=1, source_target_pairs={{0,8},{1,9},{2,10},{3,11},{4,20},{5,21},{6,22},{7,23},{8,0},{9,1},... | collective-permute-start | bytes 786440 | tf_op jit(solution)/shard_map/ppermute | solution.py:269
  16.1 13.1 %collective-permute-start.6 = (f32[256,256]{1,0:T(8,128)S(1)}, f32[256,256]{1,0:T(8,128)S(1)}, u32[]{:S(2)}, u32[]{:S(2)}) collective-permute-start(f32[256,256]{1,0:T(8,128)S(1)} %shard_map.79.after), channel_id=1, source_target_pairs={{0,2},{1,3},{2,0},{3,1},{4,5},{5,4},{6,7},{7,6},{8,10},{9,11},{10,... | collective-permute-start | bytes 786440 | tf_op jit(solution)/shard_map/ppermute | solution.py:269
  22.1 11.3 %collective-permute-start.10 = (f32[256,256]{1,0:T(8,128)S(1)}, f32[256,256]{1,0:T(8,128)S(1)}, u32[]{:S(2)}, u32[]{:S(2)}) collective-permute-start(f32[256,256]{1,0:T(8,128)S(1)} %shard_map.86), channel_id=1, source_target_pairs={{0,8},{1,9},{2,10},{3,11},{4,20},{5,21},{6,22},{7,23},{8,0},{9,1},... | collective-permute-start | bytes 786440 | tf_op jit(solution)/shard_map/ppermute | solution.py:269
  22.8 12.0 %collective-permute-start.5 = (f32[256,256]{1,0:T(8,128)S(1)}, f32[256,256]{1,0:T(8,128)S(1)}, u32[]{:S(2)}, u32[]{:S(2)}) collective-permute-start(f32[256,256]{1,0:T(8,128)S(1)} %shard_map.80), channel_id=1, source_target_pairs={{0,16},{1,17},{2,18},{3,19},{4,12},{5,13},{6,14},{7,15},{8,24},{9,... | collective-permute-start | bytes 786440 | tf_op jit(solution)/shard_map/ppermute | solution.py:269
  29.2 5.6 %collective-permute-start.7 = (f32[256,128]{1,0:T(8,128)S(1)}, f32[256,128]{1,0:T(8,128)S(1)}, u32[]{:S(2)}, u32[]{:S(2)}) collective-permute-start(f32[256,128]{1,0:T(8,128)S(1)} %get-tuple-element.50), channel_id=1, source_target_pairs={{0,16},{1,17},{2,18},{3,19},{4,12},{5,13},{6,14},{7,15},{8,24},{9,... | collective-permute-start | bytes 393224 | tf_op jit(solution)/shard_map/ppermute | solution.py:269
  29.5 6.1 %collective-permute-start.8 = (f32[256,128]{1,0:T(8,128)S(1)}, f32[256,128]{1,0:T(8,128)S(1)}, u32[]{:S(2)}, u32[]{:S(2)}) collective-permute-start(f32[256,128]{1,0:T(8,128)S(1)} %get-tuple-element.51), channel_id=1, source_target_pairs={{0,16},{1,17},{2,18},{3,19},{4,12},{5,13},{6,14},{7,15},{8,24},{9,... | collective-permute-start | bytes 393224 | tf_op jit(solution)/shard_map/ppermute | solution.py:269
  36.5 6.5 %collective-permute-start.12 = (f32[136,256]{1,0:T(8,128)S(1)}, f32[136,256]{1,0:T(8,128)S(1)}, u32[]{:S(2)}, u32[]{:S(2)}) collective-permute-start(f32[136,256]{1,0:T(8,128)S(1)} %get-tuple-element.69), channel_id=1, source_target_pairs={{0,8},{1,9},{2,10},{3,11},{4,20},{5,21},{6,22},{7,23},{8,0},{9,1},... | collective-permute-start | bytes 417800 | tf_op jit(solution)/shard_map/ppermute | solution.py:269
  37.4 8.7 %collective-permute-start.11 = (f32[136,256]{1,0:T(8,128)S(1)}, f32[136,256]{1,0:T(8,128)S(1)}, u32[]{:S(2)}, u32[]{:S(2)}) collective-permute-start(f32[136,256]{1,0:T(8,128)S(1)} %get-tuple-element.67), channel_id=1, source_target_pairs={{0,9},{1,8},{2,11},{3,10},{4,22},{5,23},{6,20},{7,21},{8,1},{9,0},... | collective-permute-start | bytes 417800 | tf_op jit(solution)/shard_map/ppermute | solution.py:269
  40.7 5.9 %collective-permute-start.9 = (f32[136,256]{1,0:T(8,128)S(1)}, f32[136,256]{1,0:T(8,128)S(1)}, u32[]{:S(2)}, u32[]{:S(2)}) collective-permute-start(f32[136,256]{1,0:T(8,128)S(1)} %get-tuple-element.64), channel_id=1, source_target_pairs={{0,1},{1,0},{2,3},{3,2},{4,6},{5,7},{6,4},{7,5},{8,9},{9,8},{10,11... | collective-permute-start | bytes 417800 | tf_op jit(solution)/shard_map/ppermute | solution.py:269
  42.3 8.1 %collective-permute-start.14 = (f32[136,256]{1,0:T(8,128)S(1)}, f32[136,256]{1,0:T(8,128)S(1)}, u32[]{:S(2)}, u32[]{:S(2)}) collective-permute-start(f32[136,256]{1,0:T(8,128)S(1)} %get-tuple-element.71), channel_id=1, source_target_pairs={{0,8},{1,9},{2,10},{3,11},{4,20},{5,21},{6,22},{7,23},{8,0},{9,1},... | collective-permute-start | bytes 417800 | tf_op jit(solution)/shard_map/ppermute | solution.py:269
  43.5 6.9 %collective-permute-start.13 = (f32[136,256]{1,0:T(8,128)S(1)}, f32[136,256]{1,0:T(8,128)S(1)}, u32[]{:S(2)}, u32[]{:S(2)}) collective-permute-start(f32[136,256]{1,0:T(8,128)S(1)} %shard_map.90), channel_id=1, source_target_pairs={{0,5},{1,4},{2,7},{3,6},{4,2},{5,3},{6,0},{7,1},{8,13},{9,12},{10,... | collective-permute-start | bytes 417800 | tf_op jit(solution)/shard_map/ppermute | solution.py:269
  43.5 6.9 %collective-permute-start.15 = (f32[136,256]{1,0:T(8,128)S(1)}, f32[136,256]{1,0:T(8,128)S(1)}, u32[]{:S(2)}, u32[]{:S(2)}) collective-permute-start(f32[136,256]{1,0:T(8,128)S(1)} %get-tuple-element.74), channel_id=1, source_target_pairs={{0,12},{1,13},{2,14},{3,15},{4,16},{5,17},{6,18},{7,19},{8,4},{9,5... | collective-permute-start | bytes 417800 | tf_op jit(solution)/shard_map/ppermute | solution.py:269
  46.1 4.3 %collective-permute-start.16 = (f32[136,256]{1,0:T(8,128)S(1)}, f32[136,256]{1,0:T(8,128)S(1)}, u32[]{:S(2)}, u32[]{:S(2)}) collective-permute-start(f32[136,256]{1,0:T(8,128)S(1)} %get-tuple-element.75), channel_id=1, source_target_pairs={{0,4},{1,5},{2,6},{3,7},{4,0},{5,1},{6,2},{7,3},{8,12},{9,13},{10,... | collective-permute-start | bytes 417800 | tf_op jit(solution)/shard_map/ppermute | solution.py:269
